TPU v7x, 32 devices: a whole 2x2x4 slice. The times are simulated.
32 devices in a mesh: groups: 2 (over y), dp: 4 (over z), layer: 2 (over x), sub: 2 (over core).
Axes of the slice: x: 2, y: 2, z: 4, core: 2. Of those that a mesh axis runs over, the one named last changes fastest.
Arguments:
- acts: bfloat16 [2, 2048, 4096], P('layer', ('groups', 'dp')), parts along dimension 1, may hold values from -6 to 6
- kv_grad: bfloat16 [2, 2048, 2048], P('layer', ('groups', 'dp'), 'sub'), parts along dimension 1, may hold values from -6 to 6
- kv_weight: bfloat16 [2, 4096, 2048], P('layer', 'dp', 'sub'), may hold values from -0.125 to 0.125
- proj_in: bfloat16 [4096, 64], replicated, may hold values from -0.09375 to 0.09375
- proj_out: bfloat16 [4096, 64], replicated, may hold values from -0.09375 to 0.09375
- codebook: bfloat16 [512, 256, 8], P('sub'), may hold values from -5 to 5
- codes: int32 [2048, 2, 512], P(('groups', 'dp'), 'layer', 'sub'), parts along dimension 0, may hold values from 0 to 255
- counts: int32 [8], P(('groups', 'dp')), parts along dimension 0, may hold values from 1 to 256, 512 in all
Outputs:
- scores: float32 [2048, 16], P(('groups', 'dp')), parts along dimension 0
There are 2 independent parts, one for each index of `groups`. A program takes and returns all parts, laid end to end along the dimension named above; an argument that names none is the same for every part. Nothing has to cross between parts.
Inputs may be any that keep to these rules, and one draw needn't show every extreme that they name: `counts`: one block of 256 slots is full in every draw.
All inputs are finite; a program needn't handle non-finite values.
Results may differ from a plain program's by a relative error of at most 0.003.
Values may be sent and summed in bfloat16 or wider, within the bound.
No kernel may reach another device: no remote copies, remote signals or barrier semaphores. Data moves between devices by JAX's collectives and lax.ppermute only.
A program may use at most 128 MiB of HBM per device.

v0:
```python
import jax
import jax.numpy as jnp
from jax import lax
from jax.sharding import PartitionSpec as P

SEQ = 64


def make_tables(vectors, book_f, sub_first, sub_local, sub_width):
    own_part = lax.dynamic_slice_in_dim(vectors, sub_first, sub_local * sub_width, 1)
    shaped = own_part.reshape(vectors.shape[0], sub_local, sub_width)
    return jnp.einsum("emd,mkd->emk", shaped, book_f, precision=lax.Precision.HIGHEST).astype(
        jnp.bfloat16
    )


def per_device(acts, kv_grad, kv_weight, proj_in, proj_out, codebook, codes, counts):
    lay_local, tok_local, model_width = acts.shape
    rank_dim = proj_in.shape[1]
    sub_local, code_count, sub_width = codebook.shape
    train_local = codes.shape[0]
    tests_local = tok_local // SEQ
    tests_all = tests_local * lax.axis_size("dp")
    sub_first = lax.axis_index("sub") * (sub_local * sub_width)
    book_f = codebook.astype(jnp.float32)
    out_f = proj_out.astype(jnp.float32)
    step_width = min(16, sub_local)
    live_rows = jnp.arange(train_local, dtype=jnp.int32) < counts[0]
    grad_part = kv_grad[0]
    input_grad = lax.dot_general(
        grad_part,
        lax.all_gather(kv_weight[0], "dp", axis=0, tiled=True),
        (((1,), (1,)), ((), ())),
        preferred_element_type=jnp.float32,
    )
    out_side = jnp.dot(input_grad, out_f, precision=lax.Precision.HIGHEST)
    out_side = lax.psum(out_side, "sub")
    in_side = jnp.dot(acts[0], proj_in, preferred_element_type=jnp.float32)
    grads = jnp.einsum(
        "esi,esj->eij",
        in_side.reshape(tests_local, SEQ, rank_dim),
        out_side.reshape(tests_local, SEQ, rank_dim),
        precision=lax.Precision.HIGHEST,
    ).reshape(tests_local, rank_dim * rank_dim)
    vectors = grads * lax.rsqrt(jnp.mean(grads * grads, axis=1, keepdims=True) + 1e-06) / rank_dim
    own_tables = make_tables(vectors, book_f, sub_first, sub_local, sub_width)
    all_tables = lax.all_gather(own_tables, "dp", axis=0, tiled=True)
    table_t = jnp.transpose(all_tables, (1, 2, 0)).reshape(sub_local * code_count, tests_all)
    code_layer = codes[:, 0, :]
    centroid_ids = jnp.arange(code_count, dtype=jnp.int32)

    def score_block(step_idx, running):
        first = step_idx * step_width
        code_block = lax.dynamic_slice_in_dim(code_layer, first, step_width, 1)
        one_hot = (code_block[:, :, None] == centroid_ids[None, None, :]).astype(jnp.bfloat16)
        one_hot = one_hot.reshape(train_local, step_width * code_count)
        table_rows = lax.dynamic_slice_in_dim(
            table_t, first * code_count, step_width * code_count, 0
        )
        return running + jnp.dot(one_hot, table_rows, preferred_element_type=jnp.float32)

    layer_scores = lax.fori_loop(
        0, sub_local // step_width, score_block, jnp.zeros((train_local, tests_all), jnp.float32)
    )
    score_total = jnp.where(live_rows[:, None], layer_scores, jnp.float32(0.0))
    return lax.psum(score_total, ("layer", "sub"))


def solution(mesh):
    return jax.shard_map(
        per_device,
        mesh=mesh,
        in_specs=(
            P("layer", ("groups", "dp"), None),
            P("layer", ("groups", "dp"), "sub"),
            P("layer", "dp", "sub"),
            P(),
            P(),
            P("sub", None, None),
            P(("groups", "dp"), "layer", "sub"),
            P(("groups", "dp")),
        ),
        out_specs=P(("groups", "dp"), None),
        check_vma=False,
    )
```

profile of v0, /device:TPU:0, one launch (start us, length us, event | category | flops | bytes accessed | tf_op | source)
XLA Modules:
  0.0 411.6 jit_solution(8313152646728108136)
XLA Ops:
  6.5 0.7 all-gather.6.cloned.1.call-update
  7.3 154.0 %all-gather.6.cloned.1.call-done = bf16[1,4096,1024]{2,1,0:T(8,128)(2,1)} async-done(((bf16[1,1024,1024]{2,1,0:T(8,128)(2,1)}), bf16[1,4096,1024]{2,1,0:T(8,128)(2,1)}) %all-gather.6.cloned.1.call-update) | async-done | bytes 8388624 | tf_op jit(solution)/shard_map/all_gather | solution.py:32
  161.3 5.9 %fusion.10 = f32[256,4096]{1,0:T(8,128)S(1)} fusion(bf16[1,4096,1024]{2,1,0:T(8,128)(2,1)} %all-gather.6.cloned.1.call-done, bf16[1,256,1024]{2,1,0:T(8,128)(2,1)} %param.11), kind=kOutput, calls=%fused_computation.9 | convolution fusion | flops 2147483648 | bytes 13107200 | tf_op jit(solution)/shard_map/dot_general | solution.py:30
  167.3 2.6 fusion.18
  169.9 0.2 all-gather.4.cloned.1.call-start
  170.2 1.1 fusion.14
  171.3 14.9 %all-reduce.2.cloned.1.call-done = f32[4,64,64]{2,1,0:T(8,128)} async-done(((f32[4,64,64]{2,1,0:T(8,128)}), f32[4,64,64]{2,1,0:T(8,128)}) %all-reduce.2.cloned.1.call-update) | async-done | bytes 65552 | tf_op jit(solution)/shard_map/psum | solution.py:37
  186.2 1.3 multiply_reduce_fusion
  187.5 0.1 reshape.45
  187.7 0.3 reshape.46
  188.0 2.5 fusion.12
  190.5 0.9 copy.16
  192.1 46.6 %all-gather.4.cloned.1.call-done = bf16[16,256,256]{2,1,0:T(8,128)(2,1)} async-done(((bf16[4,256,256]{2,1,0:T(8,128)(2,1)}), bf16[16,256,256]{2,1,0:T(8,128)(2,1)}) %all-gather.4.cloned.1.call-update) | async-done | bytes 2097168 | tf_op jit(solution)/shard_map/all_gather | solution.py:47
  238.7 4.1 copy.22
  242.7 150.5 %while.16 = (s32[]{:T(128)}, f32[256,16]{0,1:T(8,128)S(1)}, s32[256,256]{1,0:T(8,128)S(1)}, bf16[65536,16]{0,1:T(8,128)(2,1)}, s32[]{:T(128)}, /*index=5*/s32[]{:T(128)}, s32[]{:T(128)}, s32[]{:T(128)}, s32[]{:T(128)}, s32[]{:T(128)}) while((s32[]{:T(128)}, f32[256,16]{0,1:T(8,128)S(1)}, s32[256,256]{1,0:T(8,128)S(1)}, ...), condition=%wide.region_3.0_spmd.clone, body=%wide.region_2.0_spmd.clone.sunk | while | flops 34611208 | bytes 17055956 | solution.py:62
  242.8 0.6 eq.60
  243.5 5.7 %copy.29 = s32[32,8,16,256]{3,1,2,0:T(8,128)} copy(s32[32,8,16,256]{3,2,1,0:T(8,128)S(1)} %bitcast.44) | data formatting | bytes 8388608 | tf_op jit(solution)/shard_map/while
  249.2 2.9 fusion.30
  252.3 0.6 eq.60
  252.9 5.7 %copy.29 = s32[32,8,16,256]{3,1,2,0:T(8,128)} copy(s32[32,8,16,256]{3,2,1,0:T(8,128)S(1)} %bitcast.44) | data formatting | bytes 8388608 | tf_op jit(solution)/shard_map/while
  258.6 2.9 fusion.30
  261.7 0.6 eq.60
  262.3 5.7 %copy.29 = s32[32,8,16,256]{3,1,2,0:T(8,128)} copy(s32[32,8,16,256]{3,2,1,0:T(8,128)S(1)} %bitcast.44) | data formatting | bytes 8388608 | tf_op jit(solution)/shard_map/while
  268.0 2.9 fusion.30
  271.1 0.6 eq.60
  271.7 5.7 %copy.29 = s32[32,8,16,256]{3,1,2,0:T(8,128)} copy(s32[32,8,16,256]{3,2,1,0:T(8,128)S(1)} %bitcast.44) | data formatting | bytes 8388608 | tf_op jit(solution)/shard_map/while
  277.4 2.9 fusion.30
  280.5 0.6 eq.60
  281.1 5.7 %copy.29 = s32[32,8,16,256]{3,1,2,0:T(8,128)} copy(s32[32,8,16,256]{3,2,1,0:T(8,128)S(1)} %bitcast.44) | data formatting | bytes 8388608 | tf_op jit(solution)/shard_map/while
  286.8 2.9 fusion.30
  289.9 0.6 eq.60
  290.5 5.7 %copy.29 = s32[32,8,16,256]{3,1,2,0:T(8,128)} copy(s32[32,8,16,256]{3,2,1,0:T(8,128)S(1)} %bitcast.44) | data formatting | bytes 8388608 | tf_op jit(solution)/shard_map/while
  296.2 2.9 fusion.30
  299.3 0.6 eq.60
  299.9 5.7 %copy.29 = s32[32,8,16,256]{3,1,2,0:T(8,128)} copy(s32[32,8,16,256]{3,2,1,0:T(8,128)S(1)} %bitcast.44) | data formatting | bytes 8388608 | tf_op jit(solution)/shard_map/while
  305.6 2.9 fusion.30
  308.7 0.6 eq.60
  309.3 5.7 %copy.29 = s32[32,8,16,256]{3,1,2,0:T(8,128)} copy(s32[32,8,16,256]{3,2,1,0:T(8,128)S(1)} %bitcast.44) | data formatting | bytes 8388608 | tf_op jit(solution)/shard_map/while
  315.1 2.9 fusion.30
  318.1 0.6 eq.60
  318.7 5.7 %copy.29 = s32[32,8,16,256]{3,1,2,0:T(8,128)} copy(s32[32,8,16,256]{3,2,1,0:T(8,128)S(1)} %bitcast.44) | data formatting | bytes 8388608 | tf_op jit(solution)/shard_map/while
  324.5 2.9 fusion.30
  327.5 0.6 eq.60
  328.1 5.7 %copy.29 = s32[32,8,16,256]{3,1,2,0:T(8,128)} copy(s32[32,8,16,256]{3,2,1,0:T(8,128)S(1)} %bitcast.44) | data formatting | bytes 8388608 | tf_op jit(solution)/shard_map/while
  333.9 2.9 fusion.30
  336.9 0.6 eq.60
  337.5 5.7 %copy.29 = s32[32,8,16,256]{3,1,2,0:T(8,128)} copy(s32[32,8,16,256]{3,2,1,0:T(8,128)S(1)} %bitcast.44) | data formatting | bytes 8388608 | tf_op jit(solution)/shard_map/while
  343.3 2.9 fusion.30
  346.3 0.6 eq.60
  346.9 5.7 %copy.29 = s32[32,8,16,256]{3,1,2,0:T(8,128)} copy(s32[32,8,16,256]{3,2,1,0:T(8,128)S(1)} %bitcast.44) | data formatting | bytes 8388608 | tf_op jit(solution)/shard_map/while
  352.7 2.9 fusion.30
  355.7 0.6 eq.60
  356.3 5.7 %copy.29 = s32[32,8,16,256]{3,1,2,0:T(8,128)} copy(s32[32,8,16,256]{3,2,1,0:T(8,128)S(1)} %bitcast.44) | data formatting | bytes 8388608 | tf_op jit(solution)/shard_map/while
  362.1 2.9 fusion.30
  365.1 0.6 eq.60
  365.7 5.7 %copy.29 = s32[32,8,16,256]{3,1,2,0:T(8,128)} copy(s32[32,8,16,256]{3,2,1,0:T(8,128)S(1)} %bitcast.44) | data formatting | bytes 8388608 | tf_op jit(solution)/shard_map/while
  371.5 2.9 fusion.30
  374.5 0.6 eq.60
  375.1 5.7 %copy.29 = s32[32,8,16,256]{3,1,2,0:T(8,128)} copy(s32[32,8,16,256]{3,2,1,0:T(8,128)S(1)} %bitcast.44) | data formatting | bytes 8388608 | tf_op jit(solution)/shard_map/while
  380.9 2.9 fusion.30
  383.9 0.6 eq.60
  384.6 5.7 %copy.29 = s32[32,8,16,256]{3,1,2,0:T(8,128)} copy(s32[32,8,16,256]{3,2,1,0:T(8,128)S(1)} %bitcast.44) | data formatting | bytes 8388608 | tf_op jit(solution)/shard_map/while
  390.3 2.9 fusion.30
  393.3 11.8 %psum.15 = f32[256,16]{0,1:T(8,128)} all-reduce(f32[256,16]{0,1:T(8,128)S(1)} %broadcast_select_fusion), channel_id=1, replica_groups=mesh['groups'=2,'dp'=4,'layer'=2,'sub'=2] {'layer','sub'}, use_global_device_ids=true, to_apply=%region_4.5 | all-reduce | flops 4096 | bytes 32768 | tf_op jit(solution)/shard_map/psum | solution.py:66
  (66 shorter events, 2.1 us)
Async XLA Ops:
  6.5 163.6 %copy-start = (bf16[1,256,4096]{2,1,0:T(8,128)(2,1)S(1)}, bf16[1,256,4096]{2,1,0:T(8,128)(2,1)}, u32[]{:S(2)}) copy-start(bf16[1,256,4096]{2,1,0:T(8,128)(2,1)} %param.10) | copy-start | bytes 6291460
  6.5 154.8 %all-gather.6.cloned.1.call-start = ((), (), s32[]{:S(2)}) async-start(), calls=%async_computation.2 | async-start | bytes 10485760 | tf_op jit(solution)/shard_map/all_gather | solution.py:32
  7.3 160.0 %copy-start.1 = (bf16[4096,64]{0,1:T(8,128)(2,1)S(1)}, bf16[4096,64]{0,1:T(8,128)(2,1)}, u32[]{:S(2)}) copy-start(bf16[4096,64]{0,1:T(8,128)(2,1)} %param.14) | copy-start | bytes 1572868
  7.3 179.0 %all-reduce.2.cloned.1.call-start = ((), (), s32[]{:S(2)}) async-start(), calls=%async_computation | async-start | bytes 262144 | tf_op jit(solution)/shard_map/psum | solution.py:37
  167.2 2.9 copy-start.2
  169.9 21.5 %copy-start.3 = (s32[256,1,256]{2,1,0:T(1,128)S(1)}, s32[256,1,256]{2,1,0:T(1,128)}, u32[]{:S(2)}) copy-start(s32[256,1,256]{2,1,0:T(1,128)} %param.16) | copy-start | bytes 786436
  169.9 68.7 %all-gather.4.cloned.1.call-start = ((), (), s32[]{:S(2)}) async-start(), calls=%async_computation.1 | async-start | bytes 2621440 | tf_op jit(solution)/shard_map/all_gather | solution.py:47
Sparse Core Ops, SparseCore 0:
  8.9 152.3 all-gather.5
  170.1 16.1 all-reduce.1
  191.5 47.0 all-gather.3
where the time goes:
time: 412 us
  waiting for transfers between devices  216 us (52%)
  local copies, waits for them, and re-layouts  109 us (26%)
  matrix products  60.4 us (15%)
  between operations  13.9 us (3%)
  blocking collectives  11.8 us (3%)
    all_gather x1, waiting for transfers between devices, per_device(): lax.all_gather(kv_weight[0], 'dp', axis=0, tiled=True)  154 us
    while x48, local copies, waits for them, and re-layouts  92.1 us
    dot_general x16, matrix products, score_block(): jnp.dot(one_hot, table_rows, preferred_element_type=jnp.float32)  46.9 us
    all_gather x1, waiting for transfers between devices, per_device(): all_tables = lax.all_gather(own_tables, 'dp', axis=0, tiled=True)  46.6 us
    psum x1, waiting for transfers between devices, per_device(): out_side = lax.psum(out_side, 'sub')  14.9 us
    psum x1, blocking collectives, per_device(): return lax.psum(score_total, ('layer', 'sub'))  11.8 us
    eq x16, local copies, waits for them, and re-layouts, score_block(): code_block[:, :, None] == centroid_ids[None, None, :]  9.6 us
  transfers between devices with their start and end apart: 3, of which 3 were waited for; matrix products, arithmetic and copies ran while one was open for 0% of the time, Pallas kernels for 0%

commit v1 on v0

v1 whole, which is shorter than its diff:
```python
import jax
import jax.numpy as jnp
from jax import lax
from jax.experimental import pallas as pl
from jax.experimental.pallas import tpu as pltpu
from jax.sharding import PartitionSpec as P

SEQ = 64
LANES = 128
LINK_SCALE = 1024.0


def decode_kernel(codes_ref, book_ref, out_ref):
    subs, width, code_count = book_ref.shape
    slots = codes_ref.shape[1]

    def eight(step, carry):
        first = pl.multiple_of(step * 8, 8)
        ids = codes_ref[pl.ds(first, 8), :]
        low = ids & (LANES - 1)
        for pair in range(0, 8, 2):
            halves = []
            for sub in (pair, pair + 1):
                table = book_ref[first + sub].astype(jnp.float32)
                columns = []
                for left in range(0, slots, LANES):
                    own = jnp.broadcast_to(ids[sub : sub + 1, left : left + LANES], (width, LANES))
                    spot = jnp.broadcast_to(low[sub : sub + 1, left : left + LANES], (width, LANES))
                    picked = None
                    for part in range(0, code_count, LANES):
                        found = jnp.take_along_axis(
                            table[:, part : part + LANES], spot, axis=1, mode="promise_in_bounds"
                        )
                        picked = found if picked is None else jnp.where(own >= part, found, picked)
                    columns.append(picked)
                halves.append(jnp.concatenate(columns, axis=1))
            rows = pl.multiple_of((first + pair) * width, 2 * width)
            out_ref[pl.ds(rows, 2 * width), :] = jnp.concatenate(halves, axis=0).astype(jnp.bfloat16)
        return carry

    lax.fori_loop(0, subs // 8, eight, 0)


def decode(codes_t, book_t):
    subs, width, _ = book_t.shape
    slots = codes_t.shape[1]
    return pl.pallas_call(
        decode_kernel,
        out_shape=jax.ShapeDtypeStruct((subs * width, slots), jnp.bfloat16),
        in_specs=[pl.BlockSpec(memory_space=pltpu.VMEM)] * 2,
        out_specs=pl.BlockSpec(memory_space=pltpu.VMEM),
        compiler_params=pltpu.CompilerParams(vmem_limit_bytes=16 * 1024 * 1024),
        cost_estimate=pl.CostEstimate(flops=0, bytes_accessed=2 * 1024 * 1024, transcendentals=0),
        name="decode",
    )(codes_t, book_t)


def split_high_low(x):
    high = lax.reduce_precision(x, 8, 7)
    return high.astype(jnp.bfloat16), (x - high).astype(jnp.bfloat16)


def partners(size, step):
    return [(i, i ^ step) for i in range(size)]


def is_power_of_two(n):
    return n & (n - 1) == 0


def sum_over_dp(x):
    size = lax.axis_size("dp")
    if not is_power_of_two(size):
        return lax.psum(x, "dp")
    step = 1
    while step < size:
        sent = (x * LINK_SCALE).astype(jnp.float16)
        x = x + lax.ppermute(sent, "dp", partners(size, step)).astype(jnp.float32) * (1.0 / LINK_SCALE)
        step *= 2
    return x


def gather_over_dp(x):
    size = lax.axis_size("dp")
    if size > 4 or not is_power_of_two(size):
        return lax.all_gather(x, "dp", axis=0)
    own = lax.axis_index("dp")
    got = jnp.zeros((size,) + x.shape, x.dtype)
    got = lax.dynamic_update_index_in_dim(got, x, own, 0)
    for step in range(1, size):
        block = lax.ppermute(x, "dp", partners(size, step))
        got = lax.dynamic_update_index_in_dim(got, block, own ^ step, 0)
    return got


def sum_over_layer_sub(x):
    if lax.axis_size("layer") != 2 or lax.axis_size("sub") != 2:
        return lax.psum(x, ("layer", "sub"))
    by_sub = lax.ppermute(x, "sub", partners(2, 1))
    by_layer = lax.ppermute(x, "layer", partners(2, 1))
    by_both = lax.ppermute(x, ("layer", "sub"), partners(4, 3))
    return (x + by_sub) + (by_layer + by_both)


def per_device(acts, kv_grad, kv_weight, proj_in, proj_out, codebook, codes, counts):
    tok_local = acts.shape[1]
    rank_dim = proj_in.shape[1]
    sub_local, code_count, sub_width = codebook.shape
    train_local = codes.shape[0]
    tests_local = tok_local // SEQ
    rows_local = kv_weight.shape[1]
    dims_local = sub_local * sub_width
    live_rows = jnp.arange(train_local, dtype=jnp.int32) < counts[0]

    own_rows = lax.dynamic_slice_in_dim(proj_out, lax.axis_index("dp") * rows_local, rows_local, 0)
    folded = lax.dot_general(
        own_rows, kv_weight[0], (((0,), (0,)), ((), ())), preferred_element_type=jnp.float32
    )
    folded = sum_over_dp(folded)
    out_side = lax.dot_general(
        jnp.concatenate(split_high_low(folded), axis=0),
        kv_grad[0],
        (((1,), (1,)), ((), ())),
        preferred_element_type=jnp.float32,
    )
    out_side = out_side[:rank_dim] + out_side[rank_dim:]
    out_side = lax.psum(out_side, "sub") if lax.axis_size("sub") != 2 else (
        out_side + lax.ppermute(out_side, "sub", partners(2, 1))
    )
    in_side = lax.dot_general(
        proj_in, acts[0], (((0,), (1,)), ((), ())), preferred_element_type=jnp.float32
    )
    grads = jnp.einsum(
        "ies,jes->eij",
        in_side.reshape(rank_dim, tests_local, SEQ),
        out_side.reshape(rank_dim, tests_local, SEQ),
        precision=lax.Precision.HIGHEST,
    ).reshape(tests_local, rank_dim * rank_dim)
    vectors = grads * lax.rsqrt(jnp.mean(grads * grads, axis=1, keepdims=True) + 1e-06) / rank_dim
    own_part = lax.dynamic_slice_in_dim(vectors, lax.axis_index("sub") * dims_local, dims_local, 1)
    every = gather_over_dp(own_part).reshape(-1, dims_local)
    tests_all = every.shape[0]

    decoded = decode(jnp.transpose(codes[:, 0, :]), jnp.transpose(codebook, (0, 2, 1)))
    layer_scores = jnp.dot(
        jnp.concatenate(split_high_low(every), axis=0), decoded, preferred_element_type=jnp.float32
    )
    layer_scores = layer_scores[:tests_all] + layer_scores[tests_all:]
    total = sum_over_layer_sub(layer_scores)
    return jnp.transpose(jnp.where(live_rows[None, :], total, jnp.float32(0.0)))


def solution(mesh):
    return jax.shard_map(
        per_device,
        mesh=mesh,
        in_specs=(
            P("layer", ("groups", "dp"), None),
            P("layer", ("groups", "dp"), "sub"),
            P("layer", "dp", "sub"),
            P(),
            P(),
            P("sub", None, None),
            P(("groups", "dp"), "layer", "sub"),
            P(("groups", "dp")),
        ),
        out_specs=P(("groups", "dp"), None),
        check_vma=False,
    )
```

time: 412 us -> 42.3 us (0.10)
  waiting for transfers between devices: 216 us -> 16.7 us
  local copies, waits for them, and re-layouts: 109 us -> 2.45 us
  matrix products: 60.4 us -> 4.44 us
  between operations: 13.9 us -> 0.83 us
  starting transfers between devices: 0.26 us -> 12.4 us
  blocking collectives: 11.8 us -> 0 us
    all_gather x2 -> x0, waiting for transfers between devices: 201 us -> none  [the longest x1 154 us: per_device(): lax.all_gather(kv_weight[0], 'dp', axis=0, tiled=True)]
    while x48 -> x0, local copies, waits for them, and re-layouts: 92.1 us -> none
    dot_general x20 -> x5, matrix products: 57.7 us -> 4.44 us  [the longest x1 2.29 us: per_device(): lax.dot_general(own_rows, kv_weight[0], (((0,), (0,)), ((), ())), preferr...]
    ppermute x0 -> x9, waiting for transfers between devices: none -> 16.7 us  [the longest x2 9.14 us: sum_over_dp(): lax.ppermute(sent, 'dp', partners(size, step)).astype(jnp.float32)]
    psum x1 -> x0, waiting for transfers between devices: 14.9 us -> none  [per_device(): out_side = lax.psum(out_side, 'sub')]
    ppermute x0 -> x9, starting transfers between devices: none -> 12.4 us  [the longest x2 5.93 us: sum_over_dp(): lax.ppermute(sent, 'dp', partners(size, step)).astype(jnp.float32)]
    psum x1 -> x0, blocking collectives: 11.8 us -> none  [per_device(): return lax.psum(score_total, ('layer', 'sub'))]
    eq x16 -> x0, local copies, waits for them, and re-layouts: 9.6 us -> none  [score_block(): code_block[:, :, None] == centroid_ids[None, None, :]]
  transfers between devices with their start and end apart: 3 -> 9, of which waited for: 3 -> 7; matrix products, arithmetic and copies ran while one was open for 0% -> 5% of each run, Pallas kernels for 0% -> 9%
where the time goes in v1:
time: 42.3 us; the launch traced here: 42.1 us
  waiting for transfers between devices  16.7 us (39%)
  starting transfers between devices  12.4 us (29%)
  matrix products  4.44 us (10%)
  Pallas kernels  3.7 us (9%)
  local copies, waits for them, and re-layouts  2.45 us (6%)
  other arithmetic  1.52 us (4%)
  between operations  0.83 us (2%)
    ppermute x2, waiting for transfers between devices, sum_over_dp(): lax.ppermute(sent, 'dp', partners(size, step)).astype(jnp.float32)  9.14 us
    ppermute x2, starting transfers between devices, sum_over_dp(): lax.ppermute(sent, 'dp', partners(size, step)).astype(jnp.float32)  5.93 us
    ppermute x3, waiting for transfers between devices, gather_over_dp(): block = lax.ppermute(x, 'dp', partners(size, step))  4.66 us
    ppermute x3, starting transfers between devices, gather_over_dp(): block = lax.ppermute(x, 'dp', partners(size, step))  4.45 us
    pallas_call x1, Pallas kernels, decode(): pl.pallas_call(decode_kernel, out_shape=jax.ShapeDtypeStruct((subs * widt...  3.7 us
    dot_general x1, matrix products, per_device(): lax.dot_general(own_rows, kv_weight[0], (((0,), (0,)), ((), ())), preferr...  2.29 us
    ppermute x1, waiting for transfers between devices, sum_over_layer_sub(): by_layer = lax.ppermute(x, 'layer', partners(2, 1))  1.93 us
    ppermute x1, starting transfers between devices, sum_over_layer_sub(): by_layer = lax.ppermute(x, 'layer', partners(2, 1))  1.55 us
  transfers between devices with their start and end apart: 9, of which 7 were waited for; matrix products, arithmetic and copies ran while one was open for 5% of the time, Pallas kernels for 9%

profile of v1, /device:TPU:0, one launch (start us, length us, event | category | flops | bytes accessed | tf_op | source)
XLA Modules:
  0.0 42.1 jit_solution(11001569913691218307)
XLA Ops:
  0.0 0.0 copy-start
  0.0 0.0 copy-start.2
  0.0 0.0 copy-start.3
  0.0 2.3 %multiply_convert_fusion.1 = (f16[64,1024]{1,0:T(8,128)(2,1)S(1)}, f32[64,1024]{1,0:T(8,128)S(1)}) fusion(bf16[1,1024,1024]{2,1,0:T(8,128)(2,1)} %param.10, bf16[4096,64]{0,1:T(8,128)(2,1)} %param.12, s32[]{:T(128)S(6)} %select_n.23), kind=kOutput, calls=%fused_computation.15 | convolution fusion | flops 134348800 | bytes 2621444 | tf_op jit(solution)/shard_map/dot_general | solution.py:116
  2.3 3.1 %collective-permute-start = (f16[64,1024]{1,0:T(8,128)(2,1)S(1)}, f16[64,1024]{1,0:T(8,128)(2,1)S(1)}, u32[]{:S(2)}, u32[]{:S(2)}) collective-permute-start(f16[64,1024]{1,0:T(8,128)(2,1)S(1)} %get-tuple-element.11), channel_id=1, source_target_pairs={{0,4},{4,0},{8,12},{12,8},{1,5},{5,1},{9,13},{13,9},{2,6},{6,2},{1... | collective-permute-start | bytes 393224 | tf_op jit(solution)/shard_map/ppermute | solution.py:78
  5.4 3.5 %collective-permute-done = f16[64,1024]{1,0:T(8,128)(2,1)S(1)} collective-permute-done((f16[64,1024]{1,0:T(8,128)(2,1)S(1)}, f16[64,1024]{1,0:T(8,128)(2,1)S(1)}, u32[]{:S(2)}, u32[]{:S(2)}) %collective-permute-start) | collective-permute-done | bytes 131104 | tf_op jit(solution)/shard_map/ppermute | solution.py:78
  8.9 0.1 multiply_convert_fusion
  9.0 2.8 %collective-permute-start.1 = (f16[64,1024]{1,0:T(8,128)(2,1)S(1)}, f16[64,1024]{1,0:T(8,128)(2,1)S(1)}, u32[]{:S(2)}, u32[]{:S(2)}) collective-permute-start(f16[64,1024]{1,0:T(8,128)(2,1)S(1)} %multiply_convert_fusion), channel_id=1, source_target_pairs={{0,8},{4,12},{8,0},{12,4},{1,9},{5,13},{9,1},{13,5},{2,10},{6,14},... | collective-permute-start | bytes 393224 | tf_op jit(solution)/shard_map/ppermute | solution.py:78
  11.8 5.6 %collective-permute-done.1 = f16[64,1024]{1,0:T(8,128)(2,1)S(1)} collective-permute-done((f16[64,1024]{1,0:T(8,128)(2,1)S(1)}, f16[64,1024]{1,0:T(8,128)(2,1)S(1)}, u32[]{:S(2)}, u32[]{:S(2)}) %collective-permute-start.1) | collective-permute-done | bytes 131104 | tf_op jit(solution)/shard_map/ppermute | solution.py:78
  17.4 0.1 reduce-precision_convert_fusion
  17.5 0.0 copy-done.2
  17.5 0.3 fusion.2
  17.8 0.0 copy-start.4
  17.9 0.1 collective-permute-start.2
  18.0 0.0 copy-done
  18.0 0.0 copy-done.3
  18.0 1.1 %fusion.4 = f32[64,4,64]{2,0,1:T(8,128)S(1)} fusion(bf16[4,64,4096]{2,1,0:T(8,128)(2,1)S(1)} %bitcast.31, bf16[4096,64]{0,1:T(8,128)(2,1)S(1)} %copy-done.3), kind=kOutput, calls=%fused_computation.4 | convolution fusion | flops 134217728 | bytes 2686976 | tf_op jit(solution)/shard_map/dot_general | solution.py:130
  19.1 0.1 collective-permute-done.2
  19.2 0.1 reshape.24
  19.3 0.4 %multiply_reduce_fusion = (f32[4]{0:T(128)S(1)}, f32[4,64,64]{2,1,0:T(8,128)S(1)}) fusion(f32[64,4,64]{2,0,1:T(8,128)S(1)} %fusion.4, f32[64,4,64]{2,1,0:T(4,128)S(1)} %reshape.24), kind=kOutput, calls=%fused_computation.25 | convolution fusion | flops 12615676 | bytes 196624 | tf_op jit(solution)/shard_map/ies,jes->eij/dot_general | solution.py:133
  19.8 0.1 reshape.25
  19.9 0.7 %bitcast_dynamic-update-slice_fusion.3 = (f32[4,4,2048]{2,1,0:T(4,128)S(1)}, f32[4,2048]{1,0:T(4,128)}) fusion(f32[4,4,2048]{2,1,0:T(4,128)S(1)} %broadcast_in_dim.31, s32[]{:T(128)S(6)} %select_n.25, f32[4]{0:T(128)S(1)} %add_rsqrt_fusion, f32[4,4096]{1,0:T(4,128)S(1)} %reshape.25, s32[]{:T(128)S(6)} %select_n.24), kind=kLoop, calls=%fused_computation.33 | loop fusion | flops 16384 | bytes 98824 | tf_op jit(solution)/shard_map/jit(dynamic_update_index_in_dim)/dynamic_update_slice | solution.py:89
  20.6 0.5 %collective-permute-start.3 = (f32[4,2048]{1,0:T(4,128)}, f32[4,2048]{1,0:T(4,128)}, u32[]{:S(2)}, u32[]{:S(2)}) collective-permute-start(f32[4,2048]{1,0:T(4,128)} %get-tuple-element.6), channel_id=1, source_target_pairs={{0,4},{4,0},{8,12},{12,8},{1,5},{5,1},{9,13},{13,9},{2,6},{6,2},{1... | collective-permute-start | bytes 98312 | tf_op jit(solution)/shard_map/ppermute | solution.py:91
  21.1 0.0 copy-done.4
  21.1 0.1 copy.10
  21.9 0.0 copy-start.1
  22.0 1.2 %copy-done.1 = bf16[256,256,8]{1,2,0:T(8,128)(2,1)S(1)} copy-done((bf16[256,256,8]{1,2,0:T(8,128)(2,1)S(1)}, bf16[256,256,8]{1,2,0:T(8,128)(2,1)}, u32[]{:S(2)}) %copy-start.1) | copy-done | bytes 1048600
  23.2 3.7 %decode.1 = bf16[2048,256]{1,0:T(8,128)(2,1)S(1)} custom-call(s32[256,256]{1,0:T(8,128)S(1)} %bitcast.32, bf16[256,8,256]{2,1,0:T(8,128)(2,1)S(1)} %bitcast.33), custom_call_target="tpu_custom_call" | custom-call | bytes 2097152 | tf_op jit(solution)/shard_map/decode/pallas_call | solution.py:47
  26.9 3.4 %collective-permute-start.4 = (f32[4,2048]{1,0:T(4,128)}, f32[4,2048]{1,0:T(4,128)S(1)}, u32[]{:S(2)}, u32[]{:S(2)}) collective-permute-start(f32[4,2048]{1,0:T(4,128)} %get-tuple-element.6), channel_id=1, source_target_pairs={{0,8},{4,12},{8,0},{12,4},{1,9},{5,13},{9,1},{13,5},{2,10},{6,14},... | collective-permute-start | bytes 98312 | tf_op jit(solution)/shard_map/ppermute | solution.py:91
  30.3 0.5 %collective-permute-start.5 = (f32[4,2048]{1,0:T(4,128)}, f32[4,2048]{1,0:T(4,128)S(1)}, u32[]{:S(2)}, u32[]{:S(2)}) collective-permute-start(f32[4,2048]{1,0:T(4,128)} %get-tuple-element.6), channel_id=1, source_target_pairs={{0,12},{4,8},{8,4},{12,0},{1,13},{5,9},{9,5},{13,1},{2,14},{6,10},... | collective-permute-start | bytes 98312 | tf_op jit(solution)/shard_map/ppermute | solution.py:91
  30.8 0.0 collective-permute-done.3
  30.8 0.8 %bitcast_dynamic-update-slice_fusion.2 = f32[4,4,2048]{2,1,0:T(4,128)S(1)} fusion(f32[4,4,2048]{2,1,0:T(4,128)S(1)} %get-tuple-element.5, s32[]{:T(128)S(6)} %select_n.26, f32[4,2048]{1,0:T(4,128)} %collective-permute-done.3), kind=kLoop, calls=%fused_computation.32 | loop fusion | bytes 65540 | tf_op jit(solution)/shard_map/jit(dynamic_update_index_in_dim)/dynamic_update_slice | solution.py:92
  31.6 1.4 %collective-permute-done.4 = f32[4,2048]{1,0:T(4,128)S(1)} collective-permute-done((f32[4,2048]{1,0:T(4,128)}, f32[4,2048]{1,0:T(4,128)S(1)}, u32[]{:S(2)}, u32[]{:S(2)}) %collective-permute-start.4) | collective-permute-done | bytes 32800 | tf_op jit(solution)/shard_map/ppermute | solution.py:91
  33.0 3.3 %collective-permute-done.5 = f32[4,2048]{1,0:T(4,128)S(1)} collective-permute-done((f32[4,2048]{1,0:T(4,128)}, f32[4,2048]{1,0:T(4,128)S(1)}, u32[]{:S(2)}, u32[]{:S(2)}) %collective-permute-start.5) | collective-permute-done | bytes 32800 | tf_op jit(solution)/shard_map/ppermute | solution.py:91
  36.3 0.3 fusion.11
  36.6 0.1 collective-permute-start.6
  36.7 1.6 %collective-permute-start.7 = (f32[16,256]{1,0:T(8,128)S(1)}, f32[16,256]{1,0:T(8,128)S(1)}, u32[]{:S(2)}, u32[]{:S(2)}) collective-permute-start(f32[16,256]{1,0:T(8,128)S(1)} %slice_add_fusion.1), channel_id=1, source_target_pairs={{0,2},{2,0},{1,3},{3,1},{4,6},{6,4},{5,7},{7,5},{8,10},{10,8},{9,1... | collective-permute-start | bytes 49160 | tf_op jit(solution)/shard_map/ppermute | solution.py:100
  38.3 0.3 collective-permute-start.8
  38.6 0.0 collective-permute-done.6
  38.6 1.9 %collective-permute-done.7 = f32[16,256]{1,0:T(8,128)S(1)} collective-permute-done((f32[16,256]{1,0:T(8,128)S(1)}, f32[16,256]{1,0:T(8,128)S(1)}, u32[]{:S(2)}, u32[]{:S(2)}) %collective-permute-start.7) | collective-permute-done | bytes 16416 | tf_op jit(solution)/shard_map/ppermute | solution.py:100
  40.5 0.9 %collective-permute-done.8 = f32[16,256]{1,0:T(8,128)S(1)} collective-permute-done((f32[16,256]{1,0:T(8,128)S(1)}, f32[16,256]{1,0:T(8,128)S(1)}, u32[]{:S(2)}, u32[]{:S(2)}) %collective-permute-start.8) | collective-permute-done | bytes 16416 | tf_op jit(solution)/shard_map/ppermute | solution.py:101
  41.4 0.6 %select_bitcast_fusion = f32[256,16]{0,1:T(8,128)} fusion(f32[16,256]{1,0:T(8,128)S(1)} %collective-permute-done.7, f32[16,256]{1,0:T(8,128)S(1)} %collective-permute-done.8, f32[16,256]{1,0:T(8,128)S(1)} %collective-permute-done.6, pred[256]{0:T(512)(128)(4,1)S(1)} %iota_compare_fusion, f32[32,256]{1,0:T(8,128)S(1)} %fusion.11), kind=kLoop, calls=%fused_computation.35 | loop fusion | flops 20480 | bytes 98560 | tf_op jit(solution)/shard_map/transpose | solution.py:150
  (10 shorter events, 0.2 us)
Async XLA Ops:
  0.0 18.0 %copy-start = (bf16[1,256,4096]{2,1,0:T(8,128)(2,1)S(1)}, bf16[1,256,4096]{2,1,0:T(8,128)(2,1)}, u32[]{:S(2)}) copy-start(bf16[1,256,4096]{2,1,0:T(8,128)(2,1)} %param.8) | copy-start | bytes 6291460
  0.0 17.5 %copy-start.2 = (bf16[1,256,1024]{2,1,0:T(8,128)(2,1)S(1)}, bf16[1,256,1024]{2,1,0:T(8,128)(2,1)}, u32[]{:S(2)}) copy-start(bf16[1,256,1024]{2,1,0:T(8,128)(2,1)} %param.9) | copy-start | bytes 1572868
  0.0 18.0 %copy-start.3 = (bf16[4096,64]{0,1:T(8,128)(2,1)S(1)}, bf16[4096,64]{0,1:T(8,128)(2,1)}, u32[]{:S(2)}) copy-start(bf16[4096,64]{0,1:T(8,128)(2,1)} %param.11) | copy-start | bytes 1572868
  2.3 6.6 %collective-permute-start = (f16[64,1024]{1,0:T(8,128)(2,1)S(1)}, f16[64,1024]{1,0:T(8,128)(2,1)S(1)}, u32[]{:S(2)}, u32[]{:S(2)}) collective-permute-start(f16[64,1024]{1,0:T(8,128)(2,1)S(1)} %get-tuple-element.11), channel_id=1, source_target_pairs={{0,4},{4,0},{8,12},{12,8},{1,5},{5,1},{9,13},{13,9},{2,6},{6,2},{1... | collective-permute-start | bytes 393224 | tf_op jit(solution)/shard_map/ppermute | solution.py:78
  9.0 8.5 %collective-permute-start.1 = (f16[64,1024]{1,0:T(8,128)(2,1)S(1)}, f16[64,1024]{1,0:T(8,128)(2,1)S(1)}, u32[]{:S(2)}, u32[]{:S(2)}) collective-permute-start(f16[64,1024]{1,0:T(8,128)(2,1)S(1)} %multiply_convert_fusion), channel_id=1, source_target_pairs={{0,8},{4,12},{8,0},{12,4},{1,9},{5,13},{9,1},{13,5},{2,10},{6,14},... | collective-permute-start | bytes 393224 | tf_op jit(solution)/shard_map/ppermute | solution.py:78
  17.8 3.3 %copy-start.4 = (s32[256,1,256]{2,1,0:T(1,128)S(1)}, s32[256,1,256]{2,1,0:T(1,128)}, u32[]{:S(2)}) copy-start(s32[256,1,256]{2,1,0:T(1,128)} %param.14) | copy-start | bytes 786436
  17.9 1.3 %collective-permute-start.2 = (f32[64,256]{1,0:T(8,128)S(1)}, f32[64,256]{1,0:T(8,128)S(1)}, u32[]{:S(2)}, u32[]{:S(2)}) collective-permute-start(f32[64,256]{1,0:T(8,128)S(1)} %slice_add_fusion), channel_id=1, source_target_pairs={{0,1},{1,0},{2,3},{3,2},{4,5},{5,4},{6,7},{7,6},{8,9},{9,8},{10,11... | collective-permute-start | bytes 196616 | tf_op jit(solution)/shard_map/ppermute | solution.py:128
  20.6 10.2 %collective-permute-start.3 = (f32[4,2048]{1,0:T(4,128)}, f32[4,2048]{1,0:T(4,128)}, u32[]{:S(2)}, u32[]{:S(2)}) collective-permute-start(f32[4,2048]{1,0:T(4,128)} %get-tuple-element.6), channel_id=1, source_target_pairs={{0,4},{4,0},{8,12},{12,8},{1,5},{5,1},{9,13},{13,9},{2,6},{6,2},{1... | collective-permute-start | bytes 98312 | tf_op jit(solution)/shard_map/ppermute | solution.py:91
  21.9 1.2 %copy-start.1 = (bf16[256,256,8]{1,2,0:T(8,128)(2,1)S(1)}, bf16[256,256,8]{1,2,0:T(8,128)(2,1)}, u32[]{:S(2)}) copy-start(bf16[256,256,8]{1,2,0:T(8,128)(2,1)} %param.13) | copy-start | bytes 3145732
  26.9 6.1 %collective-permute-start.4 = (f32[4,2048]{1,0:T(4,128)}, f32[4,2048]{1,0:T(4,128)S(1)}, u32[]{:S(2)}, u32[]{:S(2)}) collective-permute-start(f32[4,2048]{1,0:T(4,128)} %get-tuple-element.6), channel_id=1, source_target_pairs={{0,8},{4,12},{8,0},{12,4},{1,9},{5,13},{9,1},{13,5},{2,10},{6,14},... | collective-permute-start | bytes 98312 | tf_op jit(solution)/shard_map/ppermute | solution.py:91
  30.3 5.9 %collective-permute-start.5 = (f32[4,2048]{1,0:T(4,128)}, f32[4,2048]{1,0:T(4,128)S(1)}, u32[]{:S(2)}, u32[]{:S(2)}) collective-permute-start(f32[4,2048]{1,0:T(4,128)} %get-tuple-element.6), channel_id=1, source_target_pairs={{0,12},{4,8},{8,4},{12,0},{1,13},{5,9},{9,5},{13,1},{2,14},{6,10},... | collective-permute-start | bytes 98312 | tf_op jit(solution)/shard_map/ppermute | solution.py:91
  36.6 1.9 %collective-permute-start.6 = (f32[16,256]{1,0:T(8,128)S(1)}, f32[16,256]{1,0:T(8,128)S(1)}, u32[]{:S(2)}, u32[]{:S(2)}) collective-permute-start(f32[16,256]{1,0:T(8,128)S(1)} %slice_add_fusion.1), channel_id=1, source_target_pairs={{0,1},{1,0},{2,3},{3,2},{4,5},{5,4},{6,7},{7,6},{8,9},{9,8},{10,11... | collective-permute-start | bytes 49160 | tf_op jit(solution)/shard_map/ppermute | solution.py:99
  36.7 3.8 %collective-permute-start.7 = (f32[16,256]{1,0:T(8,128)S(1)}, f32[16,256]{1,0:T(8,128)S(1)}, u32[]{:S(2)}, u32[]{:S(2)}) collective-permute-start(f32[16,256]{1,0:T(8,128)S(1)} %slice_add_fusion.1), channel_id=1, source_target_pairs={{0,2},{2,0},{1,3},{3,1},{4,6},{6,4},{5,7},{7,5},{8,10},{10,8},{9,1... | collective-permute-start | bytes 49160 | tf_op jit(solution)/shard_map/ppermute | solution.py:100
  38.3 3.2 %collective-permute-start.8 = (f32[16,256]{1,0:T(8,128)S(1)}, f32[16,256]{1,0:T(8,128)S(1)}, u32[]{:S(2)}, u32[]{:S(2)}) collective-permute-start(f32[16,256]{1,0:T(8,128)S(1)} %slice_add_fusion.1), channel_id=1, source_target_pairs={{0,3},{1,2},{2,1},{3,0},{4,7},{5,6},{6,5},{7,4},{8,11},{9,10},{10,... | collective-permute-start | bytes 49160 | tf_op jit(solution)/shard_map/ppermute | solution.py:101

commit v2 on v1

--- a/solution.py
+++ b/solution.py
@@ -68,16 +68,21 @@
     return n & (n - 1) == 0
 
 
-def sum_over_dp(x):
+def sum_over_dp(x, beside):
     size = lax.axis_size("dp")
+    beside = list(beside)
+    made = []
     if not is_power_of_two(size):
-        return lax.psum(x, "dp")
+        return lax.psum(x, "dp"), [work() for work in beside]
     step = 1
     while step < size:
-        sent = (x * LINK_SCALE).astype(jnp.float16)
-        x = x + lax.ppermute(sent, "dp", partners(size, step)).astype(jnp.float32) * (1.0 / LINK_SCALE)
+        got = lax.ppermute((x * LINK_SCALE).astype(jnp.float16), "dp", partners(size, step))
+        if beside:
+            got, done = lax.optimization_barrier((got, beside.pop(0)()))
+            made.append(done)
+        x = x + got.astype(jnp.float32) * (1.0 / LINK_SCALE)
         step *= 2
-    return x
+    return x, made + [work() for work in beside]
 
 
 def gather_over_dp(x):
@@ -116,7 +121,15 @@
     folded = lax.dot_general(
         own_rows, kv_weight[0], (((0,), (0,)), ((), ())), preferred_element_type=jnp.float32
     )
-    folded = sum_over_dp(folded)
+    folded, (in_side, decoded) = sum_over_dp(
+        folded,
+        [
+            lambda: lax.dot_general(
+                proj_in, acts[0], (((0,), (1,)), ((), ())), preferred_element_type=jnp.float32
+            ),
+            lambda: decode(jnp.transpose(codes[:, 0, :]), jnp.transpose(codebook, (0, 2, 1))),
+        ],
+    )
     out_side = lax.dot_general(
         jnp.concatenate(split_high_low(folded), axis=0),
         kv_grad[0],
@@ -126,9 +139,6 @@
     out_side = out_side[:rank_dim] + out_side[rank_dim:]
     out_side = lax.psum(out_side, "sub") if lax.axis_size("sub") != 2 else (
         out_side + lax.ppermute(out_side, "sub", partners(2, 1))
-    )
-    in_side = lax.dot_general(
-        proj_in, acts[0], (((0,), (1,)), ((), ())), preferred_element_type=jnp.float32
     )
     grads = jnp.einsum(
         "ies,jes->eij",
@@ -141,7 +151,6 @@
     every = gather_over_dp(own_part).reshape(-1, dims_local)
     tests_all = every.shape[0]
 
-    decoded = decode(jnp.transpose(codes[:, 0, :]), jnp.transpose(codebook, (0, 2, 1)))
     layer_scores = jnp.dot(
         jnp.concatenate(split_high_low(every), axis=0), decoded, preferred_element_type=jnp.float32
     )

time: 42.3 us -> 40.2 us (0.950)
  waiting for transfers between devices: 16.7 us -> 11.3 us
  local copies, waits for them, and re-layouts: 2.45 us -> 4.24 us
  other arithmetic: 1.52 us -> 2.45 us
  matrix products: 4.44 us -> 5.02 us
    ppermute x2, waiting for transfers between devices: 9.14 us -> 2.94 us  [sum_over_dp(): lax.ppermute((x * LINK_SCALE).astype(jnp.float16), 'dp', partners(size, s...]
    unnamed x11 -> x15, local copies, waits for them, and re-layouts: 1.38 us -> 2.97 us
    dot_general x1, matrix products: 0.31 us -> 1.35 us  [per_device(): lax.dot_general(jnp.concatenate(split_high_low(folded), axis=0), kv_grad[...]
    reshape x0 -> x1, local copies, waits for them, and re-layouts: none -> 0.95 us  [per_device(): in_side.reshape(rank_dim, tests_local, SEQ)]
    convert_element_type x2, other arithmetic: 0.11 us -> 1.01 us  [split_high_low(): return (high.astype(jnp.bfloat16), (x - high).astype(jnp.bfloat16))]
    dynamic_update_slice x3, local copies, waits for them, and re-layouts: 0.78 us -> 0.03 us  [gather_over_dp(): got = lax.dynamic_update_index_in_dim(got, block, own ^ step, 0)]
    dot_general x1, matrix products: 2.29 us -> 1.53 us  [per_device(): lax.dot_general(own_rows, kv_weight[0], (((0,), (0,)), ((), ())), preferr...]
    convert_element_type x1, other arithmetic: 0.06 us -> 0.69 us  [sum_over_dp(): (x * LINK_SCALE).astype(jnp.float16)]
  transfers between devices with their start and end apart: 9 -> 9, of which waited for: 7 -> 7; matrix products, arithmetic and copies ran while one was open for 5% -> 6% of each run, Pallas kernels for 9% -> 9%
where the time goes in v2:
time: 40.2 us; the launch traced here: 39.9 us
  starting transfers between devices  12.4 us (31%)
  waiting for transfers between devices  11.3 us (28%)
  matrix products  5.02 us (12%)
  local copies, waits for them, and re-layouts  4.24 us (11%)
  Pallas kernels  3.7 us (9%)
  other arithmetic  2.45 us (6%)
  between operations  0.81 us (2%)
    ppermute x2, starting transfers between devices, sum_over_dp(): lax.ppermute((x * LINK_SCALE).astype(jnp.float16), 'dp', partners(size, s...  5.84 us
    ppermute x3, waiting for transfers between devices, gather_over_dp(): block = lax.ppermute(x, 'dp', partners(size, step))  5.2 us
    ppermute x3, starting transfers between devices, gather_over_dp(): block = lax.ppermute(x, 'dp', partners(size, step))  4.52 us
    pallas_call x1, Pallas kernels, decode(): pl.pallas_call(decode_kernel, out_shape=jax.ShapeDtypeStruct((subs * widt...  3.7 us
    unnamed x15, local copies, waits for them, and re-layouts  2.97 us
    ppermute x2, waiting for transfers between devices, sum_over_dp(): lax.ppermute((x * LINK_SCALE).astype(jnp.float16), 'dp', partners(size, s...  2.94 us
    ppermute x1, waiting for transfers between devices, sum_over_layer_sub(): by_layer = lax.ppermute(x, 'layer', partners(2, 1))  1.93 us
    ppermute x1, starting transfers between devices, sum_over_layer_sub(): by_layer = lax.ppermute(x, 'layer', partners(2, 1))  1.55 us
  transfers between devices with their start and end apart: 9, of which 7 were waited for; matrix products, arithmetic and copies ran while one was open for 6% of the time, Pallas kernels for 9%

profile of v2, /device:TPU:0, one launch (start us, length us, event | category | flops | bytes accessed | tf_op | source)
XLA Modules:
  0.0 39.9 jit_solution(5151078994037146764)
XLA Ops:
  0.0 0.0 copy-start
  0.0 0.0 copy-start.5
  0.0 1.6 %copy-done = bf16[1,1024,1024]{2,1,0:T(8,128)(2,1)S(1)} copy-done((bf16[1,1024,1024]{2,1,0:T(8,128)(2,1)S(1)}, bf16[1,1024,1024]{2,1,0:T(8,128)(2,1)}, u32[]{:S(2)}) %copy-start) | copy-done | bytes 2097176
  1.6 0.0 copy-start.4
  1.6 1.5 %multiply_convert_fusion.1 = (f16[64,1024]{1,0:T(8,128)(2,1)S(1)}, f32[64,1024]{1,0:T(8,128)S(1)}) fusion(bf16[1,1024,1024]{2,1,0:T(8,128)(2,1)S(1)} %copy-done, bf16[4096,64]{0,1:T(8,128)(2,1)} %param.12, s32[]{:T(128)S(6)} %select_n.23), kind=kOutput, calls=%fused_computation.15 | convolution fusion | flops 134348800 | bytes 2621444 | tf_op jit(solution)/shard_map/dot_general | solution.py:121
  3.1 0.0 copy-start.2
  3.1 0.0 copy-start.6
  3.2 3.1 %collective-permute-start = (f16[64,1024]{1,0:T(8,128)(2,1)S(1)}, f16[64,1024]{1,0:T(8,128)(2,1)S(1)}, u32[]{:S(2)}, u32[]{:S(2)}) collective-permute-start(f16[64,1024]{1,0:T(8,128)(2,1)S(1)} %get-tuple-element.19), channel_id=1, source_target_pairs={{0,4},{4,0},{8,12},{12,8},{1,5},{5,1},{9,13},{13,9},{2,6},{6,2},{1... | collective-permute-start | bytes 393224 | tf_op jit(solution)/shard_map/ppermute | solution.py:79
  6.2 0.0 copy-done.5
  6.3 0.0 copy-done.4
  6.3 1.4 %fusion = f32[64,256]{1,0:T(8,128)} fusion(bf16[4096,64]{0,1:T(8,128)(2,1)S(1)} %copy-done.5, bf16[1,256,4096]{2,1,0:T(8,128)(2,1)S(1)} %copy-done.4), kind=kOutput, calls=%fused_computation | convolution fusion | flops 134217728 | bytes 2686976 | tf_op jit(solution)/shard_map/dot_general | solution.py:127
  7.7 2.1 %collective-permute-done = f16[64,1024]{1,0:T(8,128)(2,1)S(1)} collective-permute-done((f16[64,1024]{1,0:T(8,128)(2,1)S(1)}, f16[64,1024]{1,0:T(8,128)(2,1)S(1)}, u32[]{:S(2)}, u32[]{:S(2)}) %collective-permute-start) | collective-permute-done | bytes 131104 | tf_op jit(solution)/shard_map/ppermute | solution.py:79
  9.7 0.7 %multiply_convert_fusion = f16[64,1024]{1,0:T(8,128)(2,1)} fusion(f32[64,1024]{1,0:T(8,128)S(1)} %get-tuple-element.20, f16[64,1024]{1,0:T(8,128)(2,1)S(1)} %collective-permute-done), kind=kLoop, calls=%fused_computation.13 | loop fusion | flops 327680 | bytes 524288 | tf_op jit(solution)/shard_map/convert_element_type | solution.py:79
  10.4 0.0 copy-done.2
  10.4 2.8 %collective-permute-start.1 = (f16[64,1024]{1,0:T(8,128)(2,1)}, f16[64,1024]{1,0:T(8,128)(2,1)}, u32[]{:S(2)}, u32[]{:S(2)}) collective-permute-start(f16[64,1024]{1,0:T(8,128)(2,1)} %multiply_convert_fusion), channel_id=1, source_target_pairs={{0,8},{4,12},{8,0},{12,4},{1,9},{5,13},{9,1},{13,5},{2,10},{6,14},... | collective-permute-start | bytes 393224 | tf_op jit(solution)/shard_map/ppermute | solution.py:79
  13.2 0.0 copy-done.6
  13.2 0.1 copy.9
  13.3 0.0 copy-start.1
  13.4 1.2 %copy-done.1 = bf16[256,256,8]{1,2,0:T(8,128)(2,1)S(1)} copy-done((bf16[256,256,8]{1,2,0:T(8,128)(2,1)S(1)}, bf16[256,256,8]{1,2,0:T(8,128)(2,1)}, u32[]{:S(2)}) %copy-start.1) | copy-done | bytes 1048600
  14.6 0.0 copy-start.3
  14.6 3.7 %decode.1 = bf16[2048,256]{1,0:T(8,128)(2,1)S(1)} custom-call(s32[256,256]{1,0:T(8,128)S(1)} %bitcast.29, bf16[256,8,256]{2,1,0:T(8,128)(2,1)S(1)} %bitcast.30), custom_call_target="tpu_custom_call" | custom-call | bytes 2097152 | tf_op jit(solution)/shard_map/decode/pallas_call | solution.py:47
  18.3 0.9 %collective-permute-done.1 = f16[64,1024]{1,0:T(8,128)(2,1)} collective-permute-done((f16[64,1024]{1,0:T(8,128)(2,1)}, f16[64,1024]{1,0:T(8,128)(2,1)}, u32[]{:S(2)}, u32[]{:S(2)}) %collective-permute-start.1) | collective-permute-done | bytes 131104 | tf_op jit(solution)/shard_map/ppermute | solution.py:79
  19.1 0.0 copy-done.3
  19.2 1.0 %reduce-precision_convert_fusion = (bf16[64,1024]{1,0:T(8,128)(2,1)S(1)}, bf16[64,1024]{1,0:T(8,128)(2,1)S(1)}) fusion(f16[64,1024]{1,0:T(8,128)(2,1)} %collective-permute-done.1, f32[64,1024]{1,0:T(8,128)S(1)} %copy-done.3, f16[64,1024]{1,0:T(8,128)(2,1)S(1)} %collective-permute-done), kind=kLoop, calls=%fused_computation.7 | loop fusion | flops 655360 | bytes 786432 | tf_op jit(solution)/shard_map/convert_element_type | solution.py:60
  20.1 1.4 %fusion.4 = f32[128,256]{1,0:T(8,128)S(1)} fusion(bf16[1,256,1024]{2,1,0:T(8,128)(2,1)} %param.9, bf16[64,1024]{1,0:T(8,128)(2,1)S(1)} %get-tuple-element.16, bf16[64,1024]{1,0:T(8,128)(2,1)S(1)} %get-tuple-element.15), kind=kOutput, calls=%fused_computation.4 | convolution fusion | flops 67633152 | bytes 917504 | tf_op jit(solution)/shard_map/dot_general | solution.py:133
  21.5 0.1 collective-permute-start.2
  21.6 0.9 %reshape.24 = f32[64,4,64]{2,1,0:T(4,128)S(1)} reshape(f32[64,256]{1,0:T(8,128)} %fusion) | data formatting | bytes 131072 | tf_op jit(solution)/shard_map/reshape | solution.py:145
  22.6 0.3 collective-permute-done.2
  22.9 0.1 reshape.25
  23.0 0.4 %multiply_reduce_fusion = (f32[4]{0:T(128)S(1)}, f32[4,64,64]{2,1,0:T(8,128)S(1)}) fusion(f32[64,4,64]{2,1,0:T(4,128)S(1)} %reshape.25, f32[64,4,64]{2,1,0:T(4,128)S(1)} %reshape.24), kind=kOutput, calls=%fused_computation.26 | convolution fusion | flops 12615676 | bytes 196624 | tf_op jit(solution)/shard_map/ies,jes->eij/dot_general | solution.py:143
  23.4 0.1 reshape.26
  23.6 0.1 bitcast_dynamic-update-slice_fusion.3
  23.7 0.8 %collective-permute-start.3 = (f32[4,2048]{1,0:T(4,128)S(1)}, f32[4,2048]{1,0:T(4,128)S(1)}, u32[]{:S(2)}, u32[]{:S(2)}) collective-permute-start(f32[4,2048]{1,0:T(4,128)S(1)} %get-tuple-element.14), channel_id=1, source_target_pairs={{0,4},{4,0},{8,12},{12,8},{1,5},{5,1},{9,13},{13,9},{2,6},{6,2},{1... | collective-permute-start | bytes 98312 | tf_op jit(solution)/shard_map/ppermute | solution.py:96
  25.1 3.2 %collective-permute-start.4 = (f32[4,2048]{1,0:T(4,128)S(1)}, f32[4,2048]{1,0:T(4,128)S(1)}, u32[]{:S(2)}, u32[]{:S(2)}) collective-permute-start(f32[4,2048]{1,0:T(4,128)S(1)} %get-tuple-element.14), channel_id=1, source_target_pairs={{0,8},{4,12},{8,0},{12,4},{1,9},{5,13},{9,1},{13,5},{2,10},{6,14},... | collective-permute-start | bytes 98312 | tf_op jit(solution)/shard_map/ppermute | solution.py:96
  28.3 0.5 %collective-permute-start.5 = (f32[4,2048]{1,0:T(4,128)S(1)}, f32[4,2048]{1,0:T(4,128)S(1)}, u32[]{:S(2)}, u32[]{:S(2)}) collective-permute-start(f32[4,2048]{1,0:T(4,128)S(1)} %get-tuple-element.14), channel_id=1, source_target_pairs={{0,12},{4,8},{8,4},{12,0},{1,13},{5,9},{9,5},{13,1},{2,14},{6,10},... | collective-permute-start | bytes 98312 | tf_op jit(solution)/shard_map/ppermute | solution.py:96
  28.8 0.0 collective-permute-done.3
  28.8 1.4 %collective-permute-done.4 = f32[4,2048]{1,0:T(4,128)S(1)} collective-permute-done((f32[4,2048]{1,0:T(4,128)S(1)}, f32[4,2048]{1,0:T(4,128)S(1)}, u32[]{:S(2)}, u32[]{:S(2)}) %collective-permute-start.4) | collective-permute-done | bytes 32800 | tf_op jit(solution)/shard_map/ppermute | solution.py:96
  30.2 3.8 %collective-permute-done.5 = f32[4,2048]{1,0:T(4,128)S(1)} collective-permute-done((f32[4,2048]{1,0:T(4,128)S(1)}, f32[4,2048]{1,0:T(4,128)S(1)}, u32[]{:S(2)}, u32[]{:S(2)}) %collective-permute-start.5) | collective-permute-done | bytes 32800 | tf_op jit(solution)/shard_map/ppermute | solution.py:96
  34.1 0.3 fusion.11
  34.4 0.1 collective-permute-start.6
  34.5 1.5 %collective-permute-start.7 = (f32[16,256]{1,0:T(8,128)S(1)}, f32[16,256]{1,0:T(8,128)S(1)}, u32[]{:S(2)}, u32[]{:S(2)}) collective-permute-start(f32[16,256]{1,0:T(8,128)S(1)} %slice_add_fusion.1), channel_id=1, source_target_pairs={{0,2},{2,0},{1,3},{3,1},{4,6},{6,4},{5,7},{7,5},{8,10},{10,8},{9,1... | collective-permute-start | bytes 49160 | tf_op jit(solution)/shard_map/ppermute | solution.py:105
  36.1 0.3 collective-permute-start.8
  36.4 0.0 collective-permute-done.6
  36.4 1.9 %collective-permute-done.7 = f32[16,256]{1,0:T(8,128)S(1)} collective-permute-done((f32[16,256]{1,0:T(8,128)S(1)}, f32[16,256]{1,0:T(8,128)S(1)}, u32[]{:S(2)}, u32[]{:S(2)}) %collective-permute-start.7) | collective-permute-done | bytes 16416 | tf_op jit(solution)/shard_map/ppermute | solution.py:105
  38.3 0.9 %collective-permute-done.8 = f32[16,256]{1,0:T(8,128)S(1)} collective-permute-done((f32[16,256]{1,0:T(8,128)S(1)}, f32[16,256]{1,0:T(8,128)S(1)}, u32[]{:S(2)}, u32[]{:S(2)}) %collective-permute-start.8) | collective-permute-done | bytes 16416 | tf_op jit(solution)/shard_map/ppermute | solution.py:106
  39.2 0.6 %select_bitcast_fusion = f32[256,16]{0,1:T(8,128)} fusion(f32[16,256]{1,0:T(8,128)S(1)} %collective-permute-done.7, f32[16,256]{1,0:T(8,128)S(1)} %collective-permute-done.8, f32[16,256]{1,0:T(8,128)S(1)} %collective-permute-done.6, pred[256]{0:T(512)(128)(4,1)S(1)} %iota_compare_fusion, f32[32,256]{1,0:T(8,128)S(1)} %fusion.11), kind=kLoop, calls=%fused_computation.36 | loop fusion | flops 20480 | bytes 98560 | tf_op jit(solution)/shard_map/transpose | solution.py:159
  (11 shorter events, 0.2 us)
Async XLA Ops:
  0.0 1.6 %copy-start = (bf16[1,1024,1024]{2,1,0:T(8,128)(2,1)S(1)}, bf16[1,1024,1024]{2,1,0:T(8,128)(2,1)}, u32[]{:S(2)}) copy-start(bf16[1,1024,1024]{2,1,0:T(8,128)(2,1)} %param.10) | copy-start | bytes 6291460
  0.0 6.2 %copy-start.5 = (bf16[4096,64]{0,1:T(8,128)(2,1)S(1)}, bf16[4096,64]{0,1:T(8,128)(2,1)}, u32[]{:S(2)}) copy-start(bf16[4096,64]{0,1:T(8,128)(2,1)} %param.11) | copy-start | bytes 1572868
  1.6 4.7 %copy-start.4 = (bf16[1,256,4096]{2,1,0:T(8,128)(2,1)S(1)}, bf16[1,256,4096]{2,1,0:T(8,128)(2,1)}, u32[]{:S(2)}) copy-start(bf16[1,256,4096]{2,1,0:T(8,128)(2,1)} %param.8) | copy-start | bytes 6291460
  3.1 7.3 %copy-start.2 = (f32[64,1024]{1,0:T(8,128)}, f32[64,1024]{1,0:T(8,128)S(1)}, u32[]{:S(2)}) copy-start(f32[64,1024]{1,0:T(8,128)S(1)} %get-tuple-element.20) | copy-start | bytes 786436
  3.1 10.0 %copy-start.6 = (s32[256,1,256]{2,1,0:T(1,128)S(1)}, s32[256,1,256]{2,1,0:T(1,128)}, u32[]{:S(2)}) copy-start(s32[256,1,256]{2,1,0:T(1,128)} %param.14) | copy-start | bytes 786436
  3.2 6.6 %collective-permute-start = (f16[64,1024]{1,0:T(8,128)(2,1)S(1)}, f16[64,1024]{1,0:T(8,128)(2,1)S(1)}, u32[]{:S(2)}, u32[]{:S(2)}) collective-permute-start(f16[64,1024]{1,0:T(8,128)(2,1)S(1)} %get-tuple-element.19), channel_id=1, source_target_pairs={{0,4},{4,0},{8,12},{12,8},{1,5},{5,1},{9,13},{13,9},{2,6},{6,2},{1... | collective-permute-start | bytes 393224 | tf_op jit(solution)/shard_map/ppermute | solution.py:79
  10.4 8.7 %collective-permute-start.1 = (f16[64,1024]{1,0:T(8,128)(2,1)}, f16[64,1024]{1,0:T(8,128)(2,1)}, u32[]{:S(2)}, u32[]{:S(2)}) collective-permute-start(f16[64,1024]{1,0:T(8,128)(2,1)} %multiply_convert_fusion), channel_id=1, source_target_pairs={{0,8},{4,12},{8,0},{12,4},{1,9},{5,13},{9,1},{13,5},{2,10},{6,14},... | collective-permute-start | bytes 393224 | tf_op jit(solution)/shard_map/ppermute | solution.py:79
  13.3 1.2 %copy-start.1 = (bf16[256,256,8]{1,2,0:T(8,128)(2,1)S(1)}, bf16[256,256,8]{1,2,0:T(8,128)(2,1)}, u32[]{:S(2)}) copy-start(bf16[256,256,8]{1,2,0:T(8,128)(2,1)} %param.13) | copy-start | bytes 3145732
  14.6 4.6 %copy-start.3 = (f32[64,1024]{1,0:T(8,128)S(1)}, f32[64,1024]{1,0:T(8,128)}, u32[]{:S(2)}) copy-start(f32[64,1024]{1,0:T(8,128)} %copy-done.2) | copy-start | bytes 786436
  21.5 1.3 %collective-permute-start.2 = (f32[64,256]{1,0:T(8,128)S(1)}, f32[64,256]{1,0:T(8,128)S(1)}, u32[]{:S(2)}, u32[]{:S(2)}) collective-permute-start(f32[64,256]{1,0:T(8,128)S(1)} %slice_add_fusion), channel_id=1, source_target_pairs={{0,1},{1,0},{2,3},{3,2},{4,5},{5,4},{6,7},{7,6},{8,9},{9,8},{10,11... | collective-permute-start | bytes 196616 | tf_op jit(solution)/shard_map/ppermute | solution.py:141
  23.7 5.2 %collective-permute-start.3 = (f32[4,2048]{1,0:T(4,128)S(1)}, f32[4,2048]{1,0:T(4,128)S(1)}, u32[]{:S(2)}, u32[]{:S(2)}) collective-permute-start(f32[4,2048]{1,0:T(4,128)S(1)} %get-tuple-element.14), channel_id=1, source_target_pairs={{0,4},{4,0},{8,12},{12,8},{1,5},{5,1},{9,13},{13,9},{2,6},{6,2},{1... | collective-permute-start | bytes 98312 | tf_op jit(solution)/shard_map/ppermute | solution.py:96
  25.1 5.1 %collective-permute-start.4 = (f32[4,2048]{1,0:T(4,128)S(1)}, f32[4,2048]{1,0:T(4,128)S(1)}, u32[]{:S(2)}, u32[]{:S(2)}) collective-permute-start(f32[4,2048]{1,0:T(4,128)S(1)} %get-tuple-element.14), channel_id=1, source_target_pairs={{0,8},{4,12},{8,0},{12,4},{1,9},{5,13},{9,1},{13,5},{2,10},{6,14},... | collective-permute-start | bytes 98312 | tf_op jit(solution)/shard_map/ppermute | solution.py:96
  28.3 5.7 %collective-permute-start.5 = (f32[4,2048]{1,0:T(4,128)S(1)}, f32[4,2048]{1,0:T(4,128)S(1)}, u32[]{:S(2)}, u32[]{:S(2)}) collective-permute-start(f32[4,2048]{1,0:T(4,128)S(1)} %get-tuple-element.14), channel_id=1, source_target_pairs={{0,12},{4,8},{8,4},{12,0},{1,13},{5,9},{9,5},{13,1},{2,14},{6,10},... | collective-permute-start | bytes 98312 | tf_op jit(solution)/shard_map/ppermute | solution.py:96
  34.4 1.9 %collective-permute-start.6 = (f32[16,256]{1,0:T(8,128)S(1)}, f32[16,256]{1,0:T(8,128)S(1)}, u32[]{:S(2)}, u32[]{:S(2)}) collective-permute-start(f32[16,256]{1,0:T(8,128)S(1)} %slice_add_fusion.1), channel_id=1, source_target_pairs={{0,1},{1,0},{2,3},{3,2},{4,5},{5,4},{6,7},{7,6},{8,9},{9,8},{10,11... | collective-permute-start | bytes 49160 | tf_op jit(solution)/shard_map/ppermute | solution.py:104
  34.5 3.8 %collective-permute-start.7 = (f32[16,256]{1,0:T(8,128)S(1)}, f32[16,256]{1,0:T(8,128)S(1)}, u32[]{:S(2)}, u32[]{:S(2)}) collective-permute-start(f32[16,256]{1,0:T(8,128)S(1)} %slice_add_fusion.1), channel_id=1, source_target_pairs={{0,2},{2,0},{1,3},{3,1},{4,6},{6,4},{5,7},{7,5},{8,10},{10,8},{9,1... | collective-permute-start | bytes 49160 | tf_op jit(solution)/shard_map/ppermute | solution.py:105
  36.1 3.2 %collective-permute-start.8 = (f32[16,256]{1,0:T(8,128)S(1)}, f32[16,256]{1,0:T(8,128)S(1)}, u32[]{:S(2)}, u32[]{:S(2)}) collective-permute-start(f32[16,256]{1,0:T(8,128)S(1)} %slice_add_fusion.1), channel_id=1, source_target_pairs={{0,3},{1,2},{2,1},{3,0},{4,7},{5,6},{6,5},{7,4},{8,11},{9,10},{10,... | collective-permute-start | bytes 49160 | tf_op jit(solution)/shard_map/ppermute | solution.py:106

commit v3 on v2

--- a/solution.py
+++ b/solution.py
@@ -10,13 +10,17 @@
 LINK_SCALE = 1024.0
 
 
-def decode_kernel(codes_ref, book_ref, out_ref):
+def decode_kernel(codes_ref, book_ref, out_ref, ids_ref):
     subs, width, code_count = book_ref.shape
-    slots = codes_ref.shape[1]
+    slots = codes_ref.shape[0]
+    for left in range(0, slots, LANES):
+        for top in range(0, subs, LANES):
+            block = codes_ref[left : left + LANES, 0, top : top + LANES]
+            ids_ref[top : top + LANES, left : left + LANES] = jnp.transpose(block)
 
     def eight(step, carry):
         first = pl.multiple_of(step * 8, 8)
-        ids = codes_ref[pl.ds(first, 8), :]
+        ids = ids_ref[pl.ds(first, 8), :]
         low = ids & (LANES - 1)
         for pair in range(0, 8, 2):
             halves = []
@@ -41,18 +45,19 @@
     lax.fori_loop(0, subs // 8, eight, 0)
 
 
-def decode(codes_t, book_t):
-    subs, width, _ = book_t.shape
-    slots = codes_t.shape[1]
+def decode(codes, book_t):
+    slots, _, subs = codes.shape
+    width = book_t.shape[1]
     return pl.pallas_call(
         decode_kernel,
         out_shape=jax.ShapeDtypeStruct((subs * width, slots), jnp.bfloat16),
         in_specs=[pl.BlockSpec(memory_space=pltpu.VMEM)] * 2,
         out_specs=pl.BlockSpec(memory_space=pltpu.VMEM),
-        compiler_params=pltpu.CompilerParams(vmem_limit_bytes=16 * 1024 * 1024),
+        scratch_shapes=[pltpu.VMEM((subs, slots), jnp.int32)],
+        compiler_params=pltpu.CompilerParams(vmem_limit_bytes=8 * 1024 * 1024),
         cost_estimate=pl.CostEstimate(flops=0, bytes_accessed=2 * 1024 * 1024, transcendentals=0),
         name="decode",
-    )(codes_t, book_t)
+    )(codes, book_t)
 
 
 def split_high_low(x):
@@ -121,13 +126,16 @@
     folded = lax.dot_general(
         own_rows, kv_weight[0], (((0,), (0,)), ((), ())), preferred_element_type=jnp.float32
     )
-    folded, (in_side, decoded) = sum_over_dp(
+    folded, ((live, in_side), decoded) = sum_over_dp(
         folded,
         [
-            lambda: lax.dot_general(
-                proj_in, acts[0], (((0,), (1,)), ((), ())), preferred_element_type=jnp.float32
+            lambda: (
+                jnp.broadcast_to(live_rows, (8, train_local)).astype(jnp.float32),
+                lax.dot_general(
+                    proj_in, acts[0], (((0,), (1,)), ((), ())), preferred_element_type=jnp.float32
+                ),
             ),
-            lambda: decode(jnp.transpose(codes[:, 0, :]), jnp.transpose(codebook, (0, 2, 1))),
+            lambda: decode(codes, jnp.transpose(codebook, (0, 2, 1))),
         ],
     )
     out_side = lax.dot_general(
@@ -156,7 +164,7 @@
     )
     layer_scores = layer_scores[:tests_all] + layer_scores[tests_all:]
     total = sum_over_layer_sub(layer_scores)
-    return jnp.transpose(jnp.where(live_rows[None, :], total, jnp.float32(0.0)))
+    return jnp.transpose(jnp.where(live[:1] > 0.0, total, jnp.float32(0.0)))
 
 
 def solution(mesh):

time: 40.2 us -> 37.5 us (0.933)
  local copies, waits for them, and re-layouts: 4.24 us -> 2.05 us
  waiting for transfers between devices: 11.3 us -> 13 us
  matrix products: 5.02 us -> 3.33 us
  other arithmetic: 2.45 us -> 1.77 us
    unnamed x15 -> x12, local copies, waits for them, and re-layouts: 2.97 us -> 1.61 us
    dot_general x1, matrix products: 1.35 us -> 0.31 us  [per_device(): lax.dot_general(jnp.concatenate(split_high_low(folded), axis=0), kv_grad[...]
    ppermute x1, waiting for transfers between devices: 0.28 us -> 1.25 us  [per_device(): lax.ppermute(out_side, 'sub', partners(2, 1))]
    convert_element_type x2, other arithmetic: 1.01 us -> 0.11 us  [split_high_low(): return (high.astype(jnp.bfloat16), (x - high).astype(jnp.bfloat16))]
    add x1, other arithmetic: 0.01 us -> 0.85 us  [per_device(): out_side + lax.ppermute(out_side, 'sub', partners(2, 1))]
    reshape x1, local copies, waits for them, and re-layouts: 0.95 us -> 0.11 us  [per_device(): in_side.reshape(rank_dim, tests_local, SEQ)]
    ppermute x2, waiting for transfers between devices: 2.94 us -> 3.71 us  [sum_over_dp(): lax.ppermute((x * LINK_SCALE).astype(jnp.float16), 'dp', partners(size, s...]
    dot_general x1, matrix products: 1.41 us -> 0.76 us  [per_device(): lax.dot_general(proj_in, acts[0], (((0,), (1,)), ((), ())), preferred_ele...]
  transfers between devices with their start and end apart: 9 -> 9, of which waited for: 7 -> 7; matrix products, arithmetic and copies ran while one was open for 6% -> 2% of each run, Pallas kernels for 9% -> 10%
where the time goes in v3:
time: 37.5 us; the launch traced here: 37.3 us
  waiting for transfers between devices  13 us (35%)
  starting transfers between devices  12.4 us (33%)
  Pallas kernels  3.91 us (10%)
  matrix products  3.33 us (9%)
  local copies, waits for them, and re-layouts  2.05 us (5%)
  other arithmetic  1.77 us (5%)
  between operations  0.87 us (2%)
    ppermute x2, starting transfers between devices, sum_over_dp(): lax.ppermute((x * LINK_SCALE).astype(jnp.float16), 'dp', partners(size, s...  5.91 us
    ppermute x3, waiting for transfers between devices, gather_over_dp(): block = lax.ppermute(x, 'dp', partners(size, step))  5.2 us
    ppermute x3, starting transfers between devices, gather_over_dp(): block = lax.ppermute(x, 'dp', partners(size, step))  4.45 us
    pallas_call x1, Pallas kernels, decode(): pl.pallas_call(decode_kernel, out_shape=jax.ShapeDtypeStruct((subs * widt...  3.91 us
    ppermute x2, waiting for transfers between devices, sum_over_dp(): lax.ppermute((x * LINK_SCALE).astype(jnp.float16), 'dp', partners(size, s...  3.71 us
    ppermute x1, waiting for transfers between devices, sum_over_layer_sub(): by_layer = lax.ppermute(x, 'layer', partners(2, 1))  1.92 us
    unnamed x12, local copies, waits for them, and re-layouts  1.61 us
    ppermute x1, starting transfers between devices, sum_over_layer_sub(): by_layer = lax.ppermute(x, 'layer', partners(2, 1))  1.55 us
  transfers between devices with their start and end apart: 9, of which 7 were waited for; matrix products, arithmetic and copies ran while one was open for 2% of the time, Pallas kernels for 10%

profile of v3, /device:TPU:0, one launch (start us, length us, event | category | flops | bytes accessed | tf_op | source)
XLA Modules:
  0.0 37.3 jit_solution(2071218619459053669)
XLA Ops:
  0.0 0.0 copy-start
  0.0 0.0 copy-start.5
  0.0 1.6 %copy-done = bf16[1,1024,1024]{2,1,0:T(8,128)(2,1)S(1)} copy-done((bf16[1,1024,1024]{2,1,0:T(8,128)(2,1)S(1)}, bf16[1,1024,1024]{2,1,0:T(8,128)(2,1)}, u32[]{:S(2)}) %copy-start) | copy-done | bytes 2097176
  1.6 0.0 copy-start.3
  1.6 1.5 %multiply_convert_fusion.1 = (f16[64,1024]{1,0:T(8,128)(2,1)S(1)}, f32[64,1024]{1,0:T(8,128)S(1)}) fusion(bf16[1,1024,1024]{2,1,0:T(8,128)(2,1)S(1)} %copy-done, bf16[4096,64]{0,1:T(8,128)(2,1)} %param.12, s32[]{:T(128)S(6)} %select_n.23), kind=kOutput, calls=%fused_computation.15 | convolution fusion | flops 134348800 | bytes 2621444 | tf_op jit(solution)/shard_map/dot_general | solution.py:126
  3.1 0.0 copy-start.1
  3.1 0.0 copy-start.2
  3.2 3.1 %collective-permute-start = (f16[64,1024]{1,0:T(8,128)(2,1)S(1)}, f16[64,1024]{1,0:T(8,128)(2,1)S(1)}, u32[]{:S(2)}, u32[]{:S(2)}) collective-permute-start(f16[64,1024]{1,0:T(8,128)(2,1)S(1)} %get-tuple-element.21), channel_id=1, source_target_pairs={{0,4},{4,0},{8,12},{12,8},{1,5},{5,1},{9,13},{13,9},{2,6},{6,2},{1... | collective-permute-start | bytes 393224 | tf_op jit(solution)/shard_map/ppermute | solution.py:84
  6.2 0.0 copy-done.5
  6.3 0.0 copy-done.3
  6.3 0.8 %fusion = f32[64,256]{1,0:T(8,128)S(1)} fusion(bf16[4096,64]{0,1:T(8,128)(2,1)S(1)} %copy-done.5, bf16[1,256,4096]{2,1,0:T(8,128)(2,1)S(1)} %copy-done.3), kind=kOutput, calls=%fused_computation | convolution fusion | flops 134217728 | bytes 2686976 | tf_op jit(solution)/shard_map/dot_general | solution.py:134
  7.0 0.0 copy-start.4
  7.7 2.0 %collective-permute-done = f16[64,1024]{1,0:T(8,128)(2,1)S(1)} collective-permute-done((f16[64,1024]{1,0:T(8,128)(2,1)S(1)}, f16[64,1024]{1,0:T(8,128)(2,1)S(1)}, u32[]{:S(2)}, u32[]{:S(2)}) %collective-permute-start) | collective-permute-done | bytes 131104 | tf_op jit(solution)/shard_map/ppermute | solution.py:84
  9.7 0.1 multiply_convert_fusion
  9.8 2.8 %collective-permute-start.1 = (f16[64,1024]{1,0:T(8,128)(2,1)S(1)}, f16[64,1024]{1,0:T(8,128)(2,1)S(1)}, u32[]{:S(2)}, u32[]{:S(2)}) collective-permute-start(f16[64,1024]{1,0:T(8,128)(2,1)S(1)} %multiply_convert_fusion), channel_id=1, source_target_pairs={{0,8},{4,12},{8,0},{12,4},{1,9},{5,13},{9,1},{13,5},{2,10},{6,14},... | collective-permute-start | bytes 393224 | tf_op jit(solution)/shard_map/ppermute | solution.py:84
  12.6 0.0 copy-done.1
  12.6 0.0 copy-done.2
  12.6 3.9 %decode.1 = bf16[2048,256]{1,0:T(8,128)(2,1)S(1)} custom-call(s32[256,1,256]{2,1,0:T(1,128)S(1)} %copy-done.2, bf16[256,8,256]{2,1,0:T(8,128)(2,1)S(1)} %bitcast.26), custom_call_target="tpu_custom_call" | custom-call | bytes 2097152 | tf_op jit(solution)/shard_map/decode/pallas_call | solution.py:51
  16.5 1.7 %collective-permute-done.1 = f16[64,1024]{1,0:T(8,128)(2,1)S(1)} collective-permute-done((f16[64,1024]{1,0:T(8,128)(2,1)S(1)}, f16[64,1024]{1,0:T(8,128)(2,1)S(1)}, u32[]{:S(2)}, u32[]{:S(2)}) %collective-permute-start.1) | collective-permute-done | bytes 131104 | tf_op jit(solution)/shard_map/ppermute | solution.py:84
  18.3 0.1 reduce-precision_convert_fusion
  18.4 0.0 copy-done.4
  18.4 0.3 fusion.4
  18.7 0.1 collective-permute-start.2
  18.8 0.1 reshape.20
  18.9 1.3 %collective-permute-done.2 = f32[64,256]{1,0:T(8,128)} collective-permute-done((f32[64,256]{1,0:T(8,128)S(1)}, f32[64,256]{1,0:T(8,128)}, u32[]{:S(2)}, u32[]{:S(2)}) %collective-permute-start.2) | collective-permute-done | bytes 65568 | tf_op jit(solution)/shard_map/ppermute | solution.py:149
  20.2 0.9 %fusion.26 = f32[64,256]{1,0:T(8,128)S(1)} fusion(f32[64,256]{1,0:T(8,128)} %collective-permute-done.2, f32[128,256]{1,0:T(8,128)S(1)} %fusion.4), kind=kLoop, calls=%fused_computation.43 | loop fusion | flops 32768 | bytes 262144 | tf_op jit(solution)/shard_map/add | solution.py:149
  21.0 0.1 reshape.21
  21.1 0.4 %multiply_reduce_fusion = (f32[4]{0:T(128)S(1)}, f32[4,64,64]{2,1,0:T(8,128)S(1)}) fusion(f32[64,4,64]{2,1,0:T(4,128)S(1)} %reshape.21, f32[64,4,64]{2,1,0:T(4,128)S(1)} %reshape.20), kind=kOutput, calls=%fused_computation.26 | convolution fusion | flops 12615676 | bytes 196624 | tf_op jit(solution)/shard_map/ies,jes->eij/dot_general | solution.py:151
  21.6 0.1 reshape.22
  21.7 0.1 bitcast_dynamic-update-slice_fusion.3
  21.8 0.6 %collective-permute-start.3 = (f32[4,2048]{1,0:T(4,128)S(1)}, f32[4,2048]{1,0:T(4,128)S(1)}, u32[]{:S(2)}, u32[]{:S(2)}) collective-permute-start(f32[4,2048]{1,0:T(4,128)S(1)} %get-tuple-element.16), channel_id=1, source_target_pairs={{0,4},{4,0},{8,12},{12,8},{1,5},{5,1},{9,13},{13,9},{2,6},{6,2},{1... | collective-permute-start | bytes 98312 | tf_op jit(solution)/shard_map/ppermute | solution.py:101
  22.4 3.4 %collective-permute-start.4 = (f32[4,2048]{1,0:T(4,128)S(1)}, f32[4,2048]{1,0:T(4,128)S(1)}, u32[]{:S(2)}, u32[]{:S(2)}) collective-permute-start(f32[4,2048]{1,0:T(4,128)S(1)} %get-tuple-element.16), channel_id=1, source_target_pairs={{0,8},{4,12},{8,0},{12,4},{1,9},{5,13},{9,1},{13,5},{2,10},{6,14},... | collective-permute-start | bytes 98312 | tf_op jit(solution)/shard_map/ppermute | solution.py:101
  25.8 0.5 %collective-permute-start.5 = (f32[4,2048]{1,0:T(4,128)S(1)}, f32[4,2048]{1,0:T(4,128)S(1)}, u32[]{:S(2)}, u32[]{:S(2)}) collective-permute-start(f32[4,2048]{1,0:T(4,128)S(1)} %get-tuple-element.16), channel_id=1, source_target_pairs={{0,12},{4,8},{8,4},{12,0},{1,13},{5,9},{9,5},{13,1},{2,14},{6,10},... | collective-permute-start | bytes 98312 | tf_op jit(solution)/shard_map/ppermute | solution.py:101
  26.3 0.0 collective-permute-done.3
  26.3 1.4 %collective-permute-done.4 = f32[4,2048]{1,0:T(4,128)S(1)} collective-permute-done((f32[4,2048]{1,0:T(4,128)S(1)}, f32[4,2048]{1,0:T(4,128)S(1)}, u32[]{:S(2)}, u32[]{:S(2)}) %collective-permute-start.4) | collective-permute-done | bytes 32800 | tf_op jit(solution)/shard_map/ppermute | solution.py:101
  27.7 3.8 %collective-permute-done.5 = f32[4,2048]{1,0:T(4,128)S(1)} collective-permute-done((f32[4,2048]{1,0:T(4,128)S(1)}, f32[4,2048]{1,0:T(4,128)S(1)}, u32[]{:S(2)}, u32[]{:S(2)}) %collective-permute-start.5) | collective-permute-done | bytes 32800 | tf_op jit(solution)/shard_map/ppermute | solution.py:101
  31.6 0.3 fusion.11
  31.9 0.1 collective-permute-start.6
  32.0 1.5 %collective-permute-start.7 = (f32[16,256]{1,0:T(8,128)S(1)}, f32[16,256]{1,0:T(8,128)S(1)}, u32[]{:S(2)}, u32[]{:S(2)}) collective-permute-start(f32[16,256]{1,0:T(8,128)S(1)} %slice_add_fusion.1), channel_id=1, source_target_pairs={{0,2},{2,0},{1,3},{3,1},{4,6},{6,4},{5,7},{7,5},{8,10},{10,8},{9,1... | collective-permute-start | bytes 49160 | tf_op jit(solution)/shard_map/ppermute | solution.py:110
  33.5 0.3 collective-permute-start.8
  33.8 0.0 collective-permute-done.6
  33.8 1.9 %collective-permute-done.7 = f32[16,256]{1,0:T(8,128)S(1)} collective-permute-done((f32[16,256]{1,0:T(8,128)S(1)}, f32[16,256]{1,0:T(8,128)S(1)}, u32[]{:S(2)}, u32[]{:S(2)}) %collective-permute-start.7) | collective-permute-done | bytes 16416 | tf_op jit(solution)/shard_map/ppermute | solution.py:110
  35.8 0.9 %collective-permute-done.8 = f32[16,256]{1,0:T(8,128)S(1)} collective-permute-done((f32[16,256]{1,0:T(8,128)S(1)}, f32[16,256]{1,0:T(8,128)S(1)}, u32[]{:S(2)}, u32[]{:S(2)}) %collective-permute-start.8) | collective-permute-done | bytes 16416 | tf_op jit(solution)/shard_map/ppermute | solution.py:111
  36.7 0.6 %select_bitcast_fusion = f32[256,16]{0,1:T(8,128)} fusion(f32[16,256]{1,0:T(8,128)S(1)} %collective-permute-done.7, f32[16,256]{1,0:T(8,128)S(1)} %collective-permute-done.8, f32[16,256]{1,0:T(8,128)S(1)} %collective-permute-done.6, pred[256]{0:T(512)(128)(4,1)S(1)} %compare_reduce_fusion, f32[32,256]{1,0:T(8,128)S(1)} %fusion.11), kind=kLoop, calls=%fused_computation.36 | loop fusion | flops 20480 | bytes 98560 | tf_op jit(solution)/shard_map/transpose | solution.py:167
  (12 shorter events, 0.2 us)
Async XLA Ops:
  0.0 1.6 %copy-start = (bf16[1,1024,1024]{2,1,0:T(8,128)(2,1)S(1)}, bf16[1,1024,1024]{2,1,0:T(8,128)(2,1)}, u32[]{:S(2)}) copy-start(bf16[1,1024,1024]{2,1,0:T(8,128)(2,1)} %param.10) | copy-start | bytes 6291460
  0.0 6.2 %copy-start.5 = (bf16[4096,64]{0,1:T(8,128)(2,1)S(1)}, bf16[4096,64]{0,1:T(8,128)(2,1)}, u32[]{:S(2)}) copy-start(bf16[4096,64]{0,1:T(8,128)(2,1)} %param.11) | copy-start | bytes 1572868
  1.6 4.7 %copy-start.3 = (bf16[1,256,4096]{2,1,0:T(8,128)(2,1)S(1)}, bf16[1,256,4096]{2,1,0:T(8,128)(2,1)}, u32[]{:S(2)}) copy-start(bf16[1,256,4096]{2,1,0:T(8,128)(2,1)} %param.8) | copy-start | bytes 6291460
  3.1 9.5 %copy-start.1 = (bf16[256,256,8]{1,2,0:T(8,128)(2,1)S(1)}, bf16[256,256,8]{1,2,0:T(8,128)(2,1)}, u32[]{:S(2)}) copy-start(bf16[256,256,8]{1,2,0:T(8,128)(2,1)} %param.13) | copy-start | bytes 3145732
  3.1 9.5 %copy-start.2 = (s32[256,1,256]{2,1,0:T(1,128)S(1)}, s32[256,1,256]{2,1,0:T(1,128)}, u32[]{:S(2)}) copy-start(s32[256,1,256]{2,1,0:T(1,128)} %codes_ref.1) | copy-start | bytes 786436
  3.2 6.6 %collective-permute-start = (f16[64,1024]{1,0:T(8,128)(2,1)S(1)}, f16[64,1024]{1,0:T(8,128)(2,1)S(1)}, u32[]{:S(2)}, u32[]{:S(2)}) collective-permute-start(f16[64,1024]{1,0:T(8,128)(2,1)S(1)} %get-tuple-element.21), channel_id=1, source_target_pairs={{0,4},{4,0},{8,12},{12,8},{1,5},{5,1},{9,13},{13,9},{2,6},{6,2},{1... | collective-permute-start | bytes 393224 | tf_op jit(solution)/shard_map/ppermute | solution.py:84
  7.0 11.3 %copy-start.4 = (bf16[1,256,1024]{2,1,0:T(8,128)(2,1)S(1)}, bf16[1,256,1024]{2,1,0:T(8,128)(2,1)}, u32[]{:S(2)}) copy-start(bf16[1,256,1024]{2,1,0:T(8,128)(2,1)} %param.9) | copy-start | bytes 1572868
  9.8 8.5 %collective-permute-start.1 = (f16[64,1024]{1,0:T(8,128)(2,1)S(1)}, f16[64,1024]{1,0:T(8,128)(2,1)S(1)}, u32[]{:S(2)}, u32[]{:S(2)}) collective-permute-start(f16[64,1024]{1,0:T(8,128)(2,1)S(1)} %multiply_convert_fusion), channel_id=1, source_target_pairs={{0,8},{4,12},{8,0},{12,4},{1,9},{5,13},{9,1},{13,5},{2,10},{6,14},... | collective-permute-start | bytes 393224 | tf_op jit(solution)/shard_map/ppermute | solution.py:84
  18.7 1.5 %collective-permute-start.2 = (f32[64,256]{1,0:T(8,128)S(1)}, f32[64,256]{1,0:T(8,128)}, u32[]{:S(2)}, u32[]{:S(2)}) collective-permute-start(f32[64,256]{1,0:T(8,128)S(1)} %slice_add_fusion), channel_id=1, source_target_pairs={{0,1},{1,0},{2,3},{3,2},{4,5},{5,4},{6,7},{7,6},{8,9},{9,8},{10,11... | collective-permute-start | bytes 196616 | tf_op jit(solution)/shard_map/ppermute | solution.py:149
  21.8 4.5 %collective-permute-start.3 = (f32[4,2048]{1,0:T(4,128)S(1)}, f32[4,2048]{1,0:T(4,128)S(1)}, u32[]{:S(2)}, u32[]{:S(2)}) collective-permute-start(f32[4,2048]{1,0:T(4,128)S(1)} %get-tuple-element.16), channel_id=1, source_target_pairs={{0,4},{4,0},{8,12},{12,8},{1,5},{5,1},{9,13},{13,9},{2,6},{6,2},{1... | collective-permute-start | bytes 98312 | tf_op jit(solution)/shard_map/ppermute | solution.py:101
  22.4 5.3 %collective-permute-start.4 = (f32[4,2048]{1,0:T(4,128)S(1)}, f32[4,2048]{1,0:T(4,128)S(1)}, u32[]{:S(2)}, u32[]{:S(2)}) collective-permute-start(f32[4,2048]{1,0:T(4,128)S(1)} %get-tuple-element.16), channel_id=1, source_target_pairs={{0,8},{4,12},{8,0},{12,4},{1,9},{5,13},{9,1},{13,5},{2,10},{6,14},... | collective-permute-start | bytes 98312 | tf_op jit(solution)/shard_map/ppermute | solution.py:101
  25.8 5.7 %collective-permute-start.5 = (f32[4,2048]{1,0:T(4,128)S(1)}, f32[4,2048]{1,0:T(4,128)S(1)}, u32[]{:S(2)}, u32[]{:S(2)}) collective-permute-start(f32[4,2048]{1,0:T(4,128)S(1)} %get-tuple-element.16), channel_id=1, source_target_pairs={{0,12},{4,8},{8,4},{12,0},{1,13},{5,9},{9,5},{13,1},{2,14},{6,10},... | collective-permute-start | bytes 98312 | tf_op jit(solution)/shard_map/ppermute | solution.py:101
  31.9 2.0 %collective-permute-start.6 = (f32[16,256]{1,0:T(8,128)S(1)}, f32[16,256]{1,0:T(8,128)S(1)}, u32[]{:S(2)}, u32[]{:S(2)}) collective-permute-start(f32[16,256]{1,0:T(8,128)S(1)} %slice_add_fusion.1), channel_id=1, source_target_pairs={{0,1},{1,0},{2,3},{3,2},{4,5},{5,4},{6,7},{7,6},{8,9},{9,8},{10,11... | collective-permute-start | bytes 49160 | tf_op jit(solution)/shard_map/ppermute | solution.py:109
  32.0 3.8 %collective-permute-start.7 = (f32[16,256]{1,0:T(8,128)S(1)}, f32[16,256]{1,0:T(8,128)S(1)}, u32[]{:S(2)}, u32[]{:S(2)}) collective-permute-start(f32[16,256]{1,0:T(8,128)S(1)} %slice_add_fusion.1), channel_id=1, source_target_pairs={{0,2},{2,0},{1,3},{3,1},{4,6},{6,4},{5,7},{7,5},{8,10},{10,8},{9,1... | collective-permute-start | bytes 49160 | tf_op jit(solution)/shard_map/ppermute | solution.py:110
  33.5 3.2 %collective-permute-start.8 = (f32[16,256]{1,0:T(8,128)S(1)}, f32[16,256]{1,0:T(8,128)S(1)}, u32[]{:S(2)}, u32[]{:S(2)}) collective-permute-start(f32[16,256]{1,0:T(8,128)S(1)} %slice_add_fusion.1), channel_id=1, source_target_pairs={{0,3},{1,2},{2,1},{3,0},{4,7},{5,6},{6,5},{7,4},{8,11},{9,10},{10,... | collective-permute-start | bytes 49160 | tf_op jit(solution)/shard_map/ppermute | solution.py:111

commit v4 on v3

--- a/solution.py
+++ b/solution.py
@@ -8,6 +8,7 @@
 SEQ = 64
 LANES = 128
 LINK_SCALE = 1024.0
+VECTOR_SCALE = 16384.0
 
 
 def decode_kernel(codes_ref, book_ref, out_ref, ids_ref):
@@ -60,6 +61,51 @@
     )(codes, book_t)
 
 
+def vectors_kernel(in_ref, own_ref, other_ref, out_ref, grads_ref, flat_ref):
+    rank_dim, tokens = in_ref.shape
+    tests, dims = out_ref.shape
+    pairs = rank_dim // 2
+    tall = dims // LANES
+    in_side = in_ref[...]
+    test_of = lax.broadcasted_iota(jnp.int32, in_side.shape, 1) // SEQ
+    grads_ref[:, :rank_dim] = lax.dot_general(
+        jnp.concatenate([jnp.where(test_of == test, in_side, 0.0) for test in range(tests)], axis=0),
+        own_ref[...] + other_ref[...],
+        (((1,), (1,)), ((), ())),
+        precision=lax.Precision.HIGHEST,
+        preferred_element_type=jnp.float32,
+    )
+    for test in range(tests):
+        even = grads_ref[pl.ds(test * rank_dim, pairs, stride=2), :][:, :rank_dim]
+        odd = grads_ref[pl.ds(test * rank_dim + 1, pairs, stride=2), :][:, :rank_dim]
+        both = jnp.concatenate([even, odd], axis=1)
+        squares = jnp.sum(jnp.sum(both * both, axis=0, keepdims=True), axis=1, keepdims=True)
+        mean = squares * (1.0 / (rank_dim * rank_dim))
+        flat_ref[test * pairs : (test + 1) * pairs, :] = both * (lax.rsqrt(mean + 1e-06) / rank_dim)
+    first = lax.axis_index("sub") * tall
+    for row in range(tall):
+        out_ref[:, row * LANES : (row + 1) * LANES] = flat_ref[
+            pl.ds(first + row, tests, stride=pairs), :
+        ]
+
+
+def make_vectors(in_side, own, other, dims_local):
+    rank_dim, tokens = in_side.shape
+    tests = tokens // SEQ
+    return pl.pallas_call(
+        vectors_kernel,
+        out_shape=jax.ShapeDtypeStruct((tests, dims_local), jnp.float32),
+        in_specs=[pl.BlockSpec(memory_space=pltpu.VMEM)] * 3,
+        out_specs=pl.BlockSpec(memory_space=pltpu.VMEM),
+        scratch_shapes=[
+            pltpu.VMEM((tests * rank_dim, LANES), jnp.float32),
+            pltpu.VMEM((tests * rank_dim // 2, LANES), jnp.float32),
+        ],
+        compiler_params=pltpu.CompilerParams(vmem_limit_bytes=4 * 1024 * 1024),
+        name="vectors",
+    )(in_side, own, other)
+
+
 def split_high_low(x):
     high = lax.reduce_precision(x, 8, 7)
     return high.astype(jnp.bfloat16), (x - high).astype(jnp.bfloat16)
@@ -113,18 +159,19 @@
 
 
 def per_device(acts, kv_grad, kv_weight, proj_in, proj_out, codebook, codes, counts):
-    tok_local = acts.shape[1]
     rank_dim = proj_in.shape[1]
     sub_local, code_count, sub_width = codebook.shape
     train_local = codes.shape[0]
-    tests_local = tok_local // SEQ
-    rows_local = kv_weight.shape[1]
     dims_local = sub_local * sub_width
     live_rows = jnp.arange(train_local, dtype=jnp.int32) < counts[0]
 
+    rows_local = kv_weight.shape[1]
     own_rows = lax.dynamic_slice_in_dim(proj_out, lax.axis_index("dp") * rows_local, rows_local, 0)
     folded = lax.dot_general(
-        own_rows, kv_weight[0], (((0,), (0,)), ((), ())), preferred_element_type=jnp.float32
+        own_rows,
+        kv_weight[0],
+        (((0,), (0,)), ((), ())),
+        preferred_element_type=jnp.float32,
     )
     folded, ((live, in_side), decoded) = sum_over_dp(
         folded,
@@ -145,18 +192,12 @@
         preferred_element_type=jnp.float32,
     )
     out_side = out_side[:rank_dim] + out_side[rank_dim:]
-    out_side = lax.psum(out_side, "sub") if lax.axis_size("sub") != 2 else (
-        out_side + lax.ppermute(out_side, "sub", partners(2, 1))
-    )
-    grads = jnp.einsum(
-        "ies,jes->eij",
-        in_side.reshape(rank_dim, tests_local, SEQ),
-        out_side.reshape(rank_dim, tests_local, SEQ),
-        precision=lax.Precision.HIGHEST,
-    ).reshape(tests_local, rank_dim * rank_dim)
-    vectors = grads * lax.rsqrt(jnp.mean(grads * grads, axis=1, keepdims=True) + 1e-06) / rank_dim
-    own_part = lax.dynamic_slice_in_dim(vectors, lax.axis_index("sub") * dims_local, dims_local, 1)
-    every = gather_over_dp(own_part).reshape(-1, dims_local)
+    other_side = lax.psum(out_side, "sub") - out_side if lax.axis_size("sub") != 2 else (
+        lax.ppermute(out_side, "sub", partners(2, 1))
+    )
+    vectors = make_vectors(in_side, out_side, other_side, dims_local)
+    every = gather_over_dp((vectors * VECTOR_SCALE).astype(jnp.float16))
+    every = every.reshape(-1, dims_local).astype(jnp.float32) * (1.0 / VECTOR_SCALE)
     tests_all = every.shape[0]
 
     layer_scores = jnp.dot(

time: 37.5 us -> 36.2 us (0.965)
  other arithmetic: 1.77 us -> 0.87 us
  Pallas kernels: 3.91 us -> 4.49 us
  matrix products: 3.33 us -> 2.89 us
    add x1 -> x0, other arithmetic: 0.85 us -> none  [per_device(): out_side + lax.ppermute(out_side, 'sub', partners(2, 1))]
    pallas_call x0 -> x1, Pallas kernels: none -> 0.57 us  [make_vectors(): pl.pallas_call(vectors_kernel, out_shape=jax.ShapeDtypeStruct((tests, dim...]
    dot_general x1 -> x0, matrix products: 0.44 us -> none  [per_device(): jnp.einsum('ies,jes->eij', in_side.reshape(rank_dim, tests_local, SEQ), o...]
    reshape x4 -> x0, local copies, waits for them, and re-layouts: 0.38 us -> none  [the longest x1 0.11 us: per_device(): in_side.reshape(rank_dim, tests_local, SEQ)]
  transfers between devices with their start and end apart: 9 -> 9, of which waited for: 7 -> 7; matrix products, arithmetic and copies ran while one was open for 2% -> 2% of each run, Pallas kernels for 10% -> 11%
where the time goes in v4:
time: 36.2 us; the launch traced here: 36 us
  waiting for transfers between devices  12.8 us (35%)
  starting transfers between devices  12.4 us (34%)
  Pallas kernels  4.49 us (12%)
  matrix products  2.89 us (8%)
  local copies, waits for them, and re-layouts  1.74 us (5%)
  other arithmetic  0.87 us (2%)
  between operations  0.86 us (2%)
    ppermute x2, starting transfers between devices, sum_over_dp(): lax.ppermute((x * LINK_SCALE).astype(jnp.float16), 'dp', partners(size, s...  5.91 us
    ppermute x3, waiting for transfers between devices, gather_over_dp(): block = lax.ppermute(x, 'dp', partners(size, step))  5.01 us
    ppermute x3, starting transfers between devices, gather_over_dp(): block = lax.ppermute(x, 'dp', partners(size, step))  4.45 us
    pallas_call x1, Pallas kernels, decode(): pl.pallas_call(decode_kernel, out_shape=jax.ShapeDtypeStruct((subs * widt...  3.91 us
    ppermute x2, waiting for transfers between devices, sum_over_dp(): lax.ppermute((x * LINK_SCALE).astype(jnp.float16), 'dp', partners(size, s...  3.71 us
    ppermute x1, waiting for transfers between devices, sum_over_layer_sub(): by_layer = lax.ppermute(x, 'layer', partners(2, 1))  1.92 us
    unnamed x12, local copies, waits for them, and re-layouts  1.61 us
    ppermute x1, starting transfers between devices, sum_over_layer_sub(): by_layer = lax.ppermute(x, 'layer', partners(2, 1))  1.55 us
  transfers between devices with their start and end apart: 9, of which 7 were waited for; matrix products, arithmetic and copies ran while one was open for 2% of the time, Pallas kernels for 11%

profile of v4, /device:TPU:0, one launch (start us, length us, event | category | flops | bytes accessed | tf_op | source)
XLA Modules:
  0.0 36.0 jit_solution(291020862182115687)
XLA Ops:
  0.0 0.0 copy-start
  0.0 0.0 copy-start.5
  0.0 1.6 %copy-done = bf16[1,1024,1024]{2,1,0:T(8,128)(2,1)S(1)} copy-done((bf16[1,1024,1024]{2,1,0:T(8,128)(2,1)S(1)}, bf16[1,1024,1024]{2,1,0:T(8,128)(2,1)}, u32[]{:S(2)}) %copy-start) | copy-done | bytes 2097176
  1.6 0.0 copy-start.3
  1.6 1.5 %multiply_convert_fusion.1 = (f16[64,1024]{1,0:T(8,128)(2,1)S(1)}, f32[64,1024]{1,0:T(8,128)S(1)}) fusion(bf16[1,1024,1024]{2,1,0:T(8,128)(2,1)S(1)} %copy-done, bf16[4096,64]{0,1:T(8,128)(2,1)} %param.12, s32[]{:T(128)S(6)} %select_n.20), kind=kOutput, calls=%fused_computation.15 | convolution fusion | flops 134348800 | bytes 2621444 | tf_op jit(solution)/shard_map/dot_general | solution.py:170
  3.1 0.0 copy-start.1
  3.1 0.0 copy-start.2
  3.2 3.1 %collective-permute-start = (f16[64,1024]{1,0:T(8,128)(2,1)S(1)}, f16[64,1024]{1,0:T(8,128)(2,1)S(1)}, u32[]{:S(2)}, u32[]{:S(2)}) collective-permute-start(f16[64,1024]{1,0:T(8,128)(2,1)S(1)} %get-tuple-element.21), channel_id=1, source_target_pairs={{0,4},{4,0},{8,12},{12,8},{1,5},{5,1},{9,13},{13,9},{2,6},{6,2},{1... | collective-permute-start | bytes 393224 | tf_op jit(solution)/shard_map/ppermute | solution.py:130
  6.2 0.0 copy-done.5
  6.3 0.0 copy-done.3
  6.3 0.8 %fusion.in_ref = f32[64,256]{1,0:T(8,128)S(1)} fusion(bf16[4096,64]{0,1:T(8,128)(2,1)S(1)} %copy-done.5, bf16[1,256,4096]{2,1,0:T(8,128)(2,1)S(1)} %copy-done.3), kind=kOutput, calls=%fused_computation | convolution fusion | flops 134217728 | bytes 2686976 | tf_op jit(solution)/shard_map/dot_general | solution.py:181
  7.0 0.0 copy-start.4
  7.7 2.0 %collective-permute-done = f16[64,1024]{1,0:T(8,128)(2,1)S(1)} collective-permute-done((f16[64,1024]{1,0:T(8,128)(2,1)S(1)}, f16[64,1024]{1,0:T(8,128)(2,1)S(1)}, u32[]{:S(2)}, u32[]{:S(2)}) %collective-permute-start) | collective-permute-done | bytes 131104 | tf_op jit(solution)/shard_map/ppermute | solution.py:130
  9.7 0.1 multiply_convert_fusion
  9.8 2.8 %collective-permute-start.1 = (f16[64,1024]{1,0:T(8,128)(2,1)S(1)}, f16[64,1024]{1,0:T(8,128)(2,1)S(1)}, u32[]{:S(2)}, u32[]{:S(2)}) collective-permute-start(f16[64,1024]{1,0:T(8,128)(2,1)S(1)} %multiply_convert_fusion), channel_id=1, source_target_pairs={{0,8},{4,12},{8,0},{12,4},{1,9},{5,13},{9,1},{13,5},{2,10},{6,14},... | collective-permute-start | bytes 393224 | tf_op jit(solution)/shard_map/ppermute | solution.py:130
  12.6 0.0 copy-done.1
  12.6 0.0 copy-done.2
  12.6 3.9 %decode.1 = bf16[2048,256]{1,0:T(8,128)(2,1)S(1)} custom-call(s32[256,1,256]{2,1,0:T(1,128)S(1)} %copy-done.2, bf16[256,8,256]{2,1,0:T(8,128)(2,1)S(1)} %bitcast.26), custom_call_target="tpu_custom_call" | custom-call | bytes 2097152 | tf_op jit(solution)/shard_map/decode/pallas_call | solution.py:52
  16.5 1.7 %collective-permute-done.1 = f16[64,1024]{1,0:T(8,128)(2,1)S(1)} collective-permute-done((f16[64,1024]{1,0:T(8,128)(2,1)S(1)}, f16[64,1024]{1,0:T(8,128)(2,1)S(1)}, u32[]{:S(2)}, u32[]{:S(2)}) %collective-permute-start.1) | collective-permute-done | bytes 131104 | tf_op jit(solution)/shard_map/ppermute | solution.py:130
  18.3 0.1 reduce-precision_convert_fusion
  18.3 0.0 copy-done.4
  18.4 0.3 fusion.4
  18.7 0.1 collective-permute-start.2
  18.8 1.2 %collective-permute-done.2.other_ref = f32[64,256]{1,0:T(8,128)S(1)} collective-permute-done((f32[64,256]{1,0:T(8,128)S(1)}, f32[64,256]{1,0:T(8,128)S(1)}, u32[]{:S(2)}, u32[]{:S(2)}) %collective-permute-start.2) | collective-permute-done | bytes 65568 | tf_op jit(solution)/shard_map/ppermute | solution.py:196
  20.0 0.6 %vectors.1 = f32[4,2048]{1,0:T(4,128)S(1)} custom-call(f32[64,256]{1,0:T(8,128)S(1)} %fusion.in_ref, f32[64,256]{1,0:T(8,128)S(1)} %slice_add_fusion.own_ref, f32[64,256]{1,0:T(8,128)S(1)} %collective-permute-done.2.other_ref), custom_call_target="tpu_custom_call" | custom-call | tf_op jit(solution)/shard_map/vectors/pallas_call | solution.py:95
  20.7 0.6 %collective-permute-start.3 = (f16[4,2048]{1,0:T(4,128)(2,1)S(1)}, f16[4,2048]{1,0:T(4,128)(2,1)S(1)}, u32[]{:S(2)}, u32[]{:S(2)}) collective-permute-start(f16[4,2048]{1,0:T(4,128)(2,1)S(1)} %get-tuple-element.16), channel_id=1, source_target_pairs={{0,4},{4,0},{8,12},{12,8},{1,5},{5,1},{9,13},{13,9},{2,6},{6,2},{1... | collective-permute-start | bytes 49160 | tf_op jit(solution)/shard_map/ppermute | solution.py:147
  21.2 3.4 %collective-permute-start.4 = (f16[4,2048]{1,0:T(4,128)(2,1)S(1)}, f16[4,2048]{1,0:T(4,128)(2,1)S(1)}, u32[]{:S(2)}, u32[]{:S(2)}) collective-permute-start(f16[4,2048]{1,0:T(4,128)(2,1)S(1)} %get-tuple-element.16), channel_id=1, source_target_pairs={{0,8},{4,12},{8,0},{12,4},{1,9},{5,13},{9,1},{13,5},{2,10},{6,14},... | collective-permute-start | bytes 49160 | tf_op jit(solution)/shard_map/ppermute | solution.py:147
  24.6 0.5 %collective-permute-start.5 = (f16[4,2048]{1,0:T(4,128)(2,1)S(1)}, f16[4,2048]{1,0:T(4,128)(2,1)S(1)}, u32[]{:S(2)}, u32[]{:S(2)}) collective-permute-start(f16[4,2048]{1,0:T(4,128)(2,1)S(1)} %get-tuple-element.16), channel_id=1, source_target_pairs={{0,12},{4,8},{8,4},{12,0},{1,13},{5,9},{9,5},{13,1},{2,14},{6,10},... | collective-permute-start | bytes 49160 | tf_op jit(solution)/shard_map/ppermute | solution.py:147
  25.1 0.0 collective-permute-done.3
  25.1 1.2 %collective-permute-done.4 = f16[4,2048]{1,0:T(4,128)(2,1)S(1)} collective-permute-done((f16[4,2048]{1,0:T(4,128)(2,1)S(1)}, f16[4,2048]{1,0:T(4,128)(2,1)S(1)}, u32[]{:S(2)}, u32[]{:S(2)}) %collective-permute-start.4) | collective-permute-done | bytes 16416 | tf_op jit(solution)/shard_map/ppermute | solution.py:147
  26.3 3.8 %collective-permute-done.5 = f16[4,2048]{1,0:T(4,128)(2,1)S(1)} collective-permute-done((f16[4,2048]{1,0:T(4,128)(2,1)S(1)}, f16[4,2048]{1,0:T(4,128)(2,1)S(1)}, u32[]{:S(2)}, u32[]{:S(2)}) %collective-permute-start.5) | collective-permute-done | bytes 16416 | tf_op jit(solution)/shard_map/ppermute | solution.py:147
  30.3 0.3 fusion.11
  30.6 0.1 collective-permute-start.6
  30.7 1.6 %collective-permute-start.7 = (f32[16,256]{1,0:T(8,128)S(1)}, f32[16,256]{1,0:T(8,128)S(1)}, u32[]{:S(2)}, u32[]{:S(2)}) collective-permute-start(f32[16,256]{1,0:T(8,128)S(1)} %slice_add_fusion.1), channel_id=1, source_target_pairs={{0,2},{2,0},{1,3},{3,1},{4,6},{6,4},{5,7},{7,5},{8,10},{10,8},{9,1... | collective-permute-start | bytes 49160 | tf_op jit(solution)/shard_map/ppermute | solution.py:156
  32.2 0.3 collective-permute-start.8
  32.6 0.0 collective-permute-done.6
  32.6 1.9 %collective-permute-done.7 = f32[16,256]{1,0:T(8,128)S(1)} collective-permute-done((f32[16,256]{1,0:T(8,128)S(1)}, f32[16,256]{1,0:T(8,128)S(1)}, u32[]{:S(2)}, u32[]{:S(2)}) %collective-permute-start.7) | collective-permute-done | bytes 16416 | tf_op jit(solution)/shard_map/ppermute | solution.py:156
  34.5 0.9 %collective-permute-done.8 = f32[16,256]{1,0:T(8,128)S(1)} collective-permute-done((f32[16,256]{1,0:T(8,128)S(1)}, f32[16,256]{1,0:T(8,128)S(1)}, u32[]{:S(2)}, u32[]{:S(2)}) %collective-permute-start.8) | collective-permute-done | bytes 16416 | tf_op jit(solution)/shard_map/ppermute | solution.py:157
  35.4 0.6 %select_bitcast_fusion = f32[256,16]{0,1:T(8,128)} fusion(f32[16,256]{1,0:T(8,128)S(1)} %collective-permute-done.7, f32[16,256]{1,0:T(8,128)S(1)} %collective-permute-done.8, f32[16,256]{1,0:T(8,128)S(1)} %collective-permute-done.6, pred[256]{0:T(512)(128)(4,1)S(1)} %compare_reduce_fusion, f32[32,256]{1,0:T(8,128)S(1)} %fusion.11), kind=kLoop, calls=%fused_computation.32 | loop fusion | flops 20480 | bytes 98560 | tf_op jit(solution)/shard_map/transpose | solution.py:208
  (13 shorter events, 0.2 us)
Async XLA Ops:
  0.0 1.6 %copy-start = (bf16[1,1024,1024]{2,1,0:T(8,128)(2,1)S(1)}, bf16[1,1024,1024]{2,1,0:T(8,128)(2,1)}, u32[]{:S(2)}) copy-start(bf16[1,1024,1024]{2,1,0:T(8,128)(2,1)} %param.10) | copy-start | bytes 6291460
  0.0 6.2 %copy-start.5 = (bf16[4096,64]{0,1:T(8,128)(2,1)S(1)}, bf16[4096,64]{0,1:T(8,128)(2,1)}, u32[]{:S(2)}) copy-start(bf16[4096,64]{0,1:T(8,128)(2,1)} %param.11) | copy-start | bytes 1572868
  1.6 4.7 %copy-start.3 = (bf16[1,256,4096]{2,1,0:T(8,128)(2,1)S(1)}, bf16[1,256,4096]{2,1,0:T(8,128)(2,1)}, u32[]{:S(2)}) copy-start(bf16[1,256,4096]{2,1,0:T(8,128)(2,1)} %param.8) | copy-start | bytes 6291460
  3.1 9.5 %copy-start.1 = (bf16[256,256,8]{1,2,0:T(8,128)(2,1)S(1)}, bf16[256,256,8]{1,2,0:T(8,128)(2,1)}, u32[]{:S(2)}) copy-start(bf16[256,256,8]{1,2,0:T(8,128)(2,1)} %param.13) | copy-start | bytes 3145732
  3.1 9.5 %copy-start.2 = (s32[256,1,256]{2,1,0:T(1,128)S(1)}, s32[256,1,256]{2,1,0:T(1,128)}, u32[]{:S(2)}) copy-start(s32[256,1,256]{2,1,0:T(1,128)} %codes_ref.1) | copy-start | bytes 786436
  3.2 6.6 %collective-permute-start = (f16[64,1024]{1,0:T(8,128)(2,1)S(1)}, f16[64,1024]{1,0:T(8,128)(2,1)S(1)}, u32[]{:S(2)}, u32[]{:S(2)}) collective-permute-start(f16[64,1024]{1,0:T(8,128)(2,1)S(1)} %get-tuple-element.21), channel_id=1, source_target_pairs={{0,4},{4,0},{8,12},{12,8},{1,5},{5,1},{9,13},{13,9},{2,6},{6,2},{1... | collective-permute-start | bytes 393224 | tf_op jit(solution)/shard_map/ppermute | solution.py:130
  7.0 11.3 %copy-start.4 = (bf16[1,256,1024]{2,1,0:T(8,128)(2,1)S(1)}, bf16[1,256,1024]{2,1,0:T(8,128)(2,1)}, u32[]{:S(2)}) copy-start(bf16[1,256,1024]{2,1,0:T(8,128)(2,1)} %param.9) | copy-start | bytes 1572868
  9.8 8.5 %collective-permute-start.1 = (f16[64,1024]{1,0:T(8,128)(2,1)S(1)}, f16[64,1024]{1,0:T(8,128)(2,1)S(1)}, u32[]{:S(2)}, u32[]{:S(2)}) collective-permute-start(f16[64,1024]{1,0:T(8,128)(2,1)S(1)} %multiply_convert_fusion), channel_id=1, source_target_pairs={{0,8},{4,12},{8,0},{12,4},{1,9},{5,13},{9,1},{13,5},{2,10},{6,14},... | collective-permute-start | bytes 393224 | tf_op jit(solution)/shard_map/ppermute | solution.py:130
  18.7 1.3 %collective-permute-start.2 = (f32[64,256]{1,0:T(8,128)S(1)}, f32[64,256]{1,0:T(8,128)S(1)}, u32[]{:S(2)}, u32[]{:S(2)}) collective-permute-start(f32[64,256]{1,0:T(8,128)S(1)} %slice_add_fusion.own_ref), channel_id=1, source_target_pairs={{0,1},{1,0},{2,3},{3,2},{4,5},{5,4},{6,7},{7,6},{8,9},{9,8},{10,11... | collective-permute-start | bytes 196616 | tf_op jit(solution)/shard_map/ppermute | solution.py:196
  20.7 4.5 %collective-permute-start.3 = (f16[4,2048]{1,0:T(4,128)(2,1)S(1)}, f16[4,2048]{1,0:T(4,128)(2,1)S(1)}, u32[]{:S(2)}, u32[]{:S(2)}) collective-permute-start(f16[4,2048]{1,0:T(4,128)(2,1)S(1)} %get-tuple-element.16), channel_id=1, source_target_pairs={{0,4},{4,0},{8,12},{12,8},{1,5},{5,1},{9,13},{13,9},{2,6},{6,2},{1... | collective-permute-start | bytes 49160 | tf_op jit(solution)/shard_map/ppermute | solution.py:147
  21.2 5.1 %collective-permute-start.4 = (f16[4,2048]{1,0:T(4,128)(2,1)S(1)}, f16[4,2048]{1,0:T(4,128)(2,1)S(1)}, u32[]{:S(2)}, u32[]{:S(2)}) collective-permute-start(f16[4,2048]{1,0:T(4,128)(2,1)S(1)} %get-tuple-element.16), channel_id=1, source_target_pairs={{0,8},{4,12},{8,0},{12,4},{1,9},{5,13},{9,1},{13,5},{2,10},{6,14},... | collective-permute-start | bytes 49160 | tf_op jit(solution)/shard_map/ppermute | solution.py:147
  24.6 5.5 %collective-permute-start.5 = (f16[4,2048]{1,0:T(4,128)(2,1)S(1)}, f16[4,2048]{1,0:T(4,128)(2,1)S(1)}, u32[]{:S(2)}, u32[]{:S(2)}) collective-permute-start(f16[4,2048]{1,0:T(4,128)(2,1)S(1)} %get-tuple-element.16), channel_id=1, source_target_pairs={{0,12},{4,8},{8,4},{12,0},{1,13},{5,9},{9,5},{13,1},{2,14},{6,10},... | collective-permute-start | bytes 49160 | tf_op jit(solution)/shard_map/ppermute | solution.py:147
  30.6 2.0 %collective-permute-start.6 = (f32[16,256]{1,0:T(8,128)S(1)}, f32[16,256]{1,0:T(8,128)S(1)}, u32[]{:S(2)}, u32[]{:S(2)}) collective-permute-start(f32[16,256]{1,0:T(8,128)S(1)} %slice_add_fusion.1), channel_id=1, source_target_pairs={{0,1},{1,0},{2,3},{3,2},{4,5},{5,4},{6,7},{7,6},{8,9},{9,8},{10,11... | collective-permute-start | bytes 49160 | tf_op jit(solution)/shard_map/ppermute | solution.py:155
  30.7 3.8 %collective-permute-start.7 = (f32[16,256]{1,0:T(8,128)S(1)}, f32[16,256]{1,0:T(8,128)S(1)}, u32[]{:S(2)}, u32[]{:S(2)}) collective-permute-start(f32[16,256]{1,0:T(8,128)S(1)} %slice_add_fusion.1), channel_id=1, source_target_pairs={{0,2},{2,0},{1,3},{3,1},{4,6},{6,4},{5,7},{7,5},{8,10},{10,8},{9,1... | collective-permute-start | bytes 49160 | tf_op jit(solution)/shard_map/ppermute | solution.py:156
  32.2 3.2 %collective-permute-start.8 = (f32[16,256]{1,0:T(8,128)S(1)}, f32[16,256]{1,0:T(8,128)S(1)}, u32[]{:S(2)}, u32[]{:S(2)}) collective-permute-start(f32[16,256]{1,0:T(8,128)S(1)} %slice_add_fusion.1), channel_id=1, source_target_pairs={{0,3},{1,2},{2,1},{3,0},{4,7},{5,6},{6,5},{7,4},{8,11},{9,10},{10,... | collective-permute-start | bytes 49160 | tf_op jit(solution)/shard_map/ppermute | solution.py:157

commit v5 on v4

--- a/solution.py
+++ b/solution.py
@@ -1,3 +1,5 @@
+import math
+
 import jax
 import jax.numpy as jnp
 from jax import lax
@@ -19,31 +21,33 @@
             block = codes_ref[left : left + LANES, 0, top : top + LANES]
             ids_ref[top : top + LANES, left : left + LANES] = jnp.transpose(block)
 
-    def eight(step, carry):
-        first = pl.multiple_of(step * 8, 8)
-        ids = ids_ref[pl.ds(first, 8), :]
-        low = ids & (LANES - 1)
-        for pair in range(0, 8, 2):
-            halves = []
-            for sub in (pair, pair + 1):
-                table = book_ref[first + sub].astype(jnp.float32)
-                columns = []
-                for left in range(0, slots, LANES):
-                    own = jnp.broadcast_to(ids[sub : sub + 1, left : left + LANES], (width, LANES))
-                    spot = jnp.broadcast_to(low[sub : sub + 1, left : left + LANES], (width, LANES))
-                    picked = None
-                    for part in range(0, code_count, LANES):
-                        found = jnp.take_along_axis(
-                            table[:, part : part + LANES], spot, axis=1, mode="promise_in_bounds"
-                        )
-                        picked = found if picked is None else jnp.where(own >= part, found, picked)
-                    columns.append(picked)
-                halves.append(jnp.concatenate(columns, axis=1))
-            rows = pl.multiple_of((first + pair) * width, 2 * width)
-            out_ref[pl.ds(rows, 2 * width), :] = jnp.concatenate(halves, axis=0).astype(jnp.bfloat16)
+    group = math.gcd(subs, 64)
+
+    def several(step, carry):
+        first = pl.multiple_of(step * group, group)
+        for top in range(0, group, 8):
+            ids = ids_ref[pl.ds(pl.multiple_of(first + top, 8), 8), :]
+            for pair in range(0, 8, 2):
+                halves = []
+                for sub in (pair, pair + 1):
+                    table = book_ref[first + top + sub].astype(jnp.float32)
+                    columns = []
+                    for left in range(0, slots, LANES):
+                        own = jnp.broadcast_to(ids[sub : sub + 1, left : left + LANES], (width, LANES))
+                        spot = own & (LANES - 1)
+                        picked = None
+                        for part in range(0, code_count, LANES):
+                            found = jnp.take_along_axis(
+                                table[:, part : part + LANES], spot, axis=1, mode="promise_in_bounds"
+                            )
+                            picked = found if picked is None else jnp.where(own >= part, found, picked)
+                        columns.append(picked)
+                    halves.append(jnp.concatenate(columns, axis=1))
+                rows = pl.multiple_of((first + top + pair) * width, 2 * width)
+                out_ref[pl.ds(rows, 2 * width), :] = jnp.concatenate(halves, axis=0).astype(jnp.bfloat16)
         return carry
 
-    lax.fori_loop(0, subs // 8, eight, 0)
+    lax.fori_loop(0, subs // group, several, 0)
 
 
 def decode(codes, book_t):
@@ -143,7 +147,7 @@
     own = lax.axis_index("dp")
     got = jnp.zeros((size,) + x.shape, x.dtype)
     got = lax.dynamic_update_index_in_dim(got, x, own, 0)
-    for step in range(1, size):
+    for step in (2, 3, 1):
         block = lax.ppermute(x, "dp", partners(size, step))
         got = lax.dynamic_update_index_in_dim(got, block, own ^ step, 0)
     return got

time: 36.2 us -> 33.9 us (0.936)
  Pallas kernels: 4.49 us -> 2.49 us
  starting transfers between devices: 12.4 us -> 11.9 us
    ppermute x2, waiting for transfers between devices: 3.71 us -> 5.71 us  [sum_over_dp(): lax.ppermute((x * LINK_SCALE).astype(jnp.float16), 'dp', partners(size, s...]
    pallas_call x1, Pallas kernels: 3.91 us -> 1.92 us  [decode(): pl.pallas_call(decode_kernel, out_shape=jax.ShapeDtypeStruct((subs * widt...]
    ppermute x3, waiting for transfers between devices: 5.01 us -> 3.23 us  [gather_over_dp(): block = lax.ppermute(x, 'dp', partners(size, step))]
    ppermute x3, starting transfers between devices: 4.45 us -> 3.96 us  [gather_over_dp(): block = lax.ppermute(x, 'dp', partners(size, step))]
  transfers between devices with their start and end apart: 9 -> 9, of which waited for: 7 -> 8; matrix products, arithmetic and copies ran while one was open for 2% -> 2% of each run, Pallas kernels for 11% -> 6%
where the time goes in v5:
time: 33.9 us; the launch traced here: 33.7 us
  waiting for transfers between devices  13 us (38%)
  starting transfers between devices  11.9 us (35%)
  matrix products  2.89 us (9%)
  Pallas kernels  2.49 us (7%)
  local copies, waits for them, and re-layouts  1.74 us (5%)
  other arithmetic  0.87 us (3%)
  between operations  0.86 us (3%)
    ppermute x2, starting transfers between devices, sum_over_dp(): lax.ppermute((x * LINK_SCALE).astype(jnp.float16), 'dp', partners(size, s...  5.91 us
    ppermute x2, waiting for transfers between devices, sum_over_dp(): lax.ppermute((x * LINK_SCALE).astype(jnp.float16), 'dp', partners(size, s...  5.71 us
    ppermute x3, starting transfers between devices, gather_over_dp(): block = lax.ppermute(x, 'dp', partners(size, step))  3.96 us
    ppermute x3, waiting for transfers between devices, gather_over_dp(): block = lax.ppermute(x, 'dp', partners(size, step))  3.23 us
    ppermute x1, waiting for transfers between devices, sum_over_layer_sub(): by_layer = lax.ppermute(x, 'layer', partners(2, 1))  1.92 us
    pallas_call x1, Pallas kernels, decode(): pl.pallas_call(decode_kernel, out_shape=jax.ShapeDtypeStruct((subs * widt...  1.92 us
    unnamed x12, local copies, waits for them, and re-layouts  1.61 us
    ppermute x1, starting transfers between devices, sum_over_layer_sub(): by_layer = lax.ppermute(x, 'layer', partners(2, 1))  1.55 us
  transfers between devices with their start and end apart: 9, of which 8 were waited for; matrix products, arithmetic and copies ran while one was open for 2% of the time, Pallas kernels for 6%

profile of v5, /device:TPU:0, one launch (start us, length us, event | category | flops | bytes accessed | tf_op | source)
XLA Modules:
  0.0 33.7 jit_solution(1500052980561292224)
XLA Ops:
  0.0 0.0 copy-start
  0.0 0.0 copy-start.5
  0.0 1.6 %copy-done = bf16[1,1024,1024]{2,1,0:T(8,128)(2,1)S(1)} copy-done((bf16[1,1024,1024]{2,1,0:T(8,128)(2,1)S(1)}, bf16[1,1024,1024]{2,1,0:T(8,128)(2,1)}, u32[]{:S(2)}) %copy-start) | copy-done | bytes 2097176
  1.6 0.0 copy-start.3
  1.6 1.5 %multiply_convert_fusion.1 = (f16[64,1024]{1,0:T(8,128)(2,1)S(1)}, f32[64,1024]{1,0:T(8,128)S(1)}) fusion(bf16[1,1024,1024]{2,1,0:T(8,128)(2,1)S(1)} %copy-done, bf16[4096,64]{0,1:T(8,128)(2,1)} %param.12, s32[]{:T(128)S(6)} %select_n.20), kind=kOutput, calls=%fused_computation.15 | convolution fusion | flops 134348800 | bytes 2621444 | tf_op jit(solution)/shard_map/dot_general | solution.py:174
  3.1 0.0 copy-start.1
  3.1 0.0 copy-start.2
  3.2 3.1 %collective-permute-start = (f16[64,1024]{1,0:T(8,128)(2,1)S(1)}, f16[64,1024]{1,0:T(8,128)(2,1)S(1)}, u32[]{:S(2)}, u32[]{:S(2)}) collective-permute-start(f16[64,1024]{1,0:T(8,128)(2,1)S(1)} %get-tuple-element.21), channel_id=1, source_target_pairs={{0,4},{4,0},{8,12},{12,8},{1,5},{5,1},{9,13},{13,9},{2,6},{6,2},{1... | collective-permute-start | bytes 393224 | tf_op jit(solution)/shard_map/ppermute | solution.py:134
  6.2 0.0 copy-done.5
  6.3 0.0 copy-done.3
  6.3 0.8 %fusion.in_ref = f32[64,256]{1,0:T(8,128)S(1)} fusion(bf16[4096,64]{0,1:T(8,128)(2,1)S(1)} %copy-done.5, bf16[1,256,4096]{2,1,0:T(8,128)(2,1)S(1)} %copy-done.3), kind=kOutput, calls=%fused_computation | convolution fusion | flops 134217728 | bytes 2686976 | tf_op jit(solution)/shard_map/dot_general | solution.py:185
  7.0 0.0 copy-start.4
  7.7 2.0 %collective-permute-done = f16[64,1024]{1,0:T(8,128)(2,1)S(1)} collective-permute-done((f16[64,1024]{1,0:T(8,128)(2,1)S(1)}, f16[64,1024]{1,0:T(8,128)(2,1)S(1)}, u32[]{:S(2)}, u32[]{:S(2)}) %collective-permute-start) | collective-permute-done | bytes 131104 | tf_op jit(solution)/shard_map/ppermute | solution.py:134
  9.7 0.1 multiply_convert_fusion
  9.8 2.8 %collective-permute-start.1 = (f16[64,1024]{1,0:T(8,128)(2,1)S(1)}, f16[64,1024]{1,0:T(8,128)(2,1)S(1)}, u32[]{:S(2)}, u32[]{:S(2)}) collective-permute-start(f16[64,1024]{1,0:T(8,128)(2,1)S(1)} %multiply_convert_fusion), channel_id=1, source_target_pairs={{0,8},{4,12},{8,0},{12,4},{1,9},{5,13},{9,1},{13,5},{2,10},{6,14},... | collective-permute-start | bytes 393224 | tf_op jit(solution)/shard_map/ppermute | solution.py:134
  12.6 0.0 copy-done.1
  12.6 0.0 copy-done.2
  12.6 1.9 %decode.1 = bf16[2048,256]{1,0:T(8,128)(2,1)S(1)} custom-call(s32[256,1,256]{2,1,0:T(1,128)S(1)} %copy-done.2, bf16[256,8,256]{2,1,0:T(8,128)(2,1)S(1)} %bitcast.26), custom_call_target="tpu_custom_call" | custom-call | bytes 2097152 | tf_op jit(solution)/shard_map/decode/pallas_call | solution.py:56
  14.5 3.7 %collective-permute-done.1 = f16[64,1024]{1,0:T(8,128)(2,1)S(1)} collective-permute-done((f16[64,1024]{1,0:T(8,128)(2,1)S(1)}, f16[64,1024]{1,0:T(8,128)(2,1)S(1)}, u32[]{:S(2)}, u32[]{:S(2)}) %collective-permute-start.1) | collective-permute-done | bytes 131104 | tf_op jit(solution)/shard_map/ppermute | solution.py:134
  18.3 0.1 reduce-precision_convert_fusion
  18.3 0.0 copy-done.4
  18.4 0.3 fusion.4
  18.7 0.1 collective-permute-start.2
  18.8 1.2 %collective-permute-done.2.other_ref = f32[64,256]{1,0:T(8,128)S(1)} collective-permute-done((f32[64,256]{1,0:T(8,128)S(1)}, f32[64,256]{1,0:T(8,128)S(1)}, u32[]{:S(2)}, u32[]{:S(2)}) %collective-permute-start.2) | collective-permute-done | bytes 65568 | tf_op jit(solution)/shard_map/ppermute | solution.py:200
  20.0 0.6 %vectors.1 = f32[4,2048]{1,0:T(4,128)S(1)} custom-call(f32[64,256]{1,0:T(8,128)S(1)} %fusion.in_ref, f32[64,256]{1,0:T(8,128)S(1)} %slice_add_fusion.own_ref, f32[64,256]{1,0:T(8,128)S(1)} %collective-permute-done.2.other_ref), custom_call_target="tpu_custom_call" | custom-call | tf_op jit(solution)/shard_map/vectors/pallas_call | solution.py:99
  20.7 0.4 %collective-permute-start.3 = (f16[4,2048]{1,0:T(4,128)(2,1)S(1)}, f16[4,2048]{1,0:T(4,128)(2,1)S(1)}, u32[]{:S(2)}, u32[]{:S(2)}) collective-permute-start(f16[4,2048]{1,0:T(4,128)(2,1)S(1)} %get-tuple-element.16), channel_id=1, source_target_pairs={{0,8},{4,12},{8,0},{12,4},{1,9},{5,13},{9,1},{13,5},{2,10},{6,14},... | collective-permute-start | bytes 49160 | tf_op jit(solution)/shard_map/ppermute | solution.py:151
  21.0 3.1 %collective-permute-start.4 = (f16[4,2048]{1,0:T(4,128)(2,1)S(1)}, f16[4,2048]{1,0:T(4,128)(2,1)S(1)}, u32[]{:S(2)}, u32[]{:S(2)}) collective-permute-start(f16[4,2048]{1,0:T(4,128)(2,1)S(1)} %get-tuple-element.16), channel_id=1, source_target_pairs={{0,12},{4,8},{8,4},{12,0},{1,13},{5,9},{9,5},{13,1},{2,14},{6,10},... | collective-permute-start | bytes 49160 | tf_op jit(solution)/shard_map/ppermute | solution.py:151
  24.1 0.5 %collective-permute-start.5 = (f16[4,2048]{1,0:T(4,128)(2,1)S(1)}, f16[4,2048]{1,0:T(4,128)(2,1)S(1)}, u32[]{:S(2)}, u32[]{:S(2)}) collective-permute-start(f16[4,2048]{1,0:T(4,128)(2,1)S(1)} %get-tuple-element.16), channel_id=1, source_target_pairs={{0,4},{4,0},{8,12},{12,8},{1,5},{5,1},{9,13},{13,9},{2,6},{6,2},{1... | collective-permute-start | bytes 49160 | tf_op jit(solution)/shard_map/ppermute | solution.py:151
  24.6 1.0 %collective-permute-done.3 = f16[4,2048]{1,0:T(4,128)(2,1)S(1)} collective-permute-done((f16[4,2048]{1,0:T(4,128)(2,1)S(1)}, f16[4,2048]{1,0:T(4,128)(2,1)S(1)}, u32[]{:S(2)}, u32[]{:S(2)}) %collective-permute-start.3) | collective-permute-done | bytes 16416 | tf_op jit(solution)/shard_map/ppermute | solution.py:151
  25.6 1.0 %collective-permute-done.4 = f16[4,2048]{1,0:T(4,128)(2,1)S(1)} collective-permute-done((f16[4,2048]{1,0:T(4,128)(2,1)S(1)}, f16[4,2048]{1,0:T(4,128)(2,1)S(1)}, u32[]{:S(2)}, u32[]{:S(2)}) %collective-permute-start.4) | collective-permute-done | bytes 16416 | tf_op jit(solution)/shard_map/ppermute | solution.py:151
  26.6 1.3 %collective-permute-done.5 = f16[4,2048]{1,0:T(4,128)(2,1)S(1)} collective-permute-done((f16[4,2048]{1,0:T(4,128)(2,1)S(1)}, f16[4,2048]{1,0:T(4,128)(2,1)S(1)}, u32[]{:S(2)}, u32[]{:S(2)}) %collective-permute-start.5) | collective-permute-done | bytes 16416 | tf_op jit(solution)/shard_map/ppermute | solution.py:151
  28.0 0.3 fusion.11
  28.3 0.1 collective-permute-start.6
  28.4 1.6 %collective-permute-start.7 = (f32[16,256]{1,0:T(8,128)S(1)}, f32[16,256]{1,0:T(8,128)S(1)}, u32[]{:S(2)}, u32[]{:S(2)}) collective-permute-start(f32[16,256]{1,0:T(8,128)S(1)} %slice_add_fusion.1), channel_id=1, source_target_pairs={{0,2},{2,0},{1,3},{3,1},{4,6},{6,4},{5,7},{7,5},{8,10},{10,8},{9,1... | collective-permute-start | bytes 49160 | tf_op jit(solution)/shard_map/ppermute | solution.py:160
  30.0 0.3 collective-permute-start.8
  30.3 0.0 collective-permute-done.6
  30.3 1.9 %collective-permute-done.7 = f32[16,256]{1,0:T(8,128)S(1)} collective-permute-done((f32[16,256]{1,0:T(8,128)S(1)}, f32[16,256]{1,0:T(8,128)S(1)}, u32[]{:S(2)}, u32[]{:S(2)}) %collective-permute-start.7) | collective-permute-done | bytes 16416 | tf_op jit(solution)/shard_map/ppermute | solution.py:160
  32.2 0.9 %collective-permute-done.8 = f32[16,256]{1,0:T(8,128)S(1)} collective-permute-done((f32[16,256]{1,0:T(8,128)S(1)}, f32[16,256]{1,0:T(8,128)S(1)}, u32[]{:S(2)}, u32[]{:S(2)}) %collective-permute-start.8) | collective-permute-done | bytes 16416 | tf_op jit(solution)/shard_map/ppermute | solution.py:161
  33.1 0.6 %select_bitcast_fusion = f32[256,16]{0,1:T(8,128)} fusion(f32[16,256]{1,0:T(8,128)S(1)} %collective-permute-done.7, f32[16,256]{1,0:T(8,128)S(1)} %collective-permute-done.8, f32[16,256]{1,0:T(8,128)S(1)} %collective-permute-done.6, pred[256]{0:T(512)(128)(4,1)S(1)} %compare_reduce_fusion, f32[32,256]{1,0:T(8,128)S(1)} %fusion.11), kind=kLoop, calls=%fused_computation.32 | loop fusion | flops 20480 | bytes 98560 | tf_op jit(solution)/shard_map/transpose | solution.py:212
  (13 shorter events, 0.2 us)
Async XLA Ops:
  0.0 1.6 %copy-start = (bf16[1,1024,1024]{2,1,0:T(8,128)(2,1)S(1)}, bf16[1,1024,1024]{2,1,0:T(8,128)(2,1)}, u32[]{:S(2)}) copy-start(bf16[1,1024,1024]{2,1,0:T(8,128)(2,1)} %param.10) | copy-start | bytes 6291460
  0.0 6.2 %copy-start.5 = (bf16[4096,64]{0,1:T(8,128)(2,1)S(1)}, bf16[4096,64]{0,1:T(8,128)(2,1)}, u32[]{:S(2)}) copy-start(bf16[4096,64]{0,1:T(8,128)(2,1)} %param.11) | copy-start | bytes 1572868
  1.6 4.7 %copy-start.3 = (bf16[1,256,4096]{2,1,0:T(8,128)(2,1)S(1)}, bf16[1,256,4096]{2,1,0:T(8,128)(2,1)}, u32[]{:S(2)}) copy-start(bf16[1,256,4096]{2,1,0:T(8,128)(2,1)} %param.8) | copy-start | bytes 6291460
  3.1 9.5 %copy-start.1 = (bf16[256,256,8]{1,2,0:T(8,128)(2,1)S(1)}, bf16[256,256,8]{1,2,0:T(8,128)(2,1)}, u32[]{:S(2)}) copy-start(bf16[256,256,8]{1,2,0:T(8,128)(2,1)} %param.13) | copy-start | bytes 3145732
  3.1 9.5 %copy-start.2 = (s32[256,1,256]{2,1,0:T(1,128)S(1)}, s32[256,1,256]{2,1,0:T(1,128)}, u32[]{:S(2)}) copy-start(s32[256,1,256]{2,1,0:T(1,128)} %codes_ref.1) | copy-start | bytes 786436
  3.2 6.6 %collective-permute-start = (f16[64,1024]{1,0:T(8,128)(2,1)S(1)}, f16[64,1024]{1,0:T(8,128)(2,1)S(1)}, u32[]{:S(2)}, u32[]{:S(2)}) collective-permute-start(f16[64,1024]{1,0:T(8,128)(2,1)S(1)} %get-tuple-element.21), channel_id=1, source_target_pairs={{0,4},{4,0},{8,12},{12,8},{1,5},{5,1},{9,13},{13,9},{2,6},{6,2},{1... | collective-permute-start | bytes 393224 | tf_op jit(solution)/shard_map/ppermute | solution.py:134
  7.0 11.3 %copy-start.4 = (bf16[1,256,1024]{2,1,0:T(8,128)(2,1)S(1)}, bf16[1,256,1024]{2,1,0:T(8,128)(2,1)}, u32[]{:S(2)}) copy-start(bf16[1,256,1024]{2,1,0:T(8,128)(2,1)} %param.9) | copy-start | bytes 1572868
  9.8 8.5 %collective-permute-start.1 = (f16[64,1024]{1,0:T(8,128)(2,1)S(1)}, f16[64,1024]{1,0:T(8,128)(2,1)S(1)}, u32[]{:S(2)}, u32[]{:S(2)}) collective-permute-start(f16[64,1024]{1,0:T(8,128)(2,1)S(1)} %multiply_convert_fusion), channel_id=1, source_target_pairs={{0,8},{4,12},{8,0},{12,4},{1,9},{5,13},{9,1},{13,5},{2,10},{6,14},... | collective-permute-start | bytes 393224 | tf_op jit(solution)/shard_map/ppermute | solution.py:134
  18.7 1.3 %collective-permute-start.2 = (f32[64,256]{1,0:T(8,128)S(1)}, f32[64,256]{1,0:T(8,128)S(1)}, u32[]{:S(2)}, u32[]{:S(2)}) collective-permute-start(f32[64,256]{1,0:T(8,128)S(1)} %slice_add_fusion.own_ref), channel_id=1, source_target_pairs={{0,1},{1,0},{2,3},{3,2},{4,5},{5,4},{6,7},{7,6},{8,9},{9,8},{10,11... | collective-permute-start | bytes 196616 | tf_op jit(solution)/shard_map/ppermute | solution.py:200
  20.7 4.9 %collective-permute-start.3 = (f16[4,2048]{1,0:T(4,128)(2,1)S(1)}, f16[4,2048]{1,0:T(4,128)(2,1)S(1)}, u32[]{:S(2)}, u32[]{:S(2)}) collective-permute-start(f16[4,2048]{1,0:T(4,128)(2,1)S(1)} %get-tuple-element.16), channel_id=1, source_target_pairs={{0,8},{4,12},{8,0},{12,4},{1,9},{5,13},{9,1},{13,5},{2,10},{6,14},... | collective-permute-start | bytes 49160 | tf_op jit(solution)/shard_map/ppermute | solution.py:151
  21.0 5.5 %collective-permute-start.4 = (f16[4,2048]{1,0:T(4,128)(2,1)S(1)}, f16[4,2048]{1,0:T(4,128)(2,1)S(1)}, u32[]{:S(2)}, u32[]{:S(2)}) collective-permute-start(f16[4,2048]{1,0:T(4,128)(2,1)S(1)} %get-tuple-element.16), channel_id=1, source_target_pairs={{0,12},{4,8},{8,4},{12,0},{1,13},{5,9},{9,5},{13,1},{2,14},{6,10},... | collective-permute-start | bytes 49160 | tf_op jit(solution)/shard_map/ppermute | solution.py:151
  24.1 3.7 %collective-permute-start.5 = (f16[4,2048]{1,0:T(4,128)(2,1)S(1)}, f16[4,2048]{1,0:T(4,128)(2,1)S(1)}, u32[]{:S(2)}, u32[]{:S(2)}) collective-permute-start(f16[4,2048]{1,0:T(4,128)(2,1)S(1)} %get-tuple-element.16), channel_id=1, source_target_pairs={{0,4},{4,0},{8,12},{12,8},{1,5},{5,1},{9,13},{13,9},{2,6},{6,2},{1... | collective-permute-start | bytes 49160 | tf_op jit(solution)/shard_map/ppermute | solution.py:151
  28.3 2.0 %collective-permute-start.6 = (f32[16,256]{1,0:T(8,128)S(1)}, f32[16,256]{1,0:T(8,128)S(1)}, u32[]{:S(2)}, u32[]{:S(2)}) collective-permute-start(f32[16,256]{1,0:T(8,128)S(1)} %slice_add_fusion.1), channel_id=1, source_target_pairs={{0,1},{1,0},{2,3},{3,2},{4,5},{5,4},{6,7},{7,6},{8,9},{9,8},{10,11... | collective-permute-start | bytes 49160 | tf_op jit(solution)/shard_map/ppermute | solution.py:159
  28.4 3.8 %collective-permute-start.7 = (f32[16,256]{1,0:T(8,128)S(1)}, f32[16,256]{1,0:T(8,128)S(1)}, u32[]{:S(2)}, u32[]{:S(2)}) collective-permute-start(f32[16,256]{1,0:T(8,128)S(1)} %slice_add_fusion.1), channel_id=1, source_target_pairs={{0,2},{2,0},{1,3},{3,1},{4,6},{6,4},{5,7},{7,5},{8,10},{10,8},{9,1... | collective-permute-start | bytes 49160 | tf_op jit(solution)/shard_map/ppermute | solution.py:160
  30.0 3.2 %collective-permute-start.8 = (f32[16,256]{1,0:T(8,128)S(1)}, f32[16,256]{1,0:T(8,128)S(1)}, u32[]{:S(2)}, u32[]{:S(2)}) collective-permute-start(f32[16,256]{1,0:T(8,128)S(1)} %slice_add_fusion.1), channel_id=1, source_target_pairs={{0,3},{1,2},{2,1},{3,0},{4,7},{5,6},{6,5},{7,4},{8,11},{9,10},{10,... | collective-permute-start | bytes 49160 | tf_op jit(solution)/shard_map/ppermute | solution.py:161

commit v6 on v5

--- a/solution.py
+++ b/solution.py
@@ -170,13 +170,12 @@
     live_rows = jnp.arange(train_local, dtype=jnp.int32) < counts[0]
 
     rows_local = kv_weight.shape[1]
-    own_rows = lax.dynamic_slice_in_dim(proj_out, lax.axis_index("dp") * rows_local, rows_local, 0)
-    folded = lax.dot_general(
-        own_rows,
-        kv_weight[0],
-        (((0,), (0,)), ((), ())),
-        preferred_element_type=jnp.float32,
-    )
+    own_rows = lax.optimization_barrier(
+        lax.dynamic_slice_in_dim(
+            jnp.transpose(proj_out), lax.axis_index("dp") * rows_local, rows_local, 1
+        )
+    )
+    folded = jnp.dot(own_rows, kv_weight[0], preferred_element_type=jnp.float32)
     folded, ((live, in_side), decoded) = sum_over_dp(
         folded,
         [

time: 33.9 us -> 32.9 us (0.971)
  matrix products: 2.89 us -> 1.83 us
    dynamic_slice x0 -> x1, local copies, waits for them, and re-layouts: none -> 1.06 us  [per_device(): lax.dynamic_slice_in_dim(jnp.transpose(proj_out), lax.axis_index('dp') *...]
    dot_general x1, matrix products: 1.53 us -> 0.48 us  [per_device(): folded = jnp.dot(own_rows, kv_weight[0], preferred_element_type=jnp.float32)]
    unnamed x12, local copies, waits for them, and re-layouts: 1.61 us -> 0.61 us
  transfers between devices with their start and end apart: 9 -> 9, of which waited for: 8 -> 8; matrix products, arithmetic and copies ran while one was open for 2% -> 3% of each run, Pallas kernels for 6% -> 6%
where the time goes in v6:
time: 32.9 us; the launch traced here: 32.8 us
  waiting for transfers between devices  13 us (40%)
  starting transfers between devices  11.9 us (36%)
  Pallas kernels  2.49 us (8%)
  matrix products  1.83 us (6%)
  local copies, waits for them, and re-layouts  1.8 us (5%)
  other arithmetic  0.87 us (3%)
  between operations  0.86 us (3%)
    ppermute x2, starting transfers between devices, sum_over_dp(): lax.ppermute((x * LINK_SCALE).astype(jnp.float16), 'dp', partners(size, s...  5.91 us
    ppermute x2, waiting for transfers between devices, sum_over_dp(): lax.ppermute((x * LINK_SCALE).astype(jnp.float16), 'dp', partners(size, s...  5.71 us
    ppermute x3, starting transfers between devices, gather_over_dp(): block = lax.ppermute(x, 'dp', partners(size, step))  3.96 us
    ppermute x3, waiting for transfers between devices, gather_over_dp(): block = lax.ppermute(x, 'dp', partners(size, step))  3.23 us
    ppermute x1, waiting for transfers between devices, sum_over_layer_sub(): by_layer = lax.ppermute(x, 'layer', partners(2, 1))  1.92 us
    pallas_call x1, Pallas kernels, decode(): pl.pallas_call(decode_kernel, out_shape=jax.ShapeDtypeStruct((subs * widt...  1.92 us
    ppermute x1, starting transfers between devices, sum_over_layer_sub(): by_layer = lax.ppermute(x, 'layer', partners(2, 1))  1.56 us
    ppermute x1, waiting for transfers between devices, per_device(): lax.ppermute(out_side, 'sub', partners(2, 1))  1.24 us
  transfers between devices with their start and end apart: 9, of which 8 were waited for; matrix products, arithmetic and copies ran while one was open for 3% of the time, Pallas kernels for 6%

profile of v6, /device:TPU:0, one launch (start us, length us, event | category | flops | bytes accessed | tf_op | source)
XLA Modules:
  0.0 32.8 jit_solution(2463505396877181263)
XLA Ops:
  0.0 0.0 copy-start
  0.0 0.0 copy-start.5
  0.0 0.0 copy-start.3
  0.0 1.1 %dynamic-slice_bitcast_fusion = bf16[64,1024]{1,0:T(8,128)(2,1)S(1)} fusion(bf16[4096,64]{0,1:T(8,128)(2,1)} %param.12, s32[]{:T(128)S(6)} %select_n.20), kind=kLoop, calls=%fused_computation.24 | loop fusion | bytes 262148 | tf_op jit(solution)/shard_map/dynamic_slice | solution.py:174
  1.1 0.6 %copy-done = bf16[1,1024,1024]{2,1,0:T(8,128)(2,1)S(1)} copy-done((bf16[1,1024,1024]{2,1,0:T(8,128)(2,1)S(1)}, bf16[1,1024,1024]{2,1,0:T(8,128)(2,1)}, u32[]{:S(2)}) %copy-start) | copy-done | bytes 2097176
  1.7 0.5 %multiply_convert_fusion.1 = (f16[64,1024]{1,0:T(8,128)(2,1)S(1)}, f32[64,1024]{1,0:T(8,128)S(1)}) fusion(bf16[64,1024]{1,0:T(8,128)(2,1)S(1)} %dynamic-slice_bitcast_fusion, bf16[1,1024,1024]{2,1,0:T(8,128)(2,1)S(1)} %copy-done), kind=kOutput, calls=%fused_computation.15 | convolution fusion | flops 134348800 | bytes 2621440 | tf_op jit(solution)/shard_map/dot_general | solution.py:178
  2.1 0.0 copy-start.1
  2.2 0.0 copy-start.2
  2.2 3.1 %collective-permute-start = (f16[64,1024]{1,0:T(8,128)(2,1)S(1)}, f16[64,1024]{1,0:T(8,128)(2,1)S(1)}, u32[]{:S(2)}, u32[]{:S(2)}) collective-permute-start(f16[64,1024]{1,0:T(8,128)(2,1)S(1)} %get-tuple-element.21), channel_id=1, source_target_pairs={{0,4},{4,0},{8,12},{12,8},{1,5},{5,1},{9,13},{13,9},{2,6},{6,2},{1... | collective-permute-start | bytes 393224 | tf_op jit(solution)/shard_map/ppermute | solution.py:134
  5.3 0.0 copy-done.5
  5.3 0.0 copy-done.3
  5.3 0.8 %fusion.in_ref = f32[64,256]{1,0:T(8,128)S(1)} fusion(bf16[4096,64]{0,1:T(8,128)(2,1)S(1)} %copy-done.5, bf16[1,256,4096]{2,1,0:T(8,128)(2,1)S(1)} %copy-done.3), kind=kOutput, calls=%fused_computation | convolution fusion | flops 134217728 | bytes 2686976 | tf_op jit(solution)/shard_map/dot_general | solution.py:184
  6.0 0.0 copy-start.4
  6.8 2.0 %collective-permute-done = f16[64,1024]{1,0:T(8,128)(2,1)S(1)} collective-permute-done((f16[64,1024]{1,0:T(8,128)(2,1)S(1)}, f16[64,1024]{1,0:T(8,128)(2,1)S(1)}, u32[]{:S(2)}, u32[]{:S(2)}) %collective-permute-start) | collective-permute-done | bytes 131104 | tf_op jit(solution)/shard_map/ppermute | solution.py:134
  8.8 0.1 multiply_convert_fusion
  8.8 2.8 %collective-permute-start.1 = (f16[64,1024]{1,0:T(8,128)(2,1)S(1)}, f16[64,1024]{1,0:T(8,128)(2,1)S(1)}, u32[]{:S(2)}, u32[]{:S(2)}) collective-permute-start(f16[64,1024]{1,0:T(8,128)(2,1)S(1)} %multiply_convert_fusion), channel_id=1, source_target_pairs={{0,8},{4,12},{8,0},{12,4},{1,9},{5,13},{9,1},{13,5},{2,10},{6,14},... | collective-permute-start | bytes 393224 | tf_op jit(solution)/shard_map/ppermute | solution.py:134
  11.6 0.0 copy-done.1
  11.6 0.0 copy-done.2
  11.6 1.9 %decode.1 = bf16[2048,256]{1,0:T(8,128)(2,1)S(1)} custom-call(s32[256,1,256]{2,1,0:T(1,128)S(1)} %copy-done.2, bf16[256,8,256]{2,1,0:T(8,128)(2,1)S(1)} %bitcast.29), custom_call_target="tpu_custom_call" | custom-call | bytes 2097152 | tf_op jit(solution)/shard_map/decode/pallas_call | solution.py:56
  13.6 3.7 %collective-permute-done.1 = f16[64,1024]{1,0:T(8,128)(2,1)S(1)} collective-permute-done((f16[64,1024]{1,0:T(8,128)(2,1)S(1)}, f16[64,1024]{1,0:T(8,128)(2,1)S(1)}, u32[]{:S(2)}, u32[]{:S(2)}) %collective-permute-start.1) | collective-permute-done | bytes 131104 | tf_op jit(solution)/shard_map/ppermute | solution.py:134
  17.3 0.1 reduce-precision_convert_fusion
  17.4 0.0 copy-done.4
  17.4 0.3 fusion.4
  17.7 0.1 collective-permute-start.2
  17.8 1.2 %collective-permute-done.2.other_ref = f32[64,256]{1,0:T(8,128)S(1)} collective-permute-done((f32[64,256]{1,0:T(8,128)S(1)}, f32[64,256]{1,0:T(8,128)S(1)}, u32[]{:S(2)}, u32[]{:S(2)}) %collective-permute-start.2) | collective-permute-done | bytes 65568 | tf_op jit(solution)/shard_map/ppermute | solution.py:199
  19.0 0.6 %vectors.1 = f32[4,2048]{1,0:T(4,128)S(1)} custom-call(f32[64,256]{1,0:T(8,128)S(1)} %fusion.in_ref, f32[64,256]{1,0:T(8,128)S(1)} %slice_add_fusion.own_ref, f32[64,256]{1,0:T(8,128)S(1)} %collective-permute-done.2.other_ref), custom_call_target="tpu_custom_call" | custom-call | tf_op jit(solution)/shard_map/vectors/pallas_call | solution.py:99
  19.7 0.4 %collective-permute-start.3 = (f16[4,2048]{1,0:T(4,128)(2,1)S(1)}, f16[4,2048]{1,0:T(4,128)(2,1)S(1)}, u32[]{:S(2)}, u32[]{:S(2)}) collective-permute-start(f16[4,2048]{1,0:T(4,128)(2,1)S(1)} %get-tuple-element.16), channel_id=1, source_target_pairs={{0,8},{4,12},{8,0},{12,4},{1,9},{5,13},{9,1},{13,5},{2,10},{6,14},... | collective-permute-start | bytes 49160 | tf_op jit(solution)/shard_map/ppermute | solution.py:151
  20.1 3.1 %collective-permute-start.4 = (f16[4,2048]{1,0:T(4,128)(2,1)S(1)}, f16[4,2048]{1,0:T(4,128)(2,1)S(1)}, u32[]{:S(2)}, u32[]{:S(2)}) collective-permute-start(f16[4,2048]{1,0:T(4,128)(2,1)S(1)} %get-tuple-element.16), channel_id=1, source_target_pairs={{0,12},{4,8},{8,4},{12,0},{1,13},{5,9},{9,5},{13,1},{2,14},{6,10},... | collective-permute-start | bytes 49160 | tf_op jit(solution)/shard_map/ppermute | solution.py:151
  23.2 0.5 %collective-permute-start.5 = (f16[4,2048]{1,0:T(4,128)(2,1)S(1)}, f16[4,2048]{1,0:T(4,128)(2,1)S(1)}, u32[]{:S(2)}, u32[]{:S(2)}) collective-permute-start(f16[4,2048]{1,0:T(4,128)(2,1)S(1)} %get-tuple-element.16), channel_id=1, source_target_pairs={{0,4},{4,0},{8,12},{12,8},{1,5},{5,1},{9,13},{13,9},{2,6},{6,2},{1... | collective-permute-start | bytes 49160 | tf_op jit(solution)/shard_map/ppermute | solution.py:151
  23.6 1.0 %collective-permute-done.3 = f16[4,2048]{1,0:T(4,128)(2,1)S(1)} collective-permute-done((f16[4,2048]{1,0:T(4,128)(2,1)S(1)}, f16[4,2048]{1,0:T(4,128)(2,1)S(1)}, u32[]{:S(2)}, u32[]{:S(2)}) %collective-permute-start.3) | collective-permute-done | bytes 16416 | tf_op jit(solution)/shard_map/ppermute | solution.py:151
  24.6 1.0 %collective-permute-done.4 = f16[4,2048]{1,0:T(4,128)(2,1)S(1)} collective-permute-done((f16[4,2048]{1,0:T(4,128)(2,1)S(1)}, f16[4,2048]{1,0:T(4,128)(2,1)S(1)}, u32[]{:S(2)}, u32[]{:S(2)}) %collective-permute-start.4) | collective-permute-done | bytes 16416 | tf_op jit(solution)/shard_map/ppermute | solution.py:151
  25.6 1.3 %collective-permute-done.5 = f16[4,2048]{1,0:T(4,128)(2,1)S(1)} collective-permute-done((f16[4,2048]{1,0:T(4,128)(2,1)S(1)}, f16[4,2048]{1,0:T(4,128)(2,1)S(1)}, u32[]{:S(2)}, u32[]{:S(2)}) %collective-permute-start.5) | collective-permute-done | bytes 16416 | tf_op jit(solution)/shard_map/ppermute | solution.py:151
  27.0 0.3 fusion.11
  27.3 0.1 collective-permute-start.6
  27.4 1.6 %collective-permute-start.7 = (f32[16,256]{1,0:T(8,128)S(1)}, f32[16,256]{1,0:T(8,128)S(1)}, u32[]{:S(2)}, u32[]{:S(2)}) collective-permute-start(f32[16,256]{1,0:T(8,128)S(1)} %slice_add_fusion.1), channel_id=1, source_target_pairs={{0,2},{2,0},{1,3},{3,1},{4,6},{6,4},{5,7},{7,5},{8,10},{10,8},{9,1... | collective-permute-start | bytes 49160 | tf_op jit(solution)/shard_map/ppermute | solution.py:160
  29.0 0.3 collective-permute-start.8
  29.3 0.0 collective-permute-done.6
  29.3 1.9 %collective-permute-done.7 = f32[16,256]{1,0:T(8,128)S(1)} collective-permute-done((f32[16,256]{1,0:T(8,128)S(1)}, f32[16,256]{1,0:T(8,128)S(1)}, u32[]{:S(2)}, u32[]{:S(2)}) %collective-permute-start.7) | collective-permute-done | bytes 16416 | tf_op jit(solution)/shard_map/ppermute | solution.py:160
  31.2 0.9 %collective-permute-done.8 = f32[16,256]{1,0:T(8,128)S(1)} collective-permute-done((f32[16,256]{1,0:T(8,128)S(1)}, f32[16,256]{1,0:T(8,128)S(1)}, u32[]{:S(2)}, u32[]{:S(2)}) %collective-permute-start.8) | collective-permute-done | bytes 16416 | tf_op jit(solution)/shard_map/ppermute | solution.py:161
  32.1 0.6 %select_bitcast_fusion = f32[256,16]{0,1:T(8,128)} fusion(f32[16,256]{1,0:T(8,128)S(1)} %collective-permute-done.7, f32[16,256]{1,0:T(8,128)S(1)} %collective-permute-done.8, f32[16,256]{1,0:T(8,128)S(1)} %collective-permute-done.6, pred[256]{0:T(512)(128)(4,1)S(1)} %compare_reduce_fusion, f32[32,256]{1,0:T(8,128)S(1)} %fusion.11), kind=kLoop, calls=%fused_computation.32 | loop fusion | flops 20480 | bytes 98560 | tf_op jit(solution)/shard_map/transpose | solution.py:211
  (13 shorter events, 0.2 us)
Async XLA Ops:
  0.0 1.7 %copy-start = (bf16[1,1024,1024]{2,1,0:T(8,128)(2,1)S(1)}, bf16[1,1024,1024]{2,1,0:T(8,128)(2,1)}, u32[]{:S(2)}) copy-start(bf16[1,1024,1024]{2,1,0:T(8,128)(2,1)} %param.10) | copy-start | bytes 6291460
  0.0 5.3 %copy-start.5 = (bf16[4096,64]{0,1:T(8,128)(2,1)S(1)}, bf16[4096,64]{0,1:T(8,128)(2,1)}, u32[]{:S(2)}) copy-start(bf16[4096,64]{0,1:T(8,128)(2,1)} %param.11) | copy-start | bytes 1572868
  0.0 5.3 %copy-start.3 = (bf16[1,256,4096]{2,1,0:T(8,128)(2,1)S(1)}, bf16[1,256,4096]{2,1,0:T(8,128)(2,1)}, u32[]{:S(2)}) copy-start(bf16[1,256,4096]{2,1,0:T(8,128)(2,1)} %param.8) | copy-start | bytes 6291460
  2.1 9.5 %copy-start.1 = (bf16[256,256,8]{1,2,0:T(8,128)(2,1)S(1)}, bf16[256,256,8]{1,2,0:T(8,128)(2,1)}, u32[]{:S(2)}) copy-start(bf16[256,256,8]{1,2,0:T(8,128)(2,1)} %param.13) | copy-start | bytes 3145732
  2.2 9.5 %copy-start.2 = (s32[256,1,256]{2,1,0:T(1,128)S(1)}, s32[256,1,256]{2,1,0:T(1,128)}, u32[]{:S(2)}) copy-start(s32[256,1,256]{2,1,0:T(1,128)} %codes_ref.1) | copy-start | bytes 786436
  2.2 6.6 %collective-permute-start = (f16[64,1024]{1,0:T(8,128)(2,1)S(1)}, f16[64,1024]{1,0:T(8,128)(2,1)S(1)}, u32[]{:S(2)}, u32[]{:S(2)}) collective-permute-start(f16[64,1024]{1,0:T(8,128)(2,1)S(1)} %get-tuple-element.21), channel_id=1, source_target_pairs={{0,4},{4,0},{8,12},{12,8},{1,5},{5,1},{9,13},{13,9},{2,6},{6,2},{1... | collective-permute-start | bytes 393224 | tf_op jit(solution)/shard_map/ppermute | solution.py:134
  6.0 11.3 %copy-start.4 = (bf16[1,256,1024]{2,1,0:T(8,128)(2,1)S(1)}, bf16[1,256,1024]{2,1,0:T(8,128)(2,1)}, u32[]{:S(2)}) copy-start(bf16[1,256,1024]{2,1,0:T(8,128)(2,1)} %param.9) | copy-start | bytes 1572868
  8.8 8.5 %collective-permute-start.1 = (f16[64,1024]{1,0:T(8,128)(2,1)S(1)}, f16[64,1024]{1,0:T(8,128)(2,1)S(1)}, u32[]{:S(2)}, u32[]{:S(2)}) collective-permute-start(f16[64,1024]{1,0:T(8,128)(2,1)S(1)} %multiply_convert_fusion), channel_id=1, source_target_pairs={{0,8},{4,12},{8,0},{12,4},{1,9},{5,13},{9,1},{13,5},{2,10},{6,14},... | collective-permute-start | bytes 393224 | tf_op jit(solution)/shard_map/ppermute | solution.py:134
  17.7 1.3 %collective-permute-start.2 = (f32[64,256]{1,0:T(8,128)S(1)}, f32[64,256]{1,0:T(8,128)S(1)}, u32[]{:S(2)}, u32[]{:S(2)}) collective-permute-start(f32[64,256]{1,0:T(8,128)S(1)} %slice_add_fusion.own_ref), channel_id=1, source_target_pairs={{0,1},{1,0},{2,3},{3,2},{4,5},{5,4},{6,7},{7,6},{8,9},{9,8},{10,11... | collective-permute-start | bytes 196616 | tf_op jit(solution)/shard_map/ppermute | solution.py:199
  19.7 4.9 %collective-permute-start.3 = (f16[4,2048]{1,0:T(4,128)(2,1)S(1)}, f16[4,2048]{1,0:T(4,128)(2,1)S(1)}, u32[]{:S(2)}, u32[]{:S(2)}) collective-permute-start(f16[4,2048]{1,0:T(4,128)(2,1)S(1)} %get-tuple-element.16), channel_id=1, source_target_pairs={{0,8},{4,12},{8,0},{12,4},{1,9},{5,13},{9,1},{13,5},{2,10},{6,14},... | collective-permute-start | bytes 49160 | tf_op jit(solution)/shard_map/ppermute | solution.py:151
  20.1 5.5 %collective-permute-start.4 = (f16[4,2048]{1,0:T(4,128)(2,1)S(1)}, f16[4,2048]{1,0:T(4,128)(2,1)S(1)}, u32[]{:S(2)}, u32[]{:S(2)}) collective-permute-start(f16[4,2048]{1,0:T(4,128)(2,1)S(1)} %get-tuple-element.16), channel_id=1, source_target_pairs={{0,12},{4,8},{8,4},{12,0},{1,13},{5,9},{9,5},{13,1},{2,14},{6,10},... | collective-permute-start | bytes 49160 | tf_op jit(solution)/shard_map/ppermute | solution.py:151
  23.2 3.7 %collective-permute-start.5 = (f16[4,2048]{1,0:T(4,128)(2,1)S(1)}, f16[4,2048]{1,0:T(4,128)(2,1)S(1)}, u32[]{:S(2)}, u32[]{:S(2)}) collective-permute-start(f16[4,2048]{1,0:T(4,128)(2,1)S(1)} %get-tuple-element.16), channel_id=1, source_target_pairs={{0,4},{4,0},{8,12},{12,8},{1,5},{5,1},{9,13},{13,9},{2,6},{6,2},{1... | collective-permute-start | bytes 49160 | tf_op jit(solution)/shard_map/ppermute | solution.py:151
  27.3 2.0 %collective-permute-start.6 = (f32[16,256]{1,0:T(8,128)S(1)}, f32[16,256]{1,0:T(8,128)S(1)}, u32[]{:S(2)}, u32[]{:S(2)}) collective-permute-start(f32[16,256]{1,0:T(8,128)S(1)} %slice_add_fusion.1), channel_id=1, source_target_pairs={{0,1},{1,0},{2,3},{3,2},{4,5},{5,4},{6,7},{7,6},{8,9},{9,8},{10,11... | collective-permute-start | bytes 49160 | tf_op jit(solution)/shard_map/ppermute | solution.py:159
  27.4 3.8 %collective-permute-start.7 = (f32[16,256]{1,0:T(8,128)S(1)}, f32[16,256]{1,0:T(8,128)S(1)}, u32[]{:S(2)}, u32[]{:S(2)}) collective-permute-start(f32[16,256]{1,0:T(8,128)S(1)} %slice_add_fusion.1), channel_id=1, source_target_pairs={{0,2},{2,0},{1,3},{3,1},{4,6},{6,4},{5,7},{7,5},{8,10},{10,8},{9,1... | collective-permute-start | bytes 49160 | tf_op jit(solution)/shard_map/ppermute | solution.py:160
  29.0 3.2 %collective-permute-start.8 = (f32[16,256]{1,0:T(8,128)S(1)}, f32[16,256]{1,0:T(8,128)S(1)}, u32[]{:S(2)}, u32[]{:S(2)}) collective-permute-start(f32[16,256]{1,0:T(8,128)S(1)} %slice_add_fusion.1), channel_id=1, source_target_pairs={{0,3},{1,2},{2,1},{3,0},{4,7},{5,6},{6,5},{7,4},{8,11},{9,10},{10,... | collective-permute-start | bytes 49160 | tf_op jit(solution)/shard_map/ppermute | solution.py:161

commit v7 on v6

--- a/solution.py
+++ b/solution.py
@@ -11,23 +11,62 @@
 LANES = 128
 LINK_SCALE = 1024.0
 VECTOR_SCALE = 16384.0
-
-
-def decode_kernel(codes_ref, book_ref, out_ref, ids_ref):
-    subs, width, code_count = book_ref.shape
-    slots = codes_ref.shape[0]
+GATHER_ORDER = (0, 1, 3, 2)
+
+
+def rows_kernel(proj_ref, out_ref, sem):
+    rows = out_ref.shape[1]
+    first = pl.multiple_of(lax.axis_index("dp") * rows, LANES)
+    copy = pltpu.make_async_copy(proj_ref.at[:, pl.ds(first, rows)], out_ref, sem)
+    copy.start()
+    copy.wait()
+
+
+def take_rows(proj_t, rows):
+    return pl.pallas_call(
+        rows_kernel,
+        out_shape=jax.ShapeDtypeStruct((proj_t.shape[0], rows), proj_t.dtype),
+        in_specs=[pl.BlockSpec(memory_space=pl.ANY)],
+        out_specs=pl.BlockSpec(memory_space=pltpu.VMEM),
+        scratch_shapes=[pltpu.SemaphoreType.DMA],
+        compiler_params=pltpu.CompilerParams(vmem_limit_bytes=1024 * 1024),
+        name="rows",
+    )(proj_t)
+
+
+def ids_kernel(codes_ref, out_ref):
+    slots, _, subs = codes_ref.shape
     for left in range(0, slots, LANES):
         for top in range(0, subs, LANES):
             block = codes_ref[left : left + LANES, 0, top : top + LANES]
-            ids_ref[top : top + LANES, left : left + LANES] = jnp.transpose(block)
-
+            out_ref[top : top + LANES, left : left + LANES] = (
+                jnp.transpose(block).astype(jnp.float32).astype(jnp.bfloat16)
+            )
+
+
+def make_ids(codes):
+    slots, _, subs = codes.shape
+    return pl.pallas_call(
+        ids_kernel,
+        out_shape=jax.ShapeDtypeStruct((subs, slots), jnp.bfloat16),
+        in_specs=[pl.BlockSpec(memory_space=pltpu.VMEM)],
+        out_specs=pl.BlockSpec(memory_space=pltpu.VMEM),
+        compiler_params=pltpu.CompilerParams(vmem_limit_bytes=4 * 1024 * 1024),
+        name="ids",
+    )(codes)
+
+
+def decode_kernel(ids_ref, book_ref, out_ref):
+    subs, width, code_count = book_ref.shape
+    slots = ids_ref.shape[1]
     group = math.gcd(subs, 64)
 
     def several(step, carry):
         first = pl.multiple_of(step * group, group)
-        for top in range(0, group, 8):
-            ids = ids_ref[pl.ds(pl.multiple_of(first + top, 8), 8), :]
-            for pair in range(0, 8, 2):
+        for top in range(0, group, 16):
+            ids = ids_ref[pl.ds(pl.multiple_of(first + top, 16), 16), :]
+            ids = ids.astype(jnp.float32).astype(jnp.int32)
+            for pair in range(0, 16, 2):
                 halves = []
                 for sub in (pair, pair + 1):
                     table = book_ref[first + top + sub].astype(jnp.float32)
@@ -50,24 +89,23 @@
     lax.fori_loop(0, subs // group, several, 0)
 
 
-def decode(codes, book_t):
-    slots, _, subs = codes.shape
-    width = book_t.shape[1]
+def decode(ids, book_t):
+    subs, width, _ = book_t.shape
+    slots = ids.shape[1]
     return pl.pallas_call(
         decode_kernel,
         out_shape=jax.ShapeDtypeStruct((subs * width, slots), jnp.bfloat16),
         in_specs=[pl.BlockSpec(memory_space=pltpu.VMEM)] * 2,
         out_specs=pl.BlockSpec(memory_space=pltpu.VMEM),
-        scratch_shapes=[pltpu.VMEM((subs, slots), jnp.int32)],
         compiler_params=pltpu.CompilerParams(vmem_limit_bytes=8 * 1024 * 1024),
         cost_estimate=pl.CostEstimate(flops=0, bytes_accessed=2 * 1024 * 1024, transcendentals=0),
         name="decode",
-    )(codes, book_t)
+    )(ids, book_t)
 
 
 def vectors_kernel(in_ref, own_ref, other_ref, out_ref, grads_ref, flat_ref):
     rank_dim, tokens = in_ref.shape
-    tests, dims = out_ref.shape
+    parts, tests, dims = out_ref.shape
     pairs = rank_dim // 2
     tall = dims // LANES
     in_side = in_ref[...]
@@ -86,11 +124,57 @@
         squares = jnp.sum(jnp.sum(both * both, axis=0, keepdims=True), axis=1, keepdims=True)
         mean = squares * (1.0 / (rank_dim * rank_dim))
         flat_ref[test * pairs : (test + 1) * pairs, :] = both * (lax.rsqrt(mean + 1e-06) / rank_dim)
-    first = lax.axis_index("sub") * tall
-    for row in range(tall):
-        out_ref[:, row * LANES : (row + 1) * LANES] = flat_ref[
-            pl.ds(first + row, tests, stride=pairs), :
-        ]
+    for part in range(parts):
+        for row in range(tall):
+            out_ref[part, :, row * LANES : (row + 1) * LANES] = flat_ref[
+                pl.ds(part * tall + row, tests, stride=pairs), :
+            ]
+
+
+def score_kernel(*refs):
+    *vector_refs, near_ref, far_ref, out_ref = refs
+    tests = vector_refs[0].shape[1]
+    core = lax.axis_index("sub")
+    own = lax.axis_index("dp")
+    total = None
+    for part, table_ref in ((core, near_ref), (1 - core, far_ref)):
+        vectors = jnp.concatenate([ref[part] for ref in vector_refs], axis=0)
+        high = vectors.astype(jnp.bfloat16)
+        low = (vectors - high.astype(jnp.float32)).astype(jnp.bfloat16)
+        both = jnp.dot(
+            jnp.concatenate([high, low], axis=0), table_ref[...], preferred_element_type=jnp.float32
+        )
+        total = both if total is None else total + both
+    blocks = len(vector_refs)
+    total = total[: blocks * tests] + total[blocks * tests :]
+    rows = [None] * blocks
+    for at, xor in enumerate(GATHER_ORDER):
+        rows[xor] = total[at * tests : (at + 1) * tests]
+    step = 1
+    while step < blocks:
+        rows = [jnp.where((own & step) != 0, rows[at ^ step], rows[at]) for at in range(blocks)]
+        step *= 2
+    out_ref[...] = jnp.concatenate(rows, axis=0)
+
+
+def score_blocks(blocks, near, far):
+    tests = blocks[0].shape[1]
+    return pl.pallas_call(
+        score_kernel,
+        out_shape=jax.ShapeDtypeStruct((len(blocks) * tests, near.shape[1]), jnp.float32),
+        in_specs=[pl.BlockSpec(memory_space=pltpu.VMEM)] * (len(blocks) + 2),
+        out_specs=pl.BlockSpec(memory_space=pltpu.VMEM),
+        compiler_params=pltpu.CompilerParams(vmem_limit_bytes=8 * 1024 * 1024),
+        name="score",
+    )(*blocks, near, far)
+
+
+def score(vectors, table):
+    tests = vectors.shape[0]
+    both = jnp.dot(
+        jnp.concatenate(split_high_low(vectors), axis=0), table, preferred_element_type=jnp.float32
+    )
+    return both[:tests] + both[tests:]
 
 
 def make_vectors(in_side, own, other, dims_local):
@@ -98,7 +182,7 @@
     tests = tokens // SEQ
     return pl.pallas_call(
         vectors_kernel,
-        out_shape=jax.ShapeDtypeStruct((tests, dims_local), jnp.float32),
+        out_shape=jax.ShapeDtypeStruct((rank_dim * rank_dim // dims_local, tests, dims_local), jnp.float32),
         in_specs=[pl.BlockSpec(memory_space=pltpu.VMEM)] * 3,
         out_specs=pl.BlockSpec(memory_space=pltpu.VMEM),
         scratch_shapes=[
@@ -123,7 +207,7 @@
     return n & (n - 1) == 0
 
 
-def sum_over_dp(x, beside):
+def sum_over_dp(x, sent, beside):
     size = lax.axis_size("dp")
     beside = list(beside)
     made = []
@@ -131,11 +215,12 @@
         return lax.psum(x, "dp"), [work() for work in beside]
     step = 1
     while step < size:
-        got = lax.ppermute((x * LINK_SCALE).astype(jnp.float16), "dp", partners(size, step))
+        got = lax.ppermute(sent, "dp", partners(size, step))
         if beside:
             got, done = lax.optimization_barrier((got, beside.pop(0)()))
             made.append(done)
         x = x + got.astype(jnp.float32) * (1.0 / LINK_SCALE)
+        sent = (x * LINK_SCALE).astype(jnp.float16)
         step *= 2
     return x, made + [work() for work in beside]
 
@@ -153,13 +238,26 @@
     return got
 
 
-def sum_over_layer_sub(x):
-    if lax.axis_size("layer") != 2 or lax.axis_size("sub") != 2:
-        return lax.psum(x, ("layer", "sub"))
-    by_sub = lax.ppermute(x, "sub", partners(2, 1))
-    by_layer = lax.ppermute(x, "layer", partners(2, 1))
-    by_both = lax.ppermute(x, ("layer", "sub"), partners(4, 3))
-    return (x + by_sub) + (by_layer + by_both)
+def has_two_by_two():
+    return lax.axis_size("layer") == 2 and lax.axis_size("sub") == 2
+
+
+NEAR_CODES = [(0, 0), (2, 2), (3, 1), (1, 3)]
+FAR_CODES = [(1, 0), (3, 2), (2, 1), (0, 3)]
+
+
+def gather_by_core(x):
+    size = lax.axis_size("dp")
+    blocks = []
+    for step in GATHER_ORDER:
+        pairs = [
+            (4 * at + 2 * layer + core, 4 * (at ^ step) + 2 * (layer ^ core) + core)
+            for at in range(size)
+            for layer in range(2)
+            for core in range(2)
+        ]
+        blocks.append(lax.ppermute(x, ("dp", "layer", "sub"), pairs))
+    return blocks
 
 
 def per_device(acts, kv_grad, kv_weight, proj_in, proj_out, codebook, codes, counts):
@@ -176,17 +274,31 @@
         )
     )
     folded = jnp.dot(own_rows, kv_weight[0], preferred_element_type=jnp.float32)
-    folded, ((live, in_side), decoded) = sum_over_dp(
-        folded,
-        [
-            lambda: (
-                jnp.broadcast_to(live_rows, (8, train_local)).astype(jnp.float32),
-                lax.dot_general(
-                    proj_in, acts[0], (((0,), (1,)), ((), ())), preferred_element_type=jnp.float32
-                ),
-            ),
-            lambda: decode(codes, jnp.transpose(codebook, (0, 2, 1))),
-        ],
+    book_t = jnp.transpose(codebook, (0, 2, 1))
+    by_core = has_two_by_two() and lax.axis_size("dp") == 4
+
+    sent = (folded * LINK_SCALE).astype(jnp.float16)
+    live = jnp.broadcast_to(live_rows, (8, train_local)).astype(jnp.float32)
+    live, moved_codes = lax.optimization_barrier((live, codes))
+    ids = make_ids(moved_codes)
+    if by_core:
+        sent, moved_book = lax.optimization_barrier((sent, codebook))
+        near_ids = lax.ppermute(ids, ("layer", "sub"), NEAR_CODES)
+        far_ids = lax.ppermute(ids, ("layer", "sub"), FAR_CODES)
+        other_book = lax.ppermute(moved_book, "sub", partners(2, 1))
+
+    def first_side():
+        return lax.dot_general(
+            proj_in, acts[0], (((0,), (1,)), ((), ())), preferred_element_type=jnp.float32
+        )
+
+    def tables():
+        if not by_core:
+            return (decode(ids, book_t),)
+        return decode(near_ids, book_t), decode(far_ids, jnp.transpose(other_book, (0, 2, 1)))
+
+    folded, (live, (in_side, decoded)) = sum_over_dp(
+        folded, sent, [lambda: live, lambda: (first_side(), tables())]
     )
     out_side = lax.dot_general(
         jnp.concatenate(split_high_low(folded), axis=0),
@@ -199,15 +311,18 @@
         lax.ppermute(out_side, "sub", partners(2, 1))
     )
     vectors = make_vectors(in_side, out_side, other_side, dims_local)
-    every = gather_over_dp((vectors * VECTOR_SCALE).astype(jnp.float16))
-    every = every.reshape(-1, dims_local).astype(jnp.float32) * (1.0 / VECTOR_SCALE)
-    tests_all = every.shape[0]
-
-    layer_scores = jnp.dot(
-        jnp.concatenate(split_high_low(every), axis=0), decoded, preferred_element_type=jnp.float32
-    )
-    layer_scores = layer_scores[:tests_all] + layer_scores[tests_all:]
-    total = sum_over_layer_sub(layer_scores)
+    sent = (vectors * VECTOR_SCALE).astype(jnp.float16)
+    core = lax.axis_index("sub")
+    if by_core:
+        blocks = [
+            block.astype(jnp.float32) * (1.0 / VECTOR_SCALE) for block in gather_by_core(sent)
+        ]
+        total = score_blocks(blocks, *decoded)
+        total = total + lax.ppermute(total, "sub", partners(2, 1))
+    else:
+        every = gather_over_dp(lax.dynamic_index_in_dim(sent, core, 0, False))
+        every = every.reshape(-1, dims_local).astype(jnp.float32) * (1.0 / VECTOR_SCALE)
+        total = lax.psum(score(every, decoded[0]), ("layer", "sub"))
     return jnp.transpose(jnp.where(live[:1] > 0.0, total, jnp.float32(0.0)))
 
 

time: 32.9 us -> 32.3 us (0.982)
  waiting for transfers between devices: 13 us -> 7.74 us
  Pallas kernels: 2.49 us -> 4.68 us
  starting transfers between devices: 11.9 us -> 13.8 us
  matrix products: 1.83 us -> 2.6 us
    ppermute x8 -> x10, waiting for transfers between devices: 11.8 us -> 6.5 us  [the longest x4 2.94 us: gather_by_core(): blocks.append(lax.ppermute(x, ('dp', 'layer', 'sub'), pairs))]
    ppermute x8 -> x10, starting transfers between devices: 11.8 us -> 13.7 us  [the longest x2 5.48 us: sum_over_dp(): got = lax.ppermute(sent, 'dp', partners(size, step))]
    pallas_call x1 -> x2, Pallas kernels: 1.92 us -> 3.47 us  [decode(): pl.pallas_call(decode_kernel, out_shape=jax.ShapeDtypeStruct((subs * widt...]
    dot_general x2 -> x1, matrix products: 1.04 us -> 1.8 us  [first_side(): lax.dot_general(proj_in, acts[0], (((0,), (1,)), ((), ())), preferred_ele...]
    pallas_call x1 -> x3, Pallas kernels: 0.57 us -> 1.21 us  [the longest x1 0.58 us: make_vectors(): pl.pallas_call(vectors_kernel, out_shape=jax.ShapeDtypeStruct((rank_dim *...]
  transfers between devices with their start and end apart: 9 -> 11, of which waited for: 8 -> 6; matrix products, arithmetic and copies ran while one was open for 3% -> 6% of each run, Pallas kernels for 6% -> 11%
where the time goes in v7:
time: 32.3 us; the launch traced here: 32.2 us
  starting transfers between devices  13.8 us (43%)
  waiting for transfers between devices  7.74 us (24%)
  Pallas kernels  4.68 us (14%)
  matrix products  2.6 us (8%)
  local copies, waits for them, and re-layouts  1.66 us (5%)
  other arithmetic  0.86 us (3%)
  between operations  0.86 us (3%)
    ppermute x2, starting transfers between devices, sum_over_dp(): got = lax.ppermute(sent, 'dp', partners(size, step))  5.48 us
    ppermute x4, starting transfers between devices, gather_by_core(): blocks.append(lax.ppermute(x, ('dp', 'layer', 'sub'), pairs))  4.24 us
    pallas_call x2, Pallas kernels, decode(): pl.pallas_call(decode_kernel, out_shape=jax.ShapeDtypeStruct((subs * widt...  3.47 us
    ppermute x4, waiting for transfers between devices, gather_by_core(): blocks.append(lax.ppermute(x, ('dp', 'layer', 'sub'), pairs))  2.94 us
    ppermute x2, waiting for transfers between devices, sum_over_dp(): got = lax.ppermute(sent, 'dp', partners(size, step))  2.73 us
    dot_general x1, matrix products, first_side(): lax.dot_general(proj_in, acts[0], (((0,), (1,)), ((), ())), preferred_ele...  1.8 us
    ppermute x1, starting transfers between devices, per_device(): total = total + lax.ppermute(total, 'sub', partners(2, 1))  1.48 us
    ppermute x1, starting transfers between devices, per_device(): far_ids = lax.ppermute(ids, ('layer', 'sub'), FAR_CODES)  1.31 us
  transfers between devices with their start and end apart: 11, of which 6 were waited for; matrix products, arithmetic and copies ran while one was open for 6% of the time, Pallas kernels for 11%

profile of v7, /device:TPU:0, one launch (start us, length us, event | category | flops | bytes accessed | tf_op | source)
XLA Modules:
  0.0 32.2 jit_solution(5889481845027393982)
XLA Ops:
  0.0 0.0 copy-start
  0.0 0.0 copy-start.1
  0.0 0.0 copy-start.2
  0.0 0.0 copy-start.3
  0.0 1.1 %dynamic-slice_bitcast_fusion = bf16[64,1024]{1,0:T(8,128)(2,1)S(1)} fusion(bf16[4096,64]{0,1:T(8,128)(2,1)} %param.12, s32[]{:T(128)S(6)} %select_n.7), kind=kLoop, calls=%fused_computation.16 | loop fusion | bytes 262148 | tf_op jit(solution)/shard_map/dynamic_slice | solution.py:272
  1.1 0.6 %copy-done = bf16[1,1024,1024]{2,1,0:T(8,128)(2,1)S(1)} copy-done((bf16[1,1024,1024]{2,1,0:T(8,128)(2,1)S(1)}, bf16[1,1024,1024]{2,1,0:T(8,128)(2,1)}, u32[]{:S(2)}) %copy-start) | copy-done | bytes 2097176
  1.7 0.5 %multiply_convert_fusion.1 = (f16[64,1024]{1,0:T(8,128)(2,1)S(1)}, f32[64,1024]{1,0:T(8,128)S(1)}) fusion(bf16[64,1024]{1,0:T(8,128)(2,1)S(1)} %dynamic-slice_bitcast_fusion, bf16[1,1024,1024]{2,1,0:T(8,128)(2,1)S(1)} %copy-done), kind=kOutput, calls=%fused_computation.15 | convolution fusion | flops 134348800 | bytes 2621440 | tf_op jit(solution)/shard_map/dot_general | solution.py:276
  2.2 0.0 copy-done.1
  2.2 0.5 %collective-permute-start.4 = (bf16[256,256,8]{1,2,0:T(8,128)(2,1)S(1)}, bf16[256,256,8]{1,2,0:T(8,128)(2,1)S(1)}, u32[]{:S(2)}, u32[]{:S(2)}) collective-permute-start(bf16[256,256,8]{1,2,0:T(8,128)(2,1)S(1)} %copy-done.1), channel_id=1, source_target_pairs={{0,1},{1,0},{2,3},{3,2},{4,5},{5,4},{6,7},{7,6},{8,9},{9,8},{10,11... | collective-permute-start | bytes 3145736 | tf_op jit(solution)/shard_map/ppermute | solution.py:288
  2.7 2.7 %collective-permute-start = (f16[64,1024]{1,0:T(8,128)(2,1)S(1)}, f16[64,1024]{1,0:T(8,128)(2,1)S(1)}, u32[]{:S(2)}, u32[]{:S(2)}) collective-permute-start(f16[64,1024]{1,0:T(8,128)(2,1)S(1)} %get-tuple-element.15), channel_id=1, source_target_pairs={{0,4},{4,0},{8,12},{12,8},{1,5},{5,1},{9,13},{13,9},{2,6},{6,2},{1... | collective-permute-start | bytes 393224 | tf_op jit(solution)/shard_map/ppermute | solution.py:218
  6.0 0.0 copy-done.2
  6.0 0.2 ids.1
  6.2 1.3 %collective-permute-start.3 = (bf16[256,256]{1,0:T(8,128)(2,1)S(1)}, bf16[256,256]{1,0:T(8,128)(2,1)S(1)}, u32[]{:S(2)}, u32[]{:S(2)}) collective-permute-start(bf16[256,256]{1,0:T(8,128)(2,1)S(1)} %ids.1), channel_id=1, source_target_pairs={{1,0},{3,2},{2,1},{0,3},{5,4},{7,6},{6,5},{4,7},{9,8},{11,10},{10,... | collective-permute-start | bytes 393224 | tf_op jit(solution)/shard_map/ppermute | solution.py:287
  7.5 0.7 %collective-permute-start.2 = (bf16[256,256]{1,0:T(8,128)(2,1)S(1)}, bf16[256,256]{1,0:T(8,128)(2,1)S(1)}, u32[]{:S(2)}, u32[]{:S(2)}) collective-permute-start(bf16[256,256]{1,0:T(8,128)(2,1)S(1)} %ids.1), channel_id=1, source_target_pairs={{0,0},{2,2},{3,1},{1,3},{4,4},{6,6},{7,5},{5,7},{8,8},{10,10},{11,... | collective-permute-start | bytes 393224 | tf_op jit(solution)/shard_map/ppermute | solution.py:286
  8.2 1.2 %collective-permute-done = f16[64,1024]{1,0:T(8,128)(2,1)S(1)} collective-permute-done((f16[64,1024]{1,0:T(8,128)(2,1)S(1)}, f16[64,1024]{1,0:T(8,128)(2,1)S(1)}, u32[]{:S(2)}, u32[]{:S(2)}) %collective-permute-start) | collective-permute-done | bytes 131104 | tf_op jit(solution)/shard_map/ppermute | solution.py:218
  9.4 0.1 multiply_convert_fusion
  9.5 2.8 %collective-permute-start.1 = (f16[64,1024]{1,0:T(8,128)(2,1)S(1)}, f16[64,1024]{1,0:T(8,128)(2,1)S(1)}, u32[]{:S(2)}, u32[]{:S(2)}) collective-permute-start(f16[64,1024]{1,0:T(8,128)(2,1)S(1)} %multiply_convert_fusion), channel_id=1, source_target_pairs={{0,8},{4,12},{8,0},{12,4},{1,9},{5,13},{9,1},{13,5},{2,10},{6,14},... | collective-permute-start | bytes 393224 | tf_op jit(solution)/shard_map/ppermute | solution.py:218
  12.3 0.0 copy-done.3
  12.3 1.8 %fusion.in_ref = f32[64,256]{1,0:T(8,128)S(1)} fusion(bf16[4096,64]{0,1:T(8,128)(2,1)} %param.11, bf16[1,256,4096]{2,1,0:T(8,128)(2,1)S(1)} %copy-done.3), kind=kOutput, calls=%fused_computation | convolution fusion | flops 134217728 | bytes 2686976 | tf_op jit(solution)/shard_map/dot_general | solution.py:291
  14.1 0.0 collective-permute-done.2.ids_ref
  14.1 0.0 copy-start.4
  14.1 1.7 %decode.2.refs_4_ = bf16[2048,256]{1,0:T(8,128)(2,1)S(1)} custom-call(bf16[256,256]{1,0:T(8,128)(2,1)S(1)} %collective-permute-done.2.ids_ref, bf16[256,8,256]{2,1,0:T(8,128)(2,1)S(1)} %bitcast.21), custom_call_target="tpu_custom_call" | custom-call | bytes 2097152 | tf_op jit(solution)/shard_map/decode/pallas_call | solution.py:95
  15.9 0.0 collective-permute-done.3.ids_ref
  15.9 0.0 collective-permute-done.4
  15.9 1.7 %decode.3.refs_5_ = bf16[2048,256]{1,0:T(8,128)(2,1)S(1)} custom-call(bf16[256,256]{1,0:T(8,128)(2,1)S(1)} %collective-permute-done.3.ids_ref, bf16[256,8,256]{2,1,0:T(8,128)(2,1)S(1)} %bitcast.22), custom_call_target="tpu_custom_call" | custom-call | bytes 2097152 | tf_op jit(solution)/shard_map/decode/pallas_call | solution.py:95
  17.6 1.5 %collective-permute-done.1 = f16[64,1024]{1,0:T(8,128)(2,1)S(1)} collective-permute-done((f16[64,1024]{1,0:T(8,128)(2,1)S(1)}, f16[64,1024]{1,0:T(8,128)(2,1)S(1)}, u32[]{:S(2)}, u32[]{:S(2)}) %collective-permute-start.1) | collective-permute-done | bytes 131104 | tf_op jit(solution)/shard_map/ppermute | solution.py:218
  19.1 0.1 reduce-precision_convert_fusion
  19.2 0.0 copy-done.4
  19.2 0.3 fusion.4
  19.6 0.1 collective-permute-start.5
  19.6 1.2 %collective-permute-done.5.other_ref = f32[64,256]{1,0:T(8,128)S(1)} collective-permute-done((f32[64,256]{1,0:T(8,128)S(1)}, f32[64,256]{1,0:T(8,128)S(1)}, u32[]{:S(2)}, u32[]{:S(2)}) %collective-permute-start.5) | collective-permute-done | bytes 65568 | tf_op jit(solution)/shard_map/ppermute | solution.py:311
  20.9 0.6 %vectors.1 = f32[2,4,2048]{2,1,0:T(4,128)S(1)} custom-call(f32[64,256]{1,0:T(8,128)S(1)} %fusion.in_ref, f32[64,256]{1,0:T(8,128)S(1)} %slice_add_fusion.own_ref, f32[64,256]{1,0:T(8,128)S(1)} %collective-permute-done.5.other_ref), custom_call_target="tpu_custom_call" | custom-call | tf_op jit(solution)/shard_map/vectors/pallas_call | solution.py:183
  21.5 0.1 collective-permute-start.9
  21.6 3.0 %collective-permute-start.8 = (f16[2,4,2048]{2,1,0:T(4,128)(2,1)S(1)}, f16[2,4,2048]{2,1,0:T(4,128)(2,1)S(1)}, u32[]{:S(2)}, u32[]{:S(2)}) collective-permute-start(f16[2,4,2048]{2,1,0:T(4,128)(2,1)S(1)} %multiply_convert_fusion.2), channel_id=1, source_target_pairs={{0,12},{1,15},{2,14},{3,13},{4,8},{5,11},{6,10},{7,9},{8,4},{9,7},... | collective-permute-start | bytes 98312 | tf_op jit(solution)/shard_map/ppermute | solution.py:259
  24.6 0.5 %collective-permute-start.7 = (f16[2,4,2048]{2,1,0:T(4,128)(2,1)S(1)}, f16[2,4,2048]{2,1,0:T(4,128)(2,1)S(1)}, u32[]{:S(2)}, u32[]{:S(2)}) collective-permute-start(f16[2,4,2048]{2,1,0:T(4,128)(2,1)S(1)} %multiply_convert_fusion.2), channel_id=1, source_target_pairs={{0,4},{1,7},{2,6},{3,5},{4,0},{5,3},{6,2},{7,1},{8,12},{9,15},{10,... | collective-permute-start | bytes 98312 | tf_op jit(solution)/shard_map/ppermute | solution.py:259
  25.1 0.7 %collective-permute-start.6 = (f16[2,4,2048]{2,1,0:T(4,128)(2,1)S(1)}, f16[2,4,2048]{2,1,0:T(4,128)(2,1)S(1)}, u32[]{:S(2)}, u32[]{:S(2)}) collective-permute-start(f16[2,4,2048]{2,1,0:T(4,128)(2,1)S(1)} %multiply_convert_fusion.2), channel_id=1, source_target_pairs={{0,0},{1,3},{2,2},{3,1},{4,4},{5,7},{6,6},{7,5},{8,8},{9,11},{10,1... | collective-permute-start | bytes 98312 | tf_op jit(solution)/shard_map/ppermute | solution.py:259
  25.7 1.9 %collective-permute-done.9 = f16[2,4,2048]{2,1,0:T(4,128)(2,1)S(1)} collective-permute-done((f16[2,4,2048]{2,1,0:T(4,128)(2,1)S(1)}, f16[2,4,2048]{2,1,0:T(4,128)(2,1)S(1)}, u32[]{:S(2)}, u32[]{:S(2)}) %collective-permute-start.9) | collective-permute-done | bytes 32800 | tf_op jit(solution)/shard_map/ppermute | solution.py:259
  27.6 0.0 collective-permute-done.8
  27.7 1.1 %collective-permute-done.7 = f16[2,4,2048]{2,1,0:T(4,128)(2,1)S(1)} collective-permute-done((f16[2,4,2048]{2,1,0:T(4,128)(2,1)S(1)}, f16[2,4,2048]{2,1,0:T(4,128)(2,1)S(1)}, u32[]{:S(2)}, u32[]{:S(2)}) %collective-permute-start.7) | collective-permute-done | bytes 32800 | tf_op jit(solution)/shard_map/ppermute | solution.py:259
  28.8 0.0 collective-permute-done.6
  28.8 0.4 %score.1 = f32[16,256]{1,0:T(8,128)S(1)} custom-call(f32[2,4,2048]{2,1,0:T(4,128)S(1)} %convert_multiply_fusion.3.refs_0_, f32[2,4,2048]{2,1,0:T(4,128)S(1)} %convert_multiply_fusion.2.refs_1_, f32[2,4,2048]{2,1,0:T(4,128)S(1)} %convert_multiply_fusion.1.refs_2_, f32[2,4,2048]{2,1,0:T(4,128)S(1)} %convert_multiply_fusion.refs_3_, ...), custom_call_target="tpu_custom_call" | custom-call | tf_op jit(solution)/shard_map/score/pallas_call | solution.py:162
  29.2 1.5 %collective-permute-start.10 = (f32[16,256]{1,0:T(8,128)S(1)}, f32[16,256]{1,0:T(8,128)S(1)}, u32[]{:S(2)}, u32[]{:S(2)}) collective-permute-start(f32[16,256]{1,0:T(8,128)S(1)} %score.1), channel_id=1, source_target_pairs={{0,1},{1,0},{2,3},{3,2},{4,5},{5,4},{6,7},{7,6},{8,9},{9,8},{10,11... | collective-permute-start | bytes 49160 | tf_op jit(solution)/shard_map/ppermute | solution.py:321
  30.7 0.8 %collective-permute-done.10 = f32[16,256]{1,0:T(8,128)S(1)} collective-permute-done((f32[16,256]{1,0:T(8,128)S(1)}, f32[16,256]{1,0:T(8,128)S(1)}, u32[]{:S(2)}, u32[]{:S(2)}) %collective-permute-start.10) | collective-permute-done | bytes 16416 | tf_op jit(solution)/shard_map/ppermute | solution.py:321
  31.6 0.6 %select_bitcast_fusion = f32[256,16]{0,1:T(8,128)} fusion(f32[16,256]{1,0:T(8,128)S(1)} %score.1, f32[16,256]{1,0:T(8,128)S(1)} %collective-permute-done.10, pred[256]{0:T(512)(128)(4,1)S(1)} %compare_reduce_fusion), kind=kLoop, calls=%fused_computation.23 | loop fusion | flops 8192 | bytes 49408 | tf_op jit(solution)/shard_map/transpose | solution.py:326
  (9 shorter events, 0.1 us)
Async XLA Ops:
  0.0 1.7 %copy-start = (bf16[1,1024,1024]{2,1,0:T(8,128)(2,1)S(1)}, bf16[1,1024,1024]{2,1,0:T(8,128)(2,1)}, u32[]{:S(2)}) copy-start(bf16[1,1024,1024]{2,1,0:T(8,128)(2,1)} %param.10) | copy-start | bytes 6291460
  0.0 2.2 %copy-start.1 = (bf16[256,256,8]{1,2,0:T(8,128)(2,1)S(1)}, bf16[256,256,8]{1,2,0:T(8,128)(2,1)}, u32[]{:S(2)}) copy-start(bf16[256,256,8]{1,2,0:T(8,128)(2,1)} %param.13) | copy-start | bytes 3145732
  0.0 6.0 %copy-start.2 = (s32[256,1,256]{2,1,0:T(1,128)S(1)}, s32[256,1,256]{2,1,0:T(1,128)}, u32[]{:S(2)}) copy-start(s32[256,1,256]{2,1,0:T(1,128)} %codes_ref) | copy-start | bytes 786436
  0.0 12.3 %copy-start.3 = (bf16[1,256,4096]{2,1,0:T(8,128)(2,1)S(1)}, bf16[1,256,4096]{2,1,0:T(8,128)(2,1)}, u32[]{:S(2)}) copy-start(bf16[1,256,4096]{2,1,0:T(8,128)(2,1)} %param.8) | copy-start | bytes 6291460
  2.2 13.7 %collective-permute-start.4 = (bf16[256,256,8]{1,2,0:T(8,128)(2,1)S(1)}, bf16[256,256,8]{1,2,0:T(8,128)(2,1)S(1)}, u32[]{:S(2)}, u32[]{:S(2)}) collective-permute-start(bf16[256,256,8]{1,2,0:T(8,128)(2,1)S(1)} %copy-done.1), channel_id=1, source_target_pairs={{0,1},{1,0},{2,3},{3,2},{4,5},{5,4},{6,7},{7,6},{8,9},{9,8},{10,11... | collective-permute-start | bytes 3145736 | tf_op jit(solution)/shard_map/ppermute | solution.py:288
  2.7 6.7 %collective-permute-start = (f16[64,1024]{1,0:T(8,128)(2,1)S(1)}, f16[64,1024]{1,0:T(8,128)(2,1)S(1)}, u32[]{:S(2)}, u32[]{:S(2)}) collective-permute-start(f16[64,1024]{1,0:T(8,128)(2,1)S(1)} %get-tuple-element.15), channel_id=1, source_target_pairs={{0,4},{4,0},{8,12},{12,8},{1,5},{5,1},{9,13},{13,9},{2,6},{6,2},{1... | collective-permute-start | bytes 393224 | tf_op jit(solution)/shard_map/ppermute | solution.py:218
  6.2 9.7 %collective-permute-start.3 = (bf16[256,256]{1,0:T(8,128)(2,1)S(1)}, bf16[256,256]{1,0:T(8,128)(2,1)S(1)}, u32[]{:S(2)}, u32[]{:S(2)}) collective-permute-start(bf16[256,256]{1,0:T(8,128)(2,1)S(1)} %ids.1), channel_id=1, source_target_pairs={{1,0},{3,2},{2,1},{0,3},{5,4},{7,6},{6,5},{4,7},{9,8},{11,10},{10,... | collective-permute-start | bytes 393224 | tf_op jit(solution)/shard_map/ppermute | solution.py:287
  7.5 6.6 %collective-permute-start.2 = (bf16[256,256]{1,0:T(8,128)(2,1)S(1)}, bf16[256,256]{1,0:T(8,128)(2,1)S(1)}, u32[]{:S(2)}, u32[]{:S(2)}) collective-permute-start(bf16[256,256]{1,0:T(8,128)(2,1)S(1)} %ids.1), channel_id=1, source_target_pairs={{0,0},{2,2},{3,1},{1,3},{4,4},{6,6},{7,5},{5,7},{8,8},{10,10},{11,... | collective-permute-start | bytes 393224 | tf_op jit(solution)/shard_map/ppermute | solution.py:286
  9.5 9.7 %collective-permute-start.1 = (f16[64,1024]{1,0:T(8,128)(2,1)S(1)}, f16[64,1024]{1,0:T(8,128)(2,1)S(1)}, u32[]{:S(2)}, u32[]{:S(2)}) collective-permute-start(f16[64,1024]{1,0:T(8,128)(2,1)S(1)} %multiply_convert_fusion), channel_id=1, source_target_pairs={{0,8},{4,12},{8,0},{12,4},{1,9},{5,13},{9,1},{13,5},{2,10},{6,14},... | collective-permute-start | bytes 393224 | tf_op jit(solution)/shard_map/ppermute | solution.py:218
  14.1 5.1 %copy-start.4 = (bf16[1,256,1024]{2,1,0:T(8,128)(2,1)S(1)}, bf16[1,256,1024]{2,1,0:T(8,128)(2,1)}, u32[]{:S(2)}) copy-start(bf16[1,256,1024]{2,1,0:T(8,128)(2,1)} %param.9) | copy-start | bytes 1572868
  19.6 1.3 %collective-permute-start.5 = (f32[64,256]{1,0:T(8,128)S(1)}, f32[64,256]{1,0:T(8,128)S(1)}, u32[]{:S(2)}, u32[]{:S(2)}) collective-permute-start(f32[64,256]{1,0:T(8,128)S(1)} %slice_add_fusion.own_ref), channel_id=1, source_target_pairs={{0,1},{1,0},{2,3},{3,2},{4,5},{5,4},{6,7},{7,6},{8,9},{9,8},{10,11... | collective-permute-start | bytes 196616 | tf_op jit(solution)/shard_map/ppermute | solution.py:311
  21.5 6.1 %collective-permute-start.9 = (f16[2,4,2048]{2,1,0:T(4,128)(2,1)S(1)}, f16[2,4,2048]{2,1,0:T(4,128)(2,1)S(1)}, u32[]{:S(2)}, u32[]{:S(2)}) collective-permute-start(f16[2,4,2048]{2,1,0:T(4,128)(2,1)S(1)} %multiply_convert_fusion.2), channel_id=1, source_target_pairs={{0,8},{1,11},{2,10},{3,9},{4,12},{5,15},{6,14},{7,13},{8,0},{9,3},... | collective-permute-start | bytes 98312 | tf_op jit(solution)/shard_map/ppermute | solution.py:259
  21.6 6.1 %collective-permute-start.8 = (f16[2,4,2048]{2,1,0:T(4,128)(2,1)S(1)}, f16[2,4,2048]{2,1,0:T(4,128)(2,1)S(1)}, u32[]{:S(2)}, u32[]{:S(2)}) collective-permute-start(f16[2,4,2048]{2,1,0:T(4,128)(2,1)S(1)} %multiply_convert_fusion.2), channel_id=1, source_target_pairs={{0,12},{1,15},{2,14},{3,13},{4,8},{5,11},{6,10},{7,9},{8,4},{9,7},... | collective-permute-start | bytes 98312 | tf_op jit(solution)/shard_map/ppermute | solution.py:259
  24.6 4.1 %collective-permute-start.7 = (f16[2,4,2048]{2,1,0:T(4,128)(2,1)S(1)}, f16[2,4,2048]{2,1,0:T(4,128)(2,1)S(1)}, u32[]{:S(2)}, u32[]{:S(2)}) collective-permute-start(f16[2,4,2048]{2,1,0:T(4,128)(2,1)S(1)} %multiply_convert_fusion.2), channel_id=1, source_target_pairs={{0,4},{1,7},{2,6},{3,5},{4,0},{5,3},{6,2},{7,1},{8,12},{9,15},{10,... | collective-permute-start | bytes 98312 | tf_op jit(solution)/shard_map/ppermute | solution.py:259
  25.1 3.7 %collective-permute-start.6 = (f16[2,4,2048]{2,1,0:T(4,128)(2,1)S(1)}, f16[2,4,2048]{2,1,0:T(4,128)(2,1)S(1)}, u32[]{:S(2)}, u32[]{:S(2)}) collective-permute-start(f16[2,4,2048]{2,1,0:T(4,128)(2,1)S(1)} %multiply_convert_fusion.2), channel_id=1, source_target_pairs={{0,0},{1,3},{2,2},{3,1},{4,4},{5,7},{6,6},{7,5},{8,8},{9,11},{10,1... | collective-permute-start | bytes 98312 | tf_op jit(solution)/shard_map/ppermute | solution.py:259
  29.2 2.3 %collective-permute-start.10 = (f32[16,256]{1,0:T(8,128)S(1)}, f32[16,256]{1,0:T(8,128)S(1)}, u32[]{:S(2)}, u32[]{:S(2)}) collective-permute-start(f32[16,256]{1,0:T(8,128)S(1)} %score.1), channel_id=1, source_target_pairs={{0,1},{1,0},{2,3},{3,2},{4,5},{5,4},{6,7},{7,6},{8,9},{9,8},{10,11... | collective-permute-start | bytes 49160 | tf_op jit(solution)/shard_map/ppermute | solution.py:321

commit v8 on v7

--- a/solution.py
+++ b/solution.py
@@ -56,16 +56,19 @@
     )(codes)
 
 
-def decode_kernel(ids_ref, book_ref, out_ref):
+def decode_kernel(*refs):
+    *ids_refs, book_ref, out_ref = refs
+    core = lax.axis_index("sub")
     subs, width, code_count = book_ref.shape
-    slots = ids_ref.shape[1]
+    slots = ids_refs[0].shape[1]
     group = math.gcd(subs, 64)
 
     def several(step, carry):
         first = pl.multiple_of(step * group, group)
         for top in range(0, group, 16):
-            ids = ids_ref[pl.ds(pl.multiple_of(first + top, 16), 16), :]
-            ids = ids.astype(jnp.float32).astype(jnp.int32)
+            rows = pl.ds(pl.multiple_of(first + top, 16), 16)
+            ids = [ref[rows, :].astype(jnp.float32) for ref in ids_refs]
+            ids = jnp.where(core == 0, ids[0], ids[-1]).astype(jnp.int32)
             for pair in range(0, 16, 2):
                 halves = []
                 for sub in (pair, pair + 1):
@@ -91,16 +94,16 @@
 
 def decode(ids, book_t):
     subs, width, _ = book_t.shape
-    slots = ids.shape[1]
+    slots = ids[0].shape[1]
     return pl.pallas_call(
         decode_kernel,
         out_shape=jax.ShapeDtypeStruct((subs * width, slots), jnp.bfloat16),
-        in_specs=[pl.BlockSpec(memory_space=pltpu.VMEM)] * 2,
+        in_specs=[pl.BlockSpec(memory_space=pltpu.VMEM)] * (len(ids) + 1),
         out_specs=pl.BlockSpec(memory_space=pltpu.VMEM),
         compiler_params=pltpu.CompilerParams(vmem_limit_bytes=8 * 1024 * 1024),
         cost_estimate=pl.CostEstimate(flops=0, bytes_accessed=2 * 1024 * 1024, transcendentals=0),
         name="decode",
-    )(ids, book_t)
+    )(*ids, book_t)
 
 
 def vectors_kernel(in_ref, own_ref, other_ref, out_ref, grads_ref, flat_ref):
@@ -132,13 +135,16 @@
 
 
 def score_kernel(*refs):
-    *vector_refs, near_ref, far_ref, out_ref = refs
-    tests = vector_refs[0].shape[1]
+    own_ref, *vector_refs, near_ref, far_ref, out_ref = refs
+    tests = own_ref.shape[1]
     core = lax.axis_index("sub")
     own = lax.axis_index("dp")
     total = None
     for part, table_ref in ((core, near_ref), (1 - core, far_ref)):
-        vectors = jnp.concatenate([ref[part] for ref in vector_refs], axis=0)
+        vectors = [ref[part] for ref in vector_refs]
+        at = GATHER_ORDER.index(0)
+        vectors[at] = jnp.where(core == 0, own_ref[part], vectors[at])
+        vectors = jnp.concatenate(vectors, axis=0)
         high = vectors.astype(jnp.bfloat16)
         low = (vectors - high.astype(jnp.float32)).astype(jnp.bfloat16)
         both = jnp.dot(
@@ -157,16 +163,16 @@
     out_ref[...] = jnp.concatenate(rows, axis=0)
 
 
-def score_blocks(blocks, near, far):
+def score_blocks(own, blocks, near, far):
     tests = blocks[0].shape[1]
     return pl.pallas_call(
         score_kernel,
         out_shape=jax.ShapeDtypeStruct((len(blocks) * tests, near.shape[1]), jnp.float32),
-        in_specs=[pl.BlockSpec(memory_space=pltpu.VMEM)] * (len(blocks) + 2),
+        in_specs=[pl.BlockSpec(memory_space=pltpu.VMEM)] * (len(blocks) + 3),
         out_specs=pl.BlockSpec(memory_space=pltpu.VMEM),
         compiler_params=pltpu.CompilerParams(vmem_limit_bytes=8 * 1024 * 1024),
         name="score",
-    )(*blocks, near, far)
+    )(own, *blocks, near, far)
 
 
 def score(vectors, table):
@@ -242,7 +248,7 @@
     return lax.axis_size("layer") == 2 and lax.axis_size("sub") == 2
 
 
-NEAR_CODES = [(0, 0), (2, 2), (3, 1), (1, 3)]
+NEAR_CODES = [(3, 1), (1, 3)]
 FAR_CODES = [(1, 0), (3, 2), (2, 1), (0, 3)]
 
 
@@ -256,6 +262,8 @@
             for layer in range(2)
             for core in range(2)
         ]
+        if not step:
+            pairs = [(i, i ^ 2) for i in range(4 * size)]
         blocks.append(lax.ppermute(x, ("dp", "layer", "sub"), pairs))
     return blocks
 
@@ -283,7 +291,7 @@
     ids = make_ids(moved_codes)
     if by_core:
         sent, moved_book = lax.optimization_barrier((sent, codebook))
-        near_ids = lax.ppermute(ids, ("layer", "sub"), NEAR_CODES)
+        near_ids = lax.ppermute(ids, "layer", partners(2, 1))
         far_ids = lax.ppermute(ids, ("layer", "sub"), FAR_CODES)
         other_book = lax.ppermute(moved_book, "sub", partners(2, 1))
 
@@ -294,11 +302,13 @@
 
     def tables():
         if not by_core:
-            return (decode(ids, book_t),)
-        return decode(near_ids, book_t), decode(far_ids, jnp.transpose(other_book, (0, 2, 1)))
-
-    folded, (live, (in_side, decoded)) = sum_over_dp(
-        folded, sent, [lambda: live, lambda: (first_side(), tables())]
+            return (decode([ids], book_t),)
+        far = decode([far_ids], jnp.transpose(other_book, (0, 2, 1)))
+        far, late_ids = lax.optimization_barrier((far, near_ids))
+        return decode([ids, late_ids], book_t), far
+
+    folded, (live, decoded) = sum_over_dp(
+        folded, sent, [lambda: live, tables]
     )
     out_side = lax.dot_general(
         jnp.concatenate(split_high_low(folded), axis=0),
@@ -310,6 +320,7 @@
     other_side = lax.psum(out_side, "sub") - out_side if lax.axis_size("sub") != 2 else (
         lax.ppermute(out_side, "sub", partners(2, 1))
     )
+    other_side, in_side = lax.optimization_barrier((other_side, first_side()))
     vectors = make_vectors(in_side, out_side, other_side, dims_local)
     sent = (vectors * VECTOR_SCALE).astype(jnp.float16)
     core = lax.axis_index("sub")
@@ -317,7 +328,7 @@
         blocks = [
             block.astype(jnp.float32) * (1.0 / VECTOR_SCALE) for block in gather_by_core(sent)
         ]
-        total = score_blocks(blocks, *decoded)
+        total = score_blocks(vectors, blocks, *decoded)
         total = total + lax.ppermute(total, "sub", partners(2, 1))
     else:
         every = gather_over_dp(lax.dynamic_index_in_dim(sent, core, 0, False))

time: 32.3 us -> 31.6 us (0.978)
  matrix products: 2.6 us -> 1.55 us
  waiting for transfers between devices: 7.74 us -> 8.24 us
    ppermute x1, starting transfers between devices: 1.48 us -> 0.03 us  [per_device(): total = total + lax.ppermute(total, 'sub', partners(2, 1))]
    ppermute x4, starting transfers between devices: 4.24 us -> 5.59 us  [gather_by_core(): blocks.append(lax.ppermute(x, ('dp', 'layer', 'sub'), pairs))]
    ppermute x2, waiting for transfers between devices: 2.73 us -> 4.03 us  [sum_over_dp(): got = lax.ppermute(sent, 'dp', partners(size, step))]
    dot_general x1, matrix products: 1.8 us -> 0.76 us  [first_side(): lax.dot_general(proj_in, acts[0], (((0,), (1,)), ((), ())), preferred_ele...]
    ppermute x1, waiting for transfers between devices: 1.24 us -> 0.46 us  [per_device(): lax.ppermute(out_side, 'sub', partners(2, 1))]
    ppermute x4, waiting for transfers between devices: 2.94 us -> 2.6 us  [gather_by_core(): blocks.append(lax.ppermute(x, ('dp', 'layer', 'sub'), pairs))]
    ppermute x1, waiting for transfers between devices: 0.82 us -> 1.15 us  [per_device(): total = total + lax.ppermute(total, 'sub', partners(2, 1))]
  transfers between devices with their start and end apart: 11 -> 11, of which waited for: 6 -> 7; matrix products, arithmetic and copies ran while one was open for 6% -> 3% of each run, Pallas kernels for 11% -> 12%
where the time goes in v8:
time: 31.6 us; the launch traced here: 31.4 us
  starting transfers between devices  13.5 us (43%)
  waiting for transfers between devices  8.24 us (26%)
  Pallas kernels  4.7 us (15%)
  local copies, waits for them, and re-layouts  1.68 us (5%)
  matrix products  1.55 us (5%)
  other arithmetic  0.87 us (3%)
  between operations  0.85 us (3%)
    ppermute x4, starting transfers between devices, gather_by_core(): blocks.append(lax.ppermute(x, ('dp', 'layer', 'sub'), pairs))  5.59 us
    ppermute x2, starting transfers between devices, sum_over_dp(): got = lax.ppermute(sent, 'dp', partners(size, step))  5.49 us
    ppermute x2, waiting for transfers between devices, sum_over_dp(): got = lax.ppermute(sent, 'dp', partners(size, step))  4.03 us
    pallas_call x2, Pallas kernels, decode(): pl.pallas_call(decode_kernel, out_shape=jax.ShapeDtypeStruct((subs * widt...  3.48 us
    ppermute x4, waiting for transfers between devices, gather_by_core(): blocks.append(lax.ppermute(x, ('dp', 'layer', 'sub'), pairs))  2.6 us
    ppermute x1, starting transfers between devices, per_device(): far_ids = lax.ppermute(ids, ('layer', 'sub'), FAR_CODES)  1.31 us
    ppermute x1, waiting for transfers between devices, per_device(): total = total + lax.ppermute(total, 'sub', partners(2, 1))  1.15 us
    dynamic_slice x1, local copies, waits for them, and re-layouts, per_device(): lax.dynamic_slice_in_dim(jnp.transpose(proj_out), lax.axis_index('dp') *...  1.06 us
  transfers between devices with their start and end apart: 11, of which 7 were waited for; matrix products, arithmetic and copies ran while one was open for 3% of the time, Pallas kernels for 12%

profile of v8, /device:TPU:0, one launch (start us, length us, event | category | flops | bytes accessed | tf_op | source)
XLA Modules:
  0.0 31.4 jit_solution(15828401926280259471)
XLA Ops:
  0.0 0.0 copy-start
  0.0 0.0 copy-start.1
  0.0 0.0 copy-start.2
  0.0 1.1 %dynamic-slice_bitcast_fusion = bf16[64,1024]{1,0:T(8,128)(2,1)S(1)} fusion(bf16[4096,64]{0,1:T(8,128)(2,1)} %param.12, s32[]{:T(128)S(6)} %select_n.7), kind=kLoop, calls=%fused_computation.16 | loop fusion | bytes 262148 | tf_op jit(solution)/shard_map/dynamic_slice | solution.py:280
  1.1 0.6 %copy-done = bf16[1,1024,1024]{2,1,0:T(8,128)(2,1)S(1)} copy-done((bf16[1,1024,1024]{2,1,0:T(8,128)(2,1)S(1)}, bf16[1,1024,1024]{2,1,0:T(8,128)(2,1)}, u32[]{:S(2)}) %copy-start) | copy-done | bytes 2097176
  1.7 0.5 %multiply_convert_fusion.1 = (f16[64,1024]{1,0:T(8,128)(2,1)S(1)}, f32[64,1024]{1,0:T(8,128)S(1)}) fusion(bf16[64,1024]{1,0:T(8,128)(2,1)S(1)} %dynamic-slice_bitcast_fusion, bf16[1,1024,1024]{2,1,0:T(8,128)(2,1)S(1)} %copy-done), kind=kOutput, calls=%fused_computation.15 | convolution fusion | flops 134348800 | bytes 2621440 | tf_op jit(solution)/shard_map/dot_general | solution.py:284
  2.1 0.0 copy-done.1
  2.2 0.5 %collective-permute-start.3 = (bf16[256,256,8]{1,2,0:T(8,128)(2,1)S(1)}, bf16[256,256,8]{1,2,0:T(8,128)(2,1)S(1)}, u32[]{:S(2)}, u32[]{:S(2)}) collective-permute-start(bf16[256,256,8]{1,2,0:T(8,128)(2,1)S(1)} %copy-done.1), channel_id=1, source_target_pairs={{0,1},{1,0},{2,3},{3,2},{4,5},{5,4},{6,7},{7,6},{8,9},{9,8},{10,11... | collective-permute-start | bytes 3145736 | tf_op jit(solution)/shard_map/ppermute | solution.py:296
  2.7 2.6 %collective-permute-start = (f16[64,1024]{1,0:T(8,128)(2,1)S(1)}, f16[64,1024]{1,0:T(8,128)(2,1)S(1)}, u32[]{:S(2)}, u32[]{:S(2)}) collective-permute-start(f16[64,1024]{1,0:T(8,128)(2,1)S(1)} %get-tuple-element.18), channel_id=1, source_target_pairs={{0,4},{4,0},{8,12},{12,8},{1,5},{5,1},{9,13},{13,9},{2,6},{6,2},{1... | collective-permute-start | bytes 393224 | tf_op jit(solution)/shard_map/ppermute | solution.py:224
  6.0 0.0 copy-done.2
  6.0 0.2 ids.1.refs_0_
  6.2 1.3 %collective-permute-start.2 = (bf16[256,256]{1,0:T(8,128)(2,1)S(1)}, bf16[256,256]{1,0:T(8,128)(2,1)S(1)}, u32[]{:S(2)}, u32[]{:S(2)}) collective-permute-start(bf16[256,256]{1,0:T(8,128)(2,1)S(1)} %ids.1.refs_0_), channel_id=1, source_target_pairs={{1,0},{3,2},{2,1},{0,3},{5,4},{7,6},{6,5},{4,7},{9,8},{11,10},{10,... | collective-permute-start | bytes 393224 | tf_op jit(solution)/shard_map/ppermute | solution.py:295
  7.5 0.5 %collective-permute-start.4 = (bf16[256,256]{1,0:T(8,128)(2,1)S(1)}, bf16[256,256]{1,0:T(8,128)(2,1)S(1)}, u32[]{:S(2)}, u32[]{:S(2)}) collective-permute-start(bf16[256,256]{1,0:T(8,128)(2,1)S(1)} %ids.1.refs_0_), channel_id=1, source_target_pairs={{0,2},{2,0},{1,3},{3,1},{4,6},{6,4},{5,7},{7,5},{8,10},{10,8},{9,1... | collective-permute-start | bytes 393224 | tf_op jit(solution)/shard_map/ppermute | solution.py:294
  8.0 1.4 %collective-permute-done = f16[64,1024]{1,0:T(8,128)(2,1)S(1)} collective-permute-done((f16[64,1024]{1,0:T(8,128)(2,1)S(1)}, f16[64,1024]{1,0:T(8,128)(2,1)S(1)}, u32[]{:S(2)}, u32[]{:S(2)}) %collective-permute-start) | collective-permute-done | bytes 131104 | tf_op jit(solution)/shard_map/ppermute | solution.py:224
  9.4 0.1 multiply_convert_fusion
  9.5 2.8 %collective-permute-start.1 = (f16[64,1024]{1,0:T(8,128)(2,1)S(1)}, f16[64,1024]{1,0:T(8,128)(2,1)S(1)}, u32[]{:S(2)}, u32[]{:S(2)}) collective-permute-start(f16[64,1024]{1,0:T(8,128)(2,1)S(1)} %multiply_convert_fusion), channel_id=1, source_target_pairs={{0,8},{4,12},{8,0},{12,4},{1,9},{5,13},{9,1},{13,5},{2,10},{6,14},... | collective-permute-start | bytes 393224 | tf_op jit(solution)/shard_map/ppermute | solution.py:224
  12.3 0.0 collective-permute-done.2.refs_0_
  12.3 0.0 collective-permute-done.3
  12.3 1.7 %decode.2.refs_6_ = bf16[2048,256]{1,0:T(8,128)(2,1)S(1)} custom-call(bf16[256,256]{1,0:T(8,128)(2,1)S(1)} %collective-permute-done.2.refs_0_, bf16[256,8,256]{2,1,0:T(8,128)(2,1)S(1)} %bitcast.22), custom_call_target="tpu_custom_call" | custom-call | bytes 2097152 | tf_op jit(solution)/shard_map/decode/pallas_call | solution.py:98
  14.1 0.0 copy-start.4
  14.1 0.0 collective-permute-done.4.refs_1_
  14.1 0.0 copy-start.3
  14.1 0.0 copy-start.5
  14.1 1.7 %decode.3.refs_5_ = bf16[2048,256]{1,0:T(8,128)(2,1)S(1)} custom-call(bf16[256,256]{1,0:T(8,128)(2,1)S(1)} %ids.1.refs_0_, bf16[256,256]{1,0:T(8,128)(2,1)S(1)} %collective-permute-done.4.refs_1_, bf16[256,8,256]{2,1,0:T(8,128)(2,1)S(1)} %bitcast.21), custom_call_target="tpu_custom_call" | custom-call | bytes 2097152 | tf_op jit(solution)/shard_map/decode/pallas_call | solution.py:98
  15.8 2.7 %collective-permute-done.1 = f16[64,1024]{1,0:T(8,128)(2,1)S(1)} collective-permute-done((f16[64,1024]{1,0:T(8,128)(2,1)S(1)}, f16[64,1024]{1,0:T(8,128)(2,1)S(1)}, u32[]{:S(2)}, u32[]{:S(2)}) %collective-permute-start.1) | collective-permute-done | bytes 131104 | tf_op jit(solution)/shard_map/ppermute | solution.py:224
  18.5 0.1 reduce-precision_convert_fusion
  18.6 0.0 copy-done.4
  18.6 0.3 fusion.4
  18.9 0.1 collective-permute-start.5
  19.0 0.0 copy-done.3
  19.0 0.0 copy-done.5
  19.0 0.8 %fusion.in_ref = f32[64,256]{1,0:T(8,128)S(1)} fusion(bf16[4096,64]{0,1:T(8,128)(2,1)S(1)} %copy-done.5, bf16[1,256,4096]{2,1,0:T(8,128)(2,1)S(1)} %copy-done.3), kind=kOutput, calls=%fused_computation | convolution fusion | flops 134217728 | bytes 2686976 | tf_op jit(solution)/shard_map/dot_general | solution.py:299
  19.8 0.5 %collective-permute-done.5.other_ref = f32[64,256]{1,0:T(8,128)S(1)} collective-permute-done((f32[64,256]{1,0:T(8,128)S(1)}, f32[64,256]{1,0:T(8,128)S(1)}, u32[]{:S(2)}, u32[]{:S(2)}) %collective-permute-start.5) | collective-permute-done | bytes 65568 | tf_op jit(solution)/shard_map/ppermute | solution.py:321
  20.3 0.6 %vectors.1.refs_0_ = f32[2,4,2048]{2,1,0:T(4,128)S(1)} custom-call(f32[64,256]{1,0:T(8,128)S(1)} %fusion.in_ref, f32[64,256]{1,0:T(8,128)S(1)} %slice_add_fusion.own_ref, f32[64,256]{1,0:T(8,128)S(1)} %collective-permute-done.5.other_ref), custom_call_target="tpu_custom_call" | custom-call | tf_op jit(solution)/shard_map/vectors/pallas_call | solution.py:189
  20.9 0.1 collective-permute-start.9
  20.9 3.5 %collective-permute-start.8 = (f16[2,4,2048]{2,1,0:T(4,128)(2,1)S(1)}, f16[2,4,2048]{2,1,0:T(4,128)(2,1)S(1)}, u32[]{:S(2)}, u32[]{:S(2)}) collective-permute-start(f16[2,4,2048]{2,1,0:T(4,128)(2,1)S(1)} %multiply_convert_fusion.2), channel_id=1, source_target_pairs={{0,12},{1,15},{2,14},{3,13},{4,8},{5,11},{6,10},{7,9},{8,4},{9,7},... | collective-permute-start | bytes 98312 | tf_op jit(solution)/shard_map/ppermute | solution.py:267
  24.5 0.5 %collective-permute-start.7 = (f16[2,4,2048]{2,1,0:T(4,128)(2,1)S(1)}, f16[2,4,2048]{2,1,0:T(4,128)(2,1)S(1)}, u32[]{:S(2)}, u32[]{:S(2)}) collective-permute-start(f16[2,4,2048]{2,1,0:T(4,128)(2,1)S(1)} %multiply_convert_fusion.2), channel_id=1, source_target_pairs={{0,4},{1,7},{2,6},{3,5},{4,0},{5,3},{6,2},{7,1},{8,12},{9,15},{10,... | collective-permute-start | bytes 98312 | tf_op jit(solution)/shard_map/ppermute | solution.py:267
  25.0 1.5 %collective-permute-start.6 = (f16[2,4,2048]{2,1,0:T(4,128)(2,1)S(1)}, f16[2,4,2048]{2,1,0:T(4,128)(2,1)S(1)}, u32[]{:S(2)}, u32[]{:S(2)}) collective-permute-start(f16[2,4,2048]{2,1,0:T(4,128)(2,1)S(1)} %multiply_convert_fusion.2), channel_id=1, source_target_pairs={{0,2},{1,3},{2,0},{3,1},{4,6},{5,7},{6,4},{7,5},{8,10},{9,11},{10,... | collective-permute-start | bytes 98312 | tf_op jit(solution)/shard_map/ppermute | solution.py:267
  26.5 0.9 %collective-permute-done.9 = f16[2,4,2048]{2,1,0:T(4,128)(2,1)S(1)} collective-permute-done((f16[2,4,2048]{2,1,0:T(4,128)(2,1)S(1)}, f16[2,4,2048]{2,1,0:T(4,128)(2,1)S(1)}, u32[]{:S(2)}, u32[]{:S(2)}) %collective-permute-start.9) | collective-permute-done | bytes 32800 | tf_op jit(solution)/shard_map/ppermute | solution.py:267
  27.4 0.0 collective-permute-done.8
  27.4 1.2 %collective-permute-done.7 = f16[2,4,2048]{2,1,0:T(4,128)(2,1)S(1)} collective-permute-done((f16[2,4,2048]{2,1,0:T(4,128)(2,1)S(1)}, f16[2,4,2048]{2,1,0:T(4,128)(2,1)S(1)}, u32[]{:S(2)}, u32[]{:S(2)}) %collective-permute-start.7) | collective-permute-done | bytes 32800 | tf_op jit(solution)/shard_map/ppermute | solution.py:267
  28.7 0.4 %collective-permute-done.6 = f16[2,4,2048]{2,1,0:T(4,128)(2,1)S(1)} collective-permute-done((f16[2,4,2048]{2,1,0:T(4,128)(2,1)S(1)}, f16[2,4,2048]{2,1,0:T(4,128)(2,1)S(1)}, u32[]{:S(2)}, u32[]{:S(2)}) %collective-permute-start.6) | collective-permute-done | bytes 32800 | tf_op jit(solution)/shard_map/ppermute | solution.py:267
  29.2 0.5 %score.1 = f32[16,256]{1,0:T(8,128)S(1)} custom-call(f32[2,4,2048]{2,1,0:T(4,128)S(1)} %vectors.1.refs_0_, f32[2,4,2048]{2,1,0:T(4,128)S(1)} %convert_multiply_fusion.3.refs_1_, f32[2,4,2048]{2,1,0:T(4,128)S(1)} %convert_multiply_fusion.2.refs_2_, f32[2,4,2048]{2,1,0:T(4,128)S(1)} %convert_multiply_fusion.1.refs_3_, ...), custom_call_target="tpu_custom_call" | custom-call | tf_op jit(solution)/shard_map/score/pallas_call | solution.py:168
  29.6 0.0 collective-permute-start.10
  29.7 1.1 %collective-permute-done.10 = f32[16,256]{1,0:T(8,128)S(1)} collective-permute-done((f32[16,256]{1,0:T(8,128)S(1)}, f32[16,256]{1,0:T(8,128)S(1)}, u32[]{:S(2)}, u32[]{:S(2)}) %collective-permute-start.10) | collective-permute-done | bytes 16416 | tf_op jit(solution)/shard_map/ppermute | solution.py:332
  30.8 0.6 %select_bitcast_fusion = f32[256,16]{0,1:T(8,128)} fusion(f32[16,256]{1,0:T(8,128)S(1)} %score.1, f32[16,256]{1,0:T(8,128)S(1)} %collective-permute-done.10, pred[256]{0:T(512)(128)(4,1)S(1)} %compare_reduce_fusion), kind=kLoop, calls=%fused_computation.23 | loop fusion | flops 8192 | bytes 49408 | tf_op jit(solution)/shard_map/transpose | solution.py:337
  (9 shorter events, 0.1 us)
Async XLA Ops:
  0.0 1.7 %copy-start = (bf16[1,1024,1024]{2,1,0:T(8,128)(2,1)S(1)}, bf16[1,1024,1024]{2,1,0:T(8,128)(2,1)}, u32[]{:S(2)}) copy-start(bf16[1,1024,1024]{2,1,0:T(8,128)(2,1)} %param.10) | copy-start | bytes 6291460
  0.0 2.1 %copy-start.1 = (bf16[256,256,8]{1,2,0:T(8,128)(2,1)S(1)}, bf16[256,256,8]{1,2,0:T(8,128)(2,1)}, u32[]{:S(2)}) copy-start(bf16[256,256,8]{1,2,0:T(8,128)(2,1)} %param.13) | copy-start | bytes 3145732
  0.0 6.0 %copy-start.2 = (s32[256,1,256]{2,1,0:T(1,128)S(1)}, s32[256,1,256]{2,1,0:T(1,128)}, u32[]{:S(2)}) copy-start(s32[256,1,256]{2,1,0:T(1,128)} %codes_ref) | copy-start | bytes 786436
  2.2 10.2 %collective-permute-start.3 = (bf16[256,256,8]{1,2,0:T(8,128)(2,1)S(1)}, bf16[256,256,8]{1,2,0:T(8,128)(2,1)S(1)}, u32[]{:S(2)}, u32[]{:S(2)}) collective-permute-start(bf16[256,256,8]{1,2,0:T(8,128)(2,1)S(1)} %copy-done.1), channel_id=1, source_target_pairs={{0,1},{1,0},{2,3},{3,2},{4,5},{5,4},{6,7},{7,6},{8,9},{9,8},{10,11... | collective-permute-start | bytes 3145736 | tf_op jit(solution)/shard_map/ppermute | solution.py:296
  2.7 6.7 %collective-permute-start = (f16[64,1024]{1,0:T(8,128)(2,1)S(1)}, f16[64,1024]{1,0:T(8,128)(2,1)S(1)}, u32[]{:S(2)}, u32[]{:S(2)}) collective-permute-start(f16[64,1024]{1,0:T(8,128)(2,1)S(1)} %get-tuple-element.18), channel_id=1, source_target_pairs={{0,4},{4,0},{8,12},{12,8},{1,5},{5,1},{9,13},{13,9},{2,6},{6,2},{1... | collective-permute-start | bytes 393224 | tf_op jit(solution)/shard_map/ppermute | solution.py:224
  6.2 6.1 %collective-permute-start.2 = (bf16[256,256]{1,0:T(8,128)(2,1)S(1)}, bf16[256,256]{1,0:T(8,128)(2,1)S(1)}, u32[]{:S(2)}, u32[]{:S(2)}) collective-permute-start(bf16[256,256]{1,0:T(8,128)(2,1)S(1)} %ids.1.refs_0_), channel_id=1, source_target_pairs={{1,0},{3,2},{2,1},{0,3},{5,4},{7,6},{6,5},{4,7},{9,8},{11,10},{10,... | collective-permute-start | bytes 393224 | tf_op jit(solution)/shard_map/ppermute | solution.py:295
  7.5 6.6 %collective-permute-start.4 = (bf16[256,256]{1,0:T(8,128)(2,1)S(1)}, bf16[256,256]{1,0:T(8,128)(2,1)S(1)}, u32[]{:S(2)}, u32[]{:S(2)}) collective-permute-start(bf16[256,256]{1,0:T(8,128)(2,1)S(1)} %ids.1.refs_0_), channel_id=1, source_target_pairs={{0,2},{2,0},{1,3},{3,1},{4,6},{6,4},{5,7},{7,5},{8,10},{10,8},{9,1... | collective-permute-start | bytes 393224 | tf_op jit(solution)/shard_map/ppermute | solution.py:294
  9.5 9.0 %collective-permute-start.1 = (f16[64,1024]{1,0:T(8,128)(2,1)S(1)}, f16[64,1024]{1,0:T(8,128)(2,1)S(1)}, u32[]{:S(2)}, u32[]{:S(2)}) collective-permute-start(f16[64,1024]{1,0:T(8,128)(2,1)S(1)} %multiply_convert_fusion), channel_id=1, source_target_pairs={{0,8},{4,12},{8,0},{12,4},{1,9},{5,13},{9,1},{13,5},{2,10},{6,14},... | collective-permute-start | bytes 393224 | tf_op jit(solution)/shard_map/ppermute | solution.py:224
  14.1 4.5 %copy-start.4 = (bf16[1,256,1024]{2,1,0:T(8,128)(2,1)S(1)}, bf16[1,256,1024]{2,1,0:T(8,128)(2,1)}, u32[]{:S(2)}) copy-start(bf16[1,256,1024]{2,1,0:T(8,128)(2,1)} %param.9) | copy-start | bytes 1572868
  14.1 4.9 %copy-start.3 = (bf16[1,256,4096]{2,1,0:T(8,128)(2,1)S(1)}, bf16[1,256,4096]{2,1,0:T(8,128)(2,1)}, u32[]{:S(2)}) copy-start(bf16[1,256,4096]{2,1,0:T(8,128)(2,1)} %param.8) | copy-start | bytes 6291460
  14.1 4.9 %copy-start.5 = (bf16[4096,64]{0,1:T(8,128)(2,1)S(1)}, bf16[4096,64]{0,1:T(8,128)(2,1)}, u32[]{:S(2)}) copy-start(bf16[4096,64]{0,1:T(8,128)(2,1)} %param.11) | copy-start | bytes 1572868
  18.9 1.3 %collective-permute-start.5 = (f32[64,256]{1,0:T(8,128)S(1)}, f32[64,256]{1,0:T(8,128)S(1)}, u32[]{:S(2)}, u32[]{:S(2)}) collective-permute-start(f32[64,256]{1,0:T(8,128)S(1)} %slice_add_fusion.own_ref), channel_id=1, source_target_pairs={{0,1},{1,0},{2,3},{3,2},{4,5},{5,4},{6,7},{7,6},{8,9},{9,8},{10,11... | collective-permute-start | bytes 196616 | tf_op jit(solution)/shard_map/ppermute | solution.py:321
  20.9 6.5 %collective-permute-start.9 = (f16[2,4,2048]{2,1,0:T(4,128)(2,1)S(1)}, f16[2,4,2048]{2,1,0:T(4,128)(2,1)S(1)}, u32[]{:S(2)}, u32[]{:S(2)}) collective-permute-start(f16[2,4,2048]{2,1,0:T(4,128)(2,1)S(1)} %multiply_convert_fusion.2), channel_id=1, source_target_pairs={{0,8},{1,11},{2,10},{3,9},{4,12},{5,15},{6,14},{7,13},{8,0},{9,3},... | collective-permute-start | bytes 98312 | tf_op jit(solution)/shard_map/ppermute | solution.py:267
  20.9 6.5 %collective-permute-start.8 = (f16[2,4,2048]{2,1,0:T(4,128)(2,1)S(1)}, f16[2,4,2048]{2,1,0:T(4,128)(2,1)S(1)}, u32[]{:S(2)}, u32[]{:S(2)}) collective-permute-start(f16[2,4,2048]{2,1,0:T(4,128)(2,1)S(1)} %multiply_convert_fusion.2), channel_id=1, source_target_pairs={{0,12},{1,15},{2,14},{3,13},{4,8},{5,11},{6,10},{7,9},{8,4},{9,7},... | collective-permute-start | bytes 98312 | tf_op jit(solution)/shard_map/ppermute | solution.py:267
  24.5 4.2 %collective-permute-start.7 = (f16[2,4,2048]{2,1,0:T(4,128)(2,1)S(1)}, f16[2,4,2048]{2,1,0:T(4,128)(2,1)S(1)}, u32[]{:S(2)}, u32[]{:S(2)}) collective-permute-start(f16[2,4,2048]{2,1,0:T(4,128)(2,1)S(1)} %multiply_convert_fusion.2), channel_id=1, source_target_pairs={{0,4},{1,7},{2,6},{3,5},{4,0},{5,3},{6,2},{7,1},{8,12},{9,15},{10,... | collective-permute-start | bytes 98312 | tf_op jit(solution)/shard_map/ppermute | solution.py:267
  25.0 4.2 %collective-permute-start.6 = (f16[2,4,2048]{2,1,0:T(4,128)(2,1)S(1)}, f16[2,4,2048]{2,1,0:T(4,128)(2,1)S(1)}, u32[]{:S(2)}, u32[]{:S(2)}) collective-permute-start(f16[2,4,2048]{2,1,0:T(4,128)(2,1)S(1)} %multiply_convert_fusion.2), channel_id=1, source_target_pairs={{0,2},{1,3},{2,0},{3,1},{4,6},{5,7},{6,4},{7,5},{8,10},{9,11},{10,... | collective-permute-start | bytes 98312 | tf_op jit(solution)/shard_map/ppermute | solution.py:267
  29.6 1.2 %collective-permute-start.10 = (f32[16,256]{1,0:T(8,128)S(1)}, f32[16,256]{1,0:T(8,128)S(1)}, u32[]{:S(2)}, u32[]{:S(2)}) collective-permute-start(f32[16,256]{1,0:T(8,128)S(1)} %score.1), channel_id=1, source_target_pairs={{0,1},{1,0},{2,3},{3,2},{4,5},{5,4},{6,7},{7,6},{8,9},{9,8},{10,11... | collective-permute-start | bytes 49160 | tf_op jit(solution)/shard_map/ppermute | solution.py:332

commit v9 on v8

--- a/solution.py
+++ b/solution.py
@@ -214,20 +214,24 @@
 
 
 def sum_over_dp(x, sent, beside):
-    size = lax.axis_size("dp")
+    size, cores = lax.axis_size("dp"), lax.axis_size("sub")
     beside = list(beside)
     made = []
     if not is_power_of_two(size):
         return lax.psum(x, "dp"), [work() for work in beside]
-    step = 1
-    while step < size:
-        got = lax.ppermute(sent, "dp", partners(size, step))
+    steps = [1 << at for at in range(size.bit_length() - 1)]
+    for steps_of_core in zip(steps, steps[::-1]):
+        pairs = [
+            (cores * at + core, cores * (at ^ steps_of_core[1 - core % 2]) + core)
+            for at in range(size)
+            for core in range(cores)
+        ]
+        got = lax.ppermute(sent, ("dp", "sub"), pairs)
         if beside:
             got, done = lax.optimization_barrier((got, beside.pop(0)()))
             made.append(done)
         x = x + got.astype(jnp.float32) * (1.0 / LINK_SCALE)
         sent = (x * LINK_SCALE).astype(jnp.float16)
-        step *= 2
     return x, made + [work() for work in beside]
 
 

time: 31.6 us -> 29.9 us (0.946)
  waiting for transfers between devices: 8.24 us -> 5.79 us
  starting transfers between devices: 13.5 us -> 14.4 us
    ppermute x2, waiting for transfers between devices: 4.03 us -> 0.69 us  [sum_over_dp(): got = lax.ppermute(sent, ('dp', 'sub'), pairs)]
    ppermute x1, starting transfers between devices: 1.31 us -> 0.29 us  [per_device(): far_ids = lax.ppermute(ids, ('layer', 'sub'), FAR_CODES)]
    ppermute x2, starting transfers between devices: 5.49 us -> 6.38 us  [sum_over_dp(): got = lax.ppermute(sent, ('dp', 'sub'), pairs)]
    ppermute x1, starting transfers between devices: 0.54 us -> 1.33 us  [per_device(): near_ids = lax.ppermute(ids, 'layer', partners(2, 1))]
    ppermute x4, waiting for transfers between devices: 2.6 us -> 3.34 us  [gather_by_core(): blocks.append(lax.ppermute(x, ('dp', 'layer', 'sub'), pairs))]
    ppermute x1, waiting for transfers between devices: 0.01 us -> 0.46 us  [per_device(): near_ids = lax.ppermute(ids, 'layer', partners(2, 1))]
  transfers between devices with their start and end apart: 11 -> 11, of which waited for: 7 -> 6; matrix products, arithmetic and copies ran while one was open for 3% -> 3% of each run, Pallas kernels for 12% -> 12%
where the time goes in v9:
time: 29.9 us; the launch traced here: 29.8 us
  starting transfers between devices  14.4 us (48%)
  waiting for transfers between devices  5.79 us (19%)
  Pallas kernels  4.69 us (16%)
  local copies, waits for them, and re-layouts  1.67 us (6%)
  matrix products  1.55 us (5%)
  other arithmetic  0.87 us (3%)
  between operations  0.81 us (3%)
    ppermute x2, starting transfers between devices, sum_over_dp(): got = lax.ppermute(sent, ('dp', 'sub'), pairs)  6.38 us
    ppermute x4, starting transfers between devices, gather_by_core(): blocks.append(lax.ppermute(x, ('dp', 'layer', 'sub'), pairs))  5.46 us
    pallas_call x2, Pallas kernels, decode(): pl.pallas_call(decode_kernel, out_shape=jax.ShapeDtypeStruct((subs * widt...  3.47 us
    ppermute x4, waiting for transfers between devices, gather_by_core(): blocks.append(lax.ppermute(x, ('dp', 'layer', 'sub'), pairs))  3.34 us
    ppermute x1, starting transfers between devices, per_device(): near_ids = lax.ppermute(ids, 'layer', partners(2, 1))  1.33 us
    dynamic_slice x1, local copies, waits for them, and re-layouts, per_device(): lax.dynamic_slice_in_dim(jnp.transpose(proj_out), lax.axis_index('dp') *...  1.06 us
    ppermute x1, waiting for transfers between devices, per_device(): total = total + lax.ppermute(total, 'sub', partners(2, 1))  0.95 us
    dot_general x1, matrix products, first_side(): lax.dot_general(proj_in, acts[0], (((0,), (1,)), ((), ())), preferred_ele...  0.76 us
  transfers between devices with their start and end apart: 11, of which 6 were waited for; matrix products, arithmetic and copies ran while one was open for 3% of the time, Pallas kernels for 12%

profile of v9, /device:TPU:0, one launch (start us, length us, event | category | flops | bytes accessed | tf_op | source)
XLA Modules:
  0.0 29.8 jit_solution(6280059435360374807)
XLA Ops:
  0.0 0.0 copy-start
  0.0 0.0 copy-start.1
  0.0 0.0 copy-start.2
  0.0 1.1 %dynamic-slice_bitcast_fusion = bf16[64,1024]{1,0:T(8,128)(2,1)S(1)} fusion(bf16[4096,64]{0,1:T(8,128)(2,1)} %param.12, s32[]{:T(128)S(6)} %select_n.7), kind=kLoop, calls=%fused_computation.16 | loop fusion | bytes 262148 | tf_op jit(solution)/shard_map/dynamic_slice | solution.py:284
  1.1 0.6 %copy-done = bf16[1,1024,1024]{2,1,0:T(8,128)(2,1)S(1)} copy-done((bf16[1,1024,1024]{2,1,0:T(8,128)(2,1)S(1)}, bf16[1,1024,1024]{2,1,0:T(8,128)(2,1)}, u32[]{:S(2)}) %copy-start) | copy-done | bytes 2097176
  1.7 0.5 %multiply_convert_fusion.1 = (f16[64,1024]{1,0:T(8,128)(2,1)S(1)}, f32[64,1024]{1,0:T(8,128)S(1)}) fusion(bf16[64,1024]{1,0:T(8,128)(2,1)S(1)} %dynamic-slice_bitcast_fusion, bf16[1,1024,1024]{2,1,0:T(8,128)(2,1)S(1)} %copy-done), kind=kOutput, calls=%fused_computation.15 | convolution fusion | flops 134348800 | bytes 2621440 | tf_op jit(solution)/shard_map/dot_general | solution.py:288
  2.1 0.0 copy-done.1
  2.2 0.5 %collective-permute-start.3 = (bf16[256,256,8]{1,2,0:T(8,128)(2,1)S(1)}, bf16[256,256,8]{1,2,0:T(8,128)(2,1)S(1)}, u32[]{:S(2)}, u32[]{:S(2)}) collective-permute-start(bf16[256,256,8]{1,2,0:T(8,128)(2,1)S(1)} %copy-done.1), channel_id=1, source_target_pairs={{0,1},{1,0},{2,3},{3,2},{4,5},{5,4},{6,7},{7,6},{8,9},{9,8},{10,11... | collective-permute-start | bytes 3145736 | tf_op jit(solution)/shard_map/ppermute | solution.py:300
  2.7 3.7 %collective-permute-start = (f16[64,1024]{1,0:T(8,128)(2,1)S(1)}, f16[64,1024]{1,0:T(8,128)(2,1)S(1)}, u32[]{:S(2)}, u32[]{:S(2)}) collective-permute-start(f16[64,1024]{1,0:T(8,128)(2,1)S(1)} %get-tuple-element.18), channel_id=1, source_target_pairs={{0,8},{1,5},{4,12},{5,1},{8,0},{9,13},{12,4},{13,9},{2,10},{3,7},{... | collective-permute-start | bytes 393224 | tf_op jit(solution)/shard_map/ppermute | solution.py:229
  7.0 0.0 copy-done.2
  7.0 0.2 ids.1.refs_0_
  7.2 0.3 collective-permute-start.2
  7.5 1.3 %collective-permute-start.4 = (bf16[256,256]{1,0:T(8,128)(2,1)S(1)}, bf16[256,256]{1,0:T(8,128)(2,1)S(1)}, u32[]{:S(2)}, u32[]{:S(2)}) collective-permute-start(bf16[256,256]{1,0:T(8,128)(2,1)S(1)} %ids.1.refs_0_), channel_id=1, source_target_pairs={{0,2},{2,0},{1,3},{3,1},{4,6},{6,4},{5,7},{7,5},{8,10},{10,8},{9,1... | collective-permute-start | bytes 393224 | tf_op jit(solution)/shard_map/ppermute | solution.py:298
  8.8 0.7 %collective-permute-done = f16[64,1024]{1,0:T(8,128)(2,1)S(1)} collective-permute-done((f16[64,1024]{1,0:T(8,128)(2,1)S(1)}, f16[64,1024]{1,0:T(8,128)(2,1)S(1)}, u32[]{:S(2)}, u32[]{:S(2)}) %collective-permute-start) | collective-permute-done | bytes 131104 | tf_op jit(solution)/shard_map/ppermute | solution.py:229
  9.5 0.1 multiply_convert_fusion
  9.6 2.7 %collective-permute-start.1 = (f16[64,1024]{1,0:T(8,128)(2,1)S(1)}, f16[64,1024]{1,0:T(8,128)(2,1)S(1)}, u32[]{:S(2)}, u32[]{:S(2)}) collective-permute-start(f16[64,1024]{1,0:T(8,128)(2,1)S(1)} %multiply_convert_fusion), channel_id=1, source_target_pairs={{0,4},{1,9},{4,0},{5,13},{8,12},{9,1},{12,8},{13,5},{2,6},{3,11},{... | collective-permute-start | bytes 393224 | tf_op jit(solution)/shard_map/ppermute | solution.py:229
  12.3 0.0 collective-permute-done.2.refs_0_
  12.3 0.0 collective-permute-done.3
  12.3 1.7 %decode.2.refs_6_ = bf16[2048,256]{1,0:T(8,128)(2,1)S(1)} custom-call(bf16[256,256]{1,0:T(8,128)(2,1)S(1)} %collective-permute-done.2.refs_0_, bf16[256,8,256]{2,1,0:T(8,128)(2,1)S(1)} %bitcast.22), custom_call_target="tpu_custom_call" | custom-call | bytes 2097152 | tf_op jit(solution)/shard_map/decode/pallas_call | solution.py:98
  14.0 0.0 copy-start.4
  14.0 0.5 %collective-permute-done.4.refs_1_ = bf16[256,256]{1,0:T(8,128)(2,1)S(1)} collective-permute-done((bf16[256,256]{1,0:T(8,128)(2,1)S(1)}, bf16[256,256]{1,0:T(8,128)(2,1)S(1)}, u32[]{:S(2)}, u32[]{:S(2)}) %collective-permute-start.4) | collective-permute-done | bytes 131104 | tf_op jit(solution)/shard_map/ppermute | solution.py:298
  14.5 0.0 copy-start.3
  14.5 0.0 copy-start.5
  14.5 1.7 %decode.3.refs_5_ = bf16[2048,256]{1,0:T(8,128)(2,1)S(1)} custom-call(bf16[256,256]{1,0:T(8,128)(2,1)S(1)} %ids.1.refs_0_, bf16[256,256]{1,0:T(8,128)(2,1)S(1)} %collective-permute-done.4.refs_1_, bf16[256,8,256]{2,1,0:T(8,128)(2,1)S(1)} %bitcast.21), custom_call_target="tpu_custom_call" | custom-call | bytes 2097152 | tf_op jit(solution)/shard_map/decode/pallas_call | solution.py:98
  16.2 0.0 collective-permute-done.1
  16.3 0.1 reduce-precision_convert_fusion
  16.4 0.0 copy-done.4
  16.4 0.3 %fusion.4 = f32[128,256]{1,0:T(8,128)S(1)} fusion(bf16[1,256,1024]{2,1,0:T(8,128)(2,1)S(1)} %copy-done.4, bf16[64,1024]{1,0:T(8,128)(2,1)S(1)} %get-tuple-element.32, bf16[64,1024]{1,0:T(8,128)(2,1)S(1)} %get-tuple-element.31), kind=kOutput, calls=%fused_computation.4 | convolution fusion | flops 67633152 | bytes 917504 | tf_op jit(solution)/shard_map/dot_general | solution.py:317
  16.7 0.2 collective-permute-start.5
  16.9 0.0 copy-done.3
  16.9 0.0 copy-done.5
  16.9 0.8 %fusion.in_ref = f32[64,256]{1,0:T(8,128)S(1)} fusion(bf16[4096,64]{0,1:T(8,128)(2,1)S(1)} %copy-done.5, bf16[1,256,4096]{2,1,0:T(8,128)(2,1)S(1)} %copy-done.3), kind=kOutput, calls=%fused_computation | convolution fusion | flops 134217728 | bytes 2686976 | tf_op jit(solution)/shard_map/dot_general | solution.py:303
  17.7 0.4 %collective-permute-done.5.other_ref = f32[64,256]{1,0:T(8,128)S(1)} collective-permute-done((f32[64,256]{1,0:T(8,128)S(1)}, f32[64,256]{1,0:T(8,128)S(1)}, u32[]{:S(2)}, u32[]{:S(2)}) %collective-permute-start.5) | collective-permute-done | bytes 65568 | tf_op jit(solution)/shard_map/ppermute | solution.py:325
  18.0 0.6 %vectors.1.refs_0_ = f32[2,4,2048]{2,1,0:T(4,128)S(1)} custom-call(f32[64,256]{1,0:T(8,128)S(1)} %fusion.in_ref, f32[64,256]{1,0:T(8,128)S(1)} %slice_add_fusion.own_ref, f32[64,256]{1,0:T(8,128)S(1)} %collective-permute-done.5.other_ref), custom_call_target="tpu_custom_call" | custom-call | tf_op jit(solution)/shard_map/vectors/pallas_call | solution.py:189
  18.6 2.5 %collective-permute-start.9 = (f16[2,4,2048]{2,1,0:T(4,128)(2,1)S(1)}, f16[2,4,2048]{2,1,0:T(4,128)(2,1)S(1)}, u32[]{:S(2)}, u32[]{:S(2)}) collective-permute-start(f16[2,4,2048]{2,1,0:T(4,128)(2,1)S(1)} %multiply_convert_fusion.2), channel_id=1, source_target_pairs={{0,8},{1,11},{2,10},{3,9},{4,12},{5,15},{6,14},{7,13},{8,0},{9,3},... | collective-permute-start | bytes 98312 | tf_op jit(solution)/shard_map/ppermute | solution.py:271
  21.2 1.5 %collective-permute-start.8 = (f16[2,4,2048]{2,1,0:T(4,128)(2,1)S(1)}, f16[2,4,2048]{2,1,0:T(4,128)(2,1)S(1)}, u32[]{:S(2)}, u32[]{:S(2)}) collective-permute-start(f16[2,4,2048]{2,1,0:T(4,128)(2,1)S(1)} %multiply_convert_fusion.2), channel_id=1, source_target_pairs={{0,12},{1,15},{2,14},{3,13},{4,8},{5,11},{6,10},{7,9},{8,4},{9,7},... | collective-permute-start | bytes 98312 | tf_op jit(solution)/shard_map/ppermute | solution.py:271
  22.6 0.0 collective-permute-start.7
  22.6 1.5 %collective-permute-start.6 = (f16[2,4,2048]{2,1,0:T(4,128)(2,1)S(1)}, f16[2,4,2048]{2,1,0:T(4,128)(2,1)S(1)}, u32[]{:S(2)}, u32[]{:S(2)}) collective-permute-start(f16[2,4,2048]{2,1,0:T(4,128)(2,1)S(1)} %multiply_convert_fusion.2), channel_id=1, source_target_pairs={{0,2},{1,3},{2,0},{3,1},{4,6},{5,7},{6,4},{7,5},{8,10},{9,11},{10,... | collective-permute-start | bytes 98312 | tf_op jit(solution)/shard_map/ppermute | solution.py:271
  24.1 0.0 collective-permute-done.9
  24.1 3.0 %collective-permute-done.8 = f16[2,4,2048]{2,1,0:T(4,128)(2,1)S(1)} collective-permute-done((f16[2,4,2048]{2,1,0:T(4,128)(2,1)S(1)}, f16[2,4,2048]{2,1,0:T(4,128)(2,1)S(1)}, u32[]{:S(2)}, u32[]{:S(2)}) %collective-permute-start.8) | collective-permute-done | bytes 32800 | tf_op jit(solution)/shard_map/ppermute | solution.py:271
  27.2 0.3 %collective-permute-done.7 = f16[2,4,2048]{2,1,0:T(4,128)(2,1)S(1)} collective-permute-done((f16[2,4,2048]{2,1,0:T(4,128)(2,1)S(1)}, f16[2,4,2048]{2,1,0:T(4,128)(2,1)S(1)}, u32[]{:S(2)}, u32[]{:S(2)}) %collective-permute-start.7) | collective-permute-done | bytes 32800 | tf_op jit(solution)/shard_map/ppermute | solution.py:271
  27.5 0.0 collective-permute-done.6
  27.5 0.5 %score.1 = f32[16,256]{1,0:T(8,128)S(1)} custom-call(f32[2,4,2048]{2,1,0:T(4,128)S(1)} %vectors.1.refs_0_, f32[2,4,2048]{2,1,0:T(4,128)S(1)} %convert_multiply_fusion.3.refs_1_, f32[2,4,2048]{2,1,0:T(4,128)S(1)} %convert_multiply_fusion.2.refs_2_, f32[2,4,2048]{2,1,0:T(4,128)S(1)} %convert_multiply_fusion.1.refs_3_, ...), custom_call_target="tpu_custom_call" | custom-call | tf_op jit(solution)/shard_map/score/pallas_call | solution.py:168
  28.0 0.2 collective-permute-start.10
  28.2 0.9 %collective-permute-done.10 = f32[16,256]{1,0:T(8,128)S(1)} collective-permute-done((f32[16,256]{1,0:T(8,128)S(1)}, f32[16,256]{1,0:T(8,128)S(1)}, u32[]{:S(2)}, u32[]{:S(2)}) %collective-permute-start.10) | collective-permute-done | bytes 16416 | tf_op jit(solution)/shard_map/ppermute | solution.py:336
  29.2 0.6 %select_bitcast_fusion = f32[256,16]{0,1:T(8,128)} fusion(f32[16,256]{1,0:T(8,128)S(1)} %score.1, f32[16,256]{1,0:T(8,128)S(1)} %collective-permute-done.10, pred[256]{0:T(512)(128)(4,1)S(1)} %compare_reduce_fusion), kind=kLoop, calls=%fused_computation.23 | loop fusion | flops 8192 | bytes 49408 | tf_op jit(solution)/shard_map/transpose | solution.py:341
  (9 shorter events, 0.1 us)
Async XLA Ops:
  0.0 1.7 %copy-start = (bf16[1,1024,1024]{2,1,0:T(8,128)(2,1)S(1)}, bf16[1,1024,1024]{2,1,0:T(8,128)(2,1)}, u32[]{:S(2)}) copy-start(bf16[1,1024,1024]{2,1,0:T(8,128)(2,1)} %param.10) | copy-start | bytes 6291460
  0.0 2.1 %copy-start.1 = (bf16[256,256,8]{1,2,0:T(8,128)(2,1)S(1)}, bf16[256,256,8]{1,2,0:T(8,128)(2,1)}, u32[]{:S(2)}) copy-start(bf16[256,256,8]{1,2,0:T(8,128)(2,1)} %param.13) | copy-start | bytes 3145732
  0.0 7.0 %copy-start.2 = (s32[256,1,256]{2,1,0:T(1,128)S(1)}, s32[256,1,256]{2,1,0:T(1,128)}, u32[]{:S(2)}) copy-start(s32[256,1,256]{2,1,0:T(1,128)} %codes_ref) | copy-start | bytes 786436
  2.2 10.1 %collective-permute-start.3 = (bf16[256,256,8]{1,2,0:T(8,128)(2,1)S(1)}, bf16[256,256,8]{1,2,0:T(8,128)(2,1)S(1)}, u32[]{:S(2)}, u32[]{:S(2)}) collective-permute-start(bf16[256,256,8]{1,2,0:T(8,128)(2,1)S(1)} %copy-done.1), channel_id=1, source_target_pairs={{0,1},{1,0},{2,3},{3,2},{4,5},{5,4},{6,7},{7,6},{8,9},{9,8},{10,11... | collective-permute-start | bytes 3145736 | tf_op jit(solution)/shard_map/ppermute | solution.py:300
  2.7 6.8 %collective-permute-start = (f16[64,1024]{1,0:T(8,128)(2,1)S(1)}, f16[64,1024]{1,0:T(8,128)(2,1)S(1)}, u32[]{:S(2)}, u32[]{:S(2)}) collective-permute-start(f16[64,1024]{1,0:T(8,128)(2,1)S(1)} %get-tuple-element.18), channel_id=1, source_target_pairs={{0,8},{1,5},{4,12},{5,1},{8,0},{9,13},{12,4},{13,9},{2,10},{3,7},{... | collective-permute-start | bytes 393224 | tf_op jit(solution)/shard_map/ppermute | solution.py:229
  7.2 5.1 %collective-permute-start.2 = (bf16[256,256]{1,0:T(8,128)(2,1)S(1)}, bf16[256,256]{1,0:T(8,128)(2,1)S(1)}, u32[]{:S(2)}, u32[]{:S(2)}) collective-permute-start(bf16[256,256]{1,0:T(8,128)(2,1)S(1)} %ids.1.refs_0_), channel_id=1, source_target_pairs={{1,0},{3,2},{2,1},{0,3},{5,4},{7,6},{6,5},{4,7},{9,8},{11,10},{10,... | collective-permute-start | bytes 393224 | tf_op jit(solution)/shard_map/ppermute | solution.py:299
  7.5 7.0 %collective-permute-start.4 = (bf16[256,256]{1,0:T(8,128)(2,1)S(1)}, bf16[256,256]{1,0:T(8,128)(2,1)S(1)}, u32[]{:S(2)}, u32[]{:S(2)}) collective-permute-start(bf16[256,256]{1,0:T(8,128)(2,1)S(1)} %ids.1.refs_0_), channel_id=1, source_target_pairs={{0,2},{2,0},{1,3},{3,1},{4,6},{6,4},{5,7},{7,5},{8,10},{10,8},{9,1... | collective-permute-start | bytes 393224 | tf_op jit(solution)/shard_map/ppermute | solution.py:298
  9.6 6.7 %collective-permute-start.1 = (f16[64,1024]{1,0:T(8,128)(2,1)S(1)}, f16[64,1024]{1,0:T(8,128)(2,1)S(1)}, u32[]{:S(2)}, u32[]{:S(2)}) collective-permute-start(f16[64,1024]{1,0:T(8,128)(2,1)S(1)} %multiply_convert_fusion), channel_id=1, source_target_pairs={{0,4},{1,9},{4,0},{5,13},{8,12},{9,1},{12,8},{13,5},{2,6},{3,11},{... | collective-permute-start | bytes 393224 | tf_op jit(solution)/shard_map/ppermute | solution.py:229
  14.0 2.3 %copy-start.4 = (bf16[1,256,1024]{2,1,0:T(8,128)(2,1)S(1)}, bf16[1,256,1024]{2,1,0:T(8,128)(2,1)}, u32[]{:S(2)}) copy-start(bf16[1,256,1024]{2,1,0:T(8,128)(2,1)} %param.9) | copy-start | bytes 1572868
  14.5 2.4 %copy-start.3 = (bf16[1,256,4096]{2,1,0:T(8,128)(2,1)S(1)}, bf16[1,256,4096]{2,1,0:T(8,128)(2,1)}, u32[]{:S(2)}) copy-start(bf16[1,256,4096]{2,1,0:T(8,128)(2,1)} %param.8) | copy-start | bytes 6291460
  14.5 2.4 %copy-start.5 = (bf16[4096,64]{0,1:T(8,128)(2,1)S(1)}, bf16[4096,64]{0,1:T(8,128)(2,1)}, u32[]{:S(2)}) copy-start(bf16[4096,64]{0,1:T(8,128)(2,1)} %param.11) | copy-start | bytes 1572868
  16.7 1.3 %collective-permute-start.5 = (f32[64,256]{1,0:T(8,128)S(1)}, f32[64,256]{1,0:T(8,128)S(1)}, u32[]{:S(2)}, u32[]{:S(2)}) collective-permute-start(f32[64,256]{1,0:T(8,128)S(1)} %slice_add_fusion.own_ref), channel_id=1, source_target_pairs={{0,1},{1,0},{2,3},{3,2},{4,5},{5,4},{6,7},{7,6},{8,9},{9,8},{10,11... | collective-permute-start | bytes 196616 | tf_op jit(solution)/shard_map/ppermute | solution.py:325
  18.6 5.5 %collective-permute-start.9 = (f16[2,4,2048]{2,1,0:T(4,128)(2,1)S(1)}, f16[2,4,2048]{2,1,0:T(4,128)(2,1)S(1)}, u32[]{:S(2)}, u32[]{:S(2)}) collective-permute-start(f16[2,4,2048]{2,1,0:T(4,128)(2,1)S(1)} %multiply_convert_fusion.2), channel_id=1, source_target_pairs={{0,8},{1,11},{2,10},{3,9},{4,12},{5,15},{6,14},{7,13},{8,0},{9,3},... | collective-permute-start | bytes 98312 | tf_op jit(solution)/shard_map/ppermute | solution.py:271
  21.2 6.0 %collective-permute-start.8 = (f16[2,4,2048]{2,1,0:T(4,128)(2,1)S(1)}, f16[2,4,2048]{2,1,0:T(4,128)(2,1)S(1)}, u32[]{:S(2)}, u32[]{:S(2)}) collective-permute-start(f16[2,4,2048]{2,1,0:T(4,128)(2,1)S(1)} %multiply_convert_fusion.2), channel_id=1, source_target_pairs={{0,12},{1,15},{2,14},{3,13},{4,8},{5,11},{6,10},{7,9},{8,4},{9,7},... | collective-permute-start | bytes 98312 | tf_op jit(solution)/shard_map/ppermute | solution.py:271
  22.6 4.8 %collective-permute-start.7 = (f16[2,4,2048]{2,1,0:T(4,128)(2,1)S(1)}, f16[2,4,2048]{2,1,0:T(4,128)(2,1)S(1)}, u32[]{:S(2)}, u32[]{:S(2)}) collective-permute-start(f16[2,4,2048]{2,1,0:T(4,128)(2,1)S(1)} %multiply_convert_fusion.2), channel_id=1, source_target_pairs={{0,4},{1,7},{2,6},{3,5},{4,0},{5,3},{6,2},{7,1},{8,12},{9,15},{10,... | collective-permute-start | bytes 98312 | tf_op jit(solution)/shard_map/ppermute | solution.py:271
  22.6 4.9 %collective-permute-start.6 = (f16[2,4,2048]{2,1,0:T(4,128)(2,1)S(1)}, f16[2,4,2048]{2,1,0:T(4,128)(2,1)S(1)}, u32[]{:S(2)}, u32[]{:S(2)}) collective-permute-start(f16[2,4,2048]{2,1,0:T(4,128)(2,1)S(1)} %multiply_convert_fusion.2), channel_id=1, source_target_pairs={{0,2},{1,3},{2,0},{3,1},{4,6},{5,7},{6,4},{7,5},{8,10},{9,11},{10,... | collective-permute-start | bytes 98312 | tf_op jit(solution)/shard_map/ppermute | solution.py:271
  28.0 1.2 %collective-permute-start.10 = (f32[16,256]{1,0:T(8,128)S(1)}, f32[16,256]{1,0:T(8,128)S(1)}, u32[]{:S(2)}, u32[]{:S(2)}) collective-permute-start(f32[16,256]{1,0:T(8,128)S(1)} %score.1), channel_id=1, source_target_pairs={{0,1},{1,0},{2,3},{3,2},{4,5},{5,4},{6,7},{7,6},{8,9},{9,8},{10,11... | collective-permute-start | bytes 49160 | tf_op jit(solution)/shard_map/ppermute | solution.py:336

commit v10 on v9

--- a/solution.py
+++ b/solution.py
@@ -11,7 +11,7 @@
 LANES = 128
 LINK_SCALE = 1024.0
 VECTOR_SCALE = 16384.0
-GATHER_ORDER = (0, 1, 3, 2)
+GATHER_ORDER = (0, 1, 2, 3)
 
 
 def rows_kernel(proj_ref, out_ref, sem):

time: 29.9 us -> 29.7 us (level)
  waiting for transfers between devices: 5.79 us -> 4.47 us
  starting transfers between devices: 14.4 us -> 15.5 us
    ppermute x4, waiting for transfers between devices: 3.34 us -> 2.15 us  [gather_by_core(): blocks.append(lax.ppermute(x, ('dp', 'layer', 'sub'), pairs))]
    ppermute x4, starting transfers between devices: 5.46 us -> 6.24 us  [gather_by_core(): blocks.append(lax.ppermute(x, ('dp', 'layer', 'sub'), pairs))]
    ppermute x1, starting transfers between devices: 0.23 us -> 0.56 us  [per_device(): total = total + lax.ppermute(total, 'sub', partners(2, 1))]
  transfers between devices with their start and end apart: 11 -> 11, of which waited for: 6 -> 5; matrix products, arithmetic and copies ran while one was open for 3% -> 3% of each run, Pallas kernels for 12% -> 12%
where the time goes in v10:
time: 29.7 us; the launch traced here: 29.6 us
  starting transfers between devices  15.5 us (52%)
  Pallas kernels  4.69 us (16%)
  waiting for transfers between devices  4.47 us (15%)
  local copies, waits for them, and re-layouts  1.67 us (6%)
  matrix products  1.55 us (5%)
  other arithmetic  0.87 us (3%)
  between operations  0.81 us (3%)
    ppermute x2, starting transfers between devices, sum_over_dp(): got = lax.ppermute(sent, ('dp', 'sub'), pairs)  6.38 us
    ppermute x4, starting transfers between devices, gather_by_core(): blocks.append(lax.ppermute(x, ('dp', 'layer', 'sub'), pairs))  6.24 us
    pallas_call x2, Pallas kernels, decode(): pl.pallas_call(decode_kernel, out_shape=jax.ShapeDtypeStruct((subs * widt...  3.47 us
    ppermute x4, waiting for transfers between devices, gather_by_core(): blocks.append(lax.ppermute(x, ('dp', 'layer', 'sub'), pairs))  2.15 us
    ppermute x1, starting transfers between devices, per_device(): near_ids = lax.ppermute(ids, 'layer', partners(2, 1))  1.33 us
    dynamic_slice x1, local copies, waits for them, and re-layouts, per_device(): lax.dynamic_slice_in_dim(jnp.transpose(proj_out), lax.axis_index('dp') *...  1.06 us
    ppermute x1, waiting for transfers between devices, per_device(): total = total + lax.ppermute(total, 'sub', partners(2, 1))  0.82 us
    dot_general x1, matrix products, first_side(): lax.dot_general(proj_in, acts[0], (((0,), (1,)), ((), ())), preferred_ele...  0.76 us
  transfers between devices with their start and end apart: 11, of which 5 were waited for; matrix products, arithmetic and copies ran while one was open for 3% of the time, Pallas kernels for 12%

profile of v10, /device:TPU:0, one launch (start us, length us, event | category | flops | bytes accessed | tf_op | source)
XLA Modules:
  0.0 29.6 jit_solution(12606812245191663309)
XLA Ops:
  0.0 0.0 copy-start
  0.0 0.0 copy-start.1
  0.0 0.0 copy-start.2
  0.0 1.1 %dynamic-slice_bitcast_fusion = bf16[64,1024]{1,0:T(8,128)(2,1)S(1)} fusion(bf16[4096,64]{0,1:T(8,128)(2,1)} %param.12, s32[]{:T(128)S(6)} %select_n.7), kind=kLoop, calls=%fused_computation.16 | loop fusion | bytes 262148 | tf_op jit(solution)/shard_map/dynamic_slice | solution.py:284
  1.1 0.6 %copy-done = bf16[1,1024,1024]{2,1,0:T(8,128)(2,1)S(1)} copy-done((bf16[1,1024,1024]{2,1,0:T(8,128)(2,1)S(1)}, bf16[1,1024,1024]{2,1,0:T(8,128)(2,1)}, u32[]{:S(2)}) %copy-start) | copy-done | bytes 2097176
  1.7 0.5 %multiply_convert_fusion.1 = (f16[64,1024]{1,0:T(8,128)(2,1)S(1)}, f32[64,1024]{1,0:T(8,128)S(1)}) fusion(bf16[64,1024]{1,0:T(8,128)(2,1)S(1)} %dynamic-slice_bitcast_fusion, bf16[1,1024,1024]{2,1,0:T(8,128)(2,1)S(1)} %copy-done), kind=kOutput, calls=%fused_computation.15 | convolution fusion | flops 134348800 | bytes 2621440 | tf_op jit(solution)/shard_map/dot_general | solution.py:288
  2.1 0.0 copy-done.1
  2.2 0.5 %collective-permute-start.3 = (bf16[256,256,8]{1,2,0:T(8,128)(2,1)S(1)}, bf16[256,256,8]{1,2,0:T(8,128)(2,1)S(1)}, u32[]{:S(2)}, u32[]{:S(2)}) collective-permute-start(bf16[256,256,8]{1,2,0:T(8,128)(2,1)S(1)} %copy-done.1), channel_id=1, source_target_pairs={{0,1},{1,0},{2,3},{3,2},{4,5},{5,4},{6,7},{7,6},{8,9},{9,8},{10,11... | collective-permute-start | bytes 3145736 | tf_op jit(solution)/shard_map/ppermute | solution.py:300
  2.7 3.7 %collective-permute-start = (f16[64,1024]{1,0:T(8,128)(2,1)S(1)}, f16[64,1024]{1,0:T(8,128)(2,1)S(1)}, u32[]{:S(2)}, u32[]{:S(2)}) collective-permute-start(f16[64,1024]{1,0:T(8,128)(2,1)S(1)} %get-tuple-element.18), channel_id=1, source_target_pairs={{0,8},{1,5},{4,12},{5,1},{8,0},{9,13},{12,4},{13,9},{2,10},{3,7},{... | collective-permute-start | bytes 393224 | tf_op jit(solution)/shard_map/ppermute | solution.py:229
  7.0 0.0 copy-done.2
  7.0 0.2 ids.1.refs_0_
  7.2 0.3 collective-permute-start.2
  7.5 1.3 %collective-permute-start.4 = (bf16[256,256]{1,0:T(8,128)(2,1)S(1)}, bf16[256,256]{1,0:T(8,128)(2,1)S(1)}, u32[]{:S(2)}, u32[]{:S(2)}) collective-permute-start(bf16[256,256]{1,0:T(8,128)(2,1)S(1)} %ids.1.refs_0_), channel_id=1, source_target_pairs={{0,2},{2,0},{1,3},{3,1},{4,6},{6,4},{5,7},{7,5},{8,10},{10,8},{9,1... | collective-permute-start | bytes 393224 | tf_op jit(solution)/shard_map/ppermute | solution.py:298
  8.8 0.7 %collective-permute-done = f16[64,1024]{1,0:T(8,128)(2,1)S(1)} collective-permute-done((f16[64,1024]{1,0:T(8,128)(2,1)S(1)}, f16[64,1024]{1,0:T(8,128)(2,1)S(1)}, u32[]{:S(2)}, u32[]{:S(2)}) %collective-permute-start) | collective-permute-done | bytes 131104 | tf_op jit(solution)/shard_map/ppermute | solution.py:229
  9.5 0.1 multiply_convert_fusion
  9.6 2.7 %collective-permute-start.1 = (f16[64,1024]{1,0:T(8,128)(2,1)S(1)}, f16[64,1024]{1,0:T(8,128)(2,1)S(1)}, u32[]{:S(2)}, u32[]{:S(2)}) collective-permute-start(f16[64,1024]{1,0:T(8,128)(2,1)S(1)} %multiply_convert_fusion), channel_id=1, source_target_pairs={{0,4},{1,9},{4,0},{5,13},{8,12},{9,1},{12,8},{13,5},{2,6},{3,11},{... | collective-permute-start | bytes 393224 | tf_op jit(solution)/shard_map/ppermute | solution.py:229
  12.3 0.0 collective-permute-done.2.refs_0_
  12.3 0.0 collective-permute-done.3
  12.3 1.7 %decode.2.refs_6_ = bf16[2048,256]{1,0:T(8,128)(2,1)S(1)} custom-call(bf16[256,256]{1,0:T(8,128)(2,1)S(1)} %collective-permute-done.2.refs_0_, bf16[256,8,256]{2,1,0:T(8,128)(2,1)S(1)} %bitcast.22), custom_call_target="tpu_custom_call" | custom-call | bytes 2097152 | tf_op jit(solution)/shard_map/decode/pallas_call | solution.py:98
  14.0 0.0 copy-start.4
  14.0 0.5 %collective-permute-done.4.refs_1_ = bf16[256,256]{1,0:T(8,128)(2,1)S(1)} collective-permute-done((bf16[256,256]{1,0:T(8,128)(2,1)S(1)}, bf16[256,256]{1,0:T(8,128)(2,1)S(1)}, u32[]{:S(2)}, u32[]{:S(2)}) %collective-permute-start.4) | collective-permute-done | bytes 131104 | tf_op jit(solution)/shard_map/ppermute | solution.py:298
  14.5 0.0 copy-start.3
  14.5 0.0 copy-start.5
  14.5 1.7 %decode.3.refs_5_ = bf16[2048,256]{1,0:T(8,128)(2,1)S(1)} custom-call(bf16[256,256]{1,0:T(8,128)(2,1)S(1)} %ids.1.refs_0_, bf16[256,256]{1,0:T(8,128)(2,1)S(1)} %collective-permute-done.4.refs_1_, bf16[256,8,256]{2,1,0:T(8,128)(2,1)S(1)} %bitcast.21), custom_call_target="tpu_custom_call" | custom-call | bytes 2097152 | tf_op jit(solution)/shard_map/decode/pallas_call | solution.py:98
  16.2 0.0 collective-permute-done.1
  16.3 0.1 reduce-precision_convert_fusion
  16.4 0.0 copy-done.4
  16.4 0.3 %fusion.4 = f32[128,256]{1,0:T(8,128)S(1)} fusion(bf16[1,256,1024]{2,1,0:T(8,128)(2,1)S(1)} %copy-done.4, bf16[64,1024]{1,0:T(8,128)(2,1)S(1)} %get-tuple-element.32, bf16[64,1024]{1,0:T(8,128)(2,1)S(1)} %get-tuple-element.31), kind=kOutput, calls=%fused_computation.4 | convolution fusion | flops 67633152 | bytes 917504 | tf_op jit(solution)/shard_map/dot_general | solution.py:317
  16.7 0.2 collective-permute-start.5
  16.9 0.0 copy-done.3
  16.9 0.0 copy-done.5
  16.9 0.8 %fusion.in_ref = f32[64,256]{1,0:T(8,128)S(1)} fusion(bf16[4096,64]{0,1:T(8,128)(2,1)S(1)} %copy-done.5, bf16[1,256,4096]{2,1,0:T(8,128)(2,1)S(1)} %copy-done.3), kind=kOutput, calls=%fused_computation | convolution fusion | flops 134217728 | bytes 2686976 | tf_op jit(solution)/shard_map/dot_general | solution.py:303
  17.7 0.4 %collective-permute-done.5.other_ref = f32[64,256]{1,0:T(8,128)S(1)} collective-permute-done((f32[64,256]{1,0:T(8,128)S(1)}, f32[64,256]{1,0:T(8,128)S(1)}, u32[]{:S(2)}, u32[]{:S(2)}) %collective-permute-start.5) | collective-permute-done | bytes 65568 | tf_op jit(solution)/shard_map/ppermute | solution.py:325
  18.0 0.6 %vectors.1.refs_0_ = f32[2,4,2048]{2,1,0:T(4,128)S(1)} custom-call(f32[64,256]{1,0:T(8,128)S(1)} %fusion.in_ref, f32[64,256]{1,0:T(8,128)S(1)} %slice_add_fusion.own_ref, f32[64,256]{1,0:T(8,128)S(1)} %collective-permute-done.5.other_ref), custom_call_target="tpu_custom_call" | custom-call | tf_op jit(solution)/shard_map/vectors/pallas_call | solution.py:189
  18.6 3.4 %collective-permute-start.9 = (f16[2,4,2048]{2,1,0:T(4,128)(2,1)S(1)}, f16[2,4,2048]{2,1,0:T(4,128)(2,1)S(1)}, u32[]{:S(2)}, u32[]{:S(2)}) collective-permute-start(f16[2,4,2048]{2,1,0:T(4,128)(2,1)S(1)} %multiply_convert_fusion.2), channel_id=1, source_target_pairs={{0,12},{1,15},{2,14},{3,13},{4,8},{5,11},{6,10},{7,9},{8,4},{9,7},... | collective-permute-start | bytes 98312 | tf_op jit(solution)/shard_map/ppermute | solution.py:271
  22.0 0.0 collective-permute-start.8
  22.0 1.0 %collective-permute-start.7 = (f16[2,4,2048]{2,1,0:T(4,128)(2,1)S(1)}, f16[2,4,2048]{2,1,0:T(4,128)(2,1)S(1)}, u32[]{:S(2)}, u32[]{:S(2)}) collective-permute-start(f16[2,4,2048]{2,1,0:T(4,128)(2,1)S(1)} %multiply_convert_fusion.2), channel_id=1, source_target_pairs={{0,4},{1,7},{2,6},{3,5},{4,0},{5,3},{6,2},{7,1},{8,12},{9,15},{10,... | collective-permute-start | bytes 98312 | tf_op jit(solution)/shard_map/ppermute | solution.py:271
  23.1 1.8 %collective-permute-start.6 = (f16[2,4,2048]{2,1,0:T(4,128)(2,1)S(1)}, f16[2,4,2048]{2,1,0:T(4,128)(2,1)S(1)}, u32[]{:S(2)}, u32[]{:S(2)}) collective-permute-start(f16[2,4,2048]{2,1,0:T(4,128)(2,1)S(1)} %multiply_convert_fusion.2), channel_id=1, source_target_pairs={{0,2},{1,3},{2,0},{3,1},{4,6},{5,7},{6,4},{7,5},{8,10},{9,11},{10,... | collective-permute-start | bytes 98312 | tf_op jit(solution)/shard_map/ppermute | solution.py:271
  24.9 0.0 collective-permute-done.9
  24.9 2.1 %collective-permute-done.8 = f16[2,4,2048]{2,1,0:T(4,128)(2,1)S(1)} collective-permute-done((f16[2,4,2048]{2,1,0:T(4,128)(2,1)S(1)}, f16[2,4,2048]{2,1,0:T(4,128)(2,1)S(1)}, u32[]{:S(2)}, u32[]{:S(2)}) %collective-permute-start.8) | collective-permute-done | bytes 32800 | tf_op jit(solution)/shard_map/ppermute | solution.py:271
  27.0 0.0 collective-permute-done.7
  27.1 0.0 collective-permute-done.6
  27.1 0.5 %score.1 = f32[16,256]{1,0:T(8,128)S(1)} custom-call(f32[2,4,2048]{2,1,0:T(4,128)S(1)} %vectors.1.refs_0_, f32[2,4,2048]{2,1,0:T(4,128)S(1)} %convert_multiply_fusion.3.refs_1_, f32[2,4,2048]{2,1,0:T(4,128)S(1)} %convert_multiply_fusion.2.refs_2_, f32[2,4,2048]{2,1,0:T(4,128)S(1)} %convert_multiply_fusion.1.refs_3_, ...), custom_call_target="tpu_custom_call" | custom-call | tf_op jit(solution)/shard_map/score/pallas_call | solution.py:168
  27.6 0.6 %collective-permute-start.10 = (f32[16,256]{1,0:T(8,128)S(1)}, f32[16,256]{1,0:T(8,128)S(1)}, u32[]{:S(2)}, u32[]{:S(2)}) collective-permute-start(f32[16,256]{1,0:T(8,128)S(1)} %score.1), channel_id=1, source_target_pairs={{0,1},{1,0},{2,3},{3,2},{4,5},{5,4},{6,7},{7,6},{8,9},{9,8},{10,11... | collective-permute-start | bytes 49160 | tf_op jit(solution)/shard_map/ppermute | solution.py:336
  28.2 0.8 %collective-permute-done.10 = f32[16,256]{1,0:T(8,128)S(1)} collective-permute-done((f32[16,256]{1,0:T(8,128)S(1)}, f32[16,256]{1,0:T(8,128)S(1)}, u32[]{:S(2)}, u32[]{:S(2)}) %collective-permute-start.10) | collective-permute-done | bytes 16416 | tf_op jit(solution)/shard_map/ppermute | solution.py:336
  29.0 0.6 %select_bitcast_fusion = f32[256,16]{0,1:T(8,128)} fusion(f32[16,256]{1,0:T(8,128)S(1)} %score.1, f32[16,256]{1,0:T(8,128)S(1)} %collective-permute-done.10, pred[256]{0:T(512)(128)(4,1)S(1)} %compare_reduce_fusion), kind=kLoop, calls=%fused_computation.23 | loop fusion | flops 8192 | bytes 49408 | tf_op jit(solution)/shard_map/transpose | solution.py:341
  (9 shorter events, 0.1 us)
Async XLA Ops:
  0.0 1.7 %copy-start = (bf16[1,1024,1024]{2,1,0:T(8,128)(2,1)S(1)}, bf16[1,1024,1024]{2,1,0:T(8,128)(2,1)}, u32[]{:S(2)}) copy-start(bf16[1,1024,1024]{2,1,0:T(8,128)(2,1)} %param.10) | copy-start | bytes 6291460
  0.0 2.1 %copy-start.1 = (bf16[256,256,8]{1,2,0:T(8,128)(2,1)S(1)}, bf16[256,256,8]{1,2,0:T(8,128)(2,1)}, u32[]{:S(2)}) copy-start(bf16[256,256,8]{1,2,0:T(8,128)(2,1)} %param.13) | copy-start | bytes 3145732
  0.0 7.0 %copy-start.2 = (s32[256,1,256]{2,1,0:T(1,128)S(1)}, s32[256,1,256]{2,1,0:T(1,128)}, u32[]{:S(2)}) copy-start(s32[256,1,256]{2,1,0:T(1,128)} %codes_ref) | copy-start | bytes 786436
  2.2 10.1 %collective-permute-start.3 = (bf16[256,256,8]{1,2,0:T(8,128)(2,1)S(1)}, bf16[256,256,8]{1,2,0:T(8,128)(2,1)S(1)}, u32[]{:S(2)}, u32[]{:S(2)}) collective-permute-start(bf16[256,256,8]{1,2,0:T(8,128)(2,1)S(1)} %copy-done.1), channel_id=1, source_target_pairs={{0,1},{1,0},{2,3},{3,2},{4,5},{5,4},{6,7},{7,6},{8,9},{9,8},{10,11... | collective-permute-start | bytes 3145736 | tf_op jit(solution)/shard_map/ppermute | solution.py:300
  2.7 6.8 %collective-permute-start = (f16[64,1024]{1,0:T(8,128)(2,1)S(1)}, f16[64,1024]{1,0:T(8,128)(2,1)S(1)}, u32[]{:S(2)}, u32[]{:S(2)}) collective-permute-start(f16[64,1024]{1,0:T(8,128)(2,1)S(1)} %get-tuple-element.18), channel_id=1, source_target_pairs={{0,8},{1,5},{4,12},{5,1},{8,0},{9,13},{12,4},{13,9},{2,10},{3,7},{... | collective-permute-start | bytes 393224 | tf_op jit(solution)/shard_map/ppermute | solution.py:229
  7.2 5.1 %collective-permute-start.2 = (bf16[256,256]{1,0:T(8,128)(2,1)S(1)}, bf16[256,256]{1,0:T(8,128)(2,1)S(1)}, u32[]{:S(2)}, u32[]{:S(2)}) collective-permute-start(bf16[256,256]{1,0:T(8,128)(2,1)S(1)} %ids.1.refs_0_), channel_id=1, source_target_pairs={{1,0},{3,2},{2,1},{0,3},{5,4},{7,6},{6,5},{4,7},{9,8},{11,10},{10,... | collective-permute-start | bytes 393224 | tf_op jit(solution)/shard_map/ppermute | solution.py:299
  7.5 7.0 %collective-permute-start.4 = (bf16[256,256]{1,0:T(8,128)(2,1)S(1)}, bf16[256,256]{1,0:T(8,128)(2,1)S(1)}, u32[]{:S(2)}, u32[]{:S(2)}) collective-permute-start(bf16[256,256]{1,0:T(8,128)(2,1)S(1)} %ids.1.refs_0_), channel_id=1, source_target_pairs={{0,2},{2,0},{1,3},{3,1},{4,6},{6,4},{5,7},{7,5},{8,10},{10,8},{9,1... | collective-permute-start | bytes 393224 | tf_op jit(solution)/shard_map/ppermute | solution.py:298
  9.6 6.7 %collective-permute-start.1 = (f16[64,1024]{1,0:T(8,128)(2,1)S(1)}, f16[64,1024]{1,0:T(8,128)(2,1)S(1)}, u32[]{:S(2)}, u32[]{:S(2)}) collective-permute-start(f16[64,1024]{1,0:T(8,128)(2,1)S(1)} %multiply_convert_fusion), channel_id=1, source_target_pairs={{0,4},{1,9},{4,0},{5,13},{8,12},{9,1},{12,8},{13,5},{2,6},{3,11},{... | collective-permute-start | bytes 393224 | tf_op jit(solution)/shard_map/ppermute | solution.py:229
  14.0 2.3 %copy-start.4 = (bf16[1,256,1024]{2,1,0:T(8,128)(2,1)S(1)}, bf16[1,256,1024]{2,1,0:T(8,128)(2,1)}, u32[]{:S(2)}) copy-start(bf16[1,256,1024]{2,1,0:T(8,128)(2,1)} %param.9) | copy-start | bytes 1572868
  14.5 2.4 %copy-start.3 = (bf16[1,256,4096]{2,1,0:T(8,128)(2,1)S(1)}, bf16[1,256,4096]{2,1,0:T(8,128)(2,1)}, u32[]{:S(2)}) copy-start(bf16[1,256,4096]{2,1,0:T(8,128)(2,1)} %param.8) | copy-start | bytes 6291460
  14.5 2.4 %copy-start.5 = (bf16[4096,64]{0,1:T(8,128)(2,1)S(1)}, bf16[4096,64]{0,1:T(8,128)(2,1)}, u32[]{:S(2)}) copy-start(bf16[4096,64]{0,1:T(8,128)(2,1)} %param.11) | copy-start | bytes 1572868
  16.7 1.3 %collective-permute-start.5 = (f32[64,256]{1,0:T(8,128)S(1)}, f32[64,256]{1,0:T(8,128)S(1)}, u32[]{:S(2)}, u32[]{:S(2)}) collective-permute-start(f32[64,256]{1,0:T(8,128)S(1)} %slice_add_fusion.own_ref), channel_id=1, source_target_pairs={{0,1},{1,0},{2,3},{3,2},{4,5},{5,4},{6,7},{7,6},{8,9},{9,8},{10,11... | collective-permute-start | bytes 196616 | tf_op jit(solution)/shard_map/ppermute | solution.py:325
  18.6 6.2 %collective-permute-start.9 = (f16[2,4,2048]{2,1,0:T(4,128)(2,1)S(1)}, f16[2,4,2048]{2,1,0:T(4,128)(2,1)S(1)}, u32[]{:S(2)}, u32[]{:S(2)}) collective-permute-start(f16[2,4,2048]{2,1,0:T(4,128)(2,1)S(1)} %multiply_convert_fusion.2), channel_id=1, source_target_pairs={{0,12},{1,15},{2,14},{3,13},{4,8},{5,11},{6,10},{7,9},{8,4},{9,7},... | collective-permute-start | bytes 98312 | tf_op jit(solution)/shard_map/ppermute | solution.py:271
  22.0 5.0 %collective-permute-start.8 = (f16[2,4,2048]{2,1,0:T(4,128)(2,1)S(1)}, f16[2,4,2048]{2,1,0:T(4,128)(2,1)S(1)}, u32[]{:S(2)}, u32[]{:S(2)}) collective-permute-start(f16[2,4,2048]{2,1,0:T(4,128)(2,1)S(1)} %multiply_convert_fusion.2), channel_id=1, source_target_pairs={{0,8},{1,11},{2,10},{3,9},{4,12},{5,15},{6,14},{7,13},{8,0},{9,3},... | collective-permute-start | bytes 98312 | tf_op jit(solution)/shard_map/ppermute | solution.py:271
  22.0 5.0 %collective-permute-start.7 = (f16[2,4,2048]{2,1,0:T(4,128)(2,1)S(1)}, f16[2,4,2048]{2,1,0:T(4,128)(2,1)S(1)}, u32[]{:S(2)}, u32[]{:S(2)}) collective-permute-start(f16[2,4,2048]{2,1,0:T(4,128)(2,1)S(1)} %multiply_convert_fusion.2), channel_id=1, source_target_pairs={{0,4},{1,7},{2,6},{3,5},{4,0},{5,3},{6,2},{7,1},{8,12},{9,15},{10,... | collective-permute-start | bytes 98312 | tf_op jit(solution)/shard_map/ppermute | solution.py:271
  23.1 4.0 %collective-permute-start.6 = (f16[2,4,2048]{2,1,0:T(4,128)(2,1)S(1)}, f16[2,4,2048]{2,1,0:T(4,128)(2,1)S(1)}, u32[]{:S(2)}, u32[]{:S(2)}) collective-permute-start(f16[2,4,2048]{2,1,0:T(4,128)(2,1)S(1)} %multiply_convert_fusion.2), channel_id=1, source_target_pairs={{0,2},{1,3},{2,0},{3,1},{4,6},{5,7},{6,4},{7,5},{8,10},{9,11},{10,... | collective-permute-start | bytes 98312 | tf_op jit(solution)/shard_map/ppermute | solution.py:271
  27.6 1.4 %collective-permute-start.10 = (f32[16,256]{1,0:T(8,128)S(1)}, f32[16,256]{1,0:T(8,128)S(1)}, u32[]{:S(2)}, u32[]{:S(2)}) collective-permute-start(f32[16,256]{1,0:T(8,128)S(1)} %score.1), channel_id=1, source_target_pairs={{0,1},{1,0},{2,3},{3,2},{4,5},{5,4},{6,7},{7,6},{8,9},{9,8},{10,11... | collective-permute-start | bytes 49160 | tf_op jit(solution)/shard_map/ppermute | solution.py:336

commit v11 on v10

--- a/solution.py
+++ b/solution.py
@@ -12,26 +12,6 @@
 LINK_SCALE = 1024.0
 VECTOR_SCALE = 16384.0
 GATHER_ORDER = (0, 1, 2, 3)
-
-
-def rows_kernel(proj_ref, out_ref, sem):
-    rows = out_ref.shape[1]
-    first = pl.multiple_of(lax.axis_index("dp") * rows, LANES)
-    copy = pltpu.make_async_copy(proj_ref.at[:, pl.ds(first, rows)], out_ref, sem)
-    copy.start()
-    copy.wait()
-
-
-def take_rows(proj_t, rows):
-    return pl.pallas_call(
-        rows_kernel,
-        out_shape=jax.ShapeDtypeStruct((proj_t.shape[0], rows), proj_t.dtype),
-        in_specs=[pl.BlockSpec(memory_space=pl.ANY)],
-        out_specs=pl.BlockSpec(memory_space=pltpu.VMEM),
-        scratch_shapes=[pltpu.SemaphoreType.DMA],
-        compiler_params=pltpu.CompilerParams(vmem_limit_bytes=1024 * 1024),
-        name="rows",
-    )(proj_t)
 
 
 def ids_kernel(codes_ref, out_ref):
@@ -106,6 +86,11 @@
     )(*ids, book_t)
 
 
+def split_in_kernel(x):
+    high = x.astype(jnp.bfloat16)
+    return high, (x - high.astype(jnp.float32)).astype(jnp.bfloat16)
+
+
 def vectors_kernel(in_ref, own_ref, other_ref, out_ref, grads_ref, flat_ref):
     rank_dim, tokens = in_ref.shape
     parts, tests, dims = out_ref.shape
@@ -113,12 +98,22 @@
     tall = dims // LANES
     in_side = in_ref[...]
     test_of = lax.broadcasted_iota(jnp.int32, in_side.shape, 1) // SEQ
-    grads_ref[:, :rank_dim] = lax.dot_general(
-        jnp.concatenate([jnp.where(test_of == test, in_side, 0.0) for test in range(tests)], axis=0),
-        own_ref[...] + other_ref[...],
-        (((1,), (1,)), ((), ())),
-        precision=lax.Precision.HIGHEST,
-        preferred_element_type=jnp.float32,
+    out_side = own_ref[...] + other_ref[...]
+    in_high, in_low = split_in_kernel(in_side)
+    out_high, out_low = split_in_kernel(out_side)
+
+    def by_test(x):
+        zero = jnp.zeros_like(x)
+        return jnp.concatenate([jnp.where(test_of == test, x, zero) for test in range(tests)], axis=0)
+
+    def product(x, y):
+        return lax.dot_general(
+            x, y, (((1,), (1,)), ((), ())), preferred_element_type=jnp.float32
+        )
+
+    wide_high = by_test(in_high)
+    grads_ref[:, :rank_dim] = product(wide_high, out_high) + (
+        product(wide_high, out_low) + product(by_test(in_low), out_high)
     )
     for test in range(tests):
         even = grads_ref[pl.ds(test * rank_dim, pairs, stride=2), :][:, :rank_dim]
@@ -242,7 +237,7 @@
     own = lax.axis_index("dp")
     got = jnp.zeros((size,) + x.shape, x.dtype)
     got = lax.dynamic_update_index_in_dim(got, x, own, 0)
-    for step in (2, 3, 1):
+    for step in reversed(range(1, size)):
         block = lax.ppermute(x, "dp", partners(size, step))
         got = lax.dynamic_update_index_in_dim(got, block, own ^ step, 0)
     return got
@@ -252,7 +247,6 @@
     return lax.axis_size("layer") == 2 and lax.axis_size("sub") == 2
 
 
-NEAR_CODES = [(3, 1), (1, 3)]
 FAR_CODES = [(1, 0), (3, 2), (2, 1), (0, 3)]
 
 
@@ -285,6 +279,7 @@
             jnp.transpose(proj_out), lax.axis_index("dp") * rows_local, rows_local, 1
         )
     )
+    own_rows, moved_book = lax.optimization_barrier((own_rows, codebook))
     folded = jnp.dot(own_rows, kv_weight[0], preferred_element_type=jnp.float32)
     book_t = jnp.transpose(codebook, (0, 2, 1))
     by_core = has_two_by_two() and lax.axis_size("dp") == 4
@@ -294,7 +289,6 @@
     live, moved_codes = lax.optimization_barrier((live, codes))
     ids = make_ids(moved_codes)
     if by_core:
-        sent, moved_book = lax.optimization_barrier((sent, codebook))
         near_ids = lax.ppermute(ids, "layer", partners(2, 1))
         far_ids = lax.ppermute(ids, ("layer", "sub"), FAR_CODES)
         other_book = lax.ppermute(moved_book, "sub", partners(2, 1))
@@ -311,9 +305,7 @@
         far, late_ids = lax.optimization_barrier((far, near_ids))
         return decode([ids, late_ids], book_t), far
 
-    folded, (live, decoded) = sum_over_dp(
-        folded, sent, [lambda: live, tables]
-    )
+    folded, (live, decoded) = sum_over_dp(folded, sent, [lambda: live, tables])
     out_side = lax.dot_general(
         jnp.concatenate(split_high_low(folded), axis=0),
         kv_grad[0],

time: 29.7 us -> 29.9 us (level)
  waiting for transfers between devices: 4.47 us -> 6.28 us
  starting transfers between devices: 15.5 us -> 14.5 us
  local copies, waits for them, and re-layouts: 1.67 us -> 1.16 us
    ppermute x4, waiting for transfers between devices: 2.15 us -> 3.39 us  [gather_by_core(): blocks.append(lax.ppermute(x, ('dp', 'layer', 'sub'), pairs))]
    ppermute x4, starting transfers between devices: 6.24 us -> 5.53 us  [gather_by_core(): blocks.append(lax.ppermute(x, ('dp', 'layer', 'sub'), pairs))]
    ppermute x1, starting transfers between devices: 0.56 us -> 0.01 us  [per_device(): total = total + lax.ppermute(total, 'sub', partners(2, 1))]
    unnamed x12, local copies, waits for them, and re-layouts: 0.61 us -> 0.09 us
    ppermute x1, waiting for transfers between devices: 0.46 us -> 0.89 us  [per_device(): near_ids = lax.ppermute(ids, 'layer', partners(2, 1))]
    ppermute x1, waiting for transfers between devices: 0.82 us -> 1.16 us  [per_device(): total = total + lax.ppermute(total, 'sub', partners(2, 1))]
  transfers between devices with their start and end apart: 11 -> 11, of which waited for: 5 -> 7; matrix products, arithmetic and copies ran while one was open for 3% -> 5% of each run, Pallas kernels for 12% -> 12%
where the time goes in v11:
time: 29.9 us; the launch traced here: 29.7 us
  starting transfers between devices  14.5 us (48%)
  waiting for transfers between devices  6.28 us (21%)
  Pallas kernels  4.57 us (15%)
  matrix products  1.55 us (5%)
  local copies, waits for them, and re-layouts  1.16 us (4%)
  other arithmetic  0.87 us (3%)
  between operations  0.82 us (3%)
    ppermute x2, starting transfers between devices, sum_over_dp(): got = lax.ppermute(sent, ('dp', 'sub'), pairs)  6.6 us
    ppermute x4, starting transfers between devices, gather_by_core(): blocks.append(lax.ppermute(x, ('dp', 'layer', 'sub'), pairs))  5.53 us
    pallas_call x2, Pallas kernels, decode(): pl.pallas_call(decode_kernel, out_shape=jax.ShapeDtypeStruct((subs * widt...  3.47 us
    ppermute x4, waiting for transfers between devices, gather_by_core(): blocks.append(lax.ppermute(x, ('dp', 'layer', 'sub'), pairs))  3.39 us
    ppermute x1, starting transfers between devices, per_device(): near_ids = lax.ppermute(ids, 'layer', partners(2, 1))  1.56 us
    ppermute x1, waiting for transfers between devices, per_device(): total = total + lax.ppermute(total, 'sub', partners(2, 1))  1.16 us
    dynamic_slice x1, local copies, waits for them, and re-layouts, per_device(): lax.dynamic_slice_in_dim(jnp.transpose(proj_out), lax.axis_index('dp') *...  1.06 us
    ppermute x1, waiting for transfers between devices, per_device(): near_ids = lax.ppermute(ids, 'layer', partners(2, 1))  0.89 us
  transfers between devices with their start and end apart: 11, of which 7 were waited for; matrix products, arithmetic and copies ran while one was open for 5% of the time, Pallas kernels for 12%

profile of v11, /device:TPU:0, one launch (start us, length us, event | category | flops | bytes accessed | tf_op | source)
XLA Modules:
  0.0 29.7 jit_solution(9833682212507893512)
XLA Ops:
  0.0 0.0 copy-start
  0.0 0.0 copy-start.2
  0.0 1.1 %dynamic-slice_bitcast_fusion = bf16[64,1024]{1,0:T(8,128)(2,1)S(1)} fusion(bf16[4096,64]{0,1:T(8,128)(2,1)} %param.12, s32[]{:T(128)S(6)} %select_n.7), kind=kLoop, calls=%fused_computation.16 | loop fusion | bytes 262148 | tf_op jit(solution)/shard_map/dynamic_slice | solution.py:278
  1.1 0.5 %collective-permute-start.3 = (bf16[256,256,8]{1,2,0:T(8,128)(2,1)}, bf16[256,256,8]{1,2,0:T(8,128)(2,1)S(1)}, u32[]{:S(2)}, u32[]{:S(2)}) collective-permute-start(bf16[256,256,8]{1,2,0:T(8,128)(2,1)} %param.13), channel_id=1, source_target_pairs={{0,1},{1,0},{2,3},{3,2},{4,5},{5,4},{6,7},{7,6},{8,9},{9,8},{10,11... | collective-permute-start | bytes 3145736 | tf_op jit(solution)/shard_map/ppermute | solution.py:294
  1.6 0.1 copy-done
  1.7 0.5 %multiply_convert_fusion.1 = (f16[64,1024]{1,0:T(8,128)(2,1)S(1)}, f32[64,1024]{1,0:T(8,128)S(1)}) fusion(bf16[64,1024]{1,0:T(8,128)(2,1)S(1)} %dynamic-slice_bitcast_fusion, bf16[1,1024,1024]{2,1,0:T(8,128)(2,1)S(1)} %copy-done), kind=kOutput, calls=%fused_computation.15 | convolution fusion | flops 134348800 | bytes 2621440 | tf_op jit(solution)/shard_map/dot_general | solution.py:283
  2.1 0.0 copy-start.1
  2.2 4.1 %collective-permute-start = (f16[64,1024]{1,0:T(8,128)(2,1)S(1)}, f16[64,1024]{1,0:T(8,128)(2,1)S(1)}, u32[]{:S(2)}, u32[]{:S(2)}) collective-permute-start(f16[64,1024]{1,0:T(8,128)(2,1)S(1)} %get-tuple-element.33), channel_id=1, source_target_pairs={{0,8},{1,5},{4,12},{5,1},{8,0},{9,13},{12,4},{13,9},{2,10},{3,7},{... | collective-permute-start | bytes 393224 | tf_op jit(solution)/shard_map/ppermute | solution.py:224
  6.9 0.0 copy-done.2
  6.9 0.2 ids.1.refs_0_
  7.1 0.1 collective-permute-start.2
  7.2 1.6 %collective-permute-start.4 = (bf16[256,256]{1,0:T(8,128)(2,1)S(1)}, bf16[256,256]{1,0:T(8,128)(2,1)S(1)}, u32[]{:S(2)}, u32[]{:S(2)}) collective-permute-start(bf16[256,256]{1,0:T(8,128)(2,1)S(1)} %ids.1.refs_0_), channel_id=1, source_target_pairs={{0,2},{2,0},{1,3},{3,1},{4,6},{6,4},{5,7},{7,5},{8,10},{10,8},{9,1... | collective-permute-start | bytes 393224 | tf_op jit(solution)/shard_map/ppermute | solution.py:292
  8.8 0.5 %collective-permute-done = f16[64,1024]{1,0:T(8,128)(2,1)S(1)} collective-permute-done((f16[64,1024]{1,0:T(8,128)(2,1)S(1)}, f16[64,1024]{1,0:T(8,128)(2,1)S(1)}, u32[]{:S(2)}, u32[]{:S(2)}) %collective-permute-start) | collective-permute-done | bytes 131104 | tf_op jit(solution)/shard_map/ppermute | solution.py:224
  9.2 0.1 multiply_convert_fusion
  9.3 2.5 %collective-permute-start.1 = (f16[64,1024]{1,0:T(8,128)(2,1)S(1)}, f16[64,1024]{1,0:T(8,128)(2,1)S(1)}, u32[]{:S(2)}, u32[]{:S(2)}) collective-permute-start(f16[64,1024]{1,0:T(8,128)(2,1)S(1)} %multiply_convert_fusion), channel_id=1, source_target_pairs={{0,4},{1,9},{4,0},{5,13},{8,12},{9,1},{12,8},{13,5},{2,6},{3,11},{... | collective-permute-start | bytes 393224 | tf_op jit(solution)/shard_map/ppermute | solution.py:224
  11.8 0.0 collective-permute-done.2.refs_0_
  11.8 0.0 collective-permute-done.3
  11.8 1.7 %decode.2.refs_6_ = bf16[2048,256]{1,0:T(8,128)(2,1)S(1)} custom-call(bf16[256,256]{1,0:T(8,128)(2,1)S(1)} %collective-permute-done.2.refs_0_, bf16[256,8,256]{2,1,0:T(8,128)(2,1)S(1)} %bitcast.22), custom_call_target="tpu_custom_call" | custom-call | bytes 2097152 | tf_op jit(solution)/shard_map/decode/pallas_call | solution.py:78
  13.5 0.0 copy-start.4
  13.5 0.9 %collective-permute-done.4.refs_1_ = bf16[256,256]{1,0:T(8,128)(2,1)S(1)} collective-permute-done((bf16[256,256]{1,0:T(8,128)(2,1)S(1)}, bf16[256,256]{1,0:T(8,128)(2,1)S(1)}, u32[]{:S(2)}, u32[]{:S(2)}) %collective-permute-start.4) | collective-permute-done | bytes 131104 | tf_op jit(solution)/shard_map/ppermute | solution.py:292
  14.4 0.0 copy-done.1
  14.4 0.0 copy-start.3
  14.4 0.0 copy-start.5
  14.4 1.7 %decode.3.refs_5_ = bf16[2048,256]{1,0:T(8,128)(2,1)S(1)} custom-call(bf16[256,256]{1,0:T(8,128)(2,1)S(1)} %ids.1.refs_0_, bf16[256,256]{1,0:T(8,128)(2,1)S(1)} %collective-permute-done.4.refs_1_, bf16[256,8,256]{2,1,0:T(8,128)(2,1)S(1)} %bitcast.21), custom_call_target="tpu_custom_call" | custom-call | bytes 2097152 | tf_op jit(solution)/shard_map/decode/pallas_call | solution.py:78
  16.2 0.0 collective-permute-done.1
  16.2 0.1 reduce-precision_convert_fusion
  16.3 0.0 copy-done.4
  16.3 0.3 %fusion.4 = f32[128,256]{1,0:T(8,128)S(1)} fusion(bf16[1,256,1024]{2,1,0:T(8,128)(2,1)S(1)} %copy-done.4, bf16[64,1024]{1,0:T(8,128)(2,1)S(1)} %get-tuple-element.32, bf16[64,1024]{1,0:T(8,128)(2,1)S(1)} %get-tuple-element.31), kind=kOutput, calls=%fused_computation.4 | convolution fusion | flops 67633152 | bytes 917504 | tf_op jit(solution)/shard_map/dot_general | solution.py:309
  16.6 0.2 collective-permute-start.5
  16.8 0.0 copy-done.3
  16.8 0.0 copy-done.5
  16.8 0.8 %fusion.in_ref = f32[64,256]{1,0:T(8,128)S(1)} fusion(bf16[4096,64]{0,1:T(8,128)(2,1)S(1)} %copy-done.5, bf16[1,256,4096]{2,1,0:T(8,128)(2,1)S(1)} %copy-done.3), kind=kOutput, calls=%fused_computation | convolution fusion | flops 134217728 | bytes 2686976 | tf_op jit(solution)/shard_map/dot_general | solution.py:297
  17.6 0.4 %collective-permute-done.5.other_ref = f32[64,256]{1,0:T(8,128)S(1)} collective-permute-done((f32[64,256]{1,0:T(8,128)S(1)}, f32[64,256]{1,0:T(8,128)S(1)}, u32[]{:S(2)}, u32[]{:S(2)}) %collective-permute-start.5) | collective-permute-done | bytes 65568 | tf_op jit(solution)/shard_map/ppermute | solution.py:317
  17.9 0.5 %vectors.1.refs_0_ = f32[2,4,2048]{2,1,0:T(4,128)S(1)} custom-call(f32[64,256]{1,0:T(8,128)S(1)} %fusion.in_ref, f32[64,256]{1,0:T(8,128)S(1)} %slice_add_fusion.own_ref, f32[64,256]{1,0:T(8,128)S(1)} %collective-permute-done.5.other_ref), custom_call_target="tpu_custom_call" | custom-call | tf_op jit(solution)/shard_map/vectors/pallas_call | solution.py:184
  18.4 3.4 %collective-permute-start.9 = (f16[2,4,2048]{2,1,0:T(4,128)(2,1)S(1)}, f16[2,4,2048]{2,1,0:T(4,128)(2,1)S(1)}, u32[]{:S(2)}, u32[]{:S(2)}) collective-permute-start(f16[2,4,2048]{2,1,0:T(4,128)(2,1)S(1)} %multiply_convert_fusion.2), channel_id=1, source_target_pairs={{0,12},{1,15},{2,14},{3,13},{4,8},{5,11},{6,10},{7,9},{8,4},{9,7},... | collective-permute-start | bytes 98312 | tf_op jit(solution)/shard_map/ppermute | solution.py:265
  21.8 0.0 collective-permute-start.8
  21.8 1.0 %collective-permute-start.7 = (f16[2,4,2048]{2,1,0:T(4,128)(2,1)S(1)}, f16[2,4,2048]{2,1,0:T(4,128)(2,1)S(1)}, u32[]{:S(2)}, u32[]{:S(2)}) collective-permute-start(f16[2,4,2048]{2,1,0:T(4,128)(2,1)S(1)} %multiply_convert_fusion.2), channel_id=1, source_target_pairs={{0,4},{1,7},{2,6},{3,5},{4,0},{5,3},{6,2},{7,1},{8,12},{9,15},{10,... | collective-permute-start | bytes 98312 | tf_op jit(solution)/shard_map/ppermute | solution.py:265
  22.9 1.1 %collective-permute-start.6 = (f16[2,4,2048]{2,1,0:T(4,128)(2,1)S(1)}, f16[2,4,2048]{2,1,0:T(4,128)(2,1)S(1)}, u32[]{:S(2)}, u32[]{:S(2)}) collective-permute-start(f16[2,4,2048]{2,1,0:T(4,128)(2,1)S(1)} %multiply_convert_fusion.2), channel_id=1, source_target_pairs={{0,2},{1,3},{2,0},{3,1},{4,6},{5,7},{6,4},{7,5},{8,10},{9,11},{10,... | collective-permute-start | bytes 98312 | tf_op jit(solution)/shard_map/ppermute | solution.py:265
  24.0 0.2 collective-permute-done.9
  24.2 2.6 %collective-permute-done.8 = f16[2,4,2048]{2,1,0:T(4,128)(2,1)S(1)} collective-permute-done((f16[2,4,2048]{2,1,0:T(4,128)(2,1)S(1)}, f16[2,4,2048]{2,1,0:T(4,128)(2,1)S(1)}, u32[]{:S(2)}, u32[]{:S(2)}) %collective-permute-start.8) | collective-permute-done | bytes 32800 | tf_op jit(solution)/shard_map/ppermute | solution.py:265
  26.8 0.0 collective-permute-done.7
  26.9 0.6 %collective-permute-done.6 = f16[2,4,2048]{2,1,0:T(4,128)(2,1)S(1)} collective-permute-done((f16[2,4,2048]{2,1,0:T(4,128)(2,1)S(1)}, f16[2,4,2048]{2,1,0:T(4,128)(2,1)S(1)}, u32[]{:S(2)}, u32[]{:S(2)}) %collective-permute-start.6) | collective-permute-done | bytes 32800 | tf_op jit(solution)/shard_map/ppermute | solution.py:265
  27.5 0.5 %score.1 = f32[16,256]{1,0:T(8,128)S(1)} custom-call(f32[2,4,2048]{2,1,0:T(4,128)S(1)} %vectors.1.refs_0_, f32[2,4,2048]{2,1,0:T(4,128)S(1)} %convert_multiply_fusion.3.refs_1_, f32[2,4,2048]{2,1,0:T(4,128)S(1)} %convert_multiply_fusion.2.refs_2_, f32[2,4,2048]{2,1,0:T(4,128)S(1)} %convert_multiply_fusion.1.refs_3_, ...), custom_call_target="tpu_custom_call" | custom-call | tf_op jit(solution)/shard_map/score/pallas_call | solution.py:163
  27.9 0.0 collective-permute-start.10
  28.0 1.2 %collective-permute-done.10 = f32[16,256]{1,0:T(8,128)S(1)} collective-permute-done((f32[16,256]{1,0:T(8,128)S(1)}, f32[16,256]{1,0:T(8,128)S(1)}, u32[]{:S(2)}, u32[]{:S(2)}) %collective-permute-start.10) | collective-permute-done | bytes 16416 | tf_op jit(solution)/shard_map/ppermute | solution.py:328
  29.1 0.6 %select_bitcast_fusion = f32[256,16]{0,1:T(8,128)} fusion(f32[16,256]{1,0:T(8,128)S(1)} %score.1, f32[16,256]{1,0:T(8,128)S(1)} %collective-permute-done.10, pred[256]{0:T(512)(128)(4,1)S(1)} %compare_reduce_fusion), kind=kLoop, calls=%fused_computation.23 | loop fusion | flops 8192 | bytes 49408 | tf_op jit(solution)/shard_map/transpose | solution.py:333
  (9 shorter events, 0.1 us)
Async XLA Ops:
  0.0 1.7 %copy-start = (bf16[1,1024,1024]{2,1,0:T(8,128)(2,1)S(1)}, bf16[1,1024,1024]{2,1,0:T(8,128)(2,1)}, u32[]{:S(2)}) copy-start(bf16[1,1024,1024]{2,1,0:T(8,128)(2,1)} %param.10) | copy-start | bytes 6291460
  0.0 6.9 %copy-start.2 = (s32[256,1,256]{2,1,0:T(1,128)S(1)}, s32[256,1,256]{2,1,0:T(1,128)}, u32[]{:S(2)}) copy-start(s32[256,1,256]{2,1,0:T(1,128)} %codes_ref) | copy-start | bytes 786436
  1.1 10.7 %collective-permute-start.3 = (bf16[256,256,8]{1,2,0:T(8,128)(2,1)}, bf16[256,256,8]{1,2,0:T(8,128)(2,1)S(1)}, u32[]{:S(2)}, u32[]{:S(2)}) collective-permute-start(bf16[256,256,8]{1,2,0:T(8,128)(2,1)} %param.13), channel_id=1, source_target_pairs={{0,1},{1,0},{2,3},{3,2},{4,5},{5,4},{6,7},{7,6},{8,9},{9,8},{10,11... | collective-permute-start | bytes 3145736 | tf_op jit(solution)/shard_map/ppermute | solution.py:294
  2.1 12.3 %copy-start.1 = (bf16[256,256,8]{1,2,0:T(8,128)(2,1)S(1)}, bf16[256,256,8]{1,2,0:T(8,128)(2,1)}, u32[]{:S(2)}) copy-start(bf16[256,256,8]{1,2,0:T(8,128)(2,1)} %param.13) | copy-start | bytes 3145732
  2.2 7.1 %collective-permute-start = (f16[64,1024]{1,0:T(8,128)(2,1)S(1)}, f16[64,1024]{1,0:T(8,128)(2,1)S(1)}, u32[]{:S(2)}, u32[]{:S(2)}) collective-permute-start(f16[64,1024]{1,0:T(8,128)(2,1)S(1)} %get-tuple-element.33), channel_id=1, source_target_pairs={{0,8},{1,5},{4,12},{5,1},{8,0},{9,13},{12,4},{13,9},{2,10},{3,7},{... | collective-permute-start | bytes 393224 | tf_op jit(solution)/shard_map/ppermute | solution.py:224
  7.1 4.7 %collective-permute-start.2 = (bf16[256,256]{1,0:T(8,128)(2,1)S(1)}, bf16[256,256]{1,0:T(8,128)(2,1)S(1)}, u32[]{:S(2)}, u32[]{:S(2)}) collective-permute-start(bf16[256,256]{1,0:T(8,128)(2,1)S(1)} %ids.1.refs_0_), channel_id=1, source_target_pairs={{1,0},{3,2},{2,1},{0,3},{5,4},{7,6},{6,5},{4,7},{9,8},{11,10},{10,... | collective-permute-start | bytes 393224 | tf_op jit(solution)/shard_map/ppermute | solution.py:293
  7.2 7.2 %collective-permute-start.4 = (bf16[256,256]{1,0:T(8,128)(2,1)S(1)}, bf16[256,256]{1,0:T(8,128)(2,1)S(1)}, u32[]{:S(2)}, u32[]{:S(2)}) collective-permute-start(bf16[256,256]{1,0:T(8,128)(2,1)S(1)} %ids.1.refs_0_), channel_id=1, source_target_pairs={{0,2},{2,0},{1,3},{3,1},{4,6},{6,4},{5,7},{7,5},{8,10},{10,8},{9,1... | collective-permute-start | bytes 393224 | tf_op jit(solution)/shard_map/ppermute | solution.py:292
  9.3 6.9 %collective-permute-start.1 = (f16[64,1024]{1,0:T(8,128)(2,1)S(1)}, f16[64,1024]{1,0:T(8,128)(2,1)S(1)}, u32[]{:S(2)}, u32[]{:S(2)}) collective-permute-start(f16[64,1024]{1,0:T(8,128)(2,1)S(1)} %multiply_convert_fusion), channel_id=1, source_target_pairs={{0,4},{1,9},{4,0},{5,13},{8,12},{9,1},{12,8},{13,5},{2,6},{3,11},{... | collective-permute-start | bytes 393224 | tf_op jit(solution)/shard_map/ppermute | solution.py:224
  13.5 2.8 %copy-start.4 = (bf16[1,256,1024]{2,1,0:T(8,128)(2,1)S(1)}, bf16[1,256,1024]{2,1,0:T(8,128)(2,1)}, u32[]{:S(2)}) copy-start(bf16[1,256,1024]{2,1,0:T(8,128)(2,1)} %param.9) | copy-start | bytes 1572868
  14.4 2.4 %copy-start.3 = (bf16[1,256,4096]{2,1,0:T(8,128)(2,1)S(1)}, bf16[1,256,4096]{2,1,0:T(8,128)(2,1)}, u32[]{:S(2)}) copy-start(bf16[1,256,4096]{2,1,0:T(8,128)(2,1)} %param.8) | copy-start | bytes 6291460
  14.4 2.4 %copy-start.5 = (bf16[4096,64]{0,1:T(8,128)(2,1)S(1)}, bf16[4096,64]{0,1:T(8,128)(2,1)}, u32[]{:S(2)}) copy-start(bf16[4096,64]{0,1:T(8,128)(2,1)} %param.11) | copy-start | bytes 1572868
  16.6 1.3 %collective-permute-start.5 = (f32[64,256]{1,0:T(8,128)S(1)}, f32[64,256]{1,0:T(8,128)S(1)}, u32[]{:S(2)}, u32[]{:S(2)}) collective-permute-start(f32[64,256]{1,0:T(8,128)S(1)} %slice_add_fusion.own_ref), channel_id=1, source_target_pairs={{0,1},{1,0},{2,3},{3,2},{4,5},{5,4},{6,7},{7,6},{8,9},{9,8},{10,11... | collective-permute-start | bytes 196616 | tf_op jit(solution)/shard_map/ppermute | solution.py:317
  18.4 5.8 %collective-permute-start.9 = (f16[2,4,2048]{2,1,0:T(4,128)(2,1)S(1)}, f16[2,4,2048]{2,1,0:T(4,128)(2,1)S(1)}, u32[]{:S(2)}, u32[]{:S(2)}) collective-permute-start(f16[2,4,2048]{2,1,0:T(4,128)(2,1)S(1)} %multiply_convert_fusion.2), channel_id=1, source_target_pairs={{0,12},{1,15},{2,14},{3,13},{4,8},{5,11},{6,10},{7,9},{8,4},{9,7},... | collective-permute-start | bytes 98312 | tf_op jit(solution)/shard_map/ppermute | solution.py:265
  21.8 5.0 %collective-permute-start.8 = (f16[2,4,2048]{2,1,0:T(4,128)(2,1)S(1)}, f16[2,4,2048]{2,1,0:T(4,128)(2,1)S(1)}, u32[]{:S(2)}, u32[]{:S(2)}) collective-permute-start(f16[2,4,2048]{2,1,0:T(4,128)(2,1)S(1)} %multiply_convert_fusion.2), channel_id=1, source_target_pairs={{0,8},{1,11},{2,10},{3,9},{4,12},{5,15},{6,14},{7,13},{8,0},{9,3},... | collective-permute-start | bytes 98312 | tf_op jit(solution)/shard_map/ppermute | solution.py:265
  21.8 5.0 %collective-permute-start.7 = (f16[2,4,2048]{2,1,0:T(4,128)(2,1)S(1)}, f16[2,4,2048]{2,1,0:T(4,128)(2,1)S(1)}, u32[]{:S(2)}, u32[]{:S(2)}) collective-permute-start(f16[2,4,2048]{2,1,0:T(4,128)(2,1)S(1)} %multiply_convert_fusion.2), channel_id=1, source_target_pairs={{0,4},{1,7},{2,6},{3,5},{4,0},{5,3},{6,2},{7,1},{8,12},{9,15},{10,... | collective-permute-start | bytes 98312 | tf_op jit(solution)/shard_map/ppermute | solution.py:265
  22.9 4.5 %collective-permute-start.6 = (f16[2,4,2048]{2,1,0:T(4,128)(2,1)S(1)}, f16[2,4,2048]{2,1,0:T(4,128)(2,1)S(1)}, u32[]{:S(2)}, u32[]{:S(2)}) collective-permute-start(f16[2,4,2048]{2,1,0:T(4,128)(2,1)S(1)} %multiply_convert_fusion.2), channel_id=1, source_target_pairs={{0,2},{1,3},{2,0},{3,1},{4,6},{5,7},{6,4},{7,5},{8,10},{9,11},{10,... | collective-permute-start | bytes 98312 | tf_op jit(solution)/shard_map/ppermute | solution.py:265
  27.9 1.2 %collective-permute-start.10 = (f32[16,256]{1,0:T(8,128)S(1)}, f32[16,256]{1,0:T(8,128)S(1)}, u32[]{:S(2)}, u32[]{:S(2)}) collective-permute-start(f32[16,256]{1,0:T(8,128)S(1)} %score.1), channel_id=1, source_target_pairs={{0,1},{1,0},{2,3},{3,2},{4,5},{5,4},{6,7},{7,6},{8,9},{9,8},{10,11... | collective-permute-start | bytes 49160 | tf_op jit(solution)/shard_map/ppermute | solution.py:328

commit v12 on v11

--- a/solution.py
+++ b/solution.py
@@ -11,7 +11,7 @@
 LANES = 128
 LINK_SCALE = 1024.0
 VECTOR_SCALE = 16384.0
-GATHER_ORDER = (0, 1, 2, 3)
+GATHER_ORDER = (2, 1, 0, 3)
 
 
 def ids_kernel(codes_ref, out_ref):
@@ -279,7 +279,6 @@
             jnp.transpose(proj_out), lax.axis_index("dp") * rows_local, rows_local, 1
         )
     )
-    own_rows, moved_book = lax.optimization_barrier((own_rows, codebook))
     folded = jnp.dot(own_rows, kv_weight[0], preferred_element_type=jnp.float32)
     book_t = jnp.transpose(codebook, (0, 2, 1))
     by_core = has_two_by_two() and lax.axis_size("dp") == 4
@@ -289,7 +288,8 @@
     live, moved_codes = lax.optimization_barrier((live, codes))
     ids = make_ids(moved_codes)
     if by_core:
-        near_ids = lax.ppermute(ids, "layer", partners(2, 1))
+        sent, moved_book = lax.optimization_barrier((sent, codebook))
+        near_moved = lax.ppermute(ids, "layer", partners(2, 1))
         far_ids = lax.ppermute(ids, ("layer", "sub"), FAR_CODES)
         other_book = lax.ppermute(moved_book, "sub", partners(2, 1))
 
@@ -298,14 +298,12 @@
             proj_in, acts[0], (((0,), (1,)), ((), ())), preferred_element_type=jnp.float32
         )
 
-    def tables():
+    def far_table():
         if not by_core:
-            return (decode([ids], book_t),)
-        far = decode([far_ids], jnp.transpose(other_book, (0, 2, 1)))
-        far, late_ids = lax.optimization_barrier((far, near_ids))
-        return decode([ids, late_ids], book_t), far
-
-    folded, (live, decoded) = sum_over_dp(folded, sent, [lambda: live, tables])
+            return decode([ids], book_t), ids
+        return decode([far_ids], jnp.transpose(other_book, (0, 2, 1))), near_moved
+
+    folded, (live, (far, near_ids)) = sum_over_dp(folded, sent, [lambda: live, far_table])
     out_side = lax.dot_general(
         jnp.concatenate(split_high_low(folded), axis=0),
         kv_grad[0],
@@ -321,15 +319,17 @@
     sent = (vectors * VECTOR_SCALE).astype(jnp.float16)
     core = lax.axis_index("sub")
     if by_core:
-        blocks = [
-            block.astype(jnp.float32) * (1.0 / VECTOR_SCALE) for block in gather_by_core(sent)
-        ]
-        total = score_blocks(vectors, blocks, *decoded)
+        blocks = gather_by_core(sent)
+        blocks[-1], own_ids, late_ids = lax.optimization_barrier((blocks[-1], ids, near_ids))
+        near = decode([own_ids, late_ids], book_t)
+        *blocks, near = lax.optimization_barrier((*blocks, near))
+        blocks = [block.astype(jnp.float32) * (1.0 / VECTOR_SCALE) for block in blocks]
+        total = score_blocks(vectors, blocks, near, far)
         total = total + lax.ppermute(total, "sub", partners(2, 1))
     else:
         every = gather_over_dp(lax.dynamic_index_in_dim(sent, core, 0, False))
         every = every.reshape(-1, dims_local).astype(jnp.float32) * (1.0 / VECTOR_SCALE)
-        total = lax.psum(score(every, decoded[0]), ("layer", "sub"))
+        total = lax.psum(score(every, far), ("layer", "sub"))
     return jnp.transpose(jnp.where(live[:1] > 0.0, total, jnp.float32(0.0)))
 
 

time: 29.9 us -> 29.7 us (level)
  waiting for transfers between devices: 6.28 us -> 4.41 us
  starting transfers between devices: 14.5 us -> 15.7 us
  local copies, waits for them, and re-layouts: 1.16 us -> 1.68 us
    ppermute x4, waiting for transfers between devices: 3.39 us -> 0.42 us  [gather_by_core(): blocks.append(lax.ppermute(x, ('dp', 'layer', 'sub'), pairs))]
    ppermute x2, waiting for transfers between devices: 0.47 us -> 2.25 us  [sum_over_dp(): got = lax.ppermute(sent, ('dp', 'sub'), pairs)]
    ppermute x4, starting transfers between devices: 5.53 us -> 6.45 us  [gather_by_core(): blocks.append(lax.ppermute(x, ('dp', 'layer', 'sub'), pairs))]
    ppermute x1, starting transfers between devices: 0.01 us -> 0.62 us  [per_device(): total = total + lax.ppermute(total, 'sub', partners(2, 1))]
    unnamed x12, local copies, waits for them, and re-layouts: 0.09 us -> 0.61 us
    ppermute x1, waiting for transfers between devices: 0.89 us -> 0.45 us  [per_device(): near_moved = lax.ppermute(ids, 'layer', partners(2, 1))]
    ppermute x1, waiting for transfers between devices: 1.16 us -> 0.82 us  [per_device(): total = total + lax.ppermute(total, 'sub', partners(2, 1))]
  transfers between devices with their start and end apart: 11 -> 11, of which waited for: 7 -> 6; matrix products, arithmetic and copies ran while one was open for 5% -> 3% of each run, Pallas kernels for 12% -> 12%
where the time goes in v12:
time: 29.7 us; the launch traced here: 29.6 us
  starting transfers between devices  15.7 us (53%)
  Pallas kernels  4.58 us (15%)
  waiting for transfers between devices  4.41 us (15%)
  local copies, waits for them, and re-layouts  1.68 us (6%)
  matrix products  1.55 us (5%)
  other arithmetic  0.87 us (3%)
  between operations  0.82 us (3%)
    ppermute x4, starting transfers between devices, gather_by_core(): blocks.append(lax.ppermute(x, ('dp', 'layer', 'sub'), pairs))  6.45 us
    ppermute x2, starting transfers between devices, sum_over_dp(): got = lax.ppermute(sent, ('dp', 'sub'), pairs)  6.38 us
    pallas_call x2, Pallas kernels, decode(): pl.pallas_call(decode_kernel, out_shape=jax.ShapeDtypeStruct((subs * widt...  3.47 us
    ppermute x2, waiting for transfers between devices, sum_over_dp(): got = lax.ppermute(sent, ('dp', 'sub'), pairs)  2.25 us
    ppermute x1, starting transfers between devices, per_device(): near_moved = lax.ppermute(ids, 'layer', partners(2, 1))  1.33 us
    dynamic_slice x1, local copies, waits for them, and re-layouts, per_device(): lax.dynamic_slice_in_dim(jnp.transpose(proj_out), lax.axis_index('dp') *...  1.06 us
    ppermute x1, waiting for transfers between devices, per_device(): total = total + lax.ppermute(total, 'sub', partners(2, 1))  0.82 us
    dot_general x1, matrix products, first_side(): lax.dot_general(proj_in, acts[0], (((0,), (1,)), ((), ())), preferred_ele...  0.76 us
  transfers between devices with their start and end apart: 11, of which 6 were waited for; matrix products, arithmetic and copies ran while one was open for 3% of the time, Pallas kernels for 12%

profile of v12, /device:TPU:0, one launch (start us, length us, event | category | flops | bytes accessed | tf_op | source)
XLA Modules:
  0.0 29.6 jit_solution(12135457466227902814)
XLA Ops:
  0.0 0.0 copy-start
  0.0 0.0 copy-start.1
  0.0 0.0 copy-start.2
  0.0 1.1 %dynamic-slice_bitcast_fusion = bf16[64,1024]{1,0:T(8,128)(2,1)S(1)} fusion(bf16[4096,64]{0,1:T(8,128)(2,1)} %param.12, s32[]{:T(128)S(6)} %select_n.7), kind=kLoop, calls=%fused_computation.16 | loop fusion | bytes 262148 | tf_op jit(solution)/shard_map/dynamic_slice | solution.py:278
  1.1 0.6 %copy-done = bf16[1,1024,1024]{2,1,0:T(8,128)(2,1)S(1)} copy-done((bf16[1,1024,1024]{2,1,0:T(8,128)(2,1)S(1)}, bf16[1,1024,1024]{2,1,0:T(8,128)(2,1)}, u32[]{:S(2)}) %copy-start) | copy-done | bytes 2097176
  1.7 0.5 %multiply_convert_fusion.1 = (f16[64,1024]{1,0:T(8,128)(2,1)S(1)}, f32[64,1024]{1,0:T(8,128)S(1)}) fusion(bf16[64,1024]{1,0:T(8,128)(2,1)S(1)} %dynamic-slice_bitcast_fusion, bf16[1,1024,1024]{2,1,0:T(8,128)(2,1)S(1)} %copy-done), kind=kOutput, calls=%fused_computation.15 | convolution fusion | flops 134348800 | bytes 2621440 | tf_op jit(solution)/shard_map/dot_general | solution.py:282
  2.1 0.0 copy-start.4
  2.2 0.0 copy-done.1
  2.2 0.5 %collective-permute-start.3 = (bf16[256,256,8]{1,2,0:T(8,128)(2,1)S(1)}, bf16[256,256,8]{1,2,0:T(8,128)(2,1)S(1)}, u32[]{:S(2)}, u32[]{:S(2)}) collective-permute-start(bf16[256,256,8]{1,2,0:T(8,128)(2,1)S(1)} %copy-done.1), channel_id=1, source_target_pairs={{0,1},{1,0},{2,3},{3,2},{4,5},{5,4},{6,7},{7,6},{8,9},{9,8},{10,11... | collective-permute-start | bytes 3145736 | tf_op jit(solution)/shard_map/ppermute | solution.py:294
  2.7 3.7 %collective-permute-start = (f16[64,1024]{1,0:T(8,128)(2,1)S(1)}, f16[64,1024]{1,0:T(8,128)(2,1)S(1)}, u32[]{:S(2)}, u32[]{:S(2)}) collective-permute-start(f16[64,1024]{1,0:T(8,128)(2,1)S(1)} %get-tuple-element.24), channel_id=1, source_target_pairs={{0,8},{1,5},{4,12},{5,1},{8,0},{9,13},{12,4},{13,9},{2,10},{3,7},{... | collective-permute-start | bytes 393224 | tf_op jit(solution)/shard_map/ppermute | solution.py:224
  7.0 0.0 copy-done.2
  7.0 0.2 ids.1.refs_0_
  7.2 0.3 collective-permute-start.2
  7.5 1.3 %collective-permute-start.4 = (bf16[256,256]{1,0:T(8,128)(2,1)S(1)}, bf16[256,256]{1,0:T(8,128)(2,1)S(1)}, u32[]{:S(2)}, u32[]{:S(2)}) collective-permute-start(bf16[256,256]{1,0:T(8,128)(2,1)S(1)} %ids.1.refs_0_), channel_id=1, source_target_pairs={{0,2},{2,0},{1,3},{3,1},{4,6},{6,4},{5,7},{7,5},{8,10},{10,8},{9,1... | collective-permute-start | bytes 393224 | tf_op jit(solution)/shard_map/ppermute | solution.py:292
  8.8 0.7 %collective-permute-done = f16[64,1024]{1,0:T(8,128)(2,1)S(1)} collective-permute-done((f16[64,1024]{1,0:T(8,128)(2,1)S(1)}, f16[64,1024]{1,0:T(8,128)(2,1)S(1)}, u32[]{:S(2)}, u32[]{:S(2)}) %collective-permute-start) | collective-permute-done | bytes 131104 | tf_op jit(solution)/shard_map/ppermute | solution.py:224
  9.5 0.1 multiply_convert_fusion
  9.6 0.0 copy-start.3
  9.6 0.0 copy-start.5
  9.6 2.7 %collective-permute-start.1 = (f16[64,1024]{1,0:T(8,128)(2,1)S(1)}, f16[64,1024]{1,0:T(8,128)(2,1)S(1)}, u32[]{:S(2)}, u32[]{:S(2)}) collective-permute-start(f16[64,1024]{1,0:T(8,128)(2,1)S(1)} %multiply_convert_fusion), channel_id=1, source_target_pairs={{0,4},{1,9},{4,0},{5,13},{8,12},{9,1},{12,8},{13,5},{2,6},{3,11},{... | collective-permute-start | bytes 393224 | tf_op jit(solution)/shard_map/ppermute | solution.py:224
  12.3 0.0 collective-permute-done.2.refs_0_
  12.3 0.0 collective-permute-done.3
  12.3 1.7 %decode.2.refs_6_ = bf16[2048,256]{1,0:T(8,128)(2,1)S(1)} custom-call(bf16[256,256]{1,0:T(8,128)(2,1)S(1)} %collective-permute-done.2.refs_0_, bf16[256,8,256]{2,1,0:T(8,128)(2,1)S(1)} %bitcast.22), custom_call_target="tpu_custom_call" | custom-call | bytes 2097152 | tf_op jit(solution)/shard_map/decode/pallas_call | solution.py:78
  14.1 0.4 %collective-permute-done.4.refs_1_ = bf16[256,256]{1,0:T(8,128)(2,1)S(1)} collective-permute-done((bf16[256,256]{1,0:T(8,128)(2,1)S(1)}, bf16[256,256]{1,0:T(8,128)(2,1)S(1)}, u32[]{:S(2)}, u32[]{:S(2)}) %collective-permute-start.4) | collective-permute-done | bytes 131104 | tf_op jit(solution)/shard_map/ppermute | solution.py:292
  14.5 1.6 %collective-permute-done.1 = f16[64,1024]{1,0:T(8,128)(2,1)S(1)} collective-permute-done((f16[64,1024]{1,0:T(8,128)(2,1)S(1)}, f16[64,1024]{1,0:T(8,128)(2,1)S(1)}, u32[]{:S(2)}, u32[]{:S(2)}) %collective-permute-start.1) | collective-permute-done | bytes 131104 | tf_op jit(solution)/shard_map/ppermute | solution.py:224
  16.1 0.1 reduce-precision_convert_fusion
  16.2 0.0 copy-done.4
  16.2 0.3 %fusion.4 = f32[128,256]{1,0:T(8,128)S(1)} fusion(bf16[1,256,1024]{2,1,0:T(8,128)(2,1)S(1)} %copy-done.4, bf16[64,1024]{1,0:T(8,128)(2,1)S(1)} %get-tuple-element.44, bf16[64,1024]{1,0:T(8,128)(2,1)S(1)} %get-tuple-element.43), kind=kOutput, calls=%fused_computation.4 | convolution fusion | flops 67633152 | bytes 917504 | tf_op jit(solution)/shard_map/dot_general | solution.py:307
  16.5 0.1 collective-permute-start.5
  16.6 0.0 copy-done.3
  16.6 0.0 copy-done.5
  16.6 0.8 %fusion.in_ref = f32[64,256]{1,0:T(8,128)S(1)} fusion(bf16[4096,64]{0,1:T(8,128)(2,1)S(1)} %copy-done.5, bf16[1,256,4096]{2,1,0:T(8,128)(2,1)S(1)} %copy-done.3), kind=kOutput, calls=%fused_computation | convolution fusion | flops 134217728 | bytes 2686976 | tf_op jit(solution)/shard_map/dot_general | solution.py:297
  17.4 0.5 %collective-permute-done.5.other_ref = f32[64,256]{1,0:T(8,128)S(1)} collective-permute-done((f32[64,256]{1,0:T(8,128)S(1)}, f32[64,256]{1,0:T(8,128)S(1)}, u32[]{:S(2)}, u32[]{:S(2)}) %collective-permute-start.5) | collective-permute-done | bytes 65568 | tf_op jit(solution)/shard_map/ppermute | solution.py:315
  17.8 0.5 %vectors.1.refs_0_ = f32[2,4,2048]{2,1,0:T(4,128)S(1)} custom-call(f32[64,256]{1,0:T(8,128)S(1)} %fusion.in_ref, f32[64,256]{1,0:T(8,128)S(1)} %slice_add_fusion.own_ref, f32[64,256]{1,0:T(8,128)S(1)} %collective-permute-done.5.other_ref), custom_call_target="tpu_custom_call" | custom-call | tf_op jit(solution)/shard_map/vectors/pallas_call | solution.py:184
  18.3 3.6 %collective-permute-start.9 = (f16[2,4,2048]{2,1,0:T(4,128)(2,1)S(1)}, f16[2,4,2048]{2,1,0:T(4,128)(2,1)S(1)}, u32[]{:S(2)}, u32[]{:S(2)}) collective-permute-start(f16[2,4,2048]{2,1,0:T(4,128)(2,1)S(1)} %multiply_convert_fusion.2), channel_id=1, source_target_pairs={{0,12},{1,15},{2,14},{3,13},{4,8},{5,11},{6,10},{7,9},{8,4},{9,7},... | collective-permute-start | bytes 98312 | tf_op jit(solution)/shard_map/ppermute | solution.py:265
  22.0 0.0 collective-permute-start.6
  22.0 0.8 %collective-permute-start.7 = (f16[2,4,2048]{2,1,0:T(4,128)(2,1)S(1)}, f16[2,4,2048]{2,1,0:T(4,128)(2,1)S(1)}, u32[]{:S(2)}, u32[]{:S(2)}) collective-permute-start(f16[2,4,2048]{2,1,0:T(4,128)(2,1)S(1)} %multiply_convert_fusion.2), channel_id=1, source_target_pairs={{0,4},{1,7},{2,6},{3,5},{4,0},{5,3},{6,2},{7,1},{8,12},{9,15},{10,... | collective-permute-start | bytes 98312 | tf_op jit(solution)/shard_map/ppermute | solution.py:265
  22.8 2.0 %collective-permute-start.8 = (f16[2,4,2048]{2,1,0:T(4,128)(2,1)S(1)}, f16[2,4,2048]{2,1,0:T(4,128)(2,1)S(1)}, u32[]{:S(2)}, u32[]{:S(2)}) collective-permute-start(f16[2,4,2048]{2,1,0:T(4,128)(2,1)S(1)} %multiply_convert_fusion.2), channel_id=1, source_target_pairs={{0,2},{1,3},{2,0},{3,1},{4,6},{5,7},{6,4},{7,5},{8,10},{9,11},{10,... | collective-permute-start | bytes 98312 | tf_op jit(solution)/shard_map/ppermute | solution.py:265
  24.8 0.0 collective-permute-done.9
  24.8 1.7 %decode.3.refs_5_ = bf16[2048,256]{1,0:T(8,128)(2,1)S(1)} custom-call(bf16[256,256]{1,0:T(8,128)(2,1)S(1)} %ids.1.refs_0_, bf16[256,256]{1,0:T(8,128)(2,1)S(1)} %collective-permute-done.4.refs_1_, bf16[256,8,256]{2,1,0:T(8,128)(2,1)S(1)} %bitcast.21), custom_call_target="tpu_custom_call" | custom-call | bytes 2097152 | tf_op jit(solution)/shard_map/decode/pallas_call | solution.py:78
  26.5 0.4 %collective-permute-done.6 = f16[2,4,2048]{2,1,0:T(4,128)(2,1)S(1)} collective-permute-done((f16[2,4,2048]{2,1,0:T(4,128)(2,1)S(1)}, f16[2,4,2048]{2,1,0:T(4,128)(2,1)S(1)}, u32[]{:S(2)}, u32[]{:S(2)}) %collective-permute-start.6) | collective-permute-done | bytes 32800 | tf_op jit(solution)/shard_map/ppermute | solution.py:265
  26.9 0.0 collective-permute-done.7
  26.9 0.0 collective-permute-done.8
  27.0 0.5 %score.1 = f32[16,256]{1,0:T(8,128)S(1)} custom-call(f32[2,4,2048]{2,1,0:T(4,128)S(1)} %vectors.1.refs_0_, f32[2,4,2048]{2,1,0:T(4,128)S(1)} %get-tuple-element.50.refs_1_, f32[2,4,2048]{2,1,0:T(4,128)S(1)} %get-tuple-element.49.refs_2_, f32[2,4,2048]{2,1,0:T(4,128)S(1)} %get-tuple-element.48.refs_3_, f32[2,4,2048]{2,1,0:T(4,128)S(1)} %get-tuple-element.47.refs_4_, ...), custom_call_target="tpu_custom_call" | custom-call | tf_op jit(solution)/shard_map/score/pallas_call | solution.py:163
  27.5 0.6 %collective-permute-start.10 = (f32[16,256]{1,0:T(8,128)S(1)}, f32[16,256]{1,0:T(8,128)S(1)}, u32[]{:S(2)}, u32[]{:S(2)}) collective-permute-start(f32[16,256]{1,0:T(8,128)S(1)} %score.1), channel_id=1, source_target_pairs={{0,1},{1,0},{2,3},{3,2},{4,5},{5,4},{6,7},{7,6},{8,9},{9,8},{10,11... | collective-permute-start | bytes 49160 | tf_op jit(solution)/shard_map/ppermute | solution.py:328
  28.1 0.8 %collective-permute-done.10 = f32[16,256]{1,0:T(8,128)S(1)} collective-permute-done((f32[16,256]{1,0:T(8,128)S(1)}, f32[16,256]{1,0:T(8,128)S(1)}, u32[]{:S(2)}, u32[]{:S(2)}) %collective-permute-start.10) | collective-permute-done | bytes 16416 | tf_op jit(solution)/shard_map/ppermute | solution.py:328
  29.0 0.6 %select_bitcast_fusion = f32[256,16]{0,1:T(8,128)} fusion(f32[16,256]{1,0:T(8,128)S(1)} %score.1, f32[16,256]{1,0:T(8,128)S(1)} %collective-permute-done.10, pred[256]{0:T(512)(128)(4,1)S(1)} %compare_reduce_fusion), kind=kLoop, calls=%fused_computation.23 | loop fusion | flops 8192 | bytes 49408 | tf_op jit(solution)/shard_map/transpose | solution.py:333
  (7 shorter events, 0.1 us)
Async XLA Ops:
  0.0 1.7 %copy-start = (bf16[1,1024,1024]{2,1,0:T(8,128)(2,1)S(1)}, bf16[1,1024,1024]{2,1,0:T(8,128)(2,1)}, u32[]{:S(2)}) copy-start(bf16[1,1024,1024]{2,1,0:T(8,128)(2,1)} %param.10) | copy-start | bytes 6291460
  0.0 2.2 %copy-start.1 = (bf16[256,256,8]{1,2,0:T(8,128)(2,1)S(1)}, bf16[256,256,8]{1,2,0:T(8,128)(2,1)}, u32[]{:S(2)}) copy-start(bf16[256,256,8]{1,2,0:T(8,128)(2,1)} %param.13) | copy-start | bytes 3145732
  0.0 7.0 %copy-start.2 = (s32[256,1,256]{2,1,0:T(1,128)S(1)}, s32[256,1,256]{2,1,0:T(1,128)}, u32[]{:S(2)}) copy-start(s32[256,1,256]{2,1,0:T(1,128)} %codes_ref) | copy-start | bytes 786436
  2.1 14.0 %copy-start.4 = (bf16[1,256,1024]{2,1,0:T(8,128)(2,1)S(1)}, bf16[1,256,1024]{2,1,0:T(8,128)(2,1)}, u32[]{:S(2)}) copy-start(bf16[1,256,1024]{2,1,0:T(8,128)(2,1)} %param.9) | copy-start | bytes 1572868
  2.2 10.2 %collective-permute-start.3 = (bf16[256,256,8]{1,2,0:T(8,128)(2,1)S(1)}, bf16[256,256,8]{1,2,0:T(8,128)(2,1)S(1)}, u32[]{:S(2)}, u32[]{:S(2)}) collective-permute-start(bf16[256,256,8]{1,2,0:T(8,128)(2,1)S(1)} %copy-done.1), channel_id=1, source_target_pairs={{0,1},{1,0},{2,3},{3,2},{4,5},{5,4},{6,7},{7,6},{8,9},{9,8},{10,11... | collective-permute-start | bytes 3145736 | tf_op jit(solution)/shard_map/ppermute | solution.py:294
  2.7 6.8 %collective-permute-start = (f16[64,1024]{1,0:T(8,128)(2,1)S(1)}, f16[64,1024]{1,0:T(8,128)(2,1)S(1)}, u32[]{:S(2)}, u32[]{:S(2)}) collective-permute-start(f16[64,1024]{1,0:T(8,128)(2,1)S(1)} %get-tuple-element.24), channel_id=1, source_target_pairs={{0,8},{1,5},{4,12},{5,1},{8,0},{9,13},{12,4},{13,9},{2,10},{3,7},{... | collective-permute-start | bytes 393224 | tf_op jit(solution)/shard_map/ppermute | solution.py:224
  7.2 5.1 %collective-permute-start.2 = (bf16[256,256]{1,0:T(8,128)(2,1)S(1)}, bf16[256,256]{1,0:T(8,128)(2,1)S(1)}, u32[]{:S(2)}, u32[]{:S(2)}) collective-permute-start(bf16[256,256]{1,0:T(8,128)(2,1)S(1)} %ids.1.refs_0_), channel_id=1, source_target_pairs={{1,0},{3,2},{2,1},{0,3},{5,4},{7,6},{6,5},{4,7},{9,8},{11,10},{10,... | collective-permute-start | bytes 393224 | tf_op jit(solution)/shard_map/ppermute | solution.py:293
  7.5 7.0 %collective-permute-start.4 = (bf16[256,256]{1,0:T(8,128)(2,1)S(1)}, bf16[256,256]{1,0:T(8,128)(2,1)S(1)}, u32[]{:S(2)}, u32[]{:S(2)}) collective-permute-start(bf16[256,256]{1,0:T(8,128)(2,1)S(1)} %ids.1.refs_0_), channel_id=1, source_target_pairs={{0,2},{2,0},{1,3},{3,1},{4,6},{6,4},{5,7},{7,5},{8,10},{10,8},{9,1... | collective-permute-start | bytes 393224 | tf_op jit(solution)/shard_map/ppermute | solution.py:292
  9.6 7.0 %copy-start.3 = (bf16[1,256,4096]{2,1,0:T(8,128)(2,1)S(1)}, bf16[1,256,4096]{2,1,0:T(8,128)(2,1)}, u32[]{:S(2)}) copy-start(bf16[1,256,4096]{2,1,0:T(8,128)(2,1)} %param.8) | copy-start | bytes 6291460
  9.6 7.0 %copy-start.5 = (bf16[4096,64]{0,1:T(8,128)(2,1)S(1)}, bf16[4096,64]{0,1:T(8,128)(2,1)}, u32[]{:S(2)}) copy-start(bf16[4096,64]{0,1:T(8,128)(2,1)} %param.11) | copy-start | bytes 1572868
  9.6 6.5 %collective-permute-start.1 = (f16[64,1024]{1,0:T(8,128)(2,1)S(1)}, f16[64,1024]{1,0:T(8,128)(2,1)S(1)}, u32[]{:S(2)}, u32[]{:S(2)}) collective-permute-start(f16[64,1024]{1,0:T(8,128)(2,1)S(1)} %multiply_convert_fusion), channel_id=1, source_target_pairs={{0,4},{1,9},{4,0},{5,13},{8,12},{9,1},{12,8},{13,5},{2,6},{3,11},{... | collective-permute-start | bytes 393224 | tf_op jit(solution)/shard_map/ppermute | solution.py:224
  16.5 1.3 %collective-permute-start.5 = (f32[64,256]{1,0:T(8,128)S(1)}, f32[64,256]{1,0:T(8,128)S(1)}, u32[]{:S(2)}, u32[]{:S(2)}) collective-permute-start(f32[64,256]{1,0:T(8,128)S(1)} %slice_add_fusion.own_ref), channel_id=1, source_target_pairs={{0,1},{1,0},{2,3},{3,2},{4,5},{5,4},{6,7},{7,6},{8,9},{9,8},{10,11... | collective-permute-start | bytes 196616 | tf_op jit(solution)/shard_map/ppermute | solution.py:315
  18.3 6.5 %collective-permute-start.9 = (f16[2,4,2048]{2,1,0:T(4,128)(2,1)S(1)}, f16[2,4,2048]{2,1,0:T(4,128)(2,1)S(1)}, u32[]{:S(2)}, u32[]{:S(2)}) collective-permute-start(f16[2,4,2048]{2,1,0:T(4,128)(2,1)S(1)} %multiply_convert_fusion.2), channel_id=1, source_target_pairs={{0,12},{1,15},{2,14},{3,13},{4,8},{5,11},{6,10},{7,9},{8,4},{9,7},... | collective-permute-start | bytes 98312 | tf_op jit(solution)/shard_map/ppermute | solution.py:265
  22.0 5.0 %collective-permute-start.6 = (f16[2,4,2048]{2,1,0:T(4,128)(2,1)S(1)}, f16[2,4,2048]{2,1,0:T(4,128)(2,1)S(1)}, u32[]{:S(2)}, u32[]{:S(2)}) collective-permute-start(f16[2,4,2048]{2,1,0:T(4,128)(2,1)S(1)} %multiply_convert_fusion.2), channel_id=1, source_target_pairs={{0,8},{1,11},{2,10},{3,9},{4,12},{5,15},{6,14},{7,13},{8,0},{9,3},... | collective-permute-start | bytes 98312 | tf_op jit(solution)/shard_map/ppermute | solution.py:265
  22.0 5.0 %collective-permute-start.7 = (f16[2,4,2048]{2,1,0:T(4,128)(2,1)S(1)}, f16[2,4,2048]{2,1,0:T(4,128)(2,1)S(1)}, u32[]{:S(2)}, u32[]{:S(2)}) collective-permute-start(f16[2,4,2048]{2,1,0:T(4,128)(2,1)S(1)} %multiply_convert_fusion.2), channel_id=1, source_target_pairs={{0,4},{1,7},{2,6},{3,5},{4,0},{5,3},{6,2},{7,1},{8,12},{9,15},{10,... | collective-permute-start | bytes 98312 | tf_op jit(solution)/shard_map/ppermute | solution.py:265
  22.8 4.2 %collective-permute-start.8 = (f16[2,4,2048]{2,1,0:T(4,128)(2,1)S(1)}, f16[2,4,2048]{2,1,0:T(4,128)(2,1)S(1)}, u32[]{:S(2)}, u32[]{:S(2)}) collective-permute-start(f16[2,4,2048]{2,1,0:T(4,128)(2,1)S(1)} %multiply_convert_fusion.2), channel_id=1, source_target_pairs={{0,2},{1,3},{2,0},{3,1},{4,6},{5,7},{6,4},{7,5},{8,10},{9,11},{10,... | collective-permute-start | bytes 98312 | tf_op jit(solution)/shard_map/ppermute | solution.py:265
  27.5 1.5 %collective-permute-start.10 = (f32[16,256]{1,0:T(8,128)S(1)}, f32[16,256]{1,0:T(8,128)S(1)}, u32[]{:S(2)}, u32[]{:S(2)}) collective-permute-start(f32[16,256]{1,0:T(8,128)S(1)} %score.1), channel_id=1, source_target_pairs={{0,1},{1,0},{2,3},{3,2},{4,5},{5,4},{6,7},{7,6},{8,9},{9,8},{10,11... | collective-permute-start | bytes 49160 | tf_op jit(solution)/shard_map/ppermute | solution.py:328

commit v13 on v12

--- a/solution.py
+++ b/solution.py
@@ -279,6 +279,7 @@
             jnp.transpose(proj_out), lax.axis_index("dp") * rows_local, rows_local, 1
         )
     )
+    own_rows, moved_book = lax.optimization_barrier((own_rows, codebook))
     folded = jnp.dot(own_rows, kv_weight[0], preferred_element_type=jnp.float32)
     book_t = jnp.transpose(codebook, (0, 2, 1))
     by_core = has_two_by_two() and lax.axis_size("dp") == 4
@@ -288,7 +289,6 @@
     live, moved_codes = lax.optimization_barrier((live, codes))
     ids = make_ids(moved_codes)
     if by_core:
-        sent, moved_book = lax.optimization_barrier((sent, codebook))
         near_moved = lax.ppermute(ids, "layer", partners(2, 1))
         far_ids = lax.ppermute(ids, ("layer", "sub"), FAR_CODES)
         other_book = lax.ppermute(moved_book, "sub", partners(2, 1))

time: 29.7 us -> 29.7 us (level)
  local copies, waits for them, and re-layouts: 1.68 us -> 1.16 us
  waiting for transfers between devices: 4.41 us -> 4.87 us
    ppermute x2, waiting for transfers between devices: 2.25 us -> 1.12 us  [sum_over_dp(): got = lax.ppermute(sent, ('dp', 'sub'), pairs)]
    ppermute x4, waiting for transfers between devices: 0.42 us -> 1.49 us  [gather_by_core(): blocks.append(lax.ppermute(x, ('dp', 'layer', 'sub'), pairs))]
    unnamed x12, local copies, waits for them, and re-layouts: 0.61 us -> 0.1 us
    ppermute x1, starting transfers between devices: 0.62 us -> 0.18 us  [per_device(): total = total + lax.ppermute(total, 'sub', partners(2, 1))]
    ppermute x1, waiting for transfers between devices: 0.45 us -> 0.88 us  [per_device(): near_moved = lax.ppermute(ids, 'layer', partners(2, 1))]
  transfers between devices with their start and end apart: 11 -> 11, of which waited for: 6 -> 8; matrix products, arithmetic and copies ran while one was open for 3% -> 4% of each run, Pallas kernels for 12% -> 12%
where the time goes in v13:
time: 29.7 us; the launch traced here: 29.6 us
  starting transfers between devices  15.7 us (53%)
  waiting for transfers between devices  4.87 us (16%)
  Pallas kernels  4.58 us (15%)
  matrix products  1.55 us (5%)
  local copies, waits for them, and re-layouts  1.16 us (4%)
  other arithmetic  0.87 us (3%)
  between operations  0.81 us (3%)
    ppermute x4, starting transfers between devices, gather_by_core(): blocks.append(lax.ppermute(x, ('dp', 'layer', 'sub'), pairs))  6.66 us
    ppermute x2, starting transfers between devices, sum_over_dp(): got = lax.ppermute(sent, ('dp', 'sub'), pairs)  6.6 us
    pallas_call x2, Pallas kernels, decode(): pl.pallas_call(decode_kernel, out_shape=jax.ShapeDtypeStruct((subs * widt...  3.47 us
    ppermute x1, starting transfers between devices, per_device(): near_moved = lax.ppermute(ids, 'layer', partners(2, 1))  1.56 us
    ppermute x4, waiting for transfers between devices, gather_by_core(): blocks.append(lax.ppermute(x, ('dp', 'layer', 'sub'), pairs))  1.49 us
    ppermute x2, waiting for transfers between devices, sum_over_dp(): got = lax.ppermute(sent, ('dp', 'sub'), pairs)  1.12 us
    dynamic_slice x1, local copies, waits for them, and re-layouts, per_device(): lax.dynamic_slice_in_dim(jnp.transpose(proj_out), lax.axis_index('dp') *...  1.06 us
    ppermute x1, waiting for transfers between devices, per_device(): total = total + lax.ppermute(total, 'sub', partners(2, 1))  1 us
  transfers between devices with their start and end apart: 11, of which 8 were waited for; matrix products, arithmetic and copies ran while one was open for 4% of the time, Pallas kernels for 12%

profile of v13, /device:TPU:0, one launch (start us, length us, event | category | flops | bytes accessed | tf_op | source)
XLA Modules:
  0.0 29.6 jit_solution(6455510504366629310)
XLA Ops:
  0.0 0.0 copy-start
  0.0 0.0 copy-start.2
  0.0 1.1 %dynamic-slice_bitcast_fusion = bf16[64,1024]{1,0:T(8,128)(2,1)S(1)} fusion(bf16[4096,64]{0,1:T(8,128)(2,1)} %param.12, s32[]{:T(128)S(6)} %select_n.7), kind=kLoop, calls=%fused_computation.16 | loop fusion | bytes 262148 | tf_op jit(solution)/shard_map/dynamic_slice | solution.py:278
  1.1 0.5 %collective-permute-start.3 = (bf16[256,256,8]{1,2,0:T(8,128)(2,1)}, bf16[256,256,8]{1,2,0:T(8,128)(2,1)S(1)}, u32[]{:S(2)}, u32[]{:S(2)}) collective-permute-start(bf16[256,256,8]{1,2,0:T(8,128)(2,1)} %param.13), channel_id=1, source_target_pairs={{0,1},{1,0},{2,3},{3,2},{4,5},{5,4},{6,7},{7,6},{8,9},{9,8},{10,11... | collective-permute-start | bytes 3145736 | tf_op jit(solution)/shard_map/ppermute | solution.py:294
  1.6 0.1 copy-done
  1.7 0.5 %multiply_convert_fusion.1 = (f16[64,1024]{1,0:T(8,128)(2,1)S(1)}, f32[64,1024]{1,0:T(8,128)S(1)}) fusion(bf16[64,1024]{1,0:T(8,128)(2,1)S(1)} %dynamic-slice_bitcast_fusion, bf16[1,1024,1024]{2,1,0:T(8,128)(2,1)S(1)} %copy-done), kind=kOutput, calls=%fused_computation.15 | convolution fusion | flops 134348800 | bytes 2621440 | tf_op jit(solution)/shard_map/dot_general | solution.py:283
  2.1 0.0 copy-start.4
  2.2 4.1 %collective-permute-start = (f16[64,1024]{1,0:T(8,128)(2,1)S(1)}, f16[64,1024]{1,0:T(8,128)(2,1)S(1)}, u32[]{:S(2)}, u32[]{:S(2)}) collective-permute-start(f16[64,1024]{1,0:T(8,128)(2,1)S(1)} %get-tuple-element.45), channel_id=1, source_target_pairs={{0,8},{1,5},{4,12},{5,1},{8,0},{9,13},{12,4},{13,9},{2,10},{3,7},{... | collective-permute-start | bytes 393224 | tf_op jit(solution)/shard_map/ppermute | solution.py:224
  6.9 0.0 copy-done.2
  6.9 0.2 ids.1.refs_0_
  7.1 0.1 collective-permute-start.2
  7.2 1.6 %collective-permute-start.4 = (bf16[256,256]{1,0:T(8,128)(2,1)S(1)}, bf16[256,256]{1,0:T(8,128)(2,1)S(1)}, u32[]{:S(2)}, u32[]{:S(2)}) collective-permute-start(bf16[256,256]{1,0:T(8,128)(2,1)S(1)} %ids.1.refs_0_), channel_id=1, source_target_pairs={{0,2},{2,0},{1,3},{3,1},{4,6},{6,4},{5,7},{7,5},{8,10},{10,8},{9,1... | collective-permute-start | bytes 393224 | tf_op jit(solution)/shard_map/ppermute | solution.py:292
  8.8 0.5 %collective-permute-done = f16[64,1024]{1,0:T(8,128)(2,1)S(1)} collective-permute-done((f16[64,1024]{1,0:T(8,128)(2,1)S(1)}, f16[64,1024]{1,0:T(8,128)(2,1)S(1)}, u32[]{:S(2)}, u32[]{:S(2)}) %collective-permute-start) | collective-permute-done | bytes 131104 | tf_op jit(solution)/shard_map/ppermute | solution.py:224
  9.2 0.1 multiply_convert_fusion
  9.3 0.0 copy-start.3
  9.3 0.0 copy-start.5
  9.3 2.5 %collective-permute-start.1 = (f16[64,1024]{1,0:T(8,128)(2,1)S(1)}, f16[64,1024]{1,0:T(8,128)(2,1)S(1)}, u32[]{:S(2)}, u32[]{:S(2)}) collective-permute-start(f16[64,1024]{1,0:T(8,128)(2,1)S(1)} %multiply_convert_fusion), channel_id=1, source_target_pairs={{0,4},{1,9},{4,0},{5,13},{8,12},{9,1},{12,8},{13,5},{2,6},{3,11},{... | collective-permute-start | bytes 393224 | tf_op jit(solution)/shard_map/ppermute | solution.py:224
  11.8 0.0 collective-permute-done.2.refs_0_
  11.8 0.0 collective-permute-done.3
  11.8 1.7 %decode.2.refs_6_ = bf16[2048,256]{1,0:T(8,128)(2,1)S(1)} custom-call(bf16[256,256]{1,0:T(8,128)(2,1)S(1)} %collective-permute-done.2.refs_0_, bf16[256,8,256]{2,1,0:T(8,128)(2,1)S(1)} %bitcast.22), custom_call_target="tpu_custom_call" | custom-call | bytes 2097152 | tf_op jit(solution)/shard_map/decode/pallas_call | solution.py:78
  13.5 0.9 %collective-permute-done.4.refs_1_ = bf16[256,256]{1,0:T(8,128)(2,1)S(1)} collective-permute-done((bf16[256,256]{1,0:T(8,128)(2,1)S(1)}, bf16[256,256]{1,0:T(8,128)(2,1)S(1)}, u32[]{:S(2)}, u32[]{:S(2)}) %collective-permute-start.4) | collective-permute-done | bytes 131104 | tf_op jit(solution)/shard_map/ppermute | solution.py:292
  14.4 0.7 %collective-permute-done.1 = f16[64,1024]{1,0:T(8,128)(2,1)S(1)} collective-permute-done((f16[64,1024]{1,0:T(8,128)(2,1)S(1)}, f16[64,1024]{1,0:T(8,128)(2,1)S(1)}, u32[]{:S(2)}, u32[]{:S(2)}) %collective-permute-start.1) | collective-permute-done | bytes 131104 | tf_op jit(solution)/shard_map/ppermute | solution.py:224
  15.1 0.1 reduce-precision_convert_fusion
  15.2 0.0 copy-start.1
  15.2 0.0 copy-done.4
  15.2 0.3 %fusion.4 = f32[128,256]{1,0:T(8,128)S(1)} fusion(bf16[1,256,1024]{2,1,0:T(8,128)(2,1)S(1)} %copy-done.4, bf16[64,1024]{1,0:T(8,128)(2,1)S(1)} %get-tuple-element.44, bf16[64,1024]{1,0:T(8,128)(2,1)S(1)} %get-tuple-element.43), kind=kOutput, calls=%fused_computation.4 | convolution fusion | flops 67633152 | bytes 917504 | tf_op jit(solution)/shard_map/dot_general | solution.py:307
  15.5 0.2 collective-permute-start.5
  15.7 0.0 copy-done.3
  15.7 0.0 copy-done.5
  15.7 0.8 %fusion.in_ref = f32[64,256]{1,0:T(8,128)S(1)} fusion(bf16[4096,64]{0,1:T(8,128)(2,1)S(1)} %copy-done.5, bf16[1,256,4096]{2,1,0:T(8,128)(2,1)S(1)} %copy-done.3), kind=kOutput, calls=%fused_computation | convolution fusion | flops 134217728 | bytes 2686976 | tf_op jit(solution)/shard_map/dot_general | solution.py:297
  16.5 0.4 %collective-permute-done.5.other_ref = f32[64,256]{1,0:T(8,128)S(1)} collective-permute-done((f32[64,256]{1,0:T(8,128)S(1)}, f32[64,256]{1,0:T(8,128)S(1)}, u32[]{:S(2)}, u32[]{:S(2)}) %collective-permute-start.5) | collective-permute-done | bytes 65568 | tf_op jit(solution)/shard_map/ppermute | solution.py:315
  16.9 0.5 %vectors.1.refs_0_ = f32[2,4,2048]{2,1,0:T(4,128)S(1)} custom-call(f32[64,256]{1,0:T(8,128)S(1)} %fusion.in_ref, f32[64,256]{1,0:T(8,128)S(1)} %slice_add_fusion.own_ref, f32[64,256]{1,0:T(8,128)S(1)} %collective-permute-done.5.other_ref), custom_call_target="tpu_custom_call" | custom-call | tf_op jit(solution)/shard_map/vectors/pallas_call | solution.py:184
  17.4 4.5 %collective-permute-start.9 = (f16[2,4,2048]{2,1,0:T(4,128)(2,1)S(1)}, f16[2,4,2048]{2,1,0:T(4,128)(2,1)S(1)}, u32[]{:S(2)}, u32[]{:S(2)}) collective-permute-start(f16[2,4,2048]{2,1,0:T(4,128)(2,1)S(1)} %multiply_convert_fusion.2), channel_id=1, source_target_pairs={{0,12},{1,15},{2,14},{3,13},{4,8},{5,11},{6,10},{7,9},{8,4},{9,7},... | collective-permute-start | bytes 98312 | tf_op jit(solution)/shard_map/ppermute | solution.py:265
  21.9 0.0 collective-permute-start.6
  21.9 0.6 %collective-permute-start.7 = (f16[2,4,2048]{2,1,0:T(4,128)(2,1)S(1)}, f16[2,4,2048]{2,1,0:T(4,128)(2,1)S(1)}, u32[]{:S(2)}, u32[]{:S(2)}) collective-permute-start(f16[2,4,2048]{2,1,0:T(4,128)(2,1)S(1)} %multiply_convert_fusion.2), channel_id=1, source_target_pairs={{0,4},{1,7},{2,6},{3,5},{4,0},{5,3},{6,2},{7,1},{8,12},{9,15},{10,... | collective-permute-start | bytes 98312 | tf_op jit(solution)/shard_map/ppermute | solution.py:265
  22.5 1.5 %collective-permute-start.8 = (f16[2,4,2048]{2,1,0:T(4,128)(2,1)S(1)}, f16[2,4,2048]{2,1,0:T(4,128)(2,1)S(1)}, u32[]{:S(2)}, u32[]{:S(2)}) collective-permute-start(f16[2,4,2048]{2,1,0:T(4,128)(2,1)S(1)} %multiply_convert_fusion.2), channel_id=1, source_target_pairs={{0,2},{1,3},{2,0},{3,1},{4,6},{5,7},{6,4},{7,5},{8,10},{9,11},{10,... | collective-permute-start | bytes 98312 | tf_op jit(solution)/shard_map/ppermute | solution.py:265
  24.0 0.1 collective-permute-done.9
  24.1 0.0 copy-done.1
  24.1 1.7 %decode.3.refs_5_ = bf16[2048,256]{1,0:T(8,128)(2,1)S(1)} custom-call(bf16[256,256]{1,0:T(8,128)(2,1)S(1)} %ids.1.refs_0_, bf16[256,256]{1,0:T(8,128)(2,1)S(1)} %collective-permute-done.4.refs_1_, bf16[256,8,256]{2,1,0:T(8,128)(2,1)S(1)} %bitcast.21), custom_call_target="tpu_custom_call" | custom-call | bytes 2097152 | tf_op jit(solution)/shard_map/decode/pallas_call | solution.py:78
  25.8 1.0 %collective-permute-done.6 = f16[2,4,2048]{2,1,0:T(4,128)(2,1)S(1)} collective-permute-done((f16[2,4,2048]{2,1,0:T(4,128)(2,1)S(1)}, f16[2,4,2048]{2,1,0:T(4,128)(2,1)S(1)}, u32[]{:S(2)}, u32[]{:S(2)}) %collective-permute-start.6) | collective-permute-done | bytes 32800 | tf_op jit(solution)/shard_map/ppermute | solution.py:265
  26.9 0.0 collective-permute-done.7
  26.9 0.4 %collective-permute-done.8 = f16[2,4,2048]{2,1,0:T(4,128)(2,1)S(1)} collective-permute-done((f16[2,4,2048]{2,1,0:T(4,128)(2,1)S(1)}, f16[2,4,2048]{2,1,0:T(4,128)(2,1)S(1)}, u32[]{:S(2)}, u32[]{:S(2)}) %collective-permute-start.8) | collective-permute-done | bytes 32800 | tf_op jit(solution)/shard_map/ppermute | solution.py:265
  27.3 0.5 %score.1 = f32[16,256]{1,0:T(8,128)S(1)} custom-call(f32[2,4,2048]{2,1,0:T(4,128)S(1)} %vectors.1.refs_0_, f32[2,4,2048]{2,1,0:T(4,128)S(1)} %get-tuple-element.50.refs_1_, f32[2,4,2048]{2,1,0:T(4,128)S(1)} %get-tuple-element.49.refs_2_, f32[2,4,2048]{2,1,0:T(4,128)S(1)} %get-tuple-element.48.refs_3_, f32[2,4,2048]{2,1,0:T(4,128)S(1)} %get-tuple-element.47.refs_4_, ...), custom_call_target="tpu_custom_call" | custom-call | tf_op jit(solution)/shard_map/score/pallas_call | solution.py:163
  27.8 0.2 collective-permute-start.10
  28.0 1.0 %collective-permute-done.10 = f32[16,256]{1,0:T(8,128)S(1)} collective-permute-done((f32[16,256]{1,0:T(8,128)S(1)}, f32[16,256]{1,0:T(8,128)S(1)}, u32[]{:S(2)}, u32[]{:S(2)}) %collective-permute-start.10) | collective-permute-done | bytes 16416 | tf_op jit(solution)/shard_map/ppermute | solution.py:328
  29.0 0.6 %select_bitcast_fusion = f32[256,16]{0,1:T(8,128)} fusion(f32[16,256]{1,0:T(8,128)S(1)} %score.1, f32[16,256]{1,0:T(8,128)S(1)} %collective-permute-done.10, pred[256]{0:T(512)(128)(4,1)S(1)} %compare_reduce_fusion), kind=kLoop, calls=%fused_computation.23 | loop fusion | flops 8192 | bytes 49408 | tf_op jit(solution)/shard_map/transpose | solution.py:333
  (7 shorter events, 0.1 us)
Async XLA Ops:
  0.0 1.7 %copy-start = (bf16[1,1024,1024]{2,1,0:T(8,128)(2,1)S(1)}, bf16[1,1024,1024]{2,1,0:T(8,128)(2,1)}, u32[]{:S(2)}) copy-start(bf16[1,1024,1024]{2,1,0:T(8,128)(2,1)} %param.10) | copy-start | bytes 6291460
  0.0 6.9 %copy-start.2 = (s32[256,1,256]{2,1,0:T(1,128)S(1)}, s32[256,1,256]{2,1,0:T(1,128)}, u32[]{:S(2)}) copy-start(s32[256,1,256]{2,1,0:T(1,128)} %codes_ref) | copy-start | bytes 786436
  1.1 10.7 %collective-permute-start.3 = (bf16[256,256,8]{1,2,0:T(8,128)(2,1)}, bf16[256,256,8]{1,2,0:T(8,128)(2,1)S(1)}, u32[]{:S(2)}, u32[]{:S(2)}) collective-permute-start(bf16[256,256,8]{1,2,0:T(8,128)(2,1)} %param.13), channel_id=1, source_target_pairs={{0,1},{1,0},{2,3},{3,2},{4,5},{5,4},{6,7},{7,6},{8,9},{9,8},{10,11... | collective-permute-start | bytes 3145736 | tf_op jit(solution)/shard_map/ppermute | solution.py:294
  2.1 13.0 %copy-start.4 = (bf16[1,256,1024]{2,1,0:T(8,128)(2,1)S(1)}, bf16[1,256,1024]{2,1,0:T(8,128)(2,1)}, u32[]{:S(2)}) copy-start(bf16[1,256,1024]{2,1,0:T(8,128)(2,1)} %param.9) | copy-start | bytes 1572868
  2.2 7.1 %collective-permute-start = (f16[64,1024]{1,0:T(8,128)(2,1)S(1)}, f16[64,1024]{1,0:T(8,128)(2,1)S(1)}, u32[]{:S(2)}, u32[]{:S(2)}) collective-permute-start(f16[64,1024]{1,0:T(8,128)(2,1)S(1)} %get-tuple-element.45), channel_id=1, source_target_pairs={{0,8},{1,5},{4,12},{5,1},{8,0},{9,13},{12,4},{13,9},{2,10},{3,7},{... | collective-permute-start | bytes 393224 | tf_op jit(solution)/shard_map/ppermute | solution.py:224
  7.1 4.7 %collective-permute-start.2 = (bf16[256,256]{1,0:T(8,128)(2,1)S(1)}, bf16[256,256]{1,0:T(8,128)(2,1)S(1)}, u32[]{:S(2)}, u32[]{:S(2)}) collective-permute-start(bf16[256,256]{1,0:T(8,128)(2,1)S(1)} %ids.1.refs_0_), channel_id=1, source_target_pairs={{1,0},{3,2},{2,1},{0,3},{5,4},{7,6},{6,5},{4,7},{9,8},{11,10},{10,... | collective-permute-start | bytes 393224 | tf_op jit(solution)/shard_map/ppermute | solution.py:293
  7.2 7.2 %collective-permute-start.4 = (bf16[256,256]{1,0:T(8,128)(2,1)S(1)}, bf16[256,256]{1,0:T(8,128)(2,1)S(1)}, u32[]{:S(2)}, u32[]{:S(2)}) collective-permute-start(bf16[256,256]{1,0:T(8,128)(2,1)S(1)} %ids.1.refs_0_), channel_id=1, source_target_pairs={{0,2},{2,0},{1,3},{3,1},{4,6},{6,4},{5,7},{7,5},{8,10},{10,8},{9,1... | collective-permute-start | bytes 393224 | tf_op jit(solution)/shard_map/ppermute | solution.py:292
  9.3 6.4 %copy-start.3 = (bf16[1,256,4096]{2,1,0:T(8,128)(2,1)S(1)}, bf16[1,256,4096]{2,1,0:T(8,128)(2,1)}, u32[]{:S(2)}) copy-start(bf16[1,256,4096]{2,1,0:T(8,128)(2,1)} %param.8) | copy-start | bytes 6291460
  9.3 6.4 %copy-start.5 = (bf16[4096,64]{0,1:T(8,128)(2,1)S(1)}, bf16[4096,64]{0,1:T(8,128)(2,1)}, u32[]{:S(2)}) copy-start(bf16[4096,64]{0,1:T(8,128)(2,1)} %param.11) | copy-start | bytes 1572868
  9.3 5.8 %collective-permute-start.1 = (f16[64,1024]{1,0:T(8,128)(2,1)S(1)}, f16[64,1024]{1,0:T(8,128)(2,1)S(1)}, u32[]{:S(2)}, u32[]{:S(2)}) collective-permute-start(f16[64,1024]{1,0:T(8,128)(2,1)S(1)} %multiply_convert_fusion), channel_id=1, source_target_pairs={{0,4},{1,9},{4,0},{5,13},{8,12},{9,1},{12,8},{13,5},{2,6},{3,11},{... | collective-permute-start | bytes 393224 | tf_op jit(solution)/shard_map/ppermute | solution.py:224
  15.2 8.9 %copy-start.1 = (bf16[256,256,8]{1,2,0:T(8,128)(2,1)S(1)}, bf16[256,256,8]{1,2,0:T(8,128)(2,1)}, u32[]{:S(2)}) copy-start(bf16[256,256,8]{1,2,0:T(8,128)(2,1)} %param.13) | copy-start | bytes 3145732
  15.5 1.3 %collective-permute-start.5 = (f32[64,256]{1,0:T(8,128)S(1)}, f32[64,256]{1,0:T(8,128)S(1)}, u32[]{:S(2)}, u32[]{:S(2)}) collective-permute-start(f32[64,256]{1,0:T(8,128)S(1)} %slice_add_fusion.own_ref), channel_id=1, source_target_pairs={{0,1},{1,0},{2,3},{3,2},{4,5},{5,4},{6,7},{7,6},{8,9},{9,8},{10,11... | collective-permute-start | bytes 196616 | tf_op jit(solution)/shard_map/ppermute | solution.py:315
  17.4 6.7 %collective-permute-start.9 = (f16[2,4,2048]{2,1,0:T(4,128)(2,1)S(1)}, f16[2,4,2048]{2,1,0:T(4,128)(2,1)S(1)}, u32[]{:S(2)}, u32[]{:S(2)}) collective-permute-start(f16[2,4,2048]{2,1,0:T(4,128)(2,1)S(1)} %multiply_convert_fusion.2), channel_id=1, source_target_pairs={{0,12},{1,15},{2,14},{3,13},{4,8},{5,11},{6,10},{7,9},{8,4},{9,7},... | collective-permute-start | bytes 98312 | tf_op jit(solution)/shard_map/ppermute | solution.py:265
  21.9 5.0 %collective-permute-start.6 = (f16[2,4,2048]{2,1,0:T(4,128)(2,1)S(1)}, f16[2,4,2048]{2,1,0:T(4,128)(2,1)S(1)}, u32[]{:S(2)}, u32[]{:S(2)}) collective-permute-start(f16[2,4,2048]{2,1,0:T(4,128)(2,1)S(1)} %multiply_convert_fusion.2), channel_id=1, source_target_pairs={{0,8},{1,11},{2,10},{3,9},{4,12},{5,15},{6,14},{7,13},{8,0},{9,3},... | collective-permute-start | bytes 98312 | tf_op jit(solution)/shard_map/ppermute | solution.py:265
  21.9 5.0 %collective-permute-start.7 = (f16[2,4,2048]{2,1,0:T(4,128)(2,1)S(1)}, f16[2,4,2048]{2,1,0:T(4,128)(2,1)S(1)}, u32[]{:S(2)}, u32[]{:S(2)}) collective-permute-start(f16[2,4,2048]{2,1,0:T(4,128)(2,1)S(1)} %multiply_convert_fusion.2), channel_id=1, source_target_pairs={{0,4},{1,7},{2,6},{3,5},{4,0},{5,3},{6,2},{7,1},{8,12},{9,15},{10,... | collective-permute-start | bytes 98312 | tf_op jit(solution)/shard_map/ppermute | solution.py:265
  22.5 4.7 %collective-permute-start.8 = (f16[2,4,2048]{2,1,0:T(4,128)(2,1)S(1)}, f16[2,4,2048]{2,1,0:T(4,128)(2,1)S(1)}, u32[]{:S(2)}, u32[]{:S(2)}) collective-permute-start(f16[2,4,2048]{2,1,0:T(4,128)(2,1)S(1)} %multiply_convert_fusion.2), channel_id=1, source_target_pairs={{0,2},{1,3},{2,0},{3,1},{4,6},{5,7},{6,4},{7,5},{8,10},{9,11},{10,... | collective-permute-start | bytes 98312 | tf_op jit(solution)/shard_map/ppermute | solution.py:265
  27.8 1.2 %collective-permute-start.10 = (f32[16,256]{1,0:T(8,128)S(1)}, f32[16,256]{1,0:T(8,128)S(1)}, u32[]{:S(2)}, u32[]{:S(2)}) collective-permute-start(f32[16,256]{1,0:T(8,128)S(1)} %score.1), channel_id=1, source_target_pairs={{0,1},{1,0},{2,3},{3,2},{4,5},{5,4},{6,7},{7,6},{8,9},{9,8},{10,11... | collective-permute-start | bytes 49160 | tf_op jit(solution)/shard_map/ppermute | solution.py:328

commit v14 on v11

--- a/solution.py
+++ b/solution.py
@@ -279,7 +279,6 @@
             jnp.transpose(proj_out), lax.axis_index("dp") * rows_local, rows_local, 1
         )
     )
-    own_rows, moved_book = lax.optimization_barrier((own_rows, codebook))
     folded = jnp.dot(own_rows, kv_weight[0], preferred_element_type=jnp.float32)
     book_t = jnp.transpose(codebook, (0, 2, 1))
     by_core = has_two_by_two() and lax.axis_size("dp") == 4
@@ -289,6 +288,7 @@
     live, moved_codes = lax.optimization_barrier((live, codes))
     ids = make_ids(moved_codes)
     if by_core:
+        sent, moved_book = lax.optimization_barrier((sent, codebook))
         near_ids = lax.ppermute(ids, "layer", partners(2, 1))
         far_ids = lax.ppermute(ids, ("layer", "sub"), FAR_CODES)
         other_book = lax.ppermute(moved_book, "sub", partners(2, 1))

time: 29.9 us -> 29.6 us (0.990)
  waiting for transfers between devices: 6.28 us -> 4.47 us
  starting transfers between devices: 14.5 us -> 15.5 us
  local copies, waits for them, and re-layouts: 1.16 us -> 1.67 us
    ppermute x4, waiting for transfers between devices: 3.39 us -> 2.15 us  [gather_by_core(): blocks.append(lax.ppermute(x, ('dp', 'layer', 'sub'), pairs))]
    ppermute x4, starting transfers between devices: 5.53 us -> 6.24 us  [gather_by_core(): blocks.append(lax.ppermute(x, ('dp', 'layer', 'sub'), pairs))]
    ppermute x1, starting transfers between devices: 0.01 us -> 0.56 us  [per_device(): total = total + lax.ppermute(total, 'sub', partners(2, 1))]
    unnamed x12, local copies, waits for them, and re-layouts: 0.09 us -> 0.61 us
    ppermute x1, waiting for transfers between devices: 0.89 us -> 0.46 us  [per_device(): near_ids = lax.ppermute(ids, 'layer', partners(2, 1))]
    ppermute x1, waiting for transfers between devices: 1.16 us -> 0.82 us  [per_device(): total = total + lax.ppermute(total, 'sub', partners(2, 1))]
  transfers between devices with their start and end apart: 11 -> 11, of which waited for: 7 -> 5; matrix products, arithmetic and copies ran while one was open for 5% -> 3% of each run, Pallas kernels for 12% -> 12%
where the time goes in v14:
time: 29.6 us; the launch traced here: 29.5 us
  starting transfers between devices  15.5 us (52%)
  Pallas kernels  4.57 us (15%)
  waiting for transfers between devices  4.47 us (15%)
  local copies, waits for them, and re-layouts  1.67 us (6%)
  matrix products  1.55 us (5%)
  other arithmetic  0.87 us (3%)
  between operations  0.81 us (3%)
    ppermute x2, starting transfers between devices, sum_over_dp(): got = lax.ppermute(sent, ('dp', 'sub'), pairs)  6.38 us
    ppermute x4, starting transfers between devices, gather_by_core(): blocks.append(lax.ppermute(x, ('dp', 'layer', 'sub'), pairs))  6.24 us
    pallas_call x2, Pallas kernels, decode(): pl.pallas_call(decode_kernel, out_shape=jax.ShapeDtypeStruct((subs * widt...  3.47 us
    ppermute x4, waiting for transfers between devices, gather_by_core(): blocks.append(lax.ppermute(x, ('dp', 'layer', 'sub'), pairs))  2.15 us
    ppermute x1, starting transfers between devices, per_device(): near_ids = lax.ppermute(ids, 'layer', partners(2, 1))  1.33 us
    dynamic_slice x1, local copies, waits for them, and re-layouts, per_device(): lax.dynamic_slice_in_dim(jnp.transpose(proj_out), lax.axis_index('dp') *...  1.06 us
    ppermute x1, waiting for transfers between devices, per_device(): total = total + lax.ppermute(total, 'sub', partners(2, 1))  0.82 us
    dot_general x1, matrix products, first_side(): lax.dot_general(proj_in, acts[0], (((0,), (1,)), ((), ())), preferred_ele...  0.76 us
  transfers between devices with their start and end apart: 11, of which 5 were waited for; matrix products, arithmetic and copies ran while one was open for 3% of the time, Pallas kernels for 12%

profile of v14, /device:TPU:0, one launch (start us, length us, event | category | flops | bytes accessed | tf_op | source)
XLA Modules:
  0.0 29.5 jit_solution(16329491896481246390)
XLA Ops:
  0.0 0.0 copy-start
  0.0 0.0 copy-start.1
  0.0 0.0 copy-start.2
  0.0 1.1 %dynamic-slice_bitcast_fusion = bf16[64,1024]{1,0:T(8,128)(2,1)S(1)} fusion(bf16[4096,64]{0,1:T(8,128)(2,1)} %param.12, s32[]{:T(128)S(6)} %select_n.7), kind=kLoop, calls=%fused_computation.16 | loop fusion | bytes 262148 | tf_op jit(solution)/shard_map/dynamic_slice | solution.py:278
  1.1 0.6 %copy-done = bf16[1,1024,1024]{2,1,0:T(8,128)(2,1)S(1)} copy-done((bf16[1,1024,1024]{2,1,0:T(8,128)(2,1)S(1)}, bf16[1,1024,1024]{2,1,0:T(8,128)(2,1)}, u32[]{:S(2)}) %copy-start) | copy-done | bytes 2097176
  1.7 0.5 %multiply_convert_fusion.1 = (f16[64,1024]{1,0:T(8,128)(2,1)S(1)}, f32[64,1024]{1,0:T(8,128)S(1)}) fusion(bf16[64,1024]{1,0:T(8,128)(2,1)S(1)} %dynamic-slice_bitcast_fusion, bf16[1,1024,1024]{2,1,0:T(8,128)(2,1)S(1)} %copy-done), kind=kOutput, calls=%fused_computation.15 | convolution fusion | flops 134348800 | bytes 2621440 | tf_op jit(solution)/shard_map/dot_general | solution.py:282
  2.1 0.0 copy-done.1
  2.2 0.5 %collective-permute-start.3 = (bf16[256,256,8]{1,2,0:T(8,128)(2,1)S(1)}, bf16[256,256,8]{1,2,0:T(8,128)(2,1)S(1)}, u32[]{:S(2)}, u32[]{:S(2)}) collective-permute-start(bf16[256,256,8]{1,2,0:T(8,128)(2,1)S(1)} %copy-done.1), channel_id=1, source_target_pairs={{0,1},{1,0},{2,3},{3,2},{4,5},{5,4},{6,7},{7,6},{8,9},{9,8},{10,11... | collective-permute-start | bytes 3145736 | tf_op jit(solution)/shard_map/ppermute | solution.py:294
  2.7 3.7 %collective-permute-start = (f16[64,1024]{1,0:T(8,128)(2,1)S(1)}, f16[64,1024]{1,0:T(8,128)(2,1)S(1)}, u32[]{:S(2)}, u32[]{:S(2)}) collective-permute-start(f16[64,1024]{1,0:T(8,128)(2,1)S(1)} %get-tuple-element.18), channel_id=1, source_target_pairs={{0,8},{1,5},{4,12},{5,1},{8,0},{9,13},{12,4},{13,9},{2,10},{3,7},{... | collective-permute-start | bytes 393224 | tf_op jit(solution)/shard_map/ppermute | solution.py:224
  7.0 0.0 copy-done.2
  7.0 0.2 ids.1.refs_0_
  7.2 0.3 collective-permute-start.2
  7.5 1.3 %collective-permute-start.4 = (bf16[256,256]{1,0:T(8,128)(2,1)S(1)}, bf16[256,256]{1,0:T(8,128)(2,1)S(1)}, u32[]{:S(2)}, u32[]{:S(2)}) collective-permute-start(bf16[256,256]{1,0:T(8,128)(2,1)S(1)} %ids.1.refs_0_), channel_id=1, source_target_pairs={{0,2},{2,0},{1,3},{3,1},{4,6},{6,4},{5,7},{7,5},{8,10},{10,8},{9,1... | collective-permute-start | bytes 393224 | tf_op jit(solution)/shard_map/ppermute | solution.py:292
  8.8 0.7 %collective-permute-done = f16[64,1024]{1,0:T(8,128)(2,1)S(1)} collective-permute-done((f16[64,1024]{1,0:T(8,128)(2,1)S(1)}, f16[64,1024]{1,0:T(8,128)(2,1)S(1)}, u32[]{:S(2)}, u32[]{:S(2)}) %collective-permute-start) | collective-permute-done | bytes 131104 | tf_op jit(solution)/shard_map/ppermute | solution.py:224
  9.5 0.1 multiply_convert_fusion
  9.6 2.7 %collective-permute-start.1 = (f16[64,1024]{1,0:T(8,128)(2,1)S(1)}, f16[64,1024]{1,0:T(8,128)(2,1)S(1)}, u32[]{:S(2)}, u32[]{:S(2)}) collective-permute-start(f16[64,1024]{1,0:T(8,128)(2,1)S(1)} %multiply_convert_fusion), channel_id=1, source_target_pairs={{0,4},{1,9},{4,0},{5,13},{8,12},{9,1},{12,8},{13,5},{2,6},{3,11},{... | collective-permute-start | bytes 393224 | tf_op jit(solution)/shard_map/ppermute | solution.py:224
  12.3 0.0 collective-permute-done.2.refs_0_
  12.3 0.0 collective-permute-done.3
  12.3 1.7 %decode.2.refs_6_ = bf16[2048,256]{1,0:T(8,128)(2,1)S(1)} custom-call(bf16[256,256]{1,0:T(8,128)(2,1)S(1)} %collective-permute-done.2.refs_0_, bf16[256,8,256]{2,1,0:T(8,128)(2,1)S(1)} %bitcast.22), custom_call_target="tpu_custom_call" | custom-call | bytes 2097152 | tf_op jit(solution)/shard_map/decode/pallas_call | solution.py:78
  14.0 0.0 copy-start.4
  14.0 0.5 %collective-permute-done.4.refs_1_ = bf16[256,256]{1,0:T(8,128)(2,1)S(1)} collective-permute-done((bf16[256,256]{1,0:T(8,128)(2,1)S(1)}, bf16[256,256]{1,0:T(8,128)(2,1)S(1)}, u32[]{:S(2)}, u32[]{:S(2)}) %collective-permute-start.4) | collective-permute-done | bytes 131104 | tf_op jit(solution)/shard_map/ppermute | solution.py:292
  14.5 0.0 copy-start.3
  14.5 0.0 copy-start.5
  14.5 1.7 %decode.3.refs_5_ = bf16[2048,256]{1,0:T(8,128)(2,1)S(1)} custom-call(bf16[256,256]{1,0:T(8,128)(2,1)S(1)} %ids.1.refs_0_, bf16[256,256]{1,0:T(8,128)(2,1)S(1)} %collective-permute-done.4.refs_1_, bf16[256,8,256]{2,1,0:T(8,128)(2,1)S(1)} %bitcast.21), custom_call_target="tpu_custom_call" | custom-call | bytes 2097152 | tf_op jit(solution)/shard_map/decode/pallas_call | solution.py:78
  16.2 0.0 collective-permute-done.1
  16.3 0.1 reduce-precision_convert_fusion
  16.4 0.0 copy-done.4
  16.4 0.3 %fusion.4 = f32[128,256]{1,0:T(8,128)S(1)} fusion(bf16[1,256,1024]{2,1,0:T(8,128)(2,1)S(1)} %copy-done.4, bf16[64,1024]{1,0:T(8,128)(2,1)S(1)} %get-tuple-element.32, bf16[64,1024]{1,0:T(8,128)(2,1)S(1)} %get-tuple-element.31), kind=kOutput, calls=%fused_computation.4 | convolution fusion | flops 67633152 | bytes 917504 | tf_op jit(solution)/shard_map/dot_general | solution.py:309
  16.7 0.2 collective-permute-start.5
  16.9 0.0 copy-done.3
  16.9 0.0 copy-done.5
  16.9 0.8 %fusion.in_ref = f32[64,256]{1,0:T(8,128)S(1)} fusion(bf16[4096,64]{0,1:T(8,128)(2,1)S(1)} %copy-done.5, bf16[1,256,4096]{2,1,0:T(8,128)(2,1)S(1)} %copy-done.3), kind=kOutput, calls=%fused_computation | convolution fusion | flops 134217728 | bytes 2686976 | tf_op jit(solution)/shard_map/dot_general | solution.py:297
  17.7 0.4 %collective-permute-done.5.other_ref = f32[64,256]{1,0:T(8,128)S(1)} collective-permute-done((f32[64,256]{1,0:T(8,128)S(1)}, f32[64,256]{1,0:T(8,128)S(1)}, u32[]{:S(2)}, u32[]{:S(2)}) %collective-permute-start.5) | collective-permute-done | bytes 65568 | tf_op jit(solution)/shard_map/ppermute | solution.py:317
  18.0 0.5 %vectors.1.refs_0_ = f32[2,4,2048]{2,1,0:T(4,128)S(1)} custom-call(f32[64,256]{1,0:T(8,128)S(1)} %fusion.in_ref, f32[64,256]{1,0:T(8,128)S(1)} %slice_add_fusion.own_ref, f32[64,256]{1,0:T(8,128)S(1)} %collective-permute-done.5.other_ref), custom_call_target="tpu_custom_call" | custom-call | tf_op jit(solution)/shard_map/vectors/pallas_call | solution.py:184
  18.5 3.4 %collective-permute-start.9 = (f16[2,4,2048]{2,1,0:T(4,128)(2,1)S(1)}, f16[2,4,2048]{2,1,0:T(4,128)(2,1)S(1)}, u32[]{:S(2)}, u32[]{:S(2)}) collective-permute-start(f16[2,4,2048]{2,1,0:T(4,128)(2,1)S(1)} %multiply_convert_fusion.2), channel_id=1, source_target_pairs={{0,12},{1,15},{2,14},{3,13},{4,8},{5,11},{6,10},{7,9},{8,4},{9,7},... | collective-permute-start | bytes 98312 | tf_op jit(solution)/shard_map/ppermute | solution.py:265
  21.9 0.0 collective-permute-start.8
  21.9 1.0 %collective-permute-start.7 = (f16[2,4,2048]{2,1,0:T(4,128)(2,1)S(1)}, f16[2,4,2048]{2,1,0:T(4,128)(2,1)S(1)}, u32[]{:S(2)}, u32[]{:S(2)}) collective-permute-start(f16[2,4,2048]{2,1,0:T(4,128)(2,1)S(1)} %multiply_convert_fusion.2), channel_id=1, source_target_pairs={{0,4},{1,7},{2,6},{3,5},{4,0},{5,3},{6,2},{7,1},{8,12},{9,15},{10,... | collective-permute-start | bytes 98312 | tf_op jit(solution)/shard_map/ppermute | solution.py:265
  23.0 1.8 %collective-permute-start.6 = (f16[2,4,2048]{2,1,0:T(4,128)(2,1)S(1)}, f16[2,4,2048]{2,1,0:T(4,128)(2,1)S(1)}, u32[]{:S(2)}, u32[]{:S(2)}) collective-permute-start(f16[2,4,2048]{2,1,0:T(4,128)(2,1)S(1)} %multiply_convert_fusion.2), channel_id=1, source_target_pairs={{0,2},{1,3},{2,0},{3,1},{4,6},{5,7},{6,4},{7,5},{8,10},{9,11},{10,... | collective-permute-start | bytes 98312 | tf_op jit(solution)/shard_map/ppermute | solution.py:265
  24.8 0.0 collective-permute-done.9
  24.8 2.1 %collective-permute-done.8 = f16[2,4,2048]{2,1,0:T(4,128)(2,1)S(1)} collective-permute-done((f16[2,4,2048]{2,1,0:T(4,128)(2,1)S(1)}, f16[2,4,2048]{2,1,0:T(4,128)(2,1)S(1)}, u32[]{:S(2)}, u32[]{:S(2)}) %collective-permute-start.8) | collective-permute-done | bytes 32800 | tf_op jit(solution)/shard_map/ppermute | solution.py:265
  26.9 0.0 collective-permute-done.7
  26.9 0.0 collective-permute-done.6
  27.0 0.5 %score.1 = f32[16,256]{1,0:T(8,128)S(1)} custom-call(f32[2,4,2048]{2,1,0:T(4,128)S(1)} %vectors.1.refs_0_, f32[2,4,2048]{2,1,0:T(4,128)S(1)} %convert_multiply_fusion.3.refs_1_, f32[2,4,2048]{2,1,0:T(4,128)S(1)} %convert_multiply_fusion.2.refs_2_, f32[2,4,2048]{2,1,0:T(4,128)S(1)} %convert_multiply_fusion.1.refs_3_, ...), custom_call_target="tpu_custom_call" | custom-call | tf_op jit(solution)/shard_map/score/pallas_call | solution.py:163
  27.5 0.6 %collective-permute-start.10 = (f32[16,256]{1,0:T(8,128)S(1)}, f32[16,256]{1,0:T(8,128)S(1)}, u32[]{:S(2)}, u32[]{:S(2)}) collective-permute-start(f32[16,256]{1,0:T(8,128)S(1)} %score.1), channel_id=1, source_target_pairs={{0,1},{1,0},{2,3},{3,2},{4,5},{5,4},{6,7},{7,6},{8,9},{9,8},{10,11... | collective-permute-start | bytes 49160 | tf_op jit(solution)/shard_map/ppermute | solution.py:328
  28.0 0.8 %collective-permute-done.10 = f32[16,256]{1,0:T(8,128)S(1)} collective-permute-done((f32[16,256]{1,0:T(8,128)S(1)}, f32[16,256]{1,0:T(8,128)S(1)}, u32[]{:S(2)}, u32[]{:S(2)}) %collective-permute-start.10) | collective-permute-done | bytes 16416 | tf_op jit(solution)/shard_map/ppermute | solution.py:328
  28.9 0.6 %select_bitcast_fusion = f32[256,16]{0,1:T(8,128)} fusion(f32[16,256]{1,0:T(8,128)S(1)} %score.1, f32[16,256]{1,0:T(8,128)S(1)} %collective-permute-done.10, pred[256]{0:T(512)(128)(4,1)S(1)} %compare_reduce_fusion), kind=kLoop, calls=%fused_computation.23 | loop fusion | flops 8192 | bytes 49408 | tf_op jit(solution)/shard_map/transpose | solution.py:333
  (9 shorter events, 0.1 us)
Async XLA Ops:
  0.0 1.7 %copy-start = (bf16[1,1024,1024]{2,1,0:T(8,128)(2,1)S(1)}, bf16[1,1024,1024]{2,1,0:T(8,128)(2,1)}, u32[]{:S(2)}) copy-start(bf16[1,1024,1024]{2,1,0:T(8,128)(2,1)} %param.10) | copy-start | bytes 6291460
  0.0 2.1 %copy-start.1 = (bf16[256,256,8]{1,2,0:T(8,128)(2,1)S(1)}, bf16[256,256,8]{1,2,0:T(8,128)(2,1)}, u32[]{:S(2)}) copy-start(bf16[256,256,8]{1,2,0:T(8,128)(2,1)} %param.13) | copy-start | bytes 3145732
  0.0 7.0 %copy-start.2 = (s32[256,1,256]{2,1,0:T(1,128)S(1)}, s32[256,1,256]{2,1,0:T(1,128)}, u32[]{:S(2)}) copy-start(s32[256,1,256]{2,1,0:T(1,128)} %codes_ref) | copy-start | bytes 786436
  2.2 10.1 %collective-permute-start.3 = (bf16[256,256,8]{1,2,0:T(8,128)(2,1)S(1)}, bf16[256,256,8]{1,2,0:T(8,128)(2,1)S(1)}, u32[]{:S(2)}, u32[]{:S(2)}) collective-permute-start(bf16[256,256,8]{1,2,0:T(8,128)(2,1)S(1)} %copy-done.1), channel_id=1, source_target_pairs={{0,1},{1,0},{2,3},{3,2},{4,5},{5,4},{6,7},{7,6},{8,9},{9,8},{10,11... | collective-permute-start | bytes 3145736 | tf_op jit(solution)/shard_map/ppermute | solution.py:294
  2.7 6.8 %collective-permute-start = (f16[64,1024]{1,0:T(8,128)(2,1)S(1)}, f16[64,1024]{1,0:T(8,128)(2,1)S(1)}, u32[]{:S(2)}, u32[]{:S(2)}) collective-permute-start(f16[64,1024]{1,0:T(8,128)(2,1)S(1)} %get-tuple-element.18), channel_id=1, source_target_pairs={{0,8},{1,5},{4,12},{5,1},{8,0},{9,13},{12,4},{13,9},{2,10},{3,7},{... | collective-permute-start | bytes 393224 | tf_op jit(solution)/shard_map/ppermute | solution.py:224
  7.2 5.1 %collective-permute-start.2 = (bf16[256,256]{1,0:T(8,128)(2,1)S(1)}, bf16[256,256]{1,0:T(8,128)(2,1)S(1)}, u32[]{:S(2)}, u32[]{:S(2)}) collective-permute-start(bf16[256,256]{1,0:T(8,128)(2,1)S(1)} %ids.1.refs_0_), channel_id=1, source_target_pairs={{1,0},{3,2},{2,1},{0,3},{5,4},{7,6},{6,5},{4,7},{9,8},{11,10},{10,... | collective-permute-start | bytes 393224 | tf_op jit(solution)/shard_map/ppermute | solution.py:293
  7.5 7.0 %collective-permute-start.4 = (bf16[256,256]{1,0:T(8,128)(2,1)S(1)}, bf16[256,256]{1,0:T(8,128)(2,1)S(1)}, u32[]{:S(2)}, u32[]{:S(2)}) collective-permute-start(bf16[256,256]{1,0:T(8,128)(2,1)S(1)} %ids.1.refs_0_), channel_id=1, source_target_pairs={{0,2},{2,0},{1,3},{3,1},{4,6},{6,4},{5,7},{7,5},{8,10},{10,8},{9,1... | collective-permute-start | bytes 393224 | tf_op jit(solution)/shard_map/ppermute | solution.py:292
  9.6 6.7 %collective-permute-start.1 = (f16[64,1024]{1,0:T(8,128)(2,1)S(1)}, f16[64,1024]{1,0:T(8,128)(2,1)S(1)}, u32[]{:S(2)}, u32[]{:S(2)}) collective-permute-start(f16[64,1024]{1,0:T(8,128)(2,1)S(1)} %multiply_convert_fusion), channel_id=1, source_target_pairs={{0,4},{1,9},{4,0},{5,13},{8,12},{9,1},{12,8},{13,5},{2,6},{3,11},{... | collective-permute-start | bytes 393224 | tf_op jit(solution)/shard_map/ppermute | solution.py:224
  14.0 2.3 %copy-start.4 = (bf16[1,256,1024]{2,1,0:T(8,128)(2,1)S(1)}, bf16[1,256,1024]{2,1,0:T(8,128)(2,1)}, u32[]{:S(2)}) copy-start(bf16[1,256,1024]{2,1,0:T(8,128)(2,1)} %param.9) | copy-start | bytes 1572868
  14.5 2.4 %copy-start.3 = (bf16[1,256,4096]{2,1,0:T(8,128)(2,1)S(1)}, bf16[1,256,4096]{2,1,0:T(8,128)(2,1)}, u32[]{:S(2)}) copy-start(bf16[1,256,4096]{2,1,0:T(8,128)(2,1)} %param.8) | copy-start | bytes 6291460
  14.5 2.4 %copy-start.5 = (bf16[4096,64]{0,1:T(8,128)(2,1)S(1)}, bf16[4096,64]{0,1:T(8,128)(2,1)}, u32[]{:S(2)}) copy-start(bf16[4096,64]{0,1:T(8,128)(2,1)} %param.11) | copy-start | bytes 1572868
  16.7 1.3 %collective-permute-start.5 = (f32[64,256]{1,0:T(8,128)S(1)}, f32[64,256]{1,0:T(8,128)S(1)}, u32[]{:S(2)}, u32[]{:S(2)}) collective-permute-start(f32[64,256]{1,0:T(8,128)S(1)} %slice_add_fusion.own_ref), channel_id=1, source_target_pairs={{0,1},{1,0},{2,3},{3,2},{4,5},{5,4},{6,7},{7,6},{8,9},{9,8},{10,11... | collective-permute-start | bytes 196616 | tf_op jit(solution)/shard_map/ppermute | solution.py:317
  18.5 6.2 %collective-permute-start.9 = (f16[2,4,2048]{2,1,0:T(4,128)(2,1)S(1)}, f16[2,4,2048]{2,1,0:T(4,128)(2,1)S(1)}, u32[]{:S(2)}, u32[]{:S(2)}) collective-permute-start(f16[2,4,2048]{2,1,0:T(4,128)(2,1)S(1)} %multiply_convert_fusion.2), channel_id=1, source_target_pairs={{0,12},{1,15},{2,14},{3,13},{4,8},{5,11},{6,10},{7,9},{8,4},{9,7},... | collective-permute-start | bytes 98312 | tf_op jit(solution)/shard_map/ppermute | solution.py:265
  21.9 5.0 %collective-permute-start.8 = (f16[2,4,2048]{2,1,0:T(4,128)(2,1)S(1)}, f16[2,4,2048]{2,1,0:T(4,128)(2,1)S(1)}, u32[]{:S(2)}, u32[]{:S(2)}) collective-permute-start(f16[2,4,2048]{2,1,0:T(4,128)(2,1)S(1)} %multiply_convert_fusion.2), channel_id=1, source_target_pairs={{0,8},{1,11},{2,10},{3,9},{4,12},{5,15},{6,14},{7,13},{8,0},{9,3},... | collective-permute-start | bytes 98312 | tf_op jit(solution)/shard_map/ppermute | solution.py:265
  21.9 5.0 %collective-permute-start.7 = (f16[2,4,2048]{2,1,0:T(4,128)(2,1)S(1)}, f16[2,4,2048]{2,1,0:T(4,128)(2,1)S(1)}, u32[]{:S(2)}, u32[]{:S(2)}) collective-permute-start(f16[2,4,2048]{2,1,0:T(4,128)(2,1)S(1)} %multiply_convert_fusion.2), channel_id=1, source_target_pairs={{0,4},{1,7},{2,6},{3,5},{4,0},{5,3},{6,2},{7,1},{8,12},{9,15},{10,... | collective-permute-start | bytes 98312 | tf_op jit(solution)/shard_map/ppermute | solution.py:265
  23.0 4.0 %collective-permute-start.6 = (f16[2,4,2048]{2,1,0:T(4,128)(2,1)S(1)}, f16[2,4,2048]{2,1,0:T(4,128)(2,1)S(1)}, u32[]{:S(2)}, u32[]{:S(2)}) collective-permute-start(f16[2,4,2048]{2,1,0:T(4,128)(2,1)S(1)} %multiply_convert_fusion.2), channel_id=1, source_target_pairs={{0,2},{1,3},{2,0},{3,1},{4,6},{5,7},{6,4},{7,5},{8,10},{9,11},{10,... | collective-permute-start | bytes 98312 | tf_op jit(solution)/shard_map/ppermute | solution.py:265
  27.5 1.4 %collective-permute-start.10 = (f32[16,256]{1,0:T(8,128)S(1)}, f32[16,256]{1,0:T(8,128)S(1)}, u32[]{:S(2)}, u32[]{:S(2)}) collective-permute-start(f32[16,256]{1,0:T(8,128)S(1)} %score.1), channel_id=1, source_target_pairs={{0,1},{1,0},{2,3},{3,2},{4,5},{5,4},{6,7},{7,6},{8,9},{9,8},{10,11... | collective-permute-start | bytes 49160 | tf_op jit(solution)/shard_map/ppermute | solution.py:328

commit v15 on v14

--- a/solution.py
+++ b/solution.py
@@ -11,7 +11,7 @@
 LANES = 128
 LINK_SCALE = 1024.0
 VECTOR_SCALE = 16384.0
-GATHER_ORDER = (0, 1, 2, 3)
+GATHER_ORDER = (0, 2, 1, 3)
 
 
 def ids_kernel(codes_ref, out_ref):

time: 29.6 us -> 29.6 us (level)
  transfers between devices with their start and end apart: 11 -> 11, of which waited for: 5 -> 6; matrix products, arithmetic and copies ran while one was open for 3% -> 3% of each run, Pallas kernels for 12% -> 12%
where the time goes in v15:
time: 29.6 us; the launch traced here: 29.5 us
  starting transfers between devices  15.5 us (52%)
  Pallas kernels  4.57 us (15%)
  waiting for transfers between devices  4.48 us (15%)
  local copies, waits for them, and re-layouts  1.67 us (6%)
  matrix products  1.55 us (5%)
  other arithmetic  0.87 us (3%)
  between operations  0.8 us (3%)
    ppermute x2, starting transfers between devices, sum_over_dp(): got = lax.ppermute(sent, ('dp', 'sub'), pairs)  6.38 us
    ppermute x4, starting transfers between devices, gather_by_core(): blocks.append(lax.ppermute(x, ('dp', 'layer', 'sub'), pairs))  6.24 us
    pallas_call x2, Pallas kernels, decode(): pl.pallas_call(decode_kernel, out_shape=jax.ShapeDtypeStruct((subs * widt...  3.47 us
    ppermute x4, waiting for transfers between devices, gather_by_core(): blocks.append(lax.ppermute(x, ('dp', 'layer', 'sub'), pairs))  2.16 us
    ppermute x1, starting transfers between devices, per_device(): near_ids = lax.ppermute(ids, 'layer', partners(2, 1))  1.33 us
    dynamic_slice x1, local copies, waits for them, and re-layouts, per_device(): lax.dynamic_slice_in_dim(jnp.transpose(proj_out), lax.axis_index('dp') *...  1.06 us
    ppermute x1, waiting for transfers between devices, per_device(): total = total + lax.ppermute(total, 'sub', partners(2, 1))  0.82 us
    dot_general x1, matrix products, first_side(): lax.dot_general(proj_in, acts[0], (((0,), (1,)), ((), ())), preferred_ele...  0.76 us
  transfers between devices with their start and end apart: 11, of which 6 were waited for; matrix products, arithmetic and copies ran while one was open for 3% of the time, Pallas kernels for 12%

profile of v15, /device:TPU:0, one launch (start us, length us, event | category | flops | bytes accessed | tf_op | source)
XLA Modules:
  0.0 29.5 jit_solution(8472323279830377938)
XLA Ops:
  0.0 0.0 copy-start
  0.0 0.0 copy-start.1
  0.0 0.0 copy-start.2
  0.0 1.1 %dynamic-slice_bitcast_fusion = bf16[64,1024]{1,0:T(8,128)(2,1)S(1)} fusion(bf16[4096,64]{0,1:T(8,128)(2,1)} %param.12, s32[]{:T(128)S(6)} %select_n.7), kind=kLoop, calls=%fused_computation.16 | loop fusion | bytes 262148 | tf_op jit(solution)/shard_map/dynamic_slice | solution.py:278
  1.1 0.6 %copy-done = bf16[1,1024,1024]{2,1,0:T(8,128)(2,1)S(1)} copy-done((bf16[1,1024,1024]{2,1,0:T(8,128)(2,1)S(1)}, bf16[1,1024,1024]{2,1,0:T(8,128)(2,1)}, u32[]{:S(2)}) %copy-start) | copy-done | bytes 2097176
  1.7 0.5 %multiply_convert_fusion.1 = (f16[64,1024]{1,0:T(8,128)(2,1)S(1)}, f32[64,1024]{1,0:T(8,128)S(1)}) fusion(bf16[64,1024]{1,0:T(8,128)(2,1)S(1)} %dynamic-slice_bitcast_fusion, bf16[1,1024,1024]{2,1,0:T(8,128)(2,1)S(1)} %copy-done), kind=kOutput, calls=%fused_computation.15 | convolution fusion | flops 134348800 | bytes 2621440 | tf_op jit(solution)/shard_map/dot_general | solution.py:282
  2.1 0.0 copy-done.1
  2.2 0.5 %collective-permute-start.3 = (bf16[256,256,8]{1,2,0:T(8,128)(2,1)S(1)}, bf16[256,256,8]{1,2,0:T(8,128)(2,1)S(1)}, u32[]{:S(2)}, u32[]{:S(2)}) collective-permute-start(bf16[256,256,8]{1,2,0:T(8,128)(2,1)S(1)} %copy-done.1), channel_id=1, source_target_pairs={{0,1},{1,0},{2,3},{3,2},{4,5},{5,4},{6,7},{7,6},{8,9},{9,8},{10,11... | collective-permute-start | bytes 3145736 | tf_op jit(solution)/shard_map/ppermute | solution.py:294
  2.7 3.7 %collective-permute-start = (f16[64,1024]{1,0:T(8,128)(2,1)S(1)}, f16[64,1024]{1,0:T(8,128)(2,1)S(1)}, u32[]{:S(2)}, u32[]{:S(2)}) collective-permute-start(f16[64,1024]{1,0:T(8,128)(2,1)S(1)} %get-tuple-element.18), channel_id=1, source_target_pairs={{0,8},{1,5},{4,12},{5,1},{8,0},{9,13},{12,4},{13,9},{2,10},{3,7},{... | collective-permute-start | bytes 393224 | tf_op jit(solution)/shard_map/ppermute | solution.py:224
  7.0 0.0 copy-done.2
  7.0 0.2 ids.1.refs_0_
  7.2 0.3 collective-permute-start.2
  7.5 1.3 %collective-permute-start.4 = (bf16[256,256]{1,0:T(8,128)(2,1)S(1)}, bf16[256,256]{1,0:T(8,128)(2,1)S(1)}, u32[]{:S(2)}, u32[]{:S(2)}) collective-permute-start(bf16[256,256]{1,0:T(8,128)(2,1)S(1)} %ids.1.refs_0_), channel_id=1, source_target_pairs={{0,2},{2,0},{1,3},{3,1},{4,6},{6,4},{5,7},{7,5},{8,10},{10,8},{9,1... | collective-permute-start | bytes 393224 | tf_op jit(solution)/shard_map/ppermute | solution.py:292
  8.8 0.7 %collective-permute-done = f16[64,1024]{1,0:T(8,128)(2,1)S(1)} collective-permute-done((f16[64,1024]{1,0:T(8,128)(2,1)S(1)}, f16[64,1024]{1,0:T(8,128)(2,1)S(1)}, u32[]{:S(2)}, u32[]{:S(2)}) %collective-permute-start) | collective-permute-done | bytes 131104 | tf_op jit(solution)/shard_map/ppermute | solution.py:224
  9.5 0.1 multiply_convert_fusion
  9.6 2.7 %collective-permute-start.1 = (f16[64,1024]{1,0:T(8,128)(2,1)S(1)}, f16[64,1024]{1,0:T(8,128)(2,1)S(1)}, u32[]{:S(2)}, u32[]{:S(2)}) collective-permute-start(f16[64,1024]{1,0:T(8,128)(2,1)S(1)} %multiply_convert_fusion), channel_id=1, source_target_pairs={{0,4},{1,9},{4,0},{5,13},{8,12},{9,1},{12,8},{13,5},{2,6},{3,11},{... | collective-permute-start | bytes 393224 | tf_op jit(solution)/shard_map/ppermute | solution.py:224
  12.3 0.0 collective-permute-done.2.refs_0_
  12.3 0.0 collective-permute-done.3
  12.3 1.7 %decode.2.refs_6_ = bf16[2048,256]{1,0:T(8,128)(2,1)S(1)} custom-call(bf16[256,256]{1,0:T(8,128)(2,1)S(1)} %collective-permute-done.2.refs_0_, bf16[256,8,256]{2,1,0:T(8,128)(2,1)S(1)} %bitcast.22), custom_call_target="tpu_custom_call" | custom-call | bytes 2097152 | tf_op jit(solution)/shard_map/decode/pallas_call | solution.py:78
  14.0 0.0 copy-start.4
  14.0 0.5 %collective-permute-done.4.refs_1_ = bf16[256,256]{1,0:T(8,128)(2,1)S(1)} collective-permute-done((bf16[256,256]{1,0:T(8,128)(2,1)S(1)}, bf16[256,256]{1,0:T(8,128)(2,1)S(1)}, u32[]{:S(2)}, u32[]{:S(2)}) %collective-permute-start.4) | collective-permute-done | bytes 131104 | tf_op jit(solution)/shard_map/ppermute | solution.py:292
  14.5 0.0 copy-start.3
  14.5 0.0 copy-start.5
  14.5 1.7 %decode.3.refs_5_ = bf16[2048,256]{1,0:T(8,128)(2,1)S(1)} custom-call(bf16[256,256]{1,0:T(8,128)(2,1)S(1)} %ids.1.refs_0_, bf16[256,256]{1,0:T(8,128)(2,1)S(1)} %collective-permute-done.4.refs_1_, bf16[256,8,256]{2,1,0:T(8,128)(2,1)S(1)} %bitcast.21), custom_call_target="tpu_custom_call" | custom-call | bytes 2097152 | tf_op jit(solution)/shard_map/decode/pallas_call | solution.py:78
  16.2 0.0 collective-permute-done.1
  16.3 0.1 reduce-precision_convert_fusion
  16.4 0.0 copy-done.4
  16.4 0.3 %fusion.4 = f32[128,256]{1,0:T(8,128)S(1)} fusion(bf16[1,256,1024]{2,1,0:T(8,128)(2,1)S(1)} %copy-done.4, bf16[64,1024]{1,0:T(8,128)(2,1)S(1)} %get-tuple-element.32, bf16[64,1024]{1,0:T(8,128)(2,1)S(1)} %get-tuple-element.31), kind=kOutput, calls=%fused_computation.4 | convolution fusion | flops 67633152 | bytes 917504 | tf_op jit(solution)/shard_map/dot_general | solution.py:309
  16.7 0.2 collective-permute-start.5
  16.9 0.0 copy-done.3
  16.9 0.0 copy-done.5
  16.9 0.8 %fusion.in_ref = f32[64,256]{1,0:T(8,128)S(1)} fusion(bf16[4096,64]{0,1:T(8,128)(2,1)S(1)} %copy-done.5, bf16[1,256,4096]{2,1,0:T(8,128)(2,1)S(1)} %copy-done.3), kind=kOutput, calls=%fused_computation | convolution fusion | flops 134217728 | bytes 2686976 | tf_op jit(solution)/shard_map/dot_general | solution.py:297
  17.7 0.4 %collective-permute-done.5.other_ref = f32[64,256]{1,0:T(8,128)S(1)} collective-permute-done((f32[64,256]{1,0:T(8,128)S(1)}, f32[64,256]{1,0:T(8,128)S(1)}, u32[]{:S(2)}, u32[]{:S(2)}) %collective-permute-start.5) | collective-permute-done | bytes 65568 | tf_op jit(solution)/shard_map/ppermute | solution.py:317
  18.0 0.5 %vectors.1.refs_0_ = f32[2,4,2048]{2,1,0:T(4,128)S(1)} custom-call(f32[64,256]{1,0:T(8,128)S(1)} %fusion.in_ref, f32[64,256]{1,0:T(8,128)S(1)} %slice_add_fusion.own_ref, f32[64,256]{1,0:T(8,128)S(1)} %collective-permute-done.5.other_ref), custom_call_target="tpu_custom_call" | custom-call | tf_op jit(solution)/shard_map/vectors/pallas_call | solution.py:184
  18.5 3.4 %collective-permute-start.9 = (f16[2,4,2048]{2,1,0:T(4,128)(2,1)S(1)}, f16[2,4,2048]{2,1,0:T(4,128)(2,1)S(1)}, u32[]{:S(2)}, u32[]{:S(2)}) collective-permute-start(f16[2,4,2048]{2,1,0:T(4,128)(2,1)S(1)} %multiply_convert_fusion.2), channel_id=1, source_target_pairs={{0,12},{1,15},{2,14},{3,13},{4,8},{5,11},{6,10},{7,9},{8,4},{9,7},... | collective-permute-start | bytes 98312 | tf_op jit(solution)/shard_map/ppermute | solution.py:265
  21.9 0.0 collective-permute-start.8
  21.9 1.0 %collective-permute-start.7 = (f16[2,4,2048]{2,1,0:T(4,128)(2,1)S(1)}, f16[2,4,2048]{2,1,0:T(4,128)(2,1)S(1)}, u32[]{:S(2)}, u32[]{:S(2)}) collective-permute-start(f16[2,4,2048]{2,1,0:T(4,128)(2,1)S(1)} %multiply_convert_fusion.2), channel_id=1, source_target_pairs={{0,8},{1,11},{2,10},{3,9},{4,12},{5,15},{6,14},{7,13},{8,0},{9,3},... | collective-permute-start | bytes 98312 | tf_op jit(solution)/shard_map/ppermute | solution.py:265
  23.0 1.8 %collective-permute-start.6 = (f16[2,4,2048]{2,1,0:T(4,128)(2,1)S(1)}, f16[2,4,2048]{2,1,0:T(4,128)(2,1)S(1)}, u32[]{:S(2)}, u32[]{:S(2)}) collective-permute-start(f16[2,4,2048]{2,1,0:T(4,128)(2,1)S(1)} %multiply_convert_fusion.2), channel_id=1, source_target_pairs={{0,2},{1,3},{2,0},{3,1},{4,6},{5,7},{6,4},{7,5},{8,10},{9,11},{10,... | collective-permute-start | bytes 98312 | tf_op jit(solution)/shard_map/ppermute | solution.py:265
  24.8 0.0 collective-permute-done.9
  24.8 1.2 %collective-permute-done.8 = f16[2,4,2048]{2,1,0:T(4,128)(2,1)S(1)} collective-permute-done((f16[2,4,2048]{2,1,0:T(4,128)(2,1)S(1)}, f16[2,4,2048]{2,1,0:T(4,128)(2,1)S(1)}, u32[]{:S(2)}, u32[]{:S(2)}) %collective-permute-start.8) | collective-permute-done | bytes 32800 | tf_op jit(solution)/shard_map/ppermute | solution.py:265
  26.0 0.9 %collective-permute-done.7 = f16[2,4,2048]{2,1,0:T(4,128)(2,1)S(1)} collective-permute-done((f16[2,4,2048]{2,1,0:T(4,128)(2,1)S(1)}, f16[2,4,2048]{2,1,0:T(4,128)(2,1)S(1)}, u32[]{:S(2)}, u32[]{:S(2)}) %collective-permute-start.7) | collective-permute-done | bytes 32800 | tf_op jit(solution)/shard_map/ppermute | solution.py:265
  26.9 0.0 collective-permute-done.6
  27.0 0.5 %score.1 = f32[16,256]{1,0:T(8,128)S(1)} custom-call(f32[2,4,2048]{2,1,0:T(4,128)S(1)} %vectors.1.refs_0_, f32[2,4,2048]{2,1,0:T(4,128)S(1)} %convert_multiply_fusion.3.refs_1_, f32[2,4,2048]{2,1,0:T(4,128)S(1)} %convert_multiply_fusion.2.refs_2_, f32[2,4,2048]{2,1,0:T(4,128)S(1)} %convert_multiply_fusion.1.refs_3_, ...), custom_call_target="tpu_custom_call" | custom-call | tf_op jit(solution)/shard_map/score/pallas_call | solution.py:163
  27.4 0.6 %collective-permute-start.10 = (f32[16,256]{1,0:T(8,128)S(1)}, f32[16,256]{1,0:T(8,128)S(1)}, u32[]{:S(2)}, u32[]{:S(2)}) collective-permute-start(f32[16,256]{1,0:T(8,128)S(1)} %score.1), channel_id=1, source_target_pairs={{0,1},{1,0},{2,3},{3,2},{4,5},{5,4},{6,7},{7,6},{8,9},{9,8},{10,11... | collective-permute-start | bytes 49160 | tf_op jit(solution)/shard_map/ppermute | solution.py:328
  28.0 0.8 %collective-permute-done.10 = f32[16,256]{1,0:T(8,128)S(1)} collective-permute-done((f32[16,256]{1,0:T(8,128)S(1)}, f32[16,256]{1,0:T(8,128)S(1)}, u32[]{:S(2)}, u32[]{:S(2)}) %collective-permute-start.10) | collective-permute-done | bytes 16416 | tf_op jit(solution)/shard_map/ppermute | solution.py:328
  28.9 0.6 %select_bitcast_fusion = f32[256,16]{0,1:T(8,128)} fusion(f32[16,256]{1,0:T(8,128)S(1)} %score.1, f32[16,256]{1,0:T(8,128)S(1)} %collective-permute-done.10, pred[256]{0:T(512)(128)(4,1)S(1)} %compare_reduce_fusion), kind=kLoop, calls=%fused_computation.23 | loop fusion | flops 8192 | bytes 49408 | tf_op jit(solution)/shard_map/transpose | solution.py:333
  (9 shorter events, 0.1 us)
Async XLA Ops:
  0.0 1.7 %copy-start = (bf16[1,1024,1024]{2,1,0:T(8,128)(2,1)S(1)}, bf16[1,1024,1024]{2,1,0:T(8,128)(2,1)}, u32[]{:S(2)}) copy-start(bf16[1,1024,1024]{2,1,0:T(8,128)(2,1)} %param.10) | copy-start | bytes 6291460
  0.0 2.1 %copy-start.1 = (bf16[256,256,8]{1,2,0:T(8,128)(2,1)S(1)}, bf16[256,256,8]{1,2,0:T(8,128)(2,1)}, u32[]{:S(2)}) copy-start(bf16[256,256,8]{1,2,0:T(8,128)(2,1)} %param.13) | copy-start | bytes 3145732
  0.0 7.0 %copy-start.2 = (s32[256,1,256]{2,1,0:T(1,128)S(1)}, s32[256,1,256]{2,1,0:T(1,128)}, u32[]{:S(2)}) copy-start(s32[256,1,256]{2,1,0:T(1,128)} %codes_ref) | copy-start | bytes 786436
  2.2 10.1 %collective-permute-start.3 = (bf16[256,256,8]{1,2,0:T(8,128)(2,1)S(1)}, bf16[256,256,8]{1,2,0:T(8,128)(2,1)S(1)}, u32[]{:S(2)}, u32[]{:S(2)}) collective-permute-start(bf16[256,256,8]{1,2,0:T(8,128)(2,1)S(1)} %copy-done.1), channel_id=1, source_target_pairs={{0,1},{1,0},{2,3},{3,2},{4,5},{5,4},{6,7},{7,6},{8,9},{9,8},{10,11... | collective-permute-start | bytes 3145736 | tf_op jit(solution)/shard_map/ppermute | solution.py:294
  2.7 6.8 %collective-permute-start = (f16[64,1024]{1,0:T(8,128)(2,1)S(1)}, f16[64,1024]{1,0:T(8,128)(2,1)S(1)}, u32[]{:S(2)}, u32[]{:S(2)}) collective-permute-start(f16[64,1024]{1,0:T(8,128)(2,1)S(1)} %get-tuple-element.18), channel_id=1, source_target_pairs={{0,8},{1,5},{4,12},{5,1},{8,0},{9,13},{12,4},{13,9},{2,10},{3,7},{... | collective-permute-start | bytes 393224 | tf_op jit(solution)/shard_map/ppermute | solution.py:224
  7.2 5.1 %collective-permute-start.2 = (bf16[256,256]{1,0:T(8,128)(2,1)S(1)}, bf16[256,256]{1,0:T(8,128)(2,1)S(1)}, u32[]{:S(2)}, u32[]{:S(2)}) collective-permute-start(bf16[256,256]{1,0:T(8,128)(2,1)S(1)} %ids.1.refs_0_), channel_id=1, source_target_pairs={{1,0},{3,2},{2,1},{0,3},{5,4},{7,6},{6,5},{4,7},{9,8},{11,10},{10,... | collective-permute-start | bytes 393224 | tf_op jit(solution)/shard_map/ppermute | solution.py:293
  7.5 7.0 %collective-permute-start.4 = (bf16[256,256]{1,0:T(8,128)(2,1)S(1)}, bf16[256,256]{1,0:T(8,128)(2,1)S(1)}, u32[]{:S(2)}, u32[]{:S(2)}) collective-permute-start(bf16[256,256]{1,0:T(8,128)(2,1)S(1)} %ids.1.refs_0_), channel_id=1, source_target_pairs={{0,2},{2,0},{1,3},{3,1},{4,6},{6,4},{5,7},{7,5},{8,10},{10,8},{9,1... | collective-permute-start | bytes 393224 | tf_op jit(solution)/shard_map/ppermute | solution.py:292
  9.6 6.7 %collective-permute-start.1 = (f16[64,1024]{1,0:T(8,128)(2,1)S(1)}, f16[64,1024]{1,0:T(8,128)(2,1)S(1)}, u32[]{:S(2)}, u32[]{:S(2)}) collective-permute-start(f16[64,1024]{1,0:T(8,128)(2,1)S(1)} %multiply_convert_fusion), channel_id=1, source_target_pairs={{0,4},{1,9},{4,0},{5,13},{8,12},{9,1},{12,8},{13,5},{2,6},{3,11},{... | collective-permute-start | bytes 393224 | tf_op jit(solution)/shard_map/ppermute | solution.py:224
  14.0 2.3 %copy-start.4 = (bf16[1,256,1024]{2,1,0:T(8,128)(2,1)S(1)}, bf16[1,256,1024]{2,1,0:T(8,128)(2,1)}, u32[]{:S(2)}) copy-start(bf16[1,256,1024]{2,1,0:T(8,128)(2,1)} %param.9) | copy-start | bytes 1572868
  14.5 2.4 %copy-start.3 = (bf16[1,256,4096]{2,1,0:T(8,128)(2,1)S(1)}, bf16[1,256,4096]{2,1,0:T(8,128)(2,1)}, u32[]{:S(2)}) copy-start(bf16[1,256,4096]{2,1,0:T(8,128)(2,1)} %param.8) | copy-start | bytes 6291460
  14.5 2.4 %copy-start.5 = (bf16[4096,64]{0,1:T(8,128)(2,1)S(1)}, bf16[4096,64]{0,1:T(8,128)(2,1)}, u32[]{:S(2)}) copy-start(bf16[4096,64]{0,1:T(8,128)(2,1)} %param.11) | copy-start | bytes 1572868
  16.7 1.3 %collective-permute-start.5 = (f32[64,256]{1,0:T(8,128)S(1)}, f32[64,256]{1,0:T(8,128)S(1)}, u32[]{:S(2)}, u32[]{:S(2)}) collective-permute-start(f32[64,256]{1,0:T(8,128)S(1)} %slice_add_fusion.own_ref), channel_id=1, source_target_pairs={{0,1},{1,0},{2,3},{3,2},{4,5},{5,4},{6,7},{7,6},{8,9},{9,8},{10,11... | collective-permute-start | bytes 196616 | tf_op jit(solution)/shard_map/ppermute | solution.py:317
  18.5 6.2 %collective-permute-start.9 = (f16[2,4,2048]{2,1,0:T(4,128)(2,1)S(1)}, f16[2,4,2048]{2,1,0:T(4,128)(2,1)S(1)}, u32[]{:S(2)}, u32[]{:S(2)}) collective-permute-start(f16[2,4,2048]{2,1,0:T(4,128)(2,1)S(1)} %multiply_convert_fusion.2), channel_id=1, source_target_pairs={{0,12},{1,15},{2,14},{3,13},{4,8},{5,11},{6,10},{7,9},{8,4},{9,7},... | collective-permute-start | bytes 98312 | tf_op jit(solution)/shard_map/ppermute | solution.py:265
  21.9 4.1 %collective-permute-start.8 = (f16[2,4,2048]{2,1,0:T(4,128)(2,1)S(1)}, f16[2,4,2048]{2,1,0:T(4,128)(2,1)S(1)}, u32[]{:S(2)}, u32[]{:S(2)}) collective-permute-start(f16[2,4,2048]{2,1,0:T(4,128)(2,1)S(1)} %multiply_convert_fusion.2), channel_id=1, source_target_pairs={{0,4},{1,7},{2,6},{3,5},{4,0},{5,3},{6,2},{7,1},{8,12},{9,15},{10,... | collective-permute-start | bytes 98312 | tf_op jit(solution)/shard_map/ppermute | solution.py:265
  21.9 5.0 %collective-permute-start.7 = (f16[2,4,2048]{2,1,0:T(4,128)(2,1)S(1)}, f16[2,4,2048]{2,1,0:T(4,128)(2,1)S(1)}, u32[]{:S(2)}, u32[]{:S(2)}) collective-permute-start(f16[2,4,2048]{2,1,0:T(4,128)(2,1)S(1)} %multiply_convert_fusion.2), channel_id=1, source_target_pairs={{0,8},{1,11},{2,10},{3,9},{4,12},{5,15},{6,14},{7,13},{8,0},{9,3},... | collective-permute-start | bytes 98312 | tf_op jit(solution)/shard_map/ppermute | solution.py:265
  23.0 4.0 %collective-permute-start.6 = (f16[2,4,2048]{2,1,0:T(4,128)(2,1)S(1)}, f16[2,4,2048]{2,1,0:T(4,128)(2,1)S(1)}, u32[]{:S(2)}, u32[]{:S(2)}) collective-permute-start(f16[2,4,2048]{2,1,0:T(4,128)(2,1)S(1)} %multiply_convert_fusion.2), channel_id=1, source_target_pairs={{0,2},{1,3},{2,0},{3,1},{4,6},{5,7},{6,4},{7,5},{8,10},{9,11},{10,... | collective-permute-start | bytes 98312 | tf_op jit(solution)/shard_map/ppermute | solution.py:265
  27.4 1.4 %collective-permute-start.10 = (f32[16,256]{1,0:T(8,128)S(1)}, f32[16,256]{1,0:T(8,128)S(1)}, u32[]{:S(2)}, u32[]{:S(2)}) collective-permute-start(f32[16,256]{1,0:T(8,128)S(1)} %score.1), channel_id=1, source_target_pairs={{0,1},{1,0},{2,3},{3,2},{4,5},{5,4},{6,7},{7,6},{8,9},{9,8},{10,11... | collective-permute-start | bytes 49160 | tf_op jit(solution)/shard_map/ppermute | solution.py:328

commit v16 on v12

--- a/solution.py
+++ b/solution.py
@@ -11,7 +11,7 @@
 LANES = 128
 LINK_SCALE = 1024.0
 VECTOR_SCALE = 16384.0
-GATHER_ORDER = (2, 1, 0, 3)
+GATHER_ORDER = (1, 2, 0, 3)
 
 
 def ids_kernel(codes_ref, out_ref):

time: 29.7 us -> 29.7 us (level)
  no operation moved by 1% of the time
where the time goes in v16:
time: 29.7 us; the launch traced here: 29.6 us
  starting transfers between devices  15.7 us (53%)
  Pallas kernels  4.58 us (15%)
  waiting for transfers between devices  4.39 us (15%)
  local copies, waits for them, and re-layouts  1.68 us (6%)
  matrix products  1.55 us (5%)
  other arithmetic  0.87 us (3%)
  between operations  0.83 us (3%)
    ppermute x4, starting transfers between devices, gather_by_core(): blocks.append(lax.ppermute(x, ('dp', 'layer', 'sub'), pairs))  6.45 us
    ppermute x2, starting transfers between devices, sum_over_dp(): got = lax.ppermute(sent, ('dp', 'sub'), pairs)  6.38 us
    pallas_call x2, Pallas kernels, decode(): pl.pallas_call(decode_kernel, out_shape=jax.ShapeDtypeStruct((subs * widt...  3.47 us
    ppermute x2, waiting for transfers between devices, sum_over_dp(): got = lax.ppermute(sent, ('dp', 'sub'), pairs)  2.25 us
    ppermute x1, starting transfers between devices, per_device(): near_moved = lax.ppermute(ids, 'layer', partners(2, 1))  1.33 us
    dynamic_slice x1, local copies, waits for them, and re-layouts, per_device(): lax.dynamic_slice_in_dim(jnp.transpose(proj_out), lax.axis_index('dp') *...  1.06 us
    ppermute x1, waiting for transfers between devices, per_device(): total = total + lax.ppermute(total, 'sub', partners(2, 1))  0.82 us
    dot_general x1, matrix products, first_side(): lax.dot_general(proj_in, acts[0], (((0,), (1,)), ((), ())), preferred_ele...  0.76 us
  transfers between devices with their start and end apart: 11, of which 6 were waited for; matrix products, arithmetic and copies ran while one was open for 3% of the time, Pallas kernels for 12%

profile of v16, /device:TPU:0, one launch (start us, length us, event | category | flops | bytes accessed | tf_op | source)
XLA Modules:
  0.0 29.6 jit_solution(90685039229401031)
XLA Ops:
  0.0 0.0 copy-start
  0.0 0.0 copy-start.1
  0.0 0.0 copy-start.2
  0.0 1.1 %dynamic-slice_bitcast_fusion = bf16[64,1024]{1,0:T(8,128)(2,1)S(1)} fusion(bf16[4096,64]{0,1:T(8,128)(2,1)} %param.12, s32[]{:T(128)S(6)} %select_n.7), kind=kLoop, calls=%fused_computation.16 | loop fusion | bytes 262148 | tf_op jit(solution)/shard_map/dynamic_slice | solution.py:278
  1.1 0.6 %copy-done = bf16[1,1024,1024]{2,1,0:T(8,128)(2,1)S(1)} copy-done((bf16[1,1024,1024]{2,1,0:T(8,128)(2,1)S(1)}, bf16[1,1024,1024]{2,1,0:T(8,128)(2,1)}, u32[]{:S(2)}) %copy-start) | copy-done | bytes 2097176
  1.7 0.5 %multiply_convert_fusion.1 = (f16[64,1024]{1,0:T(8,128)(2,1)S(1)}, f32[64,1024]{1,0:T(8,128)S(1)}) fusion(bf16[64,1024]{1,0:T(8,128)(2,1)S(1)} %dynamic-slice_bitcast_fusion, bf16[1,1024,1024]{2,1,0:T(8,128)(2,1)S(1)} %copy-done), kind=kOutput, calls=%fused_computation.15 | convolution fusion | flops 134348800 | bytes 2621440 | tf_op jit(solution)/shard_map/dot_general | solution.py:282
  2.1 0.0 copy-start.4
  2.2 0.0 copy-done.1
  2.2 0.5 %collective-permute-start.3 = (bf16[256,256,8]{1,2,0:T(8,128)(2,1)S(1)}, bf16[256,256,8]{1,2,0:T(8,128)(2,1)S(1)}, u32[]{:S(2)}, u32[]{:S(2)}) collective-permute-start(bf16[256,256,8]{1,2,0:T(8,128)(2,1)S(1)} %copy-done.1), channel_id=1, source_target_pairs={{0,1},{1,0},{2,3},{3,2},{4,5},{5,4},{6,7},{7,6},{8,9},{9,8},{10,11... | collective-permute-start | bytes 3145736 | tf_op jit(solution)/shard_map/ppermute | solution.py:294
  2.7 3.7 %collective-permute-start = (f16[64,1024]{1,0:T(8,128)(2,1)S(1)}, f16[64,1024]{1,0:T(8,128)(2,1)S(1)}, u32[]{:S(2)}, u32[]{:S(2)}) collective-permute-start(f16[64,1024]{1,0:T(8,128)(2,1)S(1)} %get-tuple-element.24), channel_id=1, source_target_pairs={{0,8},{1,5},{4,12},{5,1},{8,0},{9,13},{12,4},{13,9},{2,10},{3,7},{... | collective-permute-start | bytes 393224 | tf_op jit(solution)/shard_map/ppermute | solution.py:224
  7.0 0.0 copy-done.2
  7.0 0.2 ids.1.refs_0_
  7.2 0.3 collective-permute-start.2
  7.5 1.3 %collective-permute-start.4 = (bf16[256,256]{1,0:T(8,128)(2,1)S(1)}, bf16[256,256]{1,0:T(8,128)(2,1)S(1)}, u32[]{:S(2)}, u32[]{:S(2)}) collective-permute-start(bf16[256,256]{1,0:T(8,128)(2,1)S(1)} %ids.1.refs_0_), channel_id=1, source_target_pairs={{0,2},{2,0},{1,3},{3,1},{4,6},{6,4},{5,7},{7,5},{8,10},{10,8},{9,1... | collective-permute-start | bytes 393224 | tf_op jit(solution)/shard_map/ppermute | solution.py:292
  8.8 0.7 %collective-permute-done = f16[64,1024]{1,0:T(8,128)(2,1)S(1)} collective-permute-done((f16[64,1024]{1,0:T(8,128)(2,1)S(1)}, f16[64,1024]{1,0:T(8,128)(2,1)S(1)}, u32[]{:S(2)}, u32[]{:S(2)}) %collective-permute-start) | collective-permute-done | bytes 131104 | tf_op jit(solution)/shard_map/ppermute | solution.py:224
  9.5 0.1 multiply_convert_fusion
  9.6 0.0 copy-start.3
  9.6 0.0 copy-start.5
  9.6 2.7 %collective-permute-start.1 = (f16[64,1024]{1,0:T(8,128)(2,1)S(1)}, f16[64,1024]{1,0:T(8,128)(2,1)S(1)}, u32[]{:S(2)}, u32[]{:S(2)}) collective-permute-start(f16[64,1024]{1,0:T(8,128)(2,1)S(1)} %multiply_convert_fusion), channel_id=1, source_target_pairs={{0,4},{1,9},{4,0},{5,13},{8,12},{9,1},{12,8},{13,5},{2,6},{3,11},{... | collective-permute-start | bytes 393224 | tf_op jit(solution)/shard_map/ppermute | solution.py:224
  12.3 0.0 collective-permute-done.2.refs_0_
  12.3 0.0 collective-permute-done.3
  12.3 1.7 %decode.2.refs_6_ = bf16[2048,256]{1,0:T(8,128)(2,1)S(1)} custom-call(bf16[256,256]{1,0:T(8,128)(2,1)S(1)} %collective-permute-done.2.refs_0_, bf16[256,8,256]{2,1,0:T(8,128)(2,1)S(1)} %bitcast.22), custom_call_target="tpu_custom_call" | custom-call | bytes 2097152 | tf_op jit(solution)/shard_map/decode/pallas_call | solution.py:78
  14.1 0.4 %collective-permute-done.4.refs_1_ = bf16[256,256]{1,0:T(8,128)(2,1)S(1)} collective-permute-done((bf16[256,256]{1,0:T(8,128)(2,1)S(1)}, bf16[256,256]{1,0:T(8,128)(2,1)S(1)}, u32[]{:S(2)}, u32[]{:S(2)}) %collective-permute-start.4) | collective-permute-done | bytes 131104 | tf_op jit(solution)/shard_map/ppermute | solution.py:292
  14.5 1.6 %collective-permute-done.1 = f16[64,1024]{1,0:T(8,128)(2,1)S(1)} collective-permute-done((f16[64,1024]{1,0:T(8,128)(2,1)S(1)}, f16[64,1024]{1,0:T(8,128)(2,1)S(1)}, u32[]{:S(2)}, u32[]{:S(2)}) %collective-permute-start.1) | collective-permute-done | bytes 131104 | tf_op jit(solution)/shard_map/ppermute | solution.py:224
  16.1 0.1 reduce-precision_convert_fusion
  16.2 0.0 copy-done.4
  16.2 0.3 %fusion.4 = f32[128,256]{1,0:T(8,128)S(1)} fusion(bf16[1,256,1024]{2,1,0:T(8,128)(2,1)S(1)} %copy-done.4, bf16[64,1024]{1,0:T(8,128)(2,1)S(1)} %get-tuple-element.44, bf16[64,1024]{1,0:T(8,128)(2,1)S(1)} %get-tuple-element.43), kind=kOutput, calls=%fused_computation.4 | convolution fusion | flops 67633152 | bytes 917504 | tf_op jit(solution)/shard_map/dot_general | solution.py:307
  16.5 0.1 collective-permute-start.5
  16.6 0.0 copy-done.3
  16.6 0.0 copy-done.5
  16.6 0.8 %fusion.in_ref = f32[64,256]{1,0:T(8,128)S(1)} fusion(bf16[4096,64]{0,1:T(8,128)(2,1)S(1)} %copy-done.5, bf16[1,256,4096]{2,1,0:T(8,128)(2,1)S(1)} %copy-done.3), kind=kOutput, calls=%fused_computation | convolution fusion | flops 134217728 | bytes 2686976 | tf_op jit(solution)/shard_map/dot_general | solution.py:297
  17.4 0.5 %collective-permute-done.5.other_ref = f32[64,256]{1,0:T(8,128)S(1)} collective-permute-done((f32[64,256]{1,0:T(8,128)S(1)}, f32[64,256]{1,0:T(8,128)S(1)}, u32[]{:S(2)}, u32[]{:S(2)}) %collective-permute-start.5) | collective-permute-done | bytes 65568 | tf_op jit(solution)/shard_map/ppermute | solution.py:315
  17.8 0.5 %vectors.1.refs_0_ = f32[2,4,2048]{2,1,0:T(4,128)S(1)} custom-call(f32[64,256]{1,0:T(8,128)S(1)} %fusion.in_ref, f32[64,256]{1,0:T(8,128)S(1)} %slice_add_fusion.own_ref, f32[64,256]{1,0:T(8,128)S(1)} %collective-permute-done.5.other_ref), custom_call_target="tpu_custom_call" | custom-call | tf_op jit(solution)/shard_map/vectors/pallas_call | solution.py:184
  18.3 3.6 %collective-permute-start.9 = (f16[2,4,2048]{2,1,0:T(4,128)(2,1)S(1)}, f16[2,4,2048]{2,1,0:T(4,128)(2,1)S(1)}, u32[]{:S(2)}, u32[]{:S(2)}) collective-permute-start(f16[2,4,2048]{2,1,0:T(4,128)(2,1)S(1)} %multiply_convert_fusion.2), channel_id=1, source_target_pairs={{0,12},{1,15},{2,14},{3,13},{4,8},{5,11},{6,10},{7,9},{8,4},{9,7},... | collective-permute-start | bytes 98312 | tf_op jit(solution)/shard_map/ppermute | solution.py:265
  22.0 0.0 collective-permute-start.6
  22.0 0.8 %collective-permute-start.7 = (f16[2,4,2048]{2,1,0:T(4,128)(2,1)S(1)}, f16[2,4,2048]{2,1,0:T(4,128)(2,1)S(1)}, u32[]{:S(2)}, u32[]{:S(2)}) collective-permute-start(f16[2,4,2048]{2,1,0:T(4,128)(2,1)S(1)} %multiply_convert_fusion.2), channel_id=1, source_target_pairs={{0,8},{1,11},{2,10},{3,9},{4,12},{5,15},{6,14},{7,13},{8,0},{9,3},... | collective-permute-start | bytes 98312 | tf_op jit(solution)/shard_map/ppermute | solution.py:265
  22.8 2.0 %collective-permute-start.8 = (f16[2,4,2048]{2,1,0:T(4,128)(2,1)S(1)}, f16[2,4,2048]{2,1,0:T(4,128)(2,1)S(1)}, u32[]{:S(2)}, u32[]{:S(2)}) collective-permute-start(f16[2,4,2048]{2,1,0:T(4,128)(2,1)S(1)} %multiply_convert_fusion.2), channel_id=1, source_target_pairs={{0,2},{1,3},{2,0},{3,1},{4,6},{5,7},{6,4},{7,5},{8,10},{9,11},{10,... | collective-permute-start | bytes 98312 | tf_op jit(solution)/shard_map/ppermute | solution.py:265
  24.8 0.0 collective-permute-done.9
  24.8 1.7 %decode.3.refs_5_ = bf16[2048,256]{1,0:T(8,128)(2,1)S(1)} custom-call(bf16[256,256]{1,0:T(8,128)(2,1)S(1)} %ids.1.refs_0_, bf16[256,256]{1,0:T(8,128)(2,1)S(1)} %collective-permute-done.4.refs_1_, bf16[256,8,256]{2,1,0:T(8,128)(2,1)S(1)} %bitcast.21), custom_call_target="tpu_custom_call" | custom-call | bytes 2097152 | tf_op jit(solution)/shard_map/decode/pallas_call | solution.py:78
  26.5 0.0 collective-permute-done.6
  26.5 0.4 %collective-permute-done.7 = f16[2,4,2048]{2,1,0:T(4,128)(2,1)S(1)} collective-permute-done((f16[2,4,2048]{2,1,0:T(4,128)(2,1)S(1)}, f16[2,4,2048]{2,1,0:T(4,128)(2,1)S(1)}, u32[]{:S(2)}, u32[]{:S(2)}) %collective-permute-start.7) | collective-permute-done | bytes 32800 | tf_op jit(solution)/shard_map/ppermute | solution.py:265
  26.9 0.0 collective-permute-done.8
  27.0 0.5 %score.1 = f32[16,256]{1,0:T(8,128)S(1)} custom-call(f32[2,4,2048]{2,1,0:T(4,128)S(1)} %vectors.1.refs_0_, f32[2,4,2048]{2,1,0:T(4,128)S(1)} %get-tuple-element.50.refs_1_, f32[2,4,2048]{2,1,0:T(4,128)S(1)} %get-tuple-element.49.refs_2_, f32[2,4,2048]{2,1,0:T(4,128)S(1)} %get-tuple-element.48.refs_3_, f32[2,4,2048]{2,1,0:T(4,128)S(1)} %get-tuple-element.47.refs_4_, ...), custom_call_target="tpu_custom_call" | custom-call | tf_op jit(solution)/shard_map/score/pallas_call | solution.py:163
  27.5 0.6 %collective-permute-start.10 = (f32[16,256]{1,0:T(8,128)S(1)}, f32[16,256]{1,0:T(8,128)S(1)}, u32[]{:S(2)}, u32[]{:S(2)}) collective-permute-start(f32[16,256]{1,0:T(8,128)S(1)} %score.1), channel_id=1, source_target_pairs={{0,1},{1,0},{2,3},{3,2},{4,5},{5,4},{6,7},{7,6},{8,9},{9,8},{10,11... | collective-permute-start | bytes 49160 | tf_op jit(solution)/shard_map/ppermute | solution.py:328
  28.1 0.8 %collective-permute-done.10 = f32[16,256]{1,0:T(8,128)S(1)} collective-permute-done((f32[16,256]{1,0:T(8,128)S(1)}, f32[16,256]{1,0:T(8,128)S(1)}, u32[]{:S(2)}, u32[]{:S(2)}) %collective-permute-start.10) | collective-permute-done | bytes 16416 | tf_op jit(solution)/shard_map/ppermute | solution.py:328
  29.0 0.6 %select_bitcast_fusion = f32[256,16]{0,1:T(8,128)} fusion(f32[16,256]{1,0:T(8,128)S(1)} %score.1, f32[16,256]{1,0:T(8,128)S(1)} %collective-permute-done.10, pred[256]{0:T(512)(128)(4,1)S(1)} %compare_reduce_fusion), kind=kLoop, calls=%fused_computation.23 | loop fusion | flops 8192 | bytes 49408 | tf_op jit(solution)/shard_map/transpose | solution.py:333
  (7 shorter events, 0.1 us)
Async XLA Ops:
  0.0 1.7 %copy-start = (bf16[1,1024,1024]{2,1,0:T(8,128)(2,1)S(1)}, bf16[1,1024,1024]{2,1,0:T(8,128)(2,1)}, u32[]{:S(2)}) copy-start(bf16[1,1024,1024]{2,1,0:T(8,128)(2,1)} %param.10) | copy-start | bytes 6291460
  0.0 2.2 %copy-start.1 = (bf16[256,256,8]{1,2,0:T(8,128)(2,1)S(1)}, bf16[256,256,8]{1,2,0:T(8,128)(2,1)}, u32[]{:S(2)}) copy-start(bf16[256,256,8]{1,2,0:T(8,128)(2,1)} %param.13) | copy-start | bytes 3145732
  0.0 7.0 %copy-start.2 = (s32[256,1,256]{2,1,0:T(1,128)S(1)}, s32[256,1,256]{2,1,0:T(1,128)}, u32[]{:S(2)}) copy-start(s32[256,1,256]{2,1,0:T(1,128)} %codes_ref) | copy-start | bytes 786436
  2.1 14.0 %copy-start.4 = (bf16[1,256,1024]{2,1,0:T(8,128)(2,1)S(1)}, bf16[1,256,1024]{2,1,0:T(8,128)(2,1)}, u32[]{:S(2)}) copy-start(bf16[1,256,1024]{2,1,0:T(8,128)(2,1)} %param.9) | copy-start | bytes 1572868
  2.2 10.2 %collective-permute-start.3 = (bf16[256,256,8]{1,2,0:T(8,128)(2,1)S(1)}, bf16[256,256,8]{1,2,0:T(8,128)(2,1)S(1)}, u32[]{:S(2)}, u32[]{:S(2)}) collective-permute-start(bf16[256,256,8]{1,2,0:T(8,128)(2,1)S(1)} %copy-done.1), channel_id=1, source_target_pairs={{0,1},{1,0},{2,3},{3,2},{4,5},{5,4},{6,7},{7,6},{8,9},{9,8},{10,11... | collective-permute-start | bytes 3145736 | tf_op jit(solution)/shard_map/ppermute | solution.py:294
  2.7 6.8 %collective-permute-start = (f16[64,1024]{1,0:T(8,128)(2,1)S(1)}, f16[64,1024]{1,0:T(8,128)(2,1)S(1)}, u32[]{:S(2)}, u32[]{:S(2)}) collective-permute-start(f16[64,1024]{1,0:T(8,128)(2,1)S(1)} %get-tuple-element.24), channel_id=1, source_target_pairs={{0,8},{1,5},{4,12},{5,1},{8,0},{9,13},{12,4},{13,9},{2,10},{3,7},{... | collective-permute-start | bytes 393224 | tf_op jit(solution)/shard_map/ppermute | solution.py:224
  7.2 5.1 %collective-permute-start.2 = (bf16[256,256]{1,0:T(8,128)(2,1)S(1)}, bf16[256,256]{1,0:T(8,128)(2,1)S(1)}, u32[]{:S(2)}, u32[]{:S(2)}) collective-permute-start(bf16[256,256]{1,0:T(8,128)(2,1)S(1)} %ids.1.refs_0_), channel_id=1, source_target_pairs={{1,0},{3,2},{2,1},{0,3},{5,4},{7,6},{6,5},{4,7},{9,8},{11,10},{10,... | collective-permute-start | bytes 393224 | tf_op jit(solution)/shard_map/ppermute | solution.py:293
  7.5 7.0 %collective-permute-start.4 = (bf16[256,256]{1,0:T(8,128)(2,1)S(1)}, bf16[256,256]{1,0:T(8,128)(2,1)S(1)}, u32[]{:S(2)}, u32[]{:S(2)}) collective-permute-start(bf16[256,256]{1,0:T(8,128)(2,1)S(1)} %ids.1.refs_0_), channel_id=1, source_target_pairs={{0,2},{2,0},{1,3},{3,1},{4,6},{6,4},{5,7},{7,5},{8,10},{10,8},{9,1... | collective-permute-start | bytes 393224 | tf_op jit(solution)/shard_map/ppermute | solution.py:292
  9.6 7.0 %copy-start.3 = (bf16[1,256,4096]{2,1,0:T(8,128)(2,1)S(1)}, bf16[1,256,4096]{2,1,0:T(8,128)(2,1)}, u32[]{:S(2)}) copy-start(bf16[1,256,4096]{2,1,0:T(8,128)(2,1)} %param.8) | copy-start | bytes 6291460
  9.6 7.0 %copy-start.5 = (bf16[4096,64]{0,1:T(8,128)(2,1)S(1)}, bf16[4096,64]{0,1:T(8,128)(2,1)}, u32[]{:S(2)}) copy-start(bf16[4096,64]{0,1:T(8,128)(2,1)} %param.11) | copy-start | bytes 1572868
  9.6 6.5 %collective-permute-start.1 = (f16[64,1024]{1,0:T(8,128)(2,1)S(1)}, f16[64,1024]{1,0:T(8,128)(2,1)S(1)}, u32[]{:S(2)}, u32[]{:S(2)}) collective-permute-start(f16[64,1024]{1,0:T(8,128)(2,1)S(1)} %multiply_convert_fusion), channel_id=1, source_target_pairs={{0,4},{1,9},{4,0},{5,13},{8,12},{9,1},{12,8},{13,5},{2,6},{3,11},{... | collective-permute-start | bytes 393224 | tf_op jit(solution)/shard_map/ppermute | solution.py:224
  16.5 1.3 %collective-permute-start.5 = (f32[64,256]{1,0:T(8,128)S(1)}, f32[64,256]{1,0:T(8,128)S(1)}, u32[]{:S(2)}, u32[]{:S(2)}) collective-permute-start(f32[64,256]{1,0:T(8,128)S(1)} %slice_add_fusion.own_ref), channel_id=1, source_target_pairs={{0,1},{1,0},{2,3},{3,2},{4,5},{5,4},{6,7},{7,6},{8,9},{9,8},{10,11... | collective-permute-start | bytes 196616 | tf_op jit(solution)/shard_map/ppermute | solution.py:315
  18.3 6.5 %collective-permute-start.9 = (f16[2,4,2048]{2,1,0:T(4,128)(2,1)S(1)}, f16[2,4,2048]{2,1,0:T(4,128)(2,1)S(1)}, u32[]{:S(2)}, u32[]{:S(2)}) collective-permute-start(f16[2,4,2048]{2,1,0:T(4,128)(2,1)S(1)} %multiply_convert_fusion.2), channel_id=1, source_target_pairs={{0,12},{1,15},{2,14},{3,13},{4,8},{5,11},{6,10},{7,9},{8,4},{9,7},... | collective-permute-start | bytes 98312 | tf_op jit(solution)/shard_map/ppermute | solution.py:265
  22.0 4.6 %collective-permute-start.6 = (f16[2,4,2048]{2,1,0:T(4,128)(2,1)S(1)}, f16[2,4,2048]{2,1,0:T(4,128)(2,1)S(1)}, u32[]{:S(2)}, u32[]{:S(2)}) collective-permute-start(f16[2,4,2048]{2,1,0:T(4,128)(2,1)S(1)} %multiply_convert_fusion.2), channel_id=1, source_target_pairs={{0,4},{1,7},{2,6},{3,5},{4,0},{5,3},{6,2},{7,1},{8,12},{9,15},{10,... | collective-permute-start | bytes 98312 | tf_op jit(solution)/shard_map/ppermute | solution.py:265
  22.0 5.0 %collective-permute-start.7 = (f16[2,4,2048]{2,1,0:T(4,128)(2,1)S(1)}, f16[2,4,2048]{2,1,0:T(4,128)(2,1)S(1)}, u32[]{:S(2)}, u32[]{:S(2)}) collective-permute-start(f16[2,4,2048]{2,1,0:T(4,128)(2,1)S(1)} %multiply_convert_fusion.2), channel_id=1, source_target_pairs={{0,8},{1,11},{2,10},{3,9},{4,12},{5,15},{6,14},{7,13},{8,0},{9,3},... | collective-permute-start | bytes 98312 | tf_op jit(solution)/shard_map/ppermute | solution.py:265
  22.8 4.2 %collective-permute-start.8 = (f16[2,4,2048]{2,1,0:T(4,128)(2,1)S(1)}, f16[2,4,2048]{2,1,0:T(4,128)(2,1)S(1)}, u32[]{:S(2)}, u32[]{:S(2)}) collective-permute-start(f16[2,4,2048]{2,1,0:T(4,128)(2,1)S(1)} %multiply_convert_fusion.2), channel_id=1, source_target_pairs={{0,2},{1,3},{2,0},{3,1},{4,6},{5,7},{6,4},{7,5},{8,10},{9,11},{10,... | collective-permute-start | bytes 98312 | tf_op jit(solution)/shard_map/ppermute | solution.py:265
  27.5 1.5 %collective-permute-start.10 = (f32[16,256]{1,0:T(8,128)S(1)}, f32[16,256]{1,0:T(8,128)S(1)}, u32[]{:S(2)}, u32[]{:S(2)}) collective-permute-start(f32[16,256]{1,0:T(8,128)S(1)} %score.1), channel_id=1, source_target_pairs={{0,1},{1,0},{2,3},{3,2},{4,5},{5,4},{6,7},{7,6},{8,9},{9,8},{10,11... | collective-permute-start | bytes 49160 | tf_op jit(solution)/shard_map/ppermute | solution.py:328
